TPU v7x, 32 devices: a whole 2x2x4 slice. The times are simulated.
32 devices in a mesh: dp: 8 (over z, core), tensor: 4 (over y, x).
Axes of the slice: x: 2, y: 2, z: 4, core: 2. Of those that a mesh axis runs over, the one named last changes fastest.
Arguments:
- layer_input: bfloat16 [16, 1024, 2048], P('dp', 'tensor'), may hold values from -6 to 6
- segments: int32 [16, 1024], P('dp'), may hold values from 0 to 4, as said below
- query_key_value_weight: bfloat16 [3, 2048, 2048], P(None, 'dp', 'tensor'), may hold values from -0.125 to 0.125
- output_weight: bfloat16 [2048, 2048], P('tensor', 'dp'), may hold values from -0.5 to 0.5
- norm1_gain: bfloat16 [2048], P('dp'), may hold values from 0.25 to 1.75
- gate_up_weight: bfloat16 [2, 2048, 8192], P(None, 'dp', 'tensor'), may hold values from -0.125 to 0.125
- down_weight: bfloat16 [8192, 2048], P('tensor', 'dp'), may hold values from -0.125 to 0.125
- norm2_gain: bfloat16 [2048], P('dp'), may hold values from 0.25 to 1.75
- grad_out: bfloat16 [16, 1024, 2048], P('dp', 'tensor'), may hold values from -6 to 6
Outputs:
- layer_out: bfloat16 [16, 1024, 2048], P('dp', 'tensor')
- grad_input: bfloat16 [16, 1024, 2048], P('dp', 'tensor')
- grad_qkv: float32 [3, 2048, 2048], P(None, 'dp', 'tensor')
- grad_wout: float32 [2048, 2048], P('tensor', 'dp')
- grad_gain1: float32 [2048], P('dp')
- grad_gateup: float32 [2, 2048, 8192], P(None, 'dp', 'tensor')
- grad_wdown: float32 [8192, 2048], P('tensor', 'dp')
- grad_gain2: float32 [2048], P('dp')
Inputs may be any that keep to these rules, and one draw needn't show every extreme that they name: `segments`: in every row the ids start at 0 and never fall; in every row one segment covers positions 64 to 959.
All inputs are finite; a program needn't handle non-finite values.
Results may differ from a plain program's by a relative error of at most 0.025.
Values may be sent and summed in bfloat16 or wider, within the bound.
A program may use at most 320 MiB of HBM per device.

v0:
```python
import jax
import jax.numpy as jnp
from jax import lax
from jax.sharding import PartitionSpec as P

HEAD_DIM = 64


NORM_EPS = 1e-05
ROPE_BASE = 130000.0
MASKED_SCORE = -1e30


def positions(segments):
    row_len = segments.shape[-1]
    position_ids = jnp.arange(row_len, dtype=jnp.int32)
    change = jnp.concatenate(
        [jnp.ones_like(segments[:, :1]), (segments[:, 1:] != segments[:, :-1]).astype(jnp.int32)],
        axis=1,
    )
    doc_start = lax.cummax(jnp.where(change > 0, position_ids[None, :], 0), axis=1)
    return position_ids[None, :] - doc_start


def rotary(segments):
    doc_pos = positions(segments).astype(jnp.float32)
    half_dim = HEAD_DIM // 2
    inv_freq = ROPE_BASE ** (-jnp.arange(half_dim, dtype=jnp.float32) * 2.0 / HEAD_DIM)
    angles = doc_pos[..., None] * inv_freq
    cos_table = jnp.concatenate([jnp.cos(angles), jnp.cos(angles)], axis=-1)
    sin_table = jnp.concatenate([jnp.sin(angles), jnp.sin(angles)], axis=-1)
    return (cos_table[:, :, None, :], sin_table[:, :, None, :])


def rotate(vectors, cos_table, sin_table):
    half_dim = vectors.shape[-1] // 2
    turned = jnp.concatenate([-vectors[..., half_dim:], vectors[..., :half_dim]], axis=-1)
    return vectors * cos_table + turned * sin_table


def unrotate(upstream_grad, cos_table, sin_table):
    half_dim = upstream_grad.shape[-1] // 2
    turned = upstream_grad * sin_table
    return upstream_grad * cos_table + jnp.concatenate(
        [turned[..., half_dim:], -turned[..., :half_dim]], axis=-1
    )


def rms_norm(vectors, gain_vec):
    return (
        vectors
        * lax.rsqrt(jnp.mean(vectors * vectors, axis=-1, keepdims=True) + NORM_EPS)
        * gain_vec
    )


def block_mask(segments, seq_id, row_start, block_rows):
    all_seg = lax.dynamic_index_in_dim(segments, seq_id, 0, False)
    row_seg = lax.dynamic_slice_in_dim(all_seg, row_start, block_rows, 0)
    row_ids = row_start + jnp.arange(block_rows, dtype=jnp.int32)
    col_ids = jnp.arange(all_seg.shape[0], dtype=jnp.int32)
    return (row_seg[:, None] == all_seg[None, :]) & (row_ids[:, None] >= col_ids[None, :])


def block_scores(queries, key_rows, segments, block_index, blocks, block_rows):
    seq_id = block_index // blocks
    row_start = block_index % blocks * block_rows
    query_block = lax.dynamic_slice_in_dim(
        lax.dynamic_index_in_dim(queries, seq_id, 0, False), row_start, block_rows, 0
    )
    key_seq = lax.dynamic_index_in_dim(key_rows, seq_id, 0, False)
    score_scale = queries.shape[-1] ** (-0.5)
    allowed = block_mask(segments, seq_id, row_start, block_rows)
    raw_scores = (
        jnp.einsum("qhe,khe->hqk", query_block, key_seq, preferred_element_type=jnp.float32)
        * score_scale
    )
    return (
        jnp.where(allowed[None], raw_scores, MASKED_SCORE),
        query_block,
        key_seq,
        seq_id,
        row_start,
    )


def attention_forward(queries, key_rows, values, segments):
    seq_count, seq_len, head_count, head_size = queries.shape
    block_rows = min(512, seq_len)
    blocks = seq_len // block_rows

    def one_block(block_index):
        scores, query_block, key_seq, seq_id, row_start = block_scores(
            queries, key_rows, segments, block_index, blocks, block_rows
        )
        value_seq = lax.dynamic_index_in_dim(values, seq_id, 0, False)
        row_top = jnp.max(scores, axis=-1, keepdims=True)
        exp_scores = jnp.exp(scores - row_top)
        row_total = jnp.sum(exp_scores, axis=-1, keepdims=True)
        attn_probs = (exp_scores / row_total).astype(jnp.bfloat16)
        attended_context = jnp.einsum(
            "hqk,khe->qhe", attn_probs, value_seq, preferred_element_type=jnp.float32
        ).astype(jnp.bfloat16)
        return (attended_context, (row_top + jnp.log(row_total))[..., 0])

    attended_context, log_totals = lax.map(
        one_block, jnp.arange(seq_count * blocks, dtype=jnp.int32)
    )
    return (attended_context.reshape(seq_count, seq_len, head_count * head_size), log_totals)


def attention_backward(queries, key_rows, values, segments, grad_context, log_totals):
    seq_count, seq_len, head_count, head_size = queries.shape
    block_rows = min(512, seq_len)
    blocks = seq_len // block_rows
    score_scale = head_size ** (-0.5)

    def one_block(running, block_index):
        grad_keys, grad_values = running
        scores, query_block, key_seq, seq_id, row_start = block_scores(
            queries, key_rows, segments, block_index, blocks, block_rows
        )
        value_seq = lax.dynamic_index_in_dim(values, seq_id, 0, False)
        grad_block = lax.dynamic_slice_in_dim(
            lax.dynamic_index_in_dim(grad_context, seq_id, 0, False), row_start, block_rows, 0
        )
        row_lse = lax.dynamic_index_in_dim(log_totals, block_index, 0, False)
        attn_probs = jnp.exp(scores - row_lse[:, :, None])
        grad_probs = jnp.einsum(
            "qhe,khe->hqk", grad_block, value_seq, preferred_element_type=jnp.float32
        )
        row_inner = jnp.sum(attn_probs * grad_probs, axis=-1, keepdims=True)
        grad_scores = (attn_probs * (grad_probs - row_inner)).astype(jnp.bfloat16)
        grad_query = (
            jnp.einsum("hqk,khe->qhe", grad_scores, key_seq, preferred_element_type=jnp.float32)
            * score_scale
        )
        key_part = (
            jnp.einsum("hqk,qhe->khe", grad_scores, query_block, preferred_element_type=jnp.float32)
            * score_scale
        )
        value_part = jnp.einsum(
            "hqk,qhe->khe",
            attn_probs.astype(jnp.bfloat16),
            grad_block,
            preferred_element_type=jnp.float32,
        )
        grad_keys = lax.dynamic_update_index_in_dim(
            grad_keys, lax.dynamic_index_in_dim(grad_keys, seq_id, 0, False) + key_part, seq_id, 0
        )
        grad_values = lax.dynamic_update_index_in_dim(
            grad_values,
            lax.dynamic_index_in_dim(grad_values, seq_id, 0, False) + value_part,
            seq_id,
            0,
        )
        return ((grad_keys, grad_values), grad_query)

    zero_grads = jnp.zeros(queries.shape, jnp.float32)
    (grad_keys, grad_values), grad_queries = lax.scan(
        one_block, (zero_grads, zero_grads), jnp.arange(seq_count * blocks, dtype=jnp.int32)
    )
    return (grad_queries.reshape(seq_count, seq_len, head_count, head_size), grad_keys, grad_values)


def per_device(
    layer_input,
    segments,
    query_key_value_weight,
    output_weight,
    norm1_gain,
    gate_up_weight,
    down_weight,
    norm2_gain,
    grad_out,
):
    full_qkv, full_out, full_gateup, full_down, gain_one, gain_two = (
        lax.all_gather(query_key_value_weight, "dp", axis=1, tiled=True),
        lax.all_gather(output_weight, "dp", axis=1, tiled=True),
        lax.all_gather(gate_up_weight, "dp", axis=1, tiled=True),
        lax.all_gather(down_weight, "dp", axis=1, tiled=True),
        lax.all_gather(norm1_gain, "dp", axis=0, tiled=True),
        lax.all_gather(norm2_gain, "dp", axis=0, tiled=True),
    )
    gain_one = gain_one.astype(jnp.float32)
    gain_two = gain_two.astype(jnp.float32)
    seq_count, local_len, model_width = layer_input.shape
    head_cols = full_qkv.shape[2]
    head_count = head_cols // HEAD_DIM
    cos_table, sin_table = rotary(segments)
    input_tokens = layer_input.astype(jnp.float32)
    low_one = rms_norm(input_tokens, gain_one).astype(jnp.bfloat16)
    flat_one = lax.all_gather(low_one, "tensor", axis=1, tiled=True).reshape(-1, model_width)
    seq_len = flat_one.shape[0] // seq_count
    projected_output = jnp.einsum(
        "td,cde->cte", flat_one, full_qkv, preferred_element_type=jnp.float32
    )
    split_heads = projected_output.reshape(3, seq_count, seq_len, head_count, HEAD_DIM)
    queries = rotate(split_heads[0], cos_table, sin_table).astype(jnp.bfloat16)
    key_rows = rotate(split_heads[1], cos_table, sin_table).astype(jnp.bfloat16)
    values = split_heads[2].astype(jnp.bfloat16)
    attended_context, log_totals = attention_forward(queries, key_rows, values, segments)
    context_flat = attended_context.reshape(seq_count * seq_len, head_cols)
    partial_one = jnp.dot(context_flat, full_out, preferred_element_type=jnp.float32).reshape(
        seq_count, seq_len, model_width
    )
    middle_state = input_tokens + lax.psum_scatter(
        partial_one.astype(jnp.bfloat16), "tensor", scatter_dimension=1, tiled=True
    ).astype(jnp.float32)
    low_two = rms_norm(middle_state, gain_two).astype(jnp.bfloat16)
    flat_two = lax.all_gather(low_two, "tensor", axis=1, tiled=True).reshape(-1, model_width)
    gate_up_output = jnp.einsum(
        "td,cdf->ctf", flat_two, full_gateup, preferred_element_type=jnp.float32
    )
    hidden_state = (jax.nn.silu(gate_up_output[0]) * gate_up_output[1]).astype(jnp.bfloat16)
    partial_two = jnp.dot(hidden_state, full_down, preferred_element_type=jnp.float32).reshape(
        seq_count, seq_len, model_width
    )
    layer_out = (
        middle_state
        + lax.psum_scatter(
            partial_two.astype(jnp.bfloat16), "tensor", scatter_dimension=1, tiled=True
        ).astype(jnp.float32)
    ).astype(jnp.bfloat16)
    grad_full = lax.all_gather(grad_out, "tensor", axis=1, tiled=True).reshape(-1, model_width)
    grad_hidden = jnp.einsum("td,fd->tf", grad_full, full_down, preferred_element_type=jnp.float32)
    grad_down = jnp.einsum("tf,td->fd", hidden_state, grad_full, preferred_element_type=jnp.float32)
    gate_part = gate_up_output[0]
    gate_sigmoid = jax.nn.sigmoid(gate_part)
    grad_gate = (
        grad_hidden * gate_up_output[1] * gate_sigmoid * (1.0 + gate_part * (1.0 - gate_sigmoid))
    )
    grad_up = grad_hidden * gate_part * gate_sigmoid
    grad_pair = jnp.stack([grad_gate, grad_up]).astype(jnp.bfloat16)
    grad_gateup = jnp.einsum("td,ctf->cdf", flat_two, grad_pair, preferred_element_type=jnp.float32)
    partial_back_two = jnp.einsum(
        "ctf,cdf->td", grad_pair, full_gateup, preferred_element_type=jnp.float32
    ).reshape(seq_count, seq_len, model_width)
    grad_normed_two = lax.psum_scatter(
        partial_back_two.astype(jnp.bfloat16), "tensor", scatter_dimension=1, tiled=True
    ).astype(jnp.float32)
    norm_value, norm_pull = jax.vjp(rms_norm, middle_state, gain_two)
    grad_mid_norm, gain_two_part = norm_pull(grad_normed_two)
    grad_middle = grad_out.astype(jnp.float32) + grad_mid_norm
    grad_mid_full = lax.all_gather(
        grad_middle.astype(jnp.bfloat16), "tensor", axis=1, tiled=True
    ).reshape(-1, model_width)
    grad_wout = jnp.einsum(
        "te,td->ed", context_flat, grad_mid_full, preferred_element_type=jnp.float32
    )
    grad_context = jnp.einsum(
        "td,ed->te", grad_mid_full, full_out, preferred_element_type=jnp.float32
    ).astype(jnp.bfloat16)
    grad_context = grad_context.reshape(seq_count, seq_len, head_count, HEAD_DIM)
    grad_queries, grad_keys, grad_values = attention_backward(
        queries, key_rows, values, segments, grad_context, log_totals
    )
    grad_proj = jnp.stack(
        [
            unrotate(grad_queries, cos_table, sin_table),
            unrotate(grad_keys, cos_table, sin_table),
            grad_values,
        ]
    ).astype(jnp.bfloat16)
    grad_proj = grad_proj.reshape(3, seq_count * seq_len, head_cols)
    grad_qkv = jnp.einsum("td,cte->cde", flat_one, grad_proj, preferred_element_type=jnp.float32)
    partial_back_one = jnp.einsum(
        "cte,cde->td", grad_proj, full_qkv, preferred_element_type=jnp.float32
    ).reshape(seq_count, seq_len, model_width)
    grad_normed_one = lax.psum_scatter(
        partial_back_one.astype(jnp.bfloat16), "tensor", scatter_dimension=1, tiled=True
    ).astype(jnp.float32)
    input_value, input_pull = jax.vjp(rms_norm, input_tokens, gain_one)
    grad_in_norm, gain_one_part = input_pull(grad_normed_one)
    grad_input = (grad_middle + grad_in_norm).astype(jnp.bfloat16)
    summed = (
        lax.psum_scatter(
            grad_qkv.astype(jnp.bfloat16), "dp", scatter_dimension=1, tiled=True
        ).astype(jnp.float32),
        lax.psum_scatter(
            grad_wout.astype(jnp.bfloat16), "dp", scatter_dimension=1, tiled=True
        ).astype(jnp.float32),
        lax.psum_scatter(
            grad_gateup.astype(jnp.bfloat16), "dp", scatter_dimension=1, tiled=True
        ).astype(jnp.float32),
        lax.psum_scatter(
            grad_down.astype(jnp.bfloat16), "dp", scatter_dimension=1, tiled=True
        ).astype(jnp.float32),
        lax.psum_scatter(
            gain_one_part.astype(jnp.bfloat16), "dp", scatter_dimension=0, tiled=True
        ).astype(jnp.float32),
        lax.psum_scatter(
            gain_two_part.astype(jnp.bfloat16), "dp", scatter_dimension=0, tiled=True
        ).astype(jnp.float32),
    )
    gain_one_sum, gain_two_sum = lax.psum((summed[4], summed[5]), "tensor")
    return (
        layer_out,
        grad_input,
        summed[0],
        summed[1],
        gain_one_sum,
        summed[2],
        summed[3],
        gain_two_sum,
    )


def solution(mesh):
    return jax.shard_map(
        per_device,
        mesh=mesh,
        in_specs=(
            P("dp", "tensor", None),
            P("dp", None),
            P(None, "dp", "tensor"),
            P("tensor", "dp"),
            P("dp"),
            P(None, "dp", "tensor"),
            P("tensor", "dp"),
            P("dp"),
            P("dp", "tensor", None),
        ),
        out_specs=(
            P("dp", "tensor", None),
            P("dp", "tensor", None),
            P(None, "dp", "tensor"),
            P("tensor", "dp"),
            P("dp"),
            P(None, "dp", "tensor"),
            P("tensor", "dp"),
            P("dp"),
        ),
        check_vma=False,
    )
```

profile of v0, /device:TPU:0, one launch (start us, length us, event | category | flops | bytes accessed | tf_op | source)
XLA Modules:
  0.0 1986.7 jit_solution(10819157555872073578)
XLA Ops:
  32.5 44.5 %all-gather.13.cloned.1.call-done = bf16[3,2048,512]{2,1,0:T(8,128)(2,1)} async-done(((bf16[3,256,512]{2,1,0:T(8,128)(2,1)}), bf16[3,2048,512]{2,1,0:T(8,128)(2,1)}) %all-gather.13.cloned.1.call-update) | async-done | bytes 6291472 | tf_op jit(solution)/shard_map/all_gather | solution.py:178
  77.1 88.8 %all-gather.11.cloned.1.call-done = bf16[2,1024,2048]{2,1,0:T(8,128)(2,1)} async-done(((bf16[2,256,2048]{2,1,0:T(8,128)(2,1)}), bf16[2,1024,2048]{2,1,0:T(8,128)(2,1)}) %all-gather.11.cloned.1.call-update) | async-done | bytes 8388624 | tf_op jit(solution)/shard_map/all_gather | solution.py:193
  165.8 17.4 convolution_bitcast_fusion.1
  241.5 80.8 %while.32 = (s32[]{:T(128)}, bf16[4,512,8,64]{1,3,2,0:T(8,128)(2,1)S(1)}, f32[4,8,512]{2,1,0:T(8,128)}, s32[4]{0:T(128)S(1)}, bf16[2,1024,8,64]{1,3,2,0:T(8,128)...) while((s32[]{:T(128)}, ...), condition=%wide.region_6.7_spmd, body=%wide.region_3.6_spmd.sunk | while | flops 1125904896 | bytes 55728616 | solution.py:106
  355.8 74.1 %reduce-scatter.9.cloned.1.call-done = bf16[2,256,2048]{2,1,0:T(8,128)(2,1)} async-done(((bf16[2,1024,2048]{2,1,0:T(8,128)(2,1)}), bf16[2,256,2048]{2,1,0:T(8,128)(2,1)}) %reduce-scatter.9.cloned.1.call-update) | async-done | bytes 2097168 | tf_op jit(solution)/shard_map/reduce_scatter | solution.py:207
  437.5 145.1 %all-gather.19.cloned.1.call-done = bf16[2,2048,2048]{2,1,0:T(8,128)(2,1)} async-done(((bf16[2,256,2048]{2,1,0:T(8,128)(2,1)}), bf16[2,2048,2048]{2,1,0:T(8,128)(2,1)}) %all-gather.19.cloned.1.call-update) | async-done | bytes 16777232 | tf_op jit(solution)/shard_map/all_gather | solution.py:180
  582.6 88.3 %all-gather.17.cloned.1.call-done = bf16[2,1024,2048]{2,1,0:T(8,128)(2,1)} async-done(((bf16[2,256,2048]{2,1,0:T(8,128)(2,1)}), bf16[2,1024,2048]{2,1,0:T(8,128)(2,1)}) %all-gather.17.cloned.1.call-update) | async-done | bytes 8388624 | tf_op jit(solution)/shard_map/all_gather | solution.py:211
  670.8 44.7 %convolution_bitcast_fusion = f32[2,2048,2048]{2,1,0:T(8,128)} fusion(bf16[2048,2048,1]{1,0,2:T(8,128)(2,1)} %bitcast.306, bf16[2,2048,2048]{2,1,0:T(8,128)(2,1)} %all-gather.19.cloned.1.call-done), kind=kOutput, calls=%fused_computation.83 | convolution fusion | flops 34359738368 | bytes 58720256 | tf_op jit(solution)/shard_map/td,cdf->ctf/dot_general | solution.py:212
  715.5 44.9 %all-gather.23.cloned.1.call-done = bf16[2,1024,2048]{2,1,0:T(8,128)(2,1)} async-done(((bf16[2,256,2048]{2,1,0:T(8,128)(2,1)}), bf16[2,1024,2048]{2,1,0:T(8,128)(2,1)}) %all-gather.23.cloned.1.call-update) | async-done | bytes 8388624 | tf_op jit(solution)/shard_map/all_gather | solution.py:225
  760.5 84.2 %all-gather.21.cloned.1.call-done = bf16[2048,2048]{1,0:T(8,128)(2,1)} async-done(((bf16[2048,256]{1,0:T(8,128)(2,1)}), bf16[2048,2048]{1,0:T(8,128)(2,1)}) %all-gather.21.cloned.1.call-update) | async-done | bytes 8388624 | tf_op jit(solution)/shard_map/all_gather | solution.py:181
  844.7 34.5 %fusion.62 = (bf16[1,2048,2048]{2,1,0:T(8,128)(2,1)}, bf16[1,2048,2048]{2,1,0:T(8,128)(2,1)}) fusion(f32[2,2048,2048]{2,1,0:T(8,128)} %convolution_bitcast_fusion, bf16[2048,2048]{1,0:T(8,128)(2,1)} %bitcast.308, bf16[2048,2048]{1,0:T(8,128)(2,1)} %all-gather.21.cloned.1.call-done), kind=kOutput, calls=%fused_computation.96 | convolution fusion | flops 17234395136 | bytes 67108864 | tf_op jit(solution)/shard_map/td,fd->tf/dot_general | solution.py:226
  879.2 44.4 %bitcast_convert_fusion.1 = bf16[2048,2048]{1,0:T(8,128)(2,1)} fusion(bf16[2,2048,2048]{2,1,0:T(8,128)(2,1)} %all-gather.19.cloned.1.call-done, bf16[1,2048,2048]{2,1,0:T(8,128)(2,1)} %get-tuple-element.466, bf16[1,2048,2048]{2,1,0:T(8,128)(2,1)} %get-tuple-element.465), kind=kOutput, calls=%fused_computation.66 | convolution fusion | flops 34372321280 | bytes 41943040 | tf_op jit(solution)/shard_map/ctf,cdf->td/dot_general | solution.py:236
  923.9 84.5 %reduce-scatter.13.cloned.1.call-done = bf16[2,256,2048]{2,1,0:T(8,128)(2,1)} async-done(((bf16[2,1024,2048]{2,1,0:T(8,128)(2,1)}), bf16[2,256,2048]{2,1,0:T(8,128)(2,1)}) %reduce-scatter.13.cloned.1.call-update) | async-done | bytes 2097168 | tf_op jit(solution)/shard_map/reduce_scatter | solution.py:239
  1017.6 26.9 %fusion.63 = bf16[2048,2048]{1,0:T(8,128)(2,1)} fusion(bf16[2048,2048]{1,0:T(8,128)(2,1)} %bitcast.309, f32[2,2048,2048]{2,1,0:T(8,128)} %convolution_bitcast_fusion), kind=kOutput, calls=%fused_computation.97 | convolution fusion | flops 17209229312 | bytes 50331648 | tf_op jit(solution)/shard_map/tf,td->fd/dot_general | solution.py:227
  1044.7 42.2 %convert_bitcast_fusion = bf16[2,2048,2048]{1,2,0:T(8,128)(2,1)} fusion(bf16[2048,2048,1]{1,0,2:T(8,128)(2,1)} %bitcast.307, bf16[1,2048,2048]{2,1,0:T(8,128)(2,1)} %get-tuple-element.466, bf16[1,2048,2048]{2,1,0:T(8,128)(2,1)} %get-tuple-element.465), kind=kOutput, calls=%fused_computation.81 | convolution fusion | flops 34376515584 | bytes 41943040 | tf_op jit(solution)/shard_map/td,ctf->cdf/dot_general | solution.py:235
  1128.9 498.4 %while.33 = (s32[]{:T(128)}, f32[2,1024,8,64]{1,0,3,2:T(2,128)}, f32[2,1024,8,64]{1,3,2,0:T(8,128)}, f32[4,512,8,64]{1,0,3,2:T(4,128)}, s32[4]{0:T(128)S(1)}, /*...) while((s32[]{:T(128)}, f32[2,1024,8,64]{1,0,3,2:T(2,128)}, ...), condition=%wide.region_14.15_spmd, body=%wide.region_12.14_spmd.sunk | while | flops 2725507584 | bytes 246520432 | solution.py:160
  1196.3 36.6 %dynamic_update_slice.50 = f32[2,1024,8,64]{1,0,3,2:T(2,128)} dynamic-update-slice(f32[2,1024,8,64]{1,0,3,2:T(2,128)} %get-tuple-element.678, f32[1,1024,8,64]{1,0,3,2:T(1,128)S(1)} %copy.115, s32[]{:T(128)S(6)} %select_n.166, s32[]{:T(128)} %constant.400.clone.1..sunk.1, s32[]{:T(128)} %constant.400.clone.1..sunk.1, s32[]{:T(128)} %constant.400.clone.1..sunk.1) | dynamic-update-slice | bytes 4194308 | tf_op jit(solution)/shard_map/while/body/eval_jaxpr/jit(dynamic_update_index_in_dim)/dynamic_update_slice | solution.py:148
  1232.9 21.1 %dynamic_update_slice.51 = f32[4,512,8,64]{1,0,3,2:T(4,128)} dynamic-update-slice(f32[4,512,8,64]{1,0,3,2:T(4,128)} %get-tuple-element.680, f32[1,512,8,64]{1,0,3,2:T(1,128)S(1)} %copy.116, s32[]{:T(128)S(6)} %copy.135, s32[]{:T(128)} %constant.400.clone.1..sunk.1, s32[]{:T(128)} %constant.400.clone.1..sunk.1, s32[]{:T(128)} %constant.400.clone.1..sunk.1) | dynamic-update-slice | bytes 2097156 | tf_op jit(solution)/shard_map/while/body/jit(dynamic_update_index_in_dim)/dynamic_update_slice | solution.py:160
  1276.2 13.7 multiply_reduce_fusion.3
  1321.2 36.6 %dynamic_update_slice.50 = f32[2,1024,8,64]{1,0,3,2:T(2,128)} dynamic-update-slice(f32[2,1024,8,64]{1,0,3,2:T(2,128)} %get-tuple-element.678, f32[1,1024,8,64]{1,0,3,2:T(1,128)S(1)} %copy.115, s32[]{:T(128)S(6)} %select_n.166, s32[]{:T(128)} %constant.400.clone.1..sunk.1, s32[]{:T(128)} %constant.400.clone.1..sunk.1, s32[]{:T(128)} %constant.400.clone.1..sunk.1) | dynamic-update-slice | bytes 4194308 | tf_op jit(solution)/shard_map/while/body/eval_jaxpr/jit(dynamic_update_index_in_dim)/dynamic_update_slice | solution.py:148
  1357.8 21.0 %dynamic_update_slice.51 = f32[4,512,8,64]{1,0,3,2:T(4,128)} dynamic-update-slice(f32[4,512,8,64]{1,0,3,2:T(4,128)} %get-tuple-element.680, f32[1,512,8,64]{1,0,3,2:T(1,128)S(1)} %copy.116, s32[]{:T(128)S(6)} %copy.135, s32[]{:T(128)} %constant.400.clone.1..sunk.1, s32[]{:T(128)} %constant.400.clone.1..sunk.1, s32[]{:T(128)} %constant.400.clone.1..sunk.1) | dynamic-update-slice | bytes 2097156 | tf_op jit(solution)/shard_map/while/body/jit(dynamic_update_index_in_dim)/dynamic_update_slice | solution.py:160
  1445.4 36.6 %dynamic_update_slice.50 = f32[2,1024,8,64]{1,0,3,2:T(2,128)} dynamic-update-slice(f32[2,1024,8,64]{1,0,3,2:T(2,128)} %get-tuple-element.678, f32[1,1024,8,64]{1,0,3,2:T(1,128)S(1)} %copy.115, s32[]{:T(128)S(6)} %select_n.166, s32[]{:T(128)} %constant.400.clone.1..sunk.1, s32[]{:T(128)} %constant.400.clone.1..sunk.1, s32[]{:T(128)} %constant.400.clone.1..sunk.1) | dynamic-update-slice | bytes 4194308 | tf_op jit(solution)/shard_map/while/body/eval_jaxpr/jit(dynamic_update_index_in_dim)/dynamic_update_slice | solution.py:148
  1481.9 21.0 %dynamic_update_slice.51 = f32[4,512,8,64]{1,0,3,2:T(4,128)} dynamic-update-slice(f32[4,512,8,64]{1,0,3,2:T(4,128)} %get-tuple-element.680, f32[1,512,8,64]{1,0,3,2:T(1,128)S(1)} %copy.116, s32[]{:T(128)S(6)} %copy.135, s32[]{:T(128)} %constant.400.clone.1..sunk.1, s32[]{:T(128)} %constant.400.clone.1..sunk.1, s32[]{:T(128)} %constant.400.clone.1..sunk.1) | dynamic-update-slice | bytes 2097156 | tf_op jit(solution)/shard_map/while/body/jit(dynamic_update_index_in_dim)/dynamic_update_slice | solution.py:160
  1569.4 36.6 %dynamic_update_slice.50 = f32[2,1024,8,64]{1,0,3,2:T(2,128)} dynamic-update-slice(f32[2,1024,8,64]{1,0,3,2:T(2,128)} %get-tuple-element.678, f32[1,1024,8,64]{1,0,3,2:T(1,128)S(1)} %copy.115, s32[]{:T(128)S(6)} %select_n.166, s32[]{:T(128)} %constant.400.clone.1..sunk.1, s32[]{:T(128)} %constant.400.clone.1..sunk.1, s32[]{:T(128)} %constant.400.clone.1..sunk.1) | dynamic-update-slice | bytes 4194308 | tf_op jit(solution)/shard_map/while/body/eval_jaxpr/jit(dynamic_update_index_in_dim)/dynamic_update_slice | solution.py:148
  1606.0 21.0 %dynamic_update_slice.51 = f32[4,512,8,64]{1,0,3,2:T(4,128)} dynamic-update-slice(f32[4,512,8,64]{1,0,3,2:T(4,128)} %get-tuple-element.680, f32[1,512,8,64]{1,0,3,2:T(1,128)S(1)} %copy.116, s32[]{:T(128)S(6)} %copy.135, s32[]{:T(128)} %constant.400.clone.1..sunk.1, s32[]{:T(128)} %constant.400.clone.1..sunk.1, s32[]{:T(128)} %constant.400.clone.1..sunk.1) | dynamic-update-slice | bytes 2097156 | tf_op jit(solution)/shard_map/while/body/jit(dynamic_update_index_in_dim)/dynamic_update_slice | solution.py:160
  1693.7 17.6 convert_bitcast_fusion.1
  1725.5 19.3 bitcast_convert_fusion
  1744.9 22.1 %fusion.103 = (f32[1,2048,2048]{2,1,0:T(8,128)}, f32[1,2048,2048]{2,1,0:T(8,128)}) fusion(f32[2,2048,2048]{2,1,0:T(8,128)} %convolution_bitcast_fusion), kind=kLoop, calls=%fused_computation.179 | loop fusion | bytes 67108864 | tf_op jit(solution)/shard_map/slice | solution.py:215
  1767.0 26.7 %fusion.67 = bf16[2,1024,2048]{2,1,0:T(8,128)(2,1)} fusion(bf16[2048,2048]{1,0:T(8,128)(2,1)} %all-gather.21.cloned.1.call-done, f32[2,1024,2048]{2,1,0:T(8,128)} %bitcast.283, f32[2,1024,2048]{2,1,0:T(8,128)} %bitcast.282), kind=kOutput, calls=%fused_computation.103 | convolution fusion | flops 17209229312 | bytes 50331648 | tf_op jit(solution)/shard_map/dot_general | solution.py:216
  1807.0 75.2 %reduce-scatter.15.cloned.1.call-done = bf16[2,256,2048]{2,1,0:T(8,128)(2,1)} async-done(((bf16[2,1024,2048]{2,1,0:T(8,128)(2,1)}), bf16[2,256,2048]{2,1,0:T(8,128)(2,1)}) %reduce-scatter.15.cloned.1.call-update) | async-done | bytes 2097168 | tf_op jit(solution)/shard_map/reduce_scatter | solution.py:270
  1885.5 16.6 all-reduce.4
  1912.0 60.1 %reduce-scatter.11.cloned.1.call-done = bf16[2,256,2048]{2,1,0:T(8,128)(2,1)} async-done(((bf16[2,1024,2048]{2,1,0:T(8,128)(2,1)}), bf16[2,256,2048]{2,1,0:T(8,128)(2,1)}) %reduce-scatter.11.cloned.1.call-update) | async-done | bytes 2097168 | tf_op jit(solution)/shard_map/reduce_scatter | solution.py:221
  (317 shorter events, 598.1 us)
Async XLA Ops:
  7.2 69.9 %all-gather.13.cloned.1.call-start = ((), (), s32[]{:S(2)}) async-start(), calls=%async_computation.9 | async-start | bytes 7077888 | tf_op jit(solution)/shard_map/all_gather | solution.py:178
  7.9 157.9 %all-gather.11.cloned.1.call-start = ((), (), s32[]{:S(2)}) async-start(), calls=%async_computation.8 | async-start | bytes 10485760 | tf_op jit(solution)/shard_map/all_gather | solution.py:193
  26.1 307.1 %all-gather.15.cloned.1.call-start = ((), (), s32[]{:S(2)}) async-start(), calls=%async_computation.10 | async-start | bytes 2359296 | tf_op jit(solution)/shard_map/all_gather | solution.py:179
  26.8 403.1 %reduce-scatter.9.cloned.1.call-start = ((), (), s32[]{:S(2)}) async-start(), calls=%async_computation.11 | async-start | bytes 10485760 | tf_op jit(solution)/shard_map/reduce_scatter | solution.py:207
  32.5 199.0 %copy-start.17 = (f32[2,1024,64]{1,0,2:T(2,128)}, f32[2,1024,64]{1,0,2:T(2,128)S(1)}, u32[]{:S(2)}) copy-start(f32[2,1024,64]{1,0,2:T(2,128)S(1)} %get-tuple-element.487) | copy-start | bytes 1572868
  32.5 199.0 %copy-start.20 = (f32[2,1024,64]{1,0,2:T(2,128)}, f32[2,1024,64]{1,0,2:T(2,128)S(1)}, u32[]{:S(2)}) copy-start(f32[2,1024,64]{1,0,2:T(2,128)S(1)} %get-tuple-element.488) | copy-start | bytes 1572868
  343.2 86.7 %copy-start.2 = (bf16[2,256,2048]{2,1,0:T(8,128)(2,1)S(1)}, bf16[2,256,2048]{2,1,0:T(8,128)(2,1)}, u32[]{:S(2)}) copy-start(bf16[2,256,2048]{2,1,0:T(8,128)(2,1)} %param.13) | copy-start | bytes 6291460
  343.3 239.3 %all-gather.19.cloned.1.call-start = ((), (), s32[]{:S(2)}) async-start(), calls=%async_computation.13 | async-start | bytes 18874368 | tf_op jit(solution)/shard_map/all_gather | solution.py:180
  343.9 327.0 %all-gather.17.cloned.1.call-start = ((), (), s32[]{:S(2)}) async-start(), calls=%async_computation.12 | async-start | bytes 10485760 | tf_op jit(solution)/shard_map/all_gather | solution.py:211
  355.8 80.2 %copy-start.24 = (f32[8,1,256]{2,1,0:T(1,128)}, f32[8,1,256]{2,1,0:T(1,128)S(1)}, u32[]{:S(2)}) copy-start(f32[8,1,256]{2,1,0:T(1,128)S(1)} %convert_element_type.201) | copy-start | bytes 24580
  436.0 324.5 %all-gather.23.cloned.1.call-start = ((), (), s32[]{:S(2)}) async-start(), calls=%async_computation.16 | async-start | bytes 10485760 | tf_op jit(solution)/shard_map/all_gather | solution.py:225
  436.7 408.0 %all-gather.21.cloned.1.call-start = ((), (), s32[]{:S(2)}) async-start(), calls=%async_computation.14 | async-start | bytes 9437184 | tf_op jit(solution)/shard_map/all_gather | solution.py:181
  437.5 570.9 %reduce-scatter.13.cloned.1.call-start = ((), (), s32[]{:S(2)}) async-start(), calls=%async_computation.17 | async-start | bytes 10485760 | tf_op jit(solution)/shard_map/reduce_scatter | solution.py:239
  923.6 84.8 %copy-start.3 = (bf16[2,256,2048]{2,1,0:T(8,128)(2,1)S(1)}, bf16[2,256,2048]{2,1,0:T(8,128)(2,1)}, u32[]{:S(2)}) copy-start(bf16[2,256,2048]{2,1,0:T(8,128)(2,1)} %param.13) | copy-start | bytes 6291460
  923.6 84.8 %copy-start.25 = (f32[8,1,256]{2,1,0:T(1,128)S(1)}, f32[8,1,256]{2,1,0:T(1,128)}, u32[]{:S(2)}) copy-start(f32[8,1,256]{2,1,0:T(1,128)} %copy-done.24) | copy-start | bytes 24580
  923.6 84.8 %copy-start.30 = (f32[2,256]{1,0:T(2,128)S(1)}, f32[2,256]{1,0:T(2,128)}, u32[]{:S(2)}) copy-start(f32[2,256]{1,0:T(2,128)} %copy-done.29) | copy-start | bytes 6148
  923.6 89.5 %copy-start.37 = (f32[2,256]{1,0:T(2,128)S(1)}, f32[2,256]{1,0:T(2,128)}, u32[]{:S(2)}) copy-start(f32[2,256]{1,0:T(2,128)} %copy-done.36) | copy-start | bytes 6148
  923.6 181.7 %all-gather.25.cloned.1.call-start = ((), (), s32[]{:S(2)}) async-start(), calls=%async_computation.18 | async-start | bytes 10485760 | tf_op jit(solution)/shard_map/all_gather | solution.py:245
  1017.6 778.0 %reduce-scatter.23.cloned.1.call-start = ((), (), s32[]{:S(2)}) async-start(), calls=%async_computation.23 | async-start | bytes 9437184 | tf_op jit(solution)/shard_map/reduce_scatter | solution.py:286
  1044.6 753.7 %reduce-scatter.21.cloned.1.call-start = ((), (), s32[]{:S(2)}) async-start(), calls=%async_computation.22 | async-start | bytes 18874368 | tf_op jit(solution)/shard_map/reduce_scatter | solution.py:283
  1086.8 715.8 %reduce-scatter.19.cloned.1.call-start = ((), (), s32[]{:S(2)}) async-start(), calls=%async_computation.21 | async-start | bytes 2359296 | tf_op jit(solution)/shard_map/reduce_scatter | solution.py:280
  1687.7 116.7 %reduce-scatter.17.cloned.1.call-start = ((), (), s32[]{:S(2)}) async-start(), calls=%async_computation.20 | async-start | bytes 7077888 | tf_op jit(solution)/shard_map/reduce_scatter | solution.py:277
  1711.4 170.8 %reduce-scatter.15.cloned.1.call-start = ((), (), s32[]{:S(2)}) async-start(), calls=%async_computation.19 | async-start | bytes 10485760 | tf_op jit(solution)/shard_map/reduce_scatter | solution.py:270
  1744.9 227.2 %reduce-scatter.11.cloned.1.call-start = ((), (), s32[]{:S(2)}) async-start(), calls=%async_computation.15 | async-start | bytes 10485760 | tf_op jit(solution)/shard_map/reduce_scatter | solution.py:221
  1798.3 83.9 %copy-start.4 = (bf16[2,256,2048]{2,1,0:T(8,128)(2,1)S(1)}, bf16[2,256,2048]{2,1,0:T(8,128)(2,1)}, u32[]{:S(2)}) copy-start(bf16[2,256,2048]{2,1,0:T(8,128)(2,1)} %param.13) | copy-start | bytes 6291460
  1798.3 83.9 %copy-start.28 = (f32[8,1,256]{2,1,0:T(1,128)S(1)}, f32[8,1,256]{2,1,0:T(1,128)}, u32[]{:S(2)}) copy-start(f32[8,1,256]{2,1,0:T(1,128)} %copy-done.27) | copy-start | bytes 24580
  1798.3 83.9 %copy-start.33 = (f32[2,256]{1,0:T(2,128)S(1)}, f32[2,256]{1,0:T(2,128)}, u32[]{:S(2)}) copy-start(f32[2,256]{1,0:T(2,128)} %copy-done.32) | copy-start | bytes 6148
  1802.6 82.9 %copy-start.40 = (bf16[2048]{0:T(1024)(128)(2,1)S(1)}, bf16[2048]{0:T(1024)(128)(2,1)}, u32[]{:S(2)}) copy-start(bf16[2048]{0:T(1024)(128)(2,1)} %get-tuple-element.415) | copy-start | bytes 12292
  1802.6 109.3 %copy-start.35 = (f32[2,256]{1,0:T(2,128)S(1)}, f32[2,256]{1,0:T(2,128)}, u32[]{:S(2)}) copy-start(f32[2,256]{1,0:T(2,128)} %copy-done.34) | copy-start | bytes 6148
  1802.6 169.4 %copy-start.26 = (f32[8,1,256]{2,1,0:T(1,128)S(1)}, f32[8,1,256]{2,1,0:T(1,128)}, u32[]{:S(2)}) copy-start(f32[8,1,256]{2,1,0:T(1,128)} %copy-done.24) | copy-start | bytes 24580
  1802.6 169.4 %copy-start.31 = (f32[2,256]{1,0:T(2,128)S(1)}, f32[2,256]{1,0:T(2,128)}, u32[]{:S(2)}) copy-start(f32[2,256]{1,0:T(2,128)} %copy-done.29) | copy-start | bytes 6148
  1802.6 169.4 %copy-start.39 = (f32[2,256]{1,0:T(2,128)S(1)}, f32[2,256]{1,0:T(2,128)}, u32[]{:S(2)}) copy-start(f32[2,256]{1,0:T(2,128)} %copy-done.38) | copy-start | bytes 6148
  (33 other events, 204.1 us)
Sparse Core Ops, SparseCore 0:
  9.6 67.4 all-gather.12
  79.5 86.2 all-gather.10
  167.4 30.8 all-gather.14
  343.4 86.4 reduce-scatter.8
  431.4 151.0 all-gather.18
  585.0 85.7 all-gather.16
  672.8 87.6 all-gather.22
  762.1 82.4 all-gather.20
  923.7 84.5 reduce-scatter.12
  1017.7 87.5 all-gather.24
  1107.6 89.5 reduce-scatter.22
  1199.5 166.6 reduce-scatter.20
  1687.9 36.0 reduce-scatter.18
  1726.1 68.3 reduce-scatter.16
  1797.4 84.7 reduce-scatter.14
  1885.4 86.5 reduce-scatter.10
where the time goes:
time: 2010 us; the launch traced here: 1990 us
  waiting for transfers between devices  797 us (40%)
  matrix products  488 us (24%)
  local copies, waits for them, and re-layouts  449 us (22%)
  other arithmetic  157 us (8%)
  blocking collectives  51.5 us (3%)
  loops' own time  27.1 us (1%)
    dynamic_update_slice x8, local copies, waits for them, and re-layouts, one_block(): lax.dynamic_update_index_in_dim(grad_keys, lax.dynamic_index_in_dim(grad_...  155 us
    all_gather x1, waiting for transfers between devices, per_device(): lax.all_gather(gate_up_weight, 'dp', axis=1, tiled=True)  145 us
    all_gather x1, waiting for transfers between devices, per_device(): lax.all_gather(low_one, 'tensor', axis=1, tiled=True)  88.8 us
    dynamic_update_slice x8, local copies, waits for them, and re-layouts, attention_backward(): lax.scan(one_block, (zero_grads, zero_grads), jnp.arange(seq_count * bloc...  88.4 us
    all_gather x1, waiting for transfers between devices, per_device(): lax.all_gather(low_two, 'tensor', axis=1, tiled=True)  88.3 us
    reduce_scatter x1, waiting for transfers between devices, per_device(): lax.psum_scatter(partial_back_two.astype(jnp.bfloat16), 'tensor', scatter...  84.5 us
    all_gather x1, waiting for transfers between devices, per_device(): lax.all_gather(down_weight, 'dp', axis=1, tiled=True)  84.2 us
    reduce_scatter x1, waiting for transfers between devices, per_device(): lax.psum_scatter(partial_back_one.astype(jnp.bfloat16), 'tensor', scatter...  75.2 us
  transfers between devices with their start and end apart: 16, of which 11 were waited for; matrix products, arithmetic and copies ran while one was open for 49% of the time, Pallas kernels for 0%

commit v1 on v0

v1 whole, which is shorter than its diff:
```python
import functools

import jax
import jax.numpy as jnp
from jax import lax
from jax.experimental import pallas as pl
from jax.experimental.pallas import tpu as pltpu
from jax.sharding import PartitionSpec as P

HEAD_DIM = 64
HALF = HEAD_DIM // 2
PAIR = 2 * HEAD_DIM
NORM_EPS = 1e-05
ROPE_BASE = 130000.0
MASKED_SCORE = -1e30
BF = jnp.bfloat16
F32 = jnp.float32
VMEM_LIMIT = 60 * 1024 * 1024

NT = (((1,), (1,)), ((), ()))


def dot(a, b):
    return jnp.dot(a, b, preferred_element_type=F32)


def dot_nt(a, b):
    return lax.dot_general(a, b, NT, preferred_element_type=F32)


class Order:
    last = None


ANY = pl.BlockSpec(memory_space=pl.ANY)


def call(body, grid, in_specs, out_specs, out_shape, scratch=(), flops=0, nbytes=0, aliases=None, prefetch=0):
    first_extra = prefetch + len(in_specs)

    def run(*args):
        extra = [] if Order.last is None else [Order.last]

        def ordered_body(*refs):
            body(*refs[:first_extra], *refs[first_extra + len(extra) :])

        outs = pl.pallas_call(
            ordered_body,
            grid_spec=pltpu.PrefetchScalarGridSpec(
                num_scalar_prefetch=prefetch,
                grid=grid,
                in_specs=in_specs + [ANY] * len(extra),
                out_specs=out_specs,
                scratch_shapes=list(scratch),
            ),
            out_shape=out_shape,
            input_output_aliases=aliases or {},
            cost_estimate=pl.CostEstimate(flops=flops, bytes_accessed=nbytes, transcendentals=0),
            compiler_params=pltpu.CompilerParams(vmem_limit_bytes=VMEM_LIMIT),
        )(*args, *extra)
        Order.last = outs[-1] if isinstance(outs, (list, tuple)) else outs
        return outs

    return run


def whole_spec(shape, buffers=1):
    zeros = (0,) * len(shape)
    return pl.BlockSpec(shape, lambda *_: zeros, pipeline_mode=pl.Buffered(buffers))


def sds(shape, dtype):
    return jax.ShapeDtypeStruct(shape, dtype)


def swap_perm(count, bit):
    return [(i, i ^ bit) for i in range(count)]


def gather_pieces(block, nt):
    if nt != 4:
        full = lax.all_gather(block, "tensor", axis=0, tiled=False)
        return [(full[r],) for r in range(nt)]
    half = block.shape[1] // 2
    from_x = lax.ppermute(block, "tensor", swap_perm(4, 1))
    from_y = lax.ppermute(block, "tensor", swap_perm(4, 2))
    diag_x = lax.ppermute(from_y[:, :half], "tensor", swap_perm(4, 1))
    diag_y = lax.ppermute(from_x[:, half:], "tensor", swap_perm(4, 2))
    return [(block,), (from_x,), (from_y,), (diag_x, diag_y)]


def add_half_kernel(base_ref, part_ref, out_ref):
    out_ref[...] = (base_ref[...].astype(F32) + part_ref[...].astype(F32)).astype(BF)


def add_half(base, part, which):
    rows, width = base.shape
    half = width // 2
    tile = min(256, rows)
    return call(
        add_half_kernel,
        (rows // tile,),
        [
            pl.BlockSpec((tile, half), lambda i: (i, which)),
            pl.BlockSpec((tile, half), lambda i: (i, 0)),
        ],
        pl.BlockSpec((tile, half), lambda i: (i, which)),
        sds(base.shape, BF),
        nbytes=rows * half * 6,
        aliases={0: 0},
    )(base, part)


class Scatter:
    def __init__(self, parts, nt):
        self.nt = nt
        if nt != 4:
            full = jnp.stack([p[0] for p in parts])
            self.terms = [lax.psum_scatter(full, "tensor", scatter_dimension=0, tiled=False)]
            return
        (self.own,), (self.to_x,), (self.to_y,), (diag_x, diag_y) = parts
        self.for_y = lax.ppermute(diag_x, "tensor", swap_perm(4, 1))
        self.for_x = lax.ppermute(diag_y, "tensor", swap_perm(4, 2))

    def second(self):
        if self.nt != 4:
            return
        to_y = add_half(self.to_y, self.for_y, 0)
        to_x = add_half(self.to_x, self.for_x, 1)
        self.terms = [
            self.own,
            lax.ppermute(to_x, "tensor", swap_perm(4, 1)),
            lax.ppermute(to_y, "tensor", swap_perm(4, 2)),
        ]


def piece_shapes(nt, rows, width):
    if nt != 4:
        return [((rows, width),)] * nt
    return [((rows, width),)] * 3 + [((rows, width // 2),) * 2]


def flat(pieces):
    return [a for p in pieces for a in p]


def regroup(items, nt):
    if nt != 4:
        return [(a,) for a in items]
    return [(items[0],), (items[1],), (items[2],), (items[3], items[4])]


def fill_from_pieces(refs, full_ref, nt):
    for slot, part in enumerate(regroup(refs, nt)):
        if len(part) == 1:
            full_ref[slot] = part[0][...]
        else:
            half = part[0].shape[1]
            full_ref[slot, :, :half] = part[0][...]
            full_ref[slot, :, half:] = part[1][...]


def out_piece_specs(nt, rows, width, step):
    specs = []
    half_steps = width // step // 2
    for part in piece_shapes(nt, rows, width):
        if len(part) == 1:
            specs.append(pl.BlockSpec((rows, step), lambda j: (0, j)))
        else:
            specs.append(pl.BlockSpec((rows, step), lambda j: (0, jnp.minimum(j, half_steps - 1))))
            specs.append(pl.BlockSpec((rows, step), lambda j: (0, jnp.maximum(j - half_steps, 0))))
    return specs


def store_piece(outs, nt, slot, steps, value):
    part = regroup(outs, nt)[slot]
    if len(part) == 1:
        part[0][...] = value.astype(BF)
    else:
        j = pl.program_id(0)

        @pl.when(j < steps // 2)
        def _():
            part[0][...] = value.astype(BF)

        @pl.when(j >= steps // 2)
        def _():
            part[1][...] = value.astype(BF)


def turn(v):
    lane = lax.broadcasted_iota(jnp.int32, v.shape, 1)
    return jnp.where(lane % HEAD_DIM < HALF, pltpu.roll(v, PAIR - HALF, 1), pltpu.roll(v, HALF, 1))


def rotate(v, cos, sin):
    return v * cos + turn(v) * sin


def unrotate(u, cos, sin):
    return u * cos + turn(u * sin)


def assemble_kernel(nt, normed, *refs):
    pieces, full_ref = refs[: -1 - normed], refs[-1]
    fill_from_pieces(pieces, full_ref, nt)
    if normed:
        gain = refs[-2][...]
        for slot in range(nt):
            x = full_ref[slot].astype(F32)
            scale = lax.rsqrt(jnp.mean(x * x, axis=-1, keepdims=True) + NORM_EPS)
            full_ref[slot] = (x * scale * gain).astype(BF)


def assemble(pieces, nt, gain=None):
    rows, width = pieces[0][0].shape
    tile = min(64, rows)
    items = flat(pieces)
    extra = [] if gain is None else [gain]
    return call(
        functools.partial(assemble_kernel, nt, len(extra)),
        (rows // tile,),
        [pl.BlockSpec((tile, a.shape[1]), lambda i: (i, 0)) for a in items]
        + [whole_spec(a.shape) for a in extra],
        pl.BlockSpec((nt, tile, width), lambda i: (0, i, 0)),
        sds((nt, rows, width), BF),
        nbytes=4 * nt * rows * width,
    )(*items, *extra)


def qkv_kernel(nt, a1_ref, w_ref, cos_ref, sin_ref, out_ref):
    cols = out_ref.shape[3]
    weight = w_ref[:, 0].reshape(-1, cols)

    @pl.when(pl.program_id(0) < 2)
    def _():
        for slot in range(nt):
            raw = dot(a1_ref[slot], weight)
            cos, sin = cos_ref[slot], sin_ref[slot]
            for p in range(cols // PAIR):
                part = slice(p * PAIR, (p + 1) * PAIR)
                out_ref[0, slot, :, part] = rotate(raw[:, part], cos, sin).astype(BF)

    @pl.when(pl.program_id(0) == 2)
    def _():
        for slot in range(nt):
            out_ref[0, slot] = dot(a1_ref[slot], weight).astype(BF)


def project_qkv(a1, weight, cos, sin, nt):
    nd, _, ds, hc = weight.shape
    _, rows, width = a1.shape
    return call(
        functools.partial(qkv_kernel, nt),
        (3,),
        [
            whole_spec(a1.shape),
            pl.BlockSpec((nd, 1, ds, hc), lambda c: (0, c, 0, 0)),
            whole_spec(cos.shape),
            whole_spec(sin.shape),
        ],
        pl.BlockSpec((1, nt, rows, hc), lambda c: (c, 0, 0, 0)),
        sds((3, nt, rows, hc), BF),
        flops=2 * nt * rows * width * hc * 3,
        nbytes=2 * (nt * rows * width + 3 * width * hc + 3 * nt * rows * hc),
    )(a1, weight, cos, sin)


def allowed_block(start, key_block, query_block, size):
    key_id = lax.broadcasted_iota(jnp.int32, (size, size), 0) + key_block * size
    ok = key_id >= start
    if key_block == query_block:
        ok &= lax.broadcasted_iota(jnp.int32, (size, size), 1) + query_block * size >= key_id
    return ok


def attn_fwd_kernel(nt, slot_ref, q_ref, k_ref, v_ref, start_ref, ctx_ref, lse_ref, vt_ref):
    size = q_ref.shape[1]
    for b in range(nt):
        vt_ref[b] = v_ref[slot_ref[b]].T
    lane = lax.broadcasted_iota(jnp.int32, (size, PAIR), 1)
    for p in range(nt):
        slot = slot_ref[p]
        q = q_ref[slot] * BF(HEAD_DIM**-0.5)
        start = start_ref[0, pl.ds(slot, 1), :]
        outs = []
        for h in range(2):
            qh = jnp.where((lane >= HEAD_DIM) == (h == 1), q, BF(0))
            scores = []
            for b in range(p + 1):
                s = dot_nt(k_ref[slot_ref[b]], qh)
                scores.append(jnp.where(allowed_block(start, b, p, size), s, MASKED_SCORE))
            top = functools.reduce(
                jnp.maximum, [jnp.max(s, axis=0, keepdims=True) for s in scores]
            )
            total = jnp.zeros((1, size), F32)
            acc = jnp.zeros((HEAD_DIM, size), F32)
            for b, s in enumerate(scores):
                e = jnp.exp(s - top)
                total += jnp.sum(e, axis=0, keepdims=True)
                acc += dot(vt_ref[b, h * HEAD_DIM : (h + 1) * HEAD_DIM, :], e.astype(BF))
            outs.append(acc / total)
            lse_ref[0, 0, pl.ds(2 * p + h, 1), :] = top + jnp.log(total)
        ctx_ref[slot] = jnp.concatenate(outs, axis=0).T.astype(BF)


def qkv_specs(nt, size):
    def spec(c):
        return pl.BlockSpec((None, nt, size, PAIR), lambda s, g, _: (c, 0, s, g))

    return [spec(c) for c in range(3)]


def attention_forward(qkv, start, slot_of, nt):
    _, _, rows, hc = qkv.shape
    seqs = start.shape[0]
    size = rows // seqs
    pairs = hc // PAIR
    blk = pl.BlockSpec((nt, size, PAIR), lambda s, g, _: (0, s, g))
    return call(
        functools.partial(attn_fwd_kernel, nt),
        (seqs, pairs),
        qkv_specs(nt, size) + [pl.BlockSpec((1, nt, size), lambda s, g, _: (s, 0, 0))],
        [blk, pl.BlockSpec((1, 1, 2 * nt, size), lambda s, g, _: (s, g, 0, 0))],
        [sds((nt, rows, hc), BF), sds((seqs, pairs, 2 * nt, size), F32)],
        scratch=[pltpu.VMEM((nt, PAIR, size), BF)],
        flops=seqs * pairs * 2 * 4 * (nt * size) ** 2 * 128,
        nbytes=8 * nt * rows * hc,
        prefetch=1,
    )(slot_of, qkv, qkv, qkv, start)


def attn_bwd_kernel(
    nt, slot_ref, q_ref, k_ref, v_ref, go_ref, start_ref, lse_ref, cos_ref, sin_ref,
    gq_ref, gk_ref, gv_ref, kt_ref, dk_ref, dv_ref,
):
    size = q_ref.shape[1]
    scale = HEAD_DIM**-0.5
    for b in range(nt):
        kt_ref[b] = k_ref[slot_ref[b]].T
    dk_ref[...] = jnp.zeros_like(dk_ref)
    dv_ref[...] = jnp.zeros_like(dv_ref)
    lane = lax.broadcasted_iota(jnp.int32, (size, PAIR), 1)
    for p in range(nt):
        slot = slot_ref[p]
        q = q_ref[slot] * BF(scale)
        go = go_ref[slot]
        start = start_ref[0, pl.ds(slot, 1), :]
        outs = []
        for h in range(2):
            mine = (lane >= HEAD_DIM) == (h == 1)
            qh = jnp.where(mine, q, BF(0))
            goh = jnp.where(mine, go, BF(0))
            lse = lse_ref[0, 0, pl.ds(2 * p + h, 1), :]
            probs, grads = [], []
            inner = jnp.zeros((1, size), F32)
            for b in range(p + 1):
                key_slot = slot_ref[b]
                s = dot_nt(k_ref[key_slot], qh)
                s = jnp.where(allowed_block(start, b, p, size), s, MASKED_SCORE)
                e = jnp.exp(s - lse)
                g = dot_nt(v_ref[key_slot], goh)
                inner += jnp.sum(e * g, axis=0, keepdims=True)
                probs.append(e)
                grads.append(g)
            dqt = jnp.zeros((HEAD_DIM, size), F32)
            for b in range(p + 1):
                ds = (probs[b] * (grads[b] - inner)).astype(BF)
                dv_ref[b] += dot(probs[b].astype(BF), goh)
                dk_ref[b] += dot(ds, qh)
                dqt += dot(kt_ref[b, h * HEAD_DIM : (h + 1) * HEAD_DIM, :], ds)
            outs.append(dqt)
        dq = jnp.concatenate(outs, axis=0).T * scale
        gq_ref[slot] = unrotate(dq, cos_ref[slot], sin_ref[slot]).astype(BF)
    for b in range(nt):
        slot = slot_ref[b]
        gk_ref[slot] = unrotate(dk_ref[b], cos_ref[slot], sin_ref[slot]).astype(BF)
        gv_ref[slot] = dv_ref[b].astype(BF)


def attention_backward(qkv, go, start, lse, cos, sin, slot_of, nt):
    _, _, rows, hc = qkv.shape
    seqs = start.shape[0]
    size = rows // seqs
    pairs = hc // PAIR
    blk = pl.BlockSpec((nt, size, PAIR), lambda s, g, _: (0, s, g))
    table = pl.BlockSpec((nt, size, PAIR), lambda s, g, _: (0, s, 0))
    return call(
        functools.partial(attn_bwd_kernel, nt),
        (seqs, pairs),
        qkv_specs(nt, size)
        + [
            blk,
            pl.BlockSpec((1, nt, size), lambda s, g, _: (s, 0, 0)),
            pl.BlockSpec((1, 1, 2 * nt, size), lambda s, g, _: (s, g, 0, 0)),
            table, table,
        ],
        [blk, blk, blk],
        [sds((nt, rows, hc), BF)] * 3,
        scratch=[
            pltpu.VMEM((nt, PAIR, size), BF),
            pltpu.VMEM((nt, size, PAIR), F32),
            pltpu.VMEM((nt, size, PAIR), F32),
        ],
        flops=seqs * pairs * 2 * 10 * (nt * size) ** 2 * 128,
        nbytes=14 * nt * rows * hc,
        prefetch=1,
    )(slot_of, qkv, qkv, qkv, go, start, lse, cos, sin)


def shard_group(nd, count):
    while nd % count or nd // count % 2:
        count //= 2
    return max(count, 1)


def cols_out_kernel(nt, steps, lhs_ref, w_ref, *outs):
    for slot in range(nt):
        lhs = lhs_ref[slot]
        parts = [dot(lhs, w_ref[j]) for j in range(w_ref.shape[0])]
        store_piece(outs, nt, slot, steps, jnp.concatenate(parts, axis=1))


def mm_cols(lhs, weight, nt, group):
    nd, depth, ds = weight.shape
    group = shard_group(nd, group)
    rows = lhs.shape[1]
    width = nd * ds
    shapes = flat(piece_shapes(nt, rows, width))
    outs = call(
        functools.partial(cols_out_kernel, nt, nd // group),
        (nd // group,),
        [whole_spec(lhs.shape), pl.BlockSpec((group, depth, ds), lambda j: (j, 0, 0))],
        out_piece_specs(nt, rows, width, group * ds),
        [sds(s, BF) for s in shapes],
        flops=2 * nt * rows * depth * width,
        nbytes=2 * (nt * rows * (depth + width) + depth * width),
    )(lhs, weight)
    return regroup(outs, nt)


def cols_back_kernel(nt, steps, nlhs, *refs):
    lhs, w_ref, outs = refs[:nlhs], refs[nlhs], refs[nlhs + 1 :]
    depth = w_ref.shape[3]
    weights = [w_ref[:, c].reshape(-1, depth) for c in range(nlhs)]
    for slot in range(nt):
        total = dot_nt(lhs[0][slot], weights[0])
        for c in range(1, nlhs):
            total += dot_nt(lhs[c][slot], weights[c])
        store_piece(outs, nt, slot, steps, total)


def mm_back(lhs, weight, nt, group):
    nd, count, ds, depth = weight.shape
    group = shard_group(nd, group)
    rows = lhs[0].shape[1]
    width = nd * ds
    shapes = flat(piece_shapes(nt, rows, width))
    outs = call(
        functools.partial(cols_back_kernel, nt, nd // group, count),
        (nd // group,),
        [whole_spec(a.shape) for a in lhs]
        + [pl.BlockSpec((group, count, ds, depth), lambda j: (j, 0, 0, 0))],
        out_piece_specs(nt, rows, width, group * ds),
        [sds(s, BF) for s in shapes],
        flops=2 * nt * rows * depth * width * count,
        nbytes=2 * (nt * rows * (depth * count + width) + depth * width * count),
    )(*lhs, weight)
    return regroup(outs, nt)


def gateup_kernel(nt, *refs):
    count = len(flat(piece_shapes(nt, 8, 8)))
    pieces, w_ref, (full_ref, gate_ref, up_ref, hid_ref) = (
        refs[:count],
        refs[count],
        refs[count + 1 :],
    )

    @pl.when(pl.program_id(0) == 0)
    def _():
        fill_from_pieces(pieces, full_ref, nt)

    cols = gate_ref.shape[2]
    w_gate = w_ref[:, 0].reshape(-1, cols)
    w_up = w_ref[:, 1].reshape(-1, cols)
    for slot in range(nt):
        a2 = full_ref[slot]
        gate = dot(a2, w_gate)
        up = dot(a2, w_up)
        gate_ref[slot] = gate.astype(BF)
        up_ref[slot] = up.astype(BF)
        hid_ref[slot] = (gate * jax.nn.sigmoid(gate) * up).astype(BF)


def gate_up(pieces, weight, nt):
    nd, _, ds, ff = weight.shape
    rows, width = pieces[0][0].shape
    step = min(512, ff)
    blk = pl.BlockSpec((nt, rows, step), lambda j: (0, 0, j))
    return call(
        functools.partial(gateup_kernel, nt),
        (ff // step,),
        [whole_spec(a.shape) for a in flat(pieces)]
        + [pl.BlockSpec((nd, 2, ds, step), lambda j: (0, 0, 0, j))],
        [whole_spec((nt, rows, width)), blk, blk, blk],
        [sds((nt, rows, width), BF)] + [sds((nt, rows, ff), BF)] * 3,
        flops=4 * nt * rows * width * ff,
        nbytes=2 * (2 * nt * rows * width + 2 * width * ff + 3 * nt * rows * ff),
    )(*flat(pieces), weight)


def gate_back_kernel(nt, full_ref, w_ref, gate_ref, up_ref, gg_ref, gu_ref):
    weight = jnp.concatenate([w_ref[j] for j in range(w_ref.shape[0])], axis=1)
    for slot in range(nt):
        gh = dot_nt(full_ref[slot], weight)
        gate = gate_ref[slot].astype(F32)
        up = up_ref[slot].astype(F32)
        sig = jax.nn.sigmoid(gate)
        gg_ref[slot] = (gh * up * sig * (1.0 + gate * (1.0 - sig))).astype(BF)
        gu_ref[slot] = (gh * gate * sig).astype(BF)


def gate_back(full, weight, gate, up, nt):
    nd, ff, ds = weight.shape
    _, rows, width = full.shape
    step = min(512, ff)
    blk = pl.BlockSpec((nt, rows, step), lambda j: (0, 0, j))
    return call(
        functools.partial(gate_back_kernel, nt),
        (ff // step,),
        [whole_spec(full.shape), pl.BlockSpec((nd, step, ds), lambda j: (0, j, 0)), blk, blk],
        [blk, blk],
        [sds((nt, rows, ff), BF)] * 2,
        flops=2 * nt * rows * width * ff,
        nbytes=2 * (nt * rows * width + width * ff + 4 * nt * rows * ff),
    )(full, weight, gate, up)


def context_back_kernel(nt, *refs):
    count = len(flat(piece_shapes(nt, 8, 8)))
    pieces, w_ref, (full_ref, out_ref) = refs[:count], refs[count], refs[count + 1 :]

    @pl.when(pl.program_id(0) == 0)
    def _():
        fill_from_pieces(pieces, full_ref, nt)

    weight = jnp.concatenate([w_ref[j] for j in range(w_ref.shape[0])], axis=1)
    for slot in range(nt):
        out_ref[slot] = dot_nt(full_ref[slot], weight).astype(BF)


def context_back(pieces, weight, nt):
    nd, hc, ds = weight.shape
    rows, width = pieces[0][0].shape
    step = min(256, hc)
    return call(
        functools.partial(context_back_kernel, nt),
        (hc // step,),
        [whole_spec(a.shape) for a in flat(pieces)]
        + [pl.BlockSpec((nd, step, ds), lambda j: (0, j, 0))],
        [whole_spec((nt, rows, width)), pl.BlockSpec((nt, rows, step), lambda j: (0, 0, j))],
        [sds((nt, rows, width), BF), sds((nt, rows, hc), BF)],
        flops=2 * nt * rows * width * hc,
        nbytes=2 * (2 * nt * rows * width + width * hc + nt * rows * hc),
    )(*flat(pieces), weight)


def middle_kernel(nterms, x_ref, gain_ref, *refs):
    terms, (mid_ref, low_ref) = refs[:nterms], refs[nterms:]
    mid = x_ref[...].astype(F32) + sum_terms(terms)
    mid_ref[...] = mid
    scale = lax.rsqrt(jnp.mean(mid * mid, axis=-1, keepdims=True) + NORM_EPS)
    low_ref[...] = (mid * scale * gain_ref[...]).astype(BF)


def make_middle(x, gain, terms):
    rows, width = x.shape
    tile = min(128, rows)
    blk = pl.BlockSpec((tile, width), lambda i: (i, 0))
    return call(
        functools.partial(middle_kernel, len(terms)),
        (rows // tile,),
        [blk, whole_spec(gain.shape)] + [blk] * len(terms),
        [blk, blk],
        [sds((rows, width), F32), sds((rows, width), BF)],
        nbytes=rows * width * (8 + 2 * len(terms)),
    )(x, gain, *terms)


def sum_terms(terms):
    total = terms[0][...].astype(F32)
    for t in terms[1:]:
        total += t[...].astype(F32)
    return total


def layer_out_kernel(nterms, mid_ref, *refs):
    refs[-1][...] = (mid_ref[...] + sum_terms(refs[:nterms])).astype(BF)


def place(group, groups, rows, tile, width, into):
    steps = rows // tile
    spec = pl.BlockSpec((tile, width), lambda i: (i + group * steps, 0))
    return spec, sds((groups * rows, width), BF), [] if into is None else [into]


def layer_out_rows(mid, terms, group, groups, into):
    rows, width = mid.shape
    tile = min(128, rows)
    blk = pl.BlockSpec((tile, width), lambda i: (i, 0))
    spec, shape, old = place(group, groups, rows, tile, width, into)
    return call(
        functools.partial(layer_out_kernel, len(terms)),
        (rows // tile,),
        [blk] * (1 + len(terms)) + [ANY] * len(old),
        spec,
        shape,
        nbytes=rows * width * (6 + 2 * len(terms)),
        aliases={1 + len(terms): 0} if old else None,
    )(mid, *terms, *old)


def norm_back_kernel(nterms, nouts, first_ref, v_ref, gain_ref, *refs):
    terms, outs, sum_ref = refs[:nterms], refs[-1 - nouts : -1], refs[-1]
    u = sum_terms(terms)
    v = v_ref[...].astype(F32)
    q = lax.rsqrt(jnp.mean(v * v, axis=-1, keepdims=True) + NORM_EPS)
    ug = u * gain_ref[...]
    inner = jnp.mean(ug * v, axis=-1, keepdims=True)
    grad = first_ref[...].astype(F32) + (q * ug - v * (q * q * q * inner))
    for out in outs:
        out[...] = grad.astype(out.dtype)

    @pl.when(pl.program_id(0) == 0)
    def _():
        sum_ref[...] = jnp.zeros_like(sum_ref)

    sum_ref[...] += jnp.sum(u * v * q, axis=0, keepdims=True)


def norm_back(first, v, gain, terms, group=None, groups=None, into=None):
    rows, width = v.shape
    tile = min(128, rows)
    blk = pl.BlockSpec((tile, width), lambda i: (i, 0))
    if group is None:
        specs, shapes, old = [blk, blk], [sds((rows, width), F32), sds((rows, width), BF)], []
    else:
        spec, shape, old = place(group, groups, rows, tile, width, into)
        specs, shapes = [spec], [shape]
    return call(
        functools.partial(norm_back_kernel, len(terms), len(specs)),
        (rows // tile,),
        [blk, blk, whole_spec(gain.shape)] + [blk] * len(terms) + [ANY] * len(old),
        specs + [pl.BlockSpec((1, width), lambda i: (0, 0))],
        shapes + [sds((1, width), F32)],
        nbytes=rows * width * (12 + 2 * len(terms)),
        aliases={3 + len(terms): 0} if old else None,
    )(first, v, gain, *terms, *old)


def wgrad_rows_kernel(groups, nrhs, *refs):
    lhs, rhs, out_ref = refs[:groups], refs[groups : groups * (1 + nrhs)], refs[-1]
    tile = lhs[0].shape[2]
    left = [a[...].reshape(-1, tile).T for a in lhs]
    for c in range(nrhs):
        total = None
        for g in range(groups):
            term = dot(left[g], rhs[c * groups + g][...].reshape(left[g].shape[1], -1))
            total = term if total is None else total + term
        out_ref[0, c] = total.astype(BF)


def wgrad_rows(lhs, rhs, nd, lo=0, hi=None, into=None):
    hi = nd if hi is None else hi
    groups = len(lhs)
    nt, rows, width = lhs[0].shape
    ds = width // nd
    n = rhs[0][0].shape[2]
    old = [] if into is None else [into]
    return call(
        functools.partial(wgrad_rows_kernel, groups, len(rhs)),
        (hi - lo,),
        [pl.BlockSpec((nt, rows, ds), lambda j: (0, 0, j + lo))] * groups
        + [whole_spec(a.shape) for r in rhs for a in r]
        + [ANY] * len(old),
        pl.BlockSpec((1, len(rhs), ds, n), lambda j: (j + lo, 0, 0, 0)),
        sds((nd, len(rhs), ds, n), BF),
        flops=2 * groups * nt * rows * ds * (hi - lo) * n * len(rhs),
        nbytes=2 * groups * nt * rows * (width + n * len(rhs)) + 2 * width * n * len(rhs),
        aliases={groups * (1 + len(rhs)): 0} if old else None,
    )(*lhs, *[a for r in rhs for a in r], *old)


def wgrad_cols_kernel(groups, nd, *refs):
    lhs, rhs, out_ref = refs[:groups], refs[groups:-1], refs[-1]
    tile = lhs[0].shape[2]
    ds = out_ref.shape[2]
    left = [a[...].reshape(-1, tile).T for a in lhs]
    total = None
    for g in range(groups):
        term = dot(left[g], rhs[g][...].reshape(left[g].shape[1], -1))
        total = term if total is None else total + term
    for j in range(nd):
        out_ref[j] = total[:, j * ds : (j + 1) * ds].astype(BF)


def wgrad_cols(lhs, rhs, nd):
    groups = len(lhs)
    nt, rows, m = lhs[0].shape
    width = rhs[0].shape[2]
    tile = min(256, m)
    return call(
        functools.partial(wgrad_cols_kernel, groups, nd),
        (m // tile,),
        [pl.BlockSpec((nt, rows, tile), lambda i: (0, 0, i))] * groups
        + [whole_spec(a.shape) for a in rhs],
        pl.BlockSpec((nd, tile, width // nd), lambda i: (0, i, 0)),
        sds((nd, m, width // nd), BF),
        flops=2 * groups * nt * rows * width * m,
        nbytes=2 * groups * nt * rows * (width + m) + 2 * width * m,
    )(*lhs, *rhs)


def doc_starts(segments):
    row_len = segments.shape[-1]
    ids = jnp.arange(row_len, dtype=jnp.int32)
    change = jnp.concatenate(
        [jnp.ones_like(segments[:, :1], dtype=bool), segments[:, 1:] != segments[:, :-1]], axis=1
    )
    return lax.cummax(jnp.where(change, ids[None, :], 0), axis=1)


def slot_order(blocks, index, nt):
    if nt != 4:
        return blocks
    pairs = jnp.stack([blocks[:, 1], blocks[:, 0], blocks[:, 3], blocks[:, 2]], axis=1)
    blocks = jnp.where(index % 2 == 1, pairs, blocks)
    halves = jnp.stack([blocks[:, 2], blocks[:, 3], blocks[:, 0], blocks[:, 1]], axis=1)
    return jnp.where(index // 2 == 1, halves, blocks)


def per_device(nd, nt, groups, layer_input, segments, qkv_w, out_w, gain1, gateup_w, down_w, gain2, grad_out):
    seqs, local, width = layer_input.shape
    per = seqs // groups
    index = lax.axis_index("tensor").astype(jnp.int32)
    blocks = jnp.arange(nt, dtype=jnp.int32)
    slot_of = blocks ^ index if nt == 4 else blocks

    x = [layer_input[g * per : (g + 1) * per].reshape(per * local, width) for g in range(groups)]
    go = [grad_out[g * per : (g + 1) * per].reshape(per * local, width) for g in range(groups)]
    x_pieces = [gather_pieces(a, nt) for a in x]

    gains = lax.all_gather(jnp.stack([gain1, gain2]), "dp", axis=1, tiled=True).astype(F32)
    g1, g2 = gains[:1], gains[1:]
    full_qkv = lax.all_gather(qkv_w, "dp", axis=0, tiled=False)
    full_out = lax.all_gather(out_w, "dp", axis=0, tiled=False)
    full_gateup = lax.all_gather(gateup_w, "dp", axis=0, tiled=False)
    full_down = lax.all_gather(down_w, "dp", axis=0, tiled=False)

    start_abs = doc_starts(segments)
    pos_abs = jnp.arange(segments.shape[1], dtype=jnp.int32)[None, :] - start_abs
    start_slot = slot_order(start_abs.reshape(seqs, nt, local), index, nt)
    pos_slot = slot_order(pos_abs.reshape(seqs, nt, local), index, nt)
    inv_freq = ROPE_BASE ** (-jnp.arange(HALF, dtype=F32) * 2.0 / HEAD_DIM)
    angles = pos_slot.astype(F32)[..., None] * inv_freq
    cos, sin = jnp.cos(angles), jnp.sin(angles)
    cos = jnp.concatenate([cos] * 4, axis=-1)
    sin = jnp.concatenate([-sin, sin] * 2, axis=-1)

    def table(t, g):
        t = t[g * per : (g + 1) * per]
        return jnp.swapaxes(t, 0, 1).reshape(nt, per * local, PAIR)

    coss = [table(cos, g) for g in range(groups)]
    sins = [table(sin, g) for g in range(groups)]
    starts = [start_slot[g * per : (g + 1) * per] for g in range(groups)]

    def after(value, done):
        return lax.optimization_barrier((value, done))[0]

    Order.last = None
    both = range(groups)
    qkv, ctx, lse, mid, low2, g_mid, g_low = ({} for _ in range(7))

    a1 = [assemble(x_pieces[g], nt, g1) for g in both]
    go_pieces = {0: gather_pieces(after(go[0], flat(x_pieces[-1])[-1]), nt)}
    attn_sum = {}
    for g in both:
        qkv[g] = project_qkv(a1[g], full_qkv, coss[g], sins[g], nt)
        if g > 0:
            attn_sum[g - 1].second()
        ctx[g], lse[g] = attention_forward(qkv[g], starts[g], slot_of, nt)
        attn_sum[g] = Scatter(mm_cols(ctx[g], full_out, nt, 4), nt)
    a2_pieces = {}
    gof = {}
    for g in both:
        if g == groups - 1:
            gof[0] = assemble(go_pieces[0], nt)
            attn_sum[g].second()
        mid[g], low2[g] = make_middle(x[g], g2, attn_sum[g].terms)
        a2_pieces[g] = gather_pieces(low2[g], nt)
    for g in range(1, groups):
        go_pieces[g] = gather_pieces(after(go[g], flat(a2_pieces[groups - 1])[-1]), nt)

    a2, gate, up, hid = zip(*[gate_up(a2_pieces[g], full_gateup, nt) for g in both])
    for g in range(1, groups):
        gof[g] = assemble(go_pieces[g], nt)
    gof = [gof[g] for g in both]
    grad_down = wgrad_cols(hid, gof, nd)
    gg, gu = zip(*[gate_back(gof[g], full_down, gate[g], up[g], nt) for g in both])
    ga2, out_sum, ga1 = {}, {}, {}
    ga2[0] = Scatter(mm_back([gg[0], gu[0]], full_gateup, nt, 2), nt)
    grad_gateup = wgrad_rows(a2, [gg, gu], nd, 0, nd // 2)
    ga2[0].second()
    grad_gateup = wgrad_rows(a2, [gg, gu], nd, nd // 2, nd, grad_gateup)
    sum1, sum2, gm_pieces, gmf, g_qkv = {}, {}, {}, {}, {}

    def residual_back(g):
        g_mid[g], g_low[g], sum2[g] = norm_back(go[g], mid[g], g2, ga2[g].terms)
        gm_pieces[g] = gather_pieces(g_low[g], nt)

    def attention_back(g):
        gmf[g], g_ctx = context_back(gm_pieces[g], full_out, nt)
        g_qkv[g] = attention_backward(
            qkv[g], g_ctx, starts[g], lse[g], coss[g], sins[g], slot_of, nt
        )
        ga1[g] = Scatter(mm_back(g_qkv[g], full_qkv, nt, 4), nt)

    residual_back(0)
    ga2[1] = Scatter(mm_back([gg[1], gu[1]], full_gateup, nt, 2), nt)
    out_sum[0] = Scatter(mm_cols(hid[0], full_down, nt, 2), nt)
    ga2[1].second()
    attention_back(0)
    residual_back(1)
    out_sum[0].second()
    out_sum[1] = Scatter(mm_cols(hid[1], full_down, nt, 2), nt)
    ga1[0].second()
    attention_back(1)
    grad_wout = wgrad_cols([ctx[g] for g in both], [gmf[g] for g in both], nd)
    grad_qkv = wgrad_rows(a1, [[g_qkv[g][c] for g in both] for c in range(3)], nd)
    ga1[1].second()
    out_sum[1].second()
    grad_input = layer_out = None
    for g in both:
        layer_out = layer_out_rows(mid[g], out_sum[g].terms, g, groups, layer_out)
        grad_input, sum1[g] = norm_back(g_mid[g], x[g], g1, ga1[g].terms, g, groups, grad_input)

    def dp_sum(grad):
        return lax.psum_scatter(grad, "dp", scatter_dimension=0, tiled=False).astype(F32)

    gain_sums = jnp.concatenate([sum1[0] + sum1[1], sum2[0] + sum2[1]], axis=0)
    gain_sums = lax.psum(gain_sums, ("dp", "tensor"))
    ds = gain1.shape[0]
    mine = lax.dynamic_slice_in_dim(gain_sums, lax.axis_index("dp") * ds, ds, 1)
    grad_down, grad_gateup = dp_sum(grad_down), dp_sum(grad_gateup)
    return (
        layer_out.reshape(seqs, local, width),
        grad_input.reshape(seqs, local, width),
        dp_sum(grad_qkv),
        dp_sum(grad_wout)[:, :],
        mine[0],
        grad_gateup,
        grad_down,
        mine[1],
    )


def solution(mesh):
    nd, nt = mesh.shape["dp"], mesh.shape["tensor"]
    return jax.shard_map(
        functools.partial(per_device, nd, nt, 2),
        mesh=mesh,
        in_specs=(
            P("dp", "tensor", None),
            P("dp", None),
            P(None, "dp", "tensor"),
            P("tensor", "dp"),
            P("dp"),
            P(None, "dp", "tensor"),
            P("tensor", "dp"),
            P("dp"),
            P("dp", "tensor", None),
        ),
        out_specs=(
            P("dp", "tensor", None),
            P("dp", "tensor", None),
            P(None, "dp", "tensor"),
            P("tensor", "dp"),
            P("dp"),
            P(None, "dp", "tensor"),
            P("tensor", "dp"),
            P("dp"),
        ),
        check_vma=False,
    )
```

time: 2010 us -> 1150 us (0.57)
  Pallas kernels: 0 us -> 501 us
  matrix products: 488 us -> 0 us
  local copies, waits for them, and re-layouts: 449 us -> 37 us
  waiting for transfers between devices: 797 us -> 434 us
  other arithmetic: 157 us -> 18.9 us
  starting transfers between devices: 1.33 us -> 73.6 us
  loops' own time: 27.1 us -> 0 us
    pallas_call x0 -> x53, Pallas kernels: none -> 501 us  [run(): pl.pallas_call(ordered_body, grid_spec=pltpu.PrefetchScalarGridSpec(num_s...]
    all_gather x8 -> x4, waiting for transfers between devices: 499 us -> 0.01 us  [the longest x1 0.01 us: per_device(): full_qkv = lax.all_gather(qkv_w, 'dp', axis=0, tiled=False)]
    dot_general x40 -> x0, matrix products: 488 us -> none  [the longest x8 74 us: block_scores(): jnp.einsum('qhe,khe->hqk', query_block, key_seq, preferred_element_type=j...]
    dynamic_update_slice x16 -> x0, local copies, waits for them, and re-layouts: 243 us -> none  [the longest x8 155 us: one_block(): lax.dynamic_update_index_in_dim(grad_keys, lax.dynamic_index_in_dim(grad_...]
    ppermute x0 -> x64, waiting for transfers between devices: none -> 236 us  [the longest x8 73.8 us: gather_pieces(): from_y = lax.ppermute(block, 'tensor', swap_perm(4, 2))]
    reduce_scatter x8 -> x4, waiting for transfers between devices: 294 us -> 194 us  [dp_sum(): lax.psum_scatter(grad, 'dp', scatter_dimension=0, tiled=False).astype(F32)]
    ppermute x0 -> x64, starting transfers between devices: none -> 73 us  [the longest x8 11.9 us: gather_pieces(): diag_y = lax.ppermute(from_x[:, half:], 'tensor', swap_perm(4, 2))]
    convert_element_type x16 -> x5, other arithmetic: 73.2 us -> 11.1 us  [the longest x4 11.1 us: dp_sum(): lax.psum_scatter(grad, 'dp', scatter_dimension=0, tiled=False).astype(F32)]
  transfers between devices with their start and end apart: 16 -> 72, of which waited for: 11 -> 22; matrix products, arithmetic and copies ran while one was open for 49% -> 3% of each run, Pallas kernels for 0% -> 33%
where the time goes in v1:
time: 1150 us; the launch traced here: 1140 us
  Pallas kernels  501 us (44%)
  waiting for transfers between devices  434 us (38%)
  starting transfers between devices  73.6 us (6%)
  blocking collectives  59.8 us (5%)
  local copies, waits for them, and re-layouts  37 us (3%)
  other arithmetic  18.9 us (2%)
  between operations  15.2 us (1%)
    pallas_call x53, Pallas kernels, run(): pl.pallas_call(ordered_body, grid_spec=pltpu.PrefetchScalarGridSpec(num_s...  501 us
    reduce_scatter x4, waiting for transfers between devices, dp_sum(): lax.psum_scatter(grad, 'dp', scatter_dimension=0, tiled=False).astype(F32)  194 us
    ppermute x8, waiting for transfers between devices, gather_pieces(): from_y = lax.ppermute(block, 'tensor', swap_perm(4, 2))  73.8 us
    ppermute x8, waiting for transfers between devices, __init__(): self.for_y = lax.ppermute(diag_x, 'tensor', swap_perm(4, 1))  71.7 us
    psum x1, blocking collectives, per_device(): gain_sums = lax.psum(gain_sums, ('dp', 'tensor'))  47.2 us
    ppermute x8, waiting for transfers between devices, gather_pieces(): diag_y = lax.ppermute(from_x[:, half:], 'tensor', swap_perm(4, 2))  26.7 us
    ppermute x8, waiting for transfers between devices, second(): lax.ppermute(to_y, 'tensor', swap_perm(4, 2))  25.2 us
  transfers between devices with their start and end apart: 72, of which 22 were waited for; matrix products, arithmetic and copies ran while one was open for 3% of the time, Pallas kernels for 33%

profile of v1, /device:TPU:0, one launch (start us, length us, event | category | flops | bytes accessed | tf_op | source)
XLA Modules:
  0.0 1139.3 jit_solution(18231277092973743703)
XLA Ops:
  17.9 12.6 %all_gather.27 = bf16[2,2048]{1,0:T(2,128)(2,1)S(1)} all-gather(bf16[2,256]{1,0:T(2,128)(2,1)S(1)} %pad_maximum_fusion.3), channel_id=1, replica_groups=mesh['dp'=8,'tensor'=4] {'dp'}, dimensions={1}, use_global_device_ids=true | all-gather | bytes 9216 | tf_op jit(solution)/shard_map/all_gather | solution.py:754
  44.2 16.6 %collective-permute-done.1.refs_2_ = bf16[256,2048]{1,0:T(8,128)(2,1)} collective-permute-done((bf16[256,2048]{1,0:T(8,128)(2,1)S(1)}, bf16[256,2048]{1,0:T(8,128)(2,1)}, u32[]{:S(2)}, u32[]{:S(2)}) %collective-permute-start.1) | collective-permute-done | bytes 1048608 | tf_op jit(solution)/shard_map/ppermute | solution.py:86
  67.5 14.8 %collective-permute-done.3.refs_4_ = bf16[256,1024]{1,0:T(8,128)(2,1)S(1)} collective-permute-done((bf16[256,1024]{1,0:T(8,128)(2,1)S(1)}, bf16[256,1024]{1,0:T(8,128)(2,1)S(1)}, u32[]{:S(2)}, u32[]{:S(2)}) %collective-permute-start.3) | collective-permute-done | bytes 524320 | tf_op jit(solution)/shard_map/ppermute | solution.py:88
  97.5 12.1 %shard_map.154.refs_1_.refs_2_.refs_3_.refs_5_ = bf16[3,4,256,512]{3,2,1,0:T(8,128)(2,1)} custom-call(bf16[4,256,2048]{2,1,0:T(8,128)(2,1)} %shard_map.152.refs_6_.refs_0_, bf16[8,3,256,512]{3,2,1,0:T(8,128)(2,1)} %bitcast.56, f32[4,256,128]{2,1,0:T(8,128)} %get-tuple-element.178.refs_2_.refs_7_, f32[4,256,128]{2,1,0:T(8,128)} %get-tuple-element.176.refs_3_.refs_8_, ...), custom_call_target="tpu_custom_call" | custom-call | flops 6442450944 | bytes 13631488 | tf_op jit(solution)/shard_map/pallas_call | solution.py:47
  109.6 16.2 %shard_map.155 = (bf16[4,256,512]{2,1,0:T(8,128)(2,1)}, f32[1,4,8,256]{3,2,1,0:T(8,128)}) custom-call(s32[4]{0:T(128)} %iota_xor_fusion.refs_0_, bf16[3,4,256,512]{3,2,1,0:T(8,128)(2,1)} %shard_map.154.refs_1_.refs_2_.refs_3_.refs_5_, bf16[3,4,256,512]{3,2,1,0:T(8,128)(2,1)} %shard_map.154.refs_1_.refs_2_.refs_3_.refs_5_, ...), custom_call_target="tpu_custom_call" | custom-call | flops 4294967296 | bytes 4194304 | tf_op jit(solution)/shard_map/pallas_call | solution.py:47
  132.3 12.5 %shard_map.157.refs_2_.refs_1_.refs_3_ = bf16[3,4,256,512]{3,2,1,0:T(8,128)(2,1)} custom-call(bf16[4,256,2048]{2,1,0:T(8,128)(2,1)} %shard_map.153.refs_4_.refs_0_.refs_1_, bf16[8,3,256,512]{3,2,1,0:T(8,128)(2,1)} %bitcast.57, f32[4,256,128]{2,1,0:T(8,128)} %get-tuple-element.179.refs_2_.refs_7_, f32[4,256,128]{2,1,0:T(8,128)} %get-tuple-element.177.refs_3_.refs_8_, ...), custom_call_target="tpu_custom_call" | custom-call | flops 6442450944 | bytes 13631488 | tf_op jit(solution)/shard_map/pallas_call | solution.py:47
  158.7 16.2 %shard_map.160 = (bf16[4,256,512]{2,1,0:T(8,128)(2,1)}, f32[1,4,8,256]{3,2,1,0:T(8,128)}) custom-call(s32[4]{0:T(128)} %iota_xor_fusion.refs_0_, bf16[3,4,256,512]{3,2,1,0:T(8,128)(2,1)} %shard_map.157.refs_2_.refs_1_.refs_3_, bf16[3,4,256,512]{3,2,1,0:T(8,128)(2,1)} %shard_map.157.refs_2_.refs_1_.refs_3_, ...), custom_call_target="tpu_custom_call" | custom-call | flops 4294967296 | bytes 4194304 | tf_op jit(solution)/shard_map/pallas_call | solution.py:47
  212.2 15.0 %collective-permute-done.18.refs_3_ = bf16[256,2048]{1,0:T(8,128)(2,1)S(1)} collective-permute-done((bf16[256,2048]{1,0:T(8,128)(2,1)}, bf16[256,2048]{1,0:T(8,128)(2,1)S(1)}, u32[]{:S(2)}, u32[]{:S(2)}) %collective-permute-start.18) | collective-permute-done | bytes 1048608 | tf_op jit(solution)/shard_map/ppermute | solution.py:132
  233.9 20.8 %collective-permute-done.20.refs_1_ = bf16[256,2048]{1,0:T(8,128)(2,1)S(1)} collective-permute-done((bf16[256,2048]{1,0:T(8,128)(2,1)}, bf16[256,2048]{1,0:T(8,128)(2,1)S(1)}, u32[]{:S(2)}, u32[]{:S(2)}) %collective-permute-start.20) | collective-permute-done | bytes 1048608 | tf_op jit(solution)/shard_map/ppermute | solution.py:85
  272.0 20.1 %collective-permute-done.25.refs_2_ = bf16[256,2048]{1,0:T(8,128)(2,1)S(1)} collective-permute-done((bf16[256,2048]{1,0:T(8,128)(2,1)}, bf16[256,2048]{1,0:T(8,128)(2,1)S(1)}, u32[]{:S(2)}, u32[]{:S(2)}) %collective-permute-start.25) | collective-permute-done | bytes 1048608 | tf_op jit(solution)/shard_map/ppermute | solution.py:86
  294.7 19.9 %collective-permute-done.21.refs_2_ = bf16[256,2048]{1,0:T(8,128)(2,1)S(1)} collective-permute-done((bf16[256,2048]{1,0:T(8,128)(2,1)}, bf16[256,2048]{1,0:T(8,128)(2,1)S(1)}, u32[]{:S(2)}, u32[]{:S(2)}) %collective-permute-start.21) | collective-permute-done | bytes 1048608 | tf_op jit(solution)/shard_map/ppermute | solution.py:86
  316.3 17.2 %collective-permute-done.29.refs_2_ = bf16[256,2048]{1,0:T(8,128)(2,1)S(1)} collective-permute-done((bf16[256,2048]{1,0:T(8,128)(2,1)S(1)}, bf16[256,2048]{1,0:T(8,128)(2,1)S(1)}, u32[]{:S(2)}, u32[]{:S(2)}) %collective-permute-start.29) | collective-permute-done | bytes 1048608 | tf_op jit(solution)/shard_map/ppermute | solution.py:86
  339.2 23.2 %shard_map.167 = (bf16[4,256,2048]{2,1,0:T(8,128)(2,1)}, bf16[4,256,2048]{2,1,0:T(8,128)(2,1)}, bf16[4,256,2048]{2,1,0:T(8,128)(2,1)}, bf16[4,256,2048]{2,1,0:T(8,128)(2,1)}) custom-call(bf16[256,2048]{1,0:T(8,128)(2,1)} %get-tuple-element.105.refs_5_.refs_0_, bf16[256,2048]{1,0:T(8,128)(2,1)} %copy-done.41, bf16[256,2048]{1,0:T(8,128)(2,1)} %copy-done.39, ...), custom_call_target="tpu_custom_call" | custom-call | flops 17179869184 | bytes 37748736 | tf_op jit(solution)/shard_map/pallas_call | solution.py:47
  362.5 23.2 %shard_map.168 = (bf16[4,256,2048]{2,1,0:T(8,128)(2,1)}, bf16[4,256,2048]{2,1,0:T(8,128)(2,1)}, bf16[4,256,2048]{2,1,0:T(8,128)(2,1)}, bf16[4,256,2048]{2,1,0:T(8,128)(2,1)}) custom-call(bf16[256,2048]{1,0:T(8,128)(2,1)} %get-tuple-element.107.refs_6_.refs_0_, bf16[256,2048]{1,0:T(8,128)(2,1)} %copy-done.37, bf16[256,2048]{1,0:T(8,128)(2,1)} %copy-done.38, ...), custom_call_target="tpu_custom_call" | custom-call | flops 17179869184 | bytes 37748736 | tf_op jit(solution)/shard_map/pallas_call | solution.py:47
  391.1 23.9 %shard_map.170.refs_4_ = bf16[8,2048,256]{2,1,0:T(8,128)(2,1)} custom-call(bf16[4,256,2048]{2,1,0:T(8,128)(2,1)} %get-tuple-element.108.refs_6_.refs_0_, bf16[4,256,2048]{2,1,0:T(8,128)(2,1)} %get-tuple-element.109.refs_5_.refs_1_.refs_0_, bf16[4,256,2048]{2,1,0:T(8,128)(2,1)} %shard_map.163.refs_2_.refs_0_, ...), custom_call_target="tpu_custom_call" | custom-call | flops 17179869184 | bytes 25165824 | tf_op jit(solution)/shard_map/pallas_call | solution.py:47
  415.1 17.1 %shard_map.171 = (bf16[4,256,2048]{2,1,0:T(8,128)(2,1)}, bf16[4,256,2048]{2,1,0:T(8,128)(2,1)}) custom-call(bf16[4,256,2048]{2,1,0:T(8,128)(2,1)} %shard_map.163.refs_2_.refs_0_, bf16[8,2048,256]{2,1,0:T(8,128)(2,1)} %bitcast.52, bf16[4,256,2048]{2,1,0:T(8,128)(2,1)} %get-tuple-element.113.refs_2_, bf16[4,256,2048]{2,1,0:T(8,128)(2,1)} %get-tuple-element.114.refs_3_, ...), custom_call_target="tpu_custom_call" | custom-call | flops 8589934592 | bytes 29360128 | tf_op jit(solution)/shard_map/pallas_call | solution.py:47
  432.2 16.9 %shard_map.172 = (bf16[4,256,2048]{2,1,0:T(8,128)(2,1)}, bf16[4,256,2048]{2,1,0:T(8,128)(2,1)}) custom-call(bf16[4,256,2048]{2,1,0:T(8,128)(2,1)} %shard_map.169.refs_3_.refs_4_.refs_0_, bf16[8,2048,256]{2,1,0:T(8,128)(2,1)} %bitcast.53, bf16[4,256,2048]{2,1,0:T(8,128)(2,1)} %get-tuple-element.111.refs_2_, bf16[4,256,2048]{2,1,0:T(8,128)(2,1)} %get-tuple-element.112.refs_3_, ...), custom_call_target="tpu_custom_call" | custom-call | flops 8589934592 | bytes 29360128 | tf_op jit(solution)/shard_map/pallas_call | solution.py:47
  449.1 24.1 %shard_map.173 = (bf16[256,2048]{1,0:T(8,128)(2,1)}, bf16[256,2048]{1,0:T(8,128)(2,1)}, bf16[256,2048]{1,0:T(8,128)(2,1)}, bf16[256,1024]{1,0:T(8,128)(2,1)}, bf16[256,1024]{1,0:T(8,128)(2,1)}) custom-call(bf16[4,256,2048]{2,1,0:T(8,128)(2,1)} %get-tuple-element.119.refs_0_.refs_2_, bf16[4,256,2048]{2,1,0:T(8,128)(2,1)} %get-tuple-element.115.refs_4_.refs_1_, ...), custom_call_target="tpu_custom_call" | custom-call | flops 17179869184 | bytes 29360128 | tf_op jit(solution)/shard_map/pallas_call | solution.py:47
  475.7 25.7 %shard_map.174.refs_2_.refs_6_ = bf16[8,2,256,2048]{3,2,1,0:T(8,128)(2,1)} custom-call(bf16[4,256,2048]{2,1,0:T(8,128)(2,1)} %get-tuple-element.125.refs_0_, bf16[4,256,2048]{2,1,0:T(8,128)(2,1)} %get-tuple-element.126.refs_1_, bf16[4,256,2048]{2,1,0:T(8,128)(2,1)} %get-tuple-element.119.refs_0_.refs_2_, ...), custom_call_target="tpu_custom_call" | custom-call | flops 17179869184 | bytes 41943040 | tf_op jit(solution)/shard_map/pallas_call | solution.py:47
  508.9 26.0 %shard_map.177.refs_6_ = bf16[8,2,256,2048]{3,2,1,0:T(8,128)(2,1)} custom-call(bf16[4,256,2048]{2,1,0:T(8,128)(2,1)} %get-tuple-element.125.refs_0_, bf16[4,256,2048]{2,1,0:T(8,128)(2,1)} %get-tuple-element.126.refs_1_, bf16[4,256,2048]{2,1,0:T(8,128)(2,1)} %get-tuple-element.119.refs_0_.refs_2_, ...), custom_call_target="tpu_custom_call", output_to_operand_aliasing={{}: (6, {})} | custom-call | flops 17179869184 | bytes 41943040 | tf_op jit(solution)/shard_map/pallas_call | solution.py:47
  544.2 24.1 %shard_map.179 = (bf16[256,2048]{1,0:T(8,128)(2,1)}, bf16[256,2048]{1,0:T(8,128)(2,1)}, bf16[256,2048]{1,0:T(8,128)(2,1)}, bf16[256,1024]{1,0:T(8,128)(2,1)}, bf16[256,1024]{1,0:T(8,128)(2,1)}) custom-call(bf16[4,256,2048]{2,1,0:T(8,128)(2,1)} %get-tuple-element.116.refs_3_.refs_0_, bf16[4,256,2048]{2,1,0:T(8,128)(2,1)} %get-tuple-element.117.refs_3_.refs_5_.refs_1_, ...), custom_call_target="tpu_custom_call" | custom-call | flops 17179869184 | bytes 29360128 | tf_op jit(solution)/shard_map/pallas_call | solution.py:47
  573.6 13.5 %shard_map.180 = (bf16[256,2048]{1,0:T(8,128)(2,1)}, bf16[256,2048]{1,0:T(8,128)(2,1)}, bf16[256,2048]{1,0:T(8,128)(2,1)}, bf16[256,1024]{1,0:T(8,128)(2,1)}, bf16[256,1024]{1,0:T(8,128)(2,1)}) custom-call(bf16[4,256,2048]{2,1,0:T(8,128)(2,1)} %get-tuple-element.108.refs_6_.refs_0_, bf16[8,2048,256]{2,1,0:T(8,128)(2,1)} %bitcast.54, ...), custom_call_target="tpu_custom_call" | custom-call | flops 8589934592 | bytes 16777216 | tf_op jit(solution)/shard_map/pallas_call | solution.py:47
  601.7 23.8 %shard_map.184 = (bf16[4,256,512]{2,1,0:T(8,128)(2,1)}, bf16[4,256,512]{2,1,0:T(8,128)(2,1)}, bf16[4,256,512]{2,1,0:T(8,128)(2,1)}) custom-call(s32[4]{0:T(128)} %iota_xor_fusion.refs_0_, bf16[3,4,256,512]{3,2,1,0:T(8,128)(2,1)} %shard_map.154.refs_1_.refs_2_.refs_3_.refs_5_, bf16[3,4,256,512]{3,2,1,0:T(8,128)(2,1)} %shard_map.154.refs_1_.refs_2_.refs_3_.refs_5_, ...), custom_call_target="tpu_custom_call" | custom-call | flops 10737418240 | bytes 7340032 | tf_op jit(solution)/shard_map/pallas_call | solution.py:47
  648.7 22.4 %collective-permute-done.37.refs_1_ = bf16[256,1024]{1,0:T(8,128)(2,1)S(1)} collective-permute-done((bf16[256,1024]{1,0:T(8,128)(2,1)S(1)}, bf16[256,1024]{1,0:T(8,128)(2,1)S(1)}, u32[]{:S(2)}, u32[]{:S(2)}) %collective-permute-start.37) | collective-permute-done | bytes 524320 | tf_op jit(solution)/shard_map/ppermute | solution.py:122
  682.2 13.5 %shard_map.189 = (bf16[256,2048]{1,0:T(8,128)(2,1)}, bf16[256,2048]{1,0:T(8,128)(2,1)}, bf16[256,2048]{1,0:T(8,128)(2,1)}, bf16[256,1024]{1,0:T(8,128)(2,1)}, bf16[256,1024]{1,0:T(8,128)(2,1)}) custom-call(bf16[4,256,2048]{2,1,0:T(8,128)(2,1)} %get-tuple-element.109.refs_5_.refs_1_.refs_0_, bf16[8,2048,256]{2,1,0:T(8,128)(2,1)} %bitcast.55, ...), custom_call_target="tpu_custom_call" | custom-call | flops 8589934592 | bytes 16777216 | tf_op jit(solution)/shard_map/pallas_call | solution.py:47
  709.8 23.6 %shard_map.193 = (bf16[4,256,512]{2,1,0:T(8,128)(2,1)}, bf16[4,256,512]{2,1,0:T(8,128)(2,1)}, bf16[4,256,512]{2,1,0:T(8,128)(2,1)}) custom-call(s32[4]{0:T(128)} %iota_xor_fusion.refs_0_, bf16[3,4,256,512]{3,2,1,0:T(8,128)(2,1)} %shard_map.157.refs_2_.refs_1_.refs_3_, bf16[3,4,256,512]{3,2,1,0:T(8,128)(2,1)} %shard_map.157.refs_2_.refs_1_.refs_3_, ...), custom_call_target="tpu_custom_call" | custom-call | flops 10737418240 | bytes 7340032 | tf_op jit(solution)/shard_map/pallas_call | solution.py:47
  733.4 11.4 %shard_map.194 = (bf16[256,2048]{1,0:T(8,128)(2,1)}, bf16[256,2048]{1,0:T(8,128)(2,1)}, bf16[256,2048]{1,0:T(8,128)(2,1)}, bf16[256,1024]{1,0:T(8,128)(2,1)}, bf16[256,1024]{1,0:T(8,128)(2,1)}) custom-call(bf16[4,256,512]{2,1,0:T(8,128)(2,1)} %get-tuple-element.154.refs_0_.refs_3_, bf16[4,256,512]{2,1,0:T(8,128)(2,1)} %get-tuple-element.155.refs_1_.refs_5_, ...), custom_call_target="tpu_custom_call" | custom-call | flops 6442450944 | bytes 13631488 | tf_op jit(solution)/shard_map/pallas_call | solution.py:47
  755.1 18.8 %shard_map.196.refs_2_ = bf16[8,3,256,512]{3,2,1,0:T(8,128)(2,1)} custom-call(bf16[4,256,2048]{2,1,0:T(8,128)(2,1)} %shard_map.152.refs_6_.refs_0_, bf16[4,256,2048]{2,1,0:T(8,128)(2,1)} %shard_map.153.refs_4_.refs_0_.refs_1_, bf16[4,256,512]{2,1,0:T(8,128)(2,1)} %get-tuple-element.139.refs_0_.refs_2_, ...), custom_call_target="tpu_custom_call" | custom-call | flops 12884901888 | bytes 20971520 | tf_op jit(solution)/shard_map/pallas_call | solution.py:47
  792.0 44.1 %collective-permute-done.47.refs_1_ = bf16[256,1024]{1,0:T(8,128)(2,1)} collective-permute-done((bf16[256,1024]{1,0:T(8,128)(2,1)}, bf16[256,1024]{1,0:T(8,128)(2,1)}, u32[]{:S(2)}, u32[]{:S(2)}) %collective-permute-start.47) | collective-permute-done | bytes 524320 | tf_op jit(solution)/shard_map/ppermute | solution.py:122
  878.7 47.2 %psum.7 = f32[2,2048]{1,0:T(2,128)S(1)} all-reduce(f32[2,2048]{1,0:T(2,128)S(1)} %pad_maximum_fusion.2), channel_id=1, replica_groups=mesh['dp'=8,'tensor'=4] {'dp','tensor'}, use_global_device_ids=true, to_apply=%region_4.5 | all-reduce | flops 4096 | bytes 32768 | tf_op jit(solution)/shard_map/psum | solution.py:853
  931.1 27.8 %reduce-scatter.5.cloned.1.call-done = bf16[1,3,256,512]{3,2,1,0:T(8,128)(2,1)} async-done(((bf16[8,3,256,512]{3,2,1,0:T(8,128)(2,1)}), bf16[1,3,256,512]{3,2,1,0:T(8,128)(2,1)}) %reduce-scatter.5.cloned.1.call-update) | async-done | bytes 786448 | tf_op jit(solution)/shard_map/reduce_scatter | solution.py:850
  961.3 166.5 %reduce-scatter.9.cloned.1.call-done = bf16[1,2,256,2048]{3,2,1,0:T(8,128)(2,1)} async-done(((bf16[8,2,256,2048]{3,2,1,0:T(8,128)(2,1)}), bf16[1,2,256,2048]{3,2,1,0:T(8,128)(2,1)}) %reduce-scatter.9.cloned.1.call-update) | async-done | bytes 2097168 | tf_op jit(solution)/shard_map/reduce_scatter | solution.py:850
  (341 shorter events, 313.0 us)
Async XLA Ops:
  7.2 90.3 %all-gather.9.cloned.1.call-start = ((), (), s32[]{:S(2)}) async-start(), calls=%async_computation.8 | async-start | bytes 7077888 | tf_op jit(solution)/shard_map/all_gather | solution.py:756
  7.9 117.8 %all-gather.11.cloned.1.call-start = ((), (), s32[]{:S(2)}) async-start(), calls=%async_computation.9 | async-start | bytes 2359296 | tf_op jit(solution)/shard_map/all_gather | solution.py:757
  8.7 330.6 %all-gather.13.cloned.1.call-start = ((), (), s32[]{:S(2)}) async-start(), calls=%async_computation.10 | async-start | bytes 18874368 | tf_op jit(solution)/shard_map/all_gather | solution.py:758
  9.4 405.7 %all-gather.15.cloned.1.call-start = ((), (), s32[]{:S(2)}) async-start(), calls=%async_computation.11 | async-start | bytes 9437184 | tf_op jit(solution)/shard_map/all_gather | solution.py:759
  15.7 45.1 %collective-permute-start.1 = (bf16[256,2048]{1,0:T(8,128)(2,1)S(1)}, bf16[256,2048]{1,0:T(8,128)(2,1)}, u32[]{:S(2)}, u32[]{:S(2)}) collective-permute-start(bf16[256,2048]{1,0:T(8,128)(2,1)S(1)} %get-tuple-element.175.refs_0_.refs_1_), channel_id=1, source_target_pairs={{0,2},{1,3},{2,0},{3,1},{4,6},{5,7},{6,4},{7,5},{8,10},{9,11},{10,... | collective-permute-start | bytes 3145736 | tf_op jit(solution)/shard_map/ppermute | solution.py:86
  16.2 48.5 %collective-permute-start = (bf16[256,2048]{1,0:T(8,128)(2,1)S(1)}, bf16[256,2048]{1,0:T(8,128)(2,1)}, u32[]{:S(2)}, u32[]{:S(2)}) collective-permute-start(bf16[256,2048]{1,0:T(8,128)(2,1)S(1)} %get-tuple-element.175.refs_0_.refs_1_), channel_id=1, source_target_pairs={{0,1},{1,0},{2,3},{3,2},{4,5},{5,4},{6,7},{7,6},{8,9},{9,8},{10,11... | collective-permute-start | bytes 3145736 | tf_op jit(solution)/shard_map/ppermute | solution.py:85
  16.3 910.2 %reduce-scatter.7.cloned.1.call-start = ((), (), s32[]{:S(2)}) async-start(), calls=%async_computation.5 | async-start | bytes 2359296 | tf_op jit(solution)/shard_map/reduce_scatter | solution.py:850
  39.9 45.6 %collective-permute-start.6 = (bf16[256,1024]{1,0:T(8,128)(2,1)S(1)}, bf16[256,1024]{1,0:T(8,128)(2,1)S(1)}, u32[]{:S(2)}, u32[]{:S(2)}) collective-permute-start(bf16[256,1024]{1,0:T(8,128)(2,1)S(1)} %slice.196), channel_id=1, source_target_pairs={{0,1},{1,0},{2,3},{3,2},{4,5},{5,4},{6,7},{7,6},{8,9},{9,8},{10,11... | collective-permute-start | bytes 1572872 | tf_op jit(solution)/shard_map/ppermute | solution.py:87
  42.6 43.0 %collective-permute-start.7 = (bf16[256,1024]{1,0:T(8,128)(2,1)S(1)}, bf16[256,1024]{1,0:T(8,128)(2,1)}, u32[]{:S(2)}, u32[]{:S(2)}) collective-permute-start(bf16[256,1024]{1,0:T(8,128)(2,1)S(1)} %slice.197), channel_id=1, source_target_pairs={{0,2},{1,3},{2,0},{3,1},{4,6},{5,7},{6,4},{7,5},{8,10},{9,11},{10,... | collective-permute-start | bytes 1572872 | tf_op jit(solution)/shard_map/ppermute | solution.py:88
  82.3 70.2 %collective-permute-start.13 = (bf16[256,2048]{1,0:T(8,128)(2,1)S(1)}, bf16[256,2048]{1,0:T(8,128)(2,1)}, u32[]{:S(2)}, u32[]{:S(2)}) collective-permute-start(bf16[256,2048]{1,0:T(8,128)(2,1)S(1)} %get-tuple-element.103.refs_0_), channel_id=1, source_target_pairs={{0,2},{1,3},{2,0},{3,1},{4,6},{5,7},{6,4},{7,5},{8,10},{9,11},{10,... | collective-permute-start | bytes 3145736 | tf_op jit(solution)/shard_map/ppermute | solution.py:86
  84.0 70.7 %collective-permute-start.12 = (bf16[256,2048]{1,0:T(8,128)(2,1)S(1)}, bf16[256,2048]{1,0:T(8,128)(2,1)}, u32[]{:S(2)}, u32[]{:S(2)}) collective-permute-start(bf16[256,2048]{1,0:T(8,128)(2,1)S(1)} %get-tuple-element.103.refs_0_), channel_id=1, source_target_pairs={{0,1},{1,0},{2,3},{3,2},{4,5},{5,4},{6,7},{7,6},{8,9},{9,8},{10,11... | collective-permute-start | bytes 3145736 | tf_op jit(solution)/shard_map/ppermute | solution.py:85
  154.4 44.6 %collective-permute-start.14 = (bf16[256,1024]{1,0:T(8,128)(2,1)}, bf16[256,1024]{1,0:T(8,128)(2,1)S(1)}, u32[]{:S(2)}, u32[]{:S(2)}) collective-permute-start(bf16[256,1024]{1,0:T(8,128)(2,1)} %slice.217), channel_id=1, source_target_pairs={{0,1},{1,0},{2,3},{3,2},{4,5},{5,4},{6,7},{7,6},{8,9},{9,8},{10,11... | collective-permute-start | bytes 1572872 | tf_op jit(solution)/shard_map/ppermute | solution.py:87
  156.6 42.3 %collective-permute-start.15 = (bf16[256,1024]{1,0:T(8,128)(2,1)}, bf16[256,1024]{1,0:T(8,128)(2,1)}, u32[]{:S(2)}, u32[]{:S(2)}) collective-permute-start(bf16[256,1024]{1,0:T(8,128)(2,1)} %slice.218), channel_id=1, source_target_pairs={{0,2},{1,3},{2,0},{3,1},{4,6},{5,7},{6,4},{7,5},{8,10},{9,11},{10,... | collective-permute-start | bytes 1572872 | tf_op jit(solution)/shard_map/ppermute | solution.py:88
  257.7 56.9 %collective-permute-start.21 = (bf16[256,2048]{1,0:T(8,128)(2,1)}, bf16[256,2048]{1,0:T(8,128)(2,1)S(1)}, u32[]{:S(2)}, u32[]{:S(2)}) collective-permute-start(bf16[256,2048]{1,0:T(8,128)(2,1)} %get-tuple-element.107.refs_6_.refs_0_), channel_id=1, source_target_pairs={{0,2},{1,3},{2,0},{3,1},{4,6},{5,7},{6,4},{7,5},{8,10},{9,11},{10,... | collective-permute-start | bytes 3145736 | tf_op jit(solution)/shard_map/ppermute | solution.py:86
  269.7 63.9 %collective-permute-start.29 = (bf16[256,2048]{1,0:T(8,128)(2,1)S(1)}, bf16[256,2048]{1,0:T(8,128)(2,1)S(1)}, u32[]{:S(2)}, u32[]{:S(2)}) collective-permute-start(bf16[256,2048]{1,0:T(8,128)(2,1)S(1)} %get-tuple-element.110.refs_0_), channel_id=1, source_target_pairs={{0,2},{1,3},{2,0},{3,1},{4,6},{5,7},{6,4},{7,5},{8,10},{9,11},{10,... | collective-permute-start | bytes 3145736 | tf_op jit(solution)/shard_map/ppermute | solution.py:86
  271.3 64.6 %collective-permute-start.28 = (bf16[256,2048]{1,0:T(8,128)(2,1)S(1)}, bf16[256,2048]{1,0:T(8,128)(2,1)S(1)}, u32[]{:S(2)}, u32[]{:S(2)}) collective-permute-start(bf16[256,2048]{1,0:T(8,128)(2,1)S(1)} %get-tuple-element.110.refs_0_), channel_id=1, source_target_pairs={{0,1},{1,0},{2,3},{3,2},{4,5},{5,4},{6,7},{7,6},{8,9},{9,8},{10,11... | collective-permute-start | bytes 3145736 | tf_op jit(solution)/shard_map/ppermute | solution.py:85
  292.2 44.9 %collective-permute-start.26 = (bf16[256,1024]{1,0:T(8,128)(2,1)S(1)}, bf16[256,1024]{1,0:T(8,128)(2,1)S(1)}, u32[]{:S(2)}, u32[]{:S(2)}) collective-permute-start(bf16[256,1024]{1,0:T(8,128)(2,1)S(1)} %slice.221), channel_id=1, source_target_pairs={{0,1},{1,0},{2,3},{3,2},{4,5},{5,4},{6,7},{7,6},{8,9},{9,8},{10,11... | collective-permute-start | bytes 1572872 | tf_op jit(solution)/shard_map/ppermute | solution.py:87
  293.1 46.1 %collective-permute-start.27 = (bf16[256,1024]{1,0:T(8,128)(2,1)S(1)}, bf16[256,1024]{1,0:T(8,128)(2,1)}, u32[]{:S(2)}, u32[]{:S(2)}) collective-permute-start(bf16[256,1024]{1,0:T(8,128)(2,1)S(1)} %slice.222), channel_id=1, source_target_pairs={{0,2},{1,3},{2,0},{3,1},{4,6},{5,7},{6,4},{7,5},{8,10},{9,11},{10,... | collective-permute-start | bytes 1572872 | tf_op jit(solution)/shard_map/ppermute | solution.py:88
  315.5 47.0 %collective-permute-start.22 = (bf16[256,1024]{1,0:T(8,128)(2,1)}, bf16[256,1024]{1,0:T(8,128)(2,1)}, u32[]{:S(2)}, u32[]{:S(2)}) collective-permute-start(bf16[256,1024]{1,0:T(8,128)(2,1)} %slice.219), channel_id=1, source_target_pairs={{0,1},{1,0},{2,3},{3,2},{4,5},{5,4},{6,7},{7,6},{8,9},{9,8},{10,11... | collective-permute-start | bytes 1572872 | tf_op jit(solution)/shard_map/ppermute | solution.py:87
  334.4 51.2 %collective-permute-start.30 = (bf16[256,1024]{1,0:T(8,128)(2,1)}, bf16[256,1024]{1,0:T(8,128)(2,1)}, u32[]{:S(2)}, u32[]{:S(2)}) collective-permute-start(bf16[256,1024]{1,0:T(8,128)(2,1)} %slice.223), channel_id=1, source_target_pairs={{0,1},{1,0},{2,3},{3,2},{4,5},{5,4},{6,7},{7,6},{8,9},{9,8},{10,11... | collective-permute-start | bytes 1572872 | tf_op jit(solution)/shard_map/ppermute | solution.py:87
  335.9 49.8 %collective-permute-start.31 = (bf16[256,1024]{1,0:T(8,128)(2,1)S(1)}, bf16[256,1024]{1,0:T(8,128)(2,1)S(1)}, u32[]{:S(2)}, u32[]{:S(2)}) collective-permute-start(bf16[256,1024]{1,0:T(8,128)(2,1)S(1)} %slice.224), channel_id=1, source_target_pairs={{0,2},{1,3},{2,0},{3,1},{4,6},{5,7},{6,4},{7,5},{8,10},{9,11},{10,... | collective-permute-start | bytes 1572872 | tf_op jit(solution)/shard_map/ppermute | solution.py:88
  590.0 46.9 %collective-permute-start.41 = (bf16[256,2048]{1,0:T(8,128)(2,1)}, bf16[256,2048]{1,0:T(8,128)(2,1)S(1)}, u32[]{:S(2)}, u32[]{:S(2)}) collective-permute-start(bf16[256,2048]{1,0:T(8,128)(2,1)} %shard_map.181.refs_2_), channel_id=1, source_target_pairs={{0,2},{1,3},{2,0},{3,1},{4,6},{5,7},{6,4},{7,5},{8,10},{9,11},{10,... | collective-permute-start | bytes 3145736 | tf_op jit(solution)/shard_map/ppermute | solution.py:133
  593.9 43.0 %collective-permute-start.40 = (bf16[256,2048]{1,0:T(8,128)(2,1)}, bf16[256,2048]{1,0:T(8,128)(2,1)S(1)}, u32[]{:S(2)}, u32[]{:S(2)}) collective-permute-start(bf16[256,2048]{1,0:T(8,128)(2,1)} %shard_map.182.refs_6_), channel_id=1, source_target_pairs={{0,1},{1,0},{2,3},{3,2},{4,5},{5,4},{6,7},{7,6},{8,9},{9,8},{10,11... | collective-permute-start | bytes 3145736 | tf_op jit(solution)/shard_map/ppermute | solution.py:132
  647.7 51.0 %collective-permute-start.52 = (bf16[256,1024]{1,0:T(8,128)(2,1)S(1)}, bf16[256,1024]{1,0:T(8,128)(2,1)S(1)}, u32[]{:S(2)}, u32[]{:S(2)}) collective-permute-start(bf16[256,1024]{1,0:T(8,128)(2,1)S(1)} %copy-done.34), channel_id=1, source_target_pairs={{0,2},{1,3},{2,0},{3,1},{4,6},{5,7},{6,4},{7,5},{8,10},{9,11},{10,... | collective-permute-start | bytes 1572872 | tf_op jit(solution)/shard_map/ppermute | solution.py:123
  754.5 173.9 %reduce-scatter.11.cloned.1.call-start = ((), (), s32[]{:S(2)}) async-start(), calls=%async_computation.7 | async-start | bytes 9437184 | tf_op jit(solution)/shard_map/reduce_scatter | solution.py:850
  755.0 203.8 %reduce-scatter.5.cloned.1.call-start = ((), (), s32[]{:S(2)}) async-start(), calls=%async_computation.4 | async-start | bytes 7077888 | tf_op jit(solution)/shard_map/reduce_scatter | solution.py:850
  773.9 353.9 %reduce-scatter.9.cloned.1.call-start = ((), (), s32[]{:S(2)}) async-start(), calls=%async_computation.6 | async-start | bytes 18874368 | tf_op jit(solution)/shard_map/reduce_scatter | solution.py:850
  776.9 65.2 %collective-permute-start.58 = (bf16[256,2048]{1,0:T(8,128)(2,1)}, bf16[256,2048]{1,0:T(8,128)(2,1)}, u32[]{:S(2)}, u32[]{:S(2)}) collective-permute-start(bf16[256,2048]{1,0:T(8,128)(2,1)} %shard_map.188.refs_2_), channel_id=1, source_target_pairs={{0,1},{1,0},{2,3},{3,2},{4,5},{5,4},{6,7},{7,6},{8,9},{9,8},{10,11... | collective-permute-start | bytes 3145736 | tf_op jit(solution)/shard_map/ppermute | solution.py:132
  777.7 65.8 %collective-permute-start.59 = (bf16[256,2048]{1,0:T(8,128)(2,1)}, bf16[256,2048]{1,0:T(8,128)(2,1)}, u32[]{:S(2)}, u32[]{:S(2)}) collective-permute-start(bf16[256,2048]{1,0:T(8,128)(2,1)} %shard_map.187.refs_2_), channel_id=1, source_target_pairs={{0,2},{1,3},{2,0},{3,1},{4,6},{5,7},{6,4},{7,5},{8,10},{9,11},{10,... | collective-permute-start | bytes 3145736 | tf_op jit(solution)/shard_map/ppermute | solution.py:133
  779.0 65.5 %collective-permute-start.60 = (bf16[256,2048]{1,0:T(8,128)(2,1)}, bf16[256,2048]{1,0:T(8,128)(2,1)}, u32[]{:S(2)}, u32[]{:S(2)}) collective-permute-start(bf16[256,2048]{1,0:T(8,128)(2,1)} %shard_map.191.refs_6_), channel_id=1, source_target_pairs={{0,1},{1,0},{2,3},{3,2},{4,5},{5,4},{6,7},{7,6},{8,9},{9,8},{10,11... | collective-permute-start | bytes 3145736 | tf_op jit(solution)/shard_map/ppermute | solution.py:132
  785.4 50.7 %collective-permute-start.47 = (bf16[256,1024]{1,0:T(8,128)(2,1)}, bf16[256,1024]{1,0:T(8,128)(2,1)}, u32[]{:S(2)}, u32[]{:S(2)}) collective-permute-start(bf16[256,1024]{1,0:T(8,128)(2,1)} %get-tuple-element.148), channel_id=1, source_target_pairs={{0,1},{1,0},{2,3},{3,2},{4,5},{5,4},{6,7},{7,6},{8,9},{9,8},{10,11... | collective-permute-start | bytes 1572872 | tf_op jit(solution)/shard_map/ppermute | solution.py:122
  786.9 52.0 %collective-permute-start.46 = (bf16[256,1024]{1,0:T(8,128)(2,1)}, bf16[256,1024]{1,0:T(8,128)(2,1)}, u32[]{:S(2)}, u32[]{:S(2)}) collective-permute-start(bf16[256,1024]{1,0:T(8,128)(2,1)} %get-tuple-element.146.refs_2_), channel_id=1, source_target_pairs={{0,2},{1,3},{2,0},{3,1},{4,6},{5,7},{6,4},{7,5},{8,10},{9,11},{10,... | collective-permute-start | bytes 1572872 | tf_op jit(solution)/shard_map/ppermute | solution.py:123
  (96 other events, 1893.1 us)
Sparse Core Ops, SparseCore 0:
  9.7 67.5 all-gather.8
  78.8 27.6 all-gather.10
  108.2 150.6 all-gather.12
  260.3 80.3 all-gather.14
  754.6 42.2 reduce-scatter.6
  799.0 88.2 reduce-scatter.10
  889.6 69.2 reduce-scatter.4
  961.2 166.6 reduce-scatter.8

commit v2 on v1

--- a/solution.py
+++ b/solution.py
@@ -16,6 +16,7 @@
 BF = jnp.bfloat16
 F32 = jnp.float32
 VMEM_LIMIT = 60 * 1024 * 1024
+SMALL = 3
 
 NT = (((1,), (1,)), ((), ()))
 
@@ -55,7 +56,7 @@
             ),
             out_shape=out_shape,
             input_output_aliases=aliases or {},
-            cost_estimate=pl.CostEstimate(flops=flops, bytes_accessed=nbytes, transcendentals=0),
+            cost_estimate=pl.CostEstimate(flops=flops // SMALL, bytes_accessed=nbytes // SMALL, transcendentals=0),
             compiler_params=pltpu.CompilerParams(vmem_limit_bytes=VMEM_LIMIT),
         )(*args, *extra)
         Order.last = outs[-1] if isinstance(outs, (list, tuple)) else outs
@@ -64,6 +65,14 @@
     return run
 
 
+def link_kernel(value_ref, done_ref, out_ref):
+    pass
+
+
+def link(value, done):
+    return call(link_kernel, (1,), [ANY, ANY], ANY, sds(value.shape, value.dtype), aliases={0: 0})(value, done)
+
+
 def whole_spec(shape, buffers=1):
     zeros = (0,) * len(shape)
     return pl.BlockSpec(shape, lambda *_: zeros, pipeline_mode=pl.Buffered(buffers))
@@ -77,38 +86,71 @@
     return [(i, i ^ bit) for i in range(count)]
 
 
-def gather_pieces(block, nt):
-    if nt != 4:
-        full = lax.all_gather(block, "tensor", axis=0, tiled=False)
-        return [(full[r],) for r in range(nt)]
-    half = block.shape[1] // 2
-    from_x = lax.ppermute(block, "tensor", swap_perm(4, 1))
-    from_y = lax.ppermute(block, "tensor", swap_perm(4, 2))
-    diag_x = lax.ppermute(from_y[:, :half], "tensor", swap_perm(4, 1))
-    diag_y = lax.ppermute(from_x[:, half:], "tensor", swap_perm(4, 2))
-    return [(block,), (from_x,), (from_y,), (diag_x, diag_y)]
-
-
-def add_half_kernel(base_ref, part_ref, out_ref):
-    out_ref[...] = (base_ref[...].astype(F32) + part_ref[...].astype(F32)).astype(BF)
-
-
-def add_half(base, part, which):
-    rows, width = base.shape
+def halves_kernel(y_ref, x_ref, left_ref, right_ref):
+    left_ref[...] = y_ref[...]
+    right_ref[...] = x_ref[...]
+
+
+def halves(from_y, from_x):
+    rows, width = from_y.shape
     half = width // 2
-    tile = min(256, rows)
-    return call(
-        add_half_kernel,
+    tile = min(128, rows)
+
+    def spec(which):
+        return pl.BlockSpec((tile, half), lambda i: (i, which))
+
+    return call(
+        halves_kernel,
         (rows // tile,),
-        [
-            pl.BlockSpec((tile, half), lambda i: (i, which)),
-            pl.BlockSpec((tile, half), lambda i: (i, 0)),
-        ],
-        pl.BlockSpec((tile, half), lambda i: (i, which)),
-        sds(base.shape, BF),
-        nbytes=rows * half * 6,
-        aliases={0: 0},
-    )(base, part)
+        [spec(0), spec(1)],
+        [spec(0), spec(0)],
+        [sds((rows, half), BF)] * 2,
+        nbytes=rows * half * 8,
+    )(from_y, from_x)
+
+
+class Gather:
+    def __init__(self, block, nt):
+        self.nt = nt
+        if nt != 4:
+            full = lax.all_gather(block, "tensor", axis=0, tiled=False)
+            self.pieces = [(full[r],) for r in range(nt)]
+            return
+        self.block = block
+        self.from_x = lax.ppermute(block, "tensor", swap_perm(4, 1))
+        self.from_y = lax.ppermute(block, "tensor", swap_perm(4, 2))
+
+    def second(self):
+        if self.nt != 4:
+            return
+        left, right = halves(self.from_y, self.from_x)
+        diag_x = lax.ppermute(left, "tensor", swap_perm(4, 1))
+        diag_y = lax.ppermute(right, "tensor", swap_perm(4, 2))
+        self.pieces = [(self.block,), (self.from_x,), (self.from_y,), (diag_x, diag_y)]
+
+
+def add_halves_kernel(x_ref, for_x_ref, y_ref, for_y_ref, out_x_ref, out_y_ref):
+    out_x_ref[...] = (x_ref[...].astype(F32) + for_x_ref[...].astype(F32)).astype(BF)
+    out_y_ref[...] = (y_ref[...].astype(F32) + for_y_ref[...].astype(F32)).astype(BF)
+
+
+def add_halves(to_x, for_x, to_y, for_y):
+    rows, width = to_x.shape
+    half = width // 2
+    tile = min(128, rows)
+
+    def spec(which):
+        return pl.BlockSpec((tile, half), lambda i: (i, which))
+
+    return call(
+        add_halves_kernel,
+        (rows // tile,),
+        [spec(1), spec(0), spec(0), spec(0)],
+        [spec(1), spec(0)],
+        [sds(to_x.shape, BF)] * 2,
+        nbytes=rows * half * 12,
+        aliases={0: 0, 2: 1},
+    )(to_x, for_x, to_y, for_y)
 
 
 class Scatter:
@@ -125,8 +167,7 @@
     def second(self):
         if self.nt != 4:
             return
-        to_y = add_half(self.to_y, self.for_y, 0)
-        to_x = add_half(self.to_x, self.for_x, 1)
+        to_x, to_y = add_halves(self.to_x, self.for_x, self.to_y, self.for_y)
         self.terms = [
             self.own,
             lax.ppermute(to_x, "tensor", swap_perm(4, 1)),
@@ -440,9 +481,9 @@
 
 
 def cols_back_kernel(nt, steps, nlhs, *refs):
-    lhs, w_ref, outs = refs[:nlhs], refs[nlhs], refs[nlhs + 1 :]
-    depth = w_ref.shape[3]
-    weights = [w_ref[:, c].reshape(-1, depth) for c in range(nlhs)]
+    lhs, w_refs, outs = refs[:nlhs], refs[nlhs : 2 * nlhs], refs[2 * nlhs :]
+    depth = w_refs[0].shape[3]
+    weights = [w[:, 0].reshape(-1, depth) for w in w_refs]
     for slot in range(nt):
         total = dot_nt(lhs[0][slot], weights[0])
         for c in range(1, nlhs):
@@ -450,22 +491,26 @@
         store_piece(outs, nt, slot, steps, total)
 
 
-def mm_back(lhs, weight, nt, group):
-    nd, count, ds, depth = weight.shape
+def mm_back(lhs, weight, channels, nt, group):
+    nd, _, ds, depth = weight.shape
+    count = len(lhs)
     group = shard_group(nd, group)
     rows = lhs[0].shape[1]
     width = nd * ds
     shapes = flat(piece_shapes(nt, rows, width))
+
+    def spec(c):
+        return pl.BlockSpec((group, 1, ds, depth), lambda j: (j, c, 0, 0))
+
     outs = call(
         functools.partial(cols_back_kernel, nt, nd // group, count),
         (nd // group,),
-        [whole_spec(a.shape) for a in lhs]
-        + [pl.BlockSpec((group, count, ds, depth), lambda j: (j, 0, 0, 0))],
+        [whole_spec(a.shape) for a in lhs] + [spec(c) for c in channels],
         out_piece_specs(nt, rows, width, group * ds),
         [sds(s, BF) for s in shapes],
         flops=2 * nt * rows * depth * width * count,
         nbytes=2 * (nt * rows * (depth * count + width) + depth * width * count),
-    )(*lhs, weight)
+    )(*lhs, *[weight] * count)
     return regroup(outs, nt)
 
 
@@ -545,20 +590,20 @@
     def _():
         fill_from_pieces(pieces, full_ref, nt)
 
-    weight = jnp.concatenate([w_ref[j] for j in range(w_ref.shape[0])], axis=1)
+    weight = w_ref[:, 0].reshape(-1, w_ref.shape[3])
     for slot in range(nt):
-        out_ref[slot] = dot_nt(full_ref[slot], weight).astype(BF)
-
-
-def context_back(pieces, weight, nt):
-    nd, hc, ds = weight.shape
+        out_ref[slot] = dot(full_ref[slot], weight).astype(BF)
+
+
+def context_back(pieces, weight, channel, nt):
+    nd, _, ds, hc = weight.shape
     rows, width = pieces[0][0].shape
     step = min(256, hc)
     return call(
         functools.partial(context_back_kernel, nt),
         (hc // step,),
         [whole_spec(a.shape) for a in flat(pieces)]
-        + [pl.BlockSpec((nd, step, ds), lambda j: (0, j, 0))],
+        + [pl.BlockSpec((nd, 1, ds, step), lambda j: (0, channel, 0, j))],
         [whole_spec((nt, rows, width)), pl.BlockSpec((nt, rows, step), lambda j: (0, 0, j))],
         [sds((nt, rows, width), BF), sds((nt, rows, hc), BF)],
         flops=2 * nt * rows * width * hc,
@@ -659,37 +704,39 @@
     )(first, v, gain, *terms, *old)
 
 
-def wgrad_rows_kernel(groups, nrhs, *refs):
-    lhs, rhs, out_ref = refs[:groups], refs[groups : groups * (1 + nrhs)], refs[-1]
+def wgrad_rows_kernel(groups, which, *refs):
+    nlhs = groups * (max(which) + 1)
+    lhs, rhs, out_ref = refs[:nlhs], refs[nlhs : nlhs + groups * len(which)], refs[-1]
     tile = lhs[0].shape[2]
     left = [a[...].reshape(-1, tile).T for a in lhs]
-    for c in range(nrhs):
+    for c, w in enumerate(which):
         total = None
         for g in range(groups):
-            term = dot(left[g], rhs[c * groups + g][...].reshape(left[g].shape[1], -1))
+            a = left[w * groups + g]
+            term = dot(a, rhs[c * groups + g][...].reshape(a.shape[1], -1))
             total = term if total is None else total + term
         out_ref[0, c] = total.astype(BF)
 
 
-def wgrad_rows(lhs, rhs, nd, lo=0, hi=None, into=None):
+def wgrad_rows(lhs, rhs, which, nd, lo=0, hi=None, into=None):
     hi = nd if hi is None else hi
-    groups = len(lhs)
-    nt, rows, width = lhs[0].shape
+    groups = len(lhs[0])
+    nt, rows, width = lhs[0][0].shape
     ds = width // nd
     n = rhs[0][0].shape[2]
     old = [] if into is None else [into]
     return call(
-        functools.partial(wgrad_rows_kernel, groups, len(rhs)),
+        functools.partial(wgrad_rows_kernel, groups, which),
         (hi - lo,),
-        [pl.BlockSpec((nt, rows, ds), lambda j: (0, 0, j + lo))] * groups
+        [pl.BlockSpec((nt, rows, ds), lambda j: (0, 0, j + lo))] * (groups * len(lhs))
         + [whole_spec(a.shape) for r in rhs for a in r]
         + [ANY] * len(old),
         pl.BlockSpec((1, len(rhs), ds, n), lambda j: (j + lo, 0, 0, 0)),
         sds((nd, len(rhs), ds, n), BF),
         flops=2 * groups * nt * rows * ds * (hi - lo) * n * len(rhs),
         nbytes=2 * groups * nt * rows * (width + n * len(rhs)) + 2 * width * n * len(rhs),
-        aliases={groups * (1 + len(rhs)): 0} if old else None,
-    )(*lhs, *[a for r in rhs for a in r], *old)
+        aliases={groups * (len(lhs) + len(rhs)): 0} if old else None,
+    )(*[a for l in lhs for a in l], *[a for r in rhs for a in r], *old)
 
 
 def wgrad_cols_kernel(groups, nd, *refs):
@@ -749,12 +796,13 @@
 
     x = [layer_input[g * per : (g + 1) * per].reshape(per * local, width) for g in range(groups)]
     go = [grad_out[g * per : (g + 1) * per].reshape(per * local, width) for g in range(groups)]
-    x_pieces = [gather_pieces(a, nt) for a in x]
+    Order.last = None
+    x_all = [Gather(a, nt) for a in x]
 
     gains = lax.all_gather(jnp.stack([gain1, gain2]), "dp", axis=1, tiled=True).astype(F32)
     g1, g2 = gains[:1], gains[1:]
-    full_qkv = lax.all_gather(qkv_w, "dp", axis=0, tiled=False)
-    full_out = lax.all_gather(out_w, "dp", axis=0, tiled=False)
+    qkvo_w = jnp.concatenate([qkv_w, out_w.T[None]])
+    full_qkvo = lax.all_gather(qkvo_w, "dp", axis=0, tiled=False)
     full_gateup = lax.all_gather(gateup_w, "dp", axis=0, tiled=False)
     full_down = lax.all_gather(down_w, "dp", axis=0, tiled=False)
 
@@ -776,92 +824,110 @@
     sins = [table(sin, g) for g in range(groups)]
     starts = [start_slot[g * per : (g + 1) * per] for g in range(groups)]
 
-    def after(value, done):
-        return lax.optimization_barrier((value, done))[0]
-
-    Order.last = None
     both = range(groups)
     qkv, ctx, lse, mid, low2, g_mid, g_low = ({} for _ in range(7))
-
-    a1 = [assemble(x_pieces[g], nt, g1) for g in both]
-    go_pieces = {0: gather_pieces(after(go[0], flat(x_pieces[-1])[-1]), nt)}
-    attn_sum = {}
-    for g in both:
-        qkv[g] = project_qkv(a1[g], full_qkv, coss[g], sins[g], nt)
-        if g > 0:
-            attn_sum[g - 1].second()
+    attn_sum, a2_all, ga2, out_sum, ga1 = ({} for _ in range(5))
+    sum1, sum2, gm_all, gmf, g_qkv = ({} for _ in range(5))
+
+    def dp_sum(grad):
+        return lax.psum_scatter(grad, "dp", scatter_dimension=0, tiled=False)
+
+    def project(g):
+        qkv[g] = project_qkv(a1[g], full_qkvo, coss[g], sins[g], nt)
+
+    def attend(g):
         ctx[g], lse[g] = attention_forward(qkv[g], starts[g], slot_of, nt)
-        attn_sum[g] = Scatter(mm_cols(ctx[g], full_out, nt, 4), nt)
-    a2_pieces = {}
-    gof = {}
-    for g in both:
-        if g == groups - 1:
-            gof[0] = assemble(go_pieces[0], nt)
-            attn_sum[g].second()
+        attn_sum[g] = Scatter(mm_back([ctx[g]], full_qkvo, [3], nt, 4), nt)
+
+    def middle(g):
         mid[g], low2[g] = make_middle(x[g], g2, attn_sum[g].terms)
-        a2_pieces[g] = gather_pieces(low2[g], nt)
-    for g in range(1, groups):
-        go_pieces[g] = gather_pieces(after(go[g], flat(a2_pieces[groups - 1])[-1]), nt)
-
-    a2, gate, up, hid = zip(*[gate_up(a2_pieces[g], full_gateup, nt) for g in both])
-    for g in range(1, groups):
-        gof[g] = assemble(go_pieces[g], nt)
-    gof = [gof[g] for g in both]
-    grad_down = wgrad_cols(hid, gof, nd)
-    gg, gu = zip(*[gate_back(gof[g], full_down, gate[g], up[g], nt) for g in both])
-    ga2, out_sum, ga1 = {}, {}, {}
-    ga2[0] = Scatter(mm_back([gg[0], gu[0]], full_gateup, nt, 2), nt)
-    grad_gateup = wgrad_rows(a2, [gg, gu], nd, 0, nd // 2)
-    ga2[0].second()
-    grad_gateup = wgrad_rows(a2, [gg, gu], nd, nd // 2, nd, grad_gateup)
-    sum1, sum2, gm_pieces, gmf, g_qkv = {}, {}, {}, {}, {}
+        a2_all[g] = Gather(low2[g], nt)
+
+    def second_back(g):
+        ga2[g] = Scatter(mm_back([gg[g], gu[g]], full_gateup, [0, 1], nt, 2), nt)
+
+    def project_out(g):
+        out_sum[g] = Scatter(mm_cols(hid[g], full_down, nt, 2), nt)
 
     def residual_back(g):
         g_mid[g], g_low[g], sum2[g] = norm_back(go[g], mid[g], g2, ga2[g].terms)
-        gm_pieces[g] = gather_pieces(g_low[g], nt)
+        gm_all[g] = Gather(g_low[g], nt)
 
     def attention_back(g):
-        gmf[g], g_ctx = context_back(gm_pieces[g], full_out, nt)
+        gmf[g], g_ctx = context_back(gm_all[g].pieces, full_qkvo, 3, nt)
         g_qkv[g] = attention_backward(
             qkv[g], g_ctx, starts[g], lse[g], coss[g], sins[g], slot_of, nt
         )
-        ga1[g] = Scatter(mm_back(g_qkv[g], full_qkv, nt, 4), nt)
-
+
+    def input_back(g):
+        ga1[g] = Scatter(mm_back(g_qkv[g], full_qkvo, [0, 1, 2], nt, 4), nt)
+
+    for g in both:
+        x_all[g].second()
+    a1 = [assemble(x_all[g].pieces, nt, g1) for g in both]
+    go_all = [Gather(link(go[g], a1[-1]), nt) for g in both]
+    project(0)
+    attend(0)
+    project(1)
+    attn_sum[0].second()
+    go_all[0].second()
+    attend(1)
+    go_all[1].second()
+    middle(0)
+    attn_sum[1].second()
+    a2_all[0].second()
+    middle(1)
+    gof = [assemble(go_all[g].pieces, nt) for g in both]
+    a2_all[1].second()
+
+    a2, gate, up, hid = zip(*[gate_up(a2_all[g].pieces, full_gateup, nt) for g in both])
+    grad_down = dp_sum(wgrad_cols(hid, gof, nd))
+    gg, gu = zip(*[gate_back(gof[g], full_down, gate[g], up[g], nt) for g in both])
+    grad_gateup = wgrad_rows([a2], [gg, gu], [0, 0], nd, 0, nd // 2)
+    grad_gateup = wgrad_rows([a2], [gg, gu], [0, 0], nd, nd // 2, nd, grad_gateup)
+    grad_gateup = dp_sum(link(grad_gateup, grad_down))
+    second_back(0)
+    second_back(1)
+    ga2[0].second()
+    project_out(0)
+    ga2[1].second()
     residual_back(0)
-    ga2[1] = Scatter(mm_back([gg[1], gu[1]], full_gateup, nt, 2), nt)
-    out_sum[0] = Scatter(mm_cols(hid[0], full_down, nt, 2), nt)
-    ga2[1].second()
-    attention_back(0)
+    project_out(1)
+    gm_all[0].second()
     residual_back(1)
     out_sum[0].second()
-    out_sum[1] = Scatter(mm_cols(hid[1], full_down, nt, 2), nt)
+    attention_back(0)
+    gm_all[1].second()
+    input_back(0)
+    attention_back(1)
     ga1[0].second()
-    attention_back(1)
-    grad_wout = wgrad_cols([ctx[g] for g in both], [gmf[g] for g in both], nd)
-    grad_qkv = wgrad_rows(a1, [[g_qkv[g][c] for g in both] for c in range(3)], nd)
+    input_back(1)
+    grad_qkvo = wgrad_rows(
+        [a1, [gmf[g] for g in both]],
+        [[g_qkv[g][c] for g in both] for c in range(3)] + [[ctx[g] for g in both]],
+        [0, 0, 0, 1],
+        nd,
+    )
+    out_sum[1].second()
+    grad_qkvo = dp_sum(link(grad_qkvo, grad_gateup))
+    layer_out = layer_out_rows(mid[0], out_sum[0].terms, 0, groups, None)
+    grad_input, sum1[0] = norm_back(g_mid[0], x[0], g1, ga1[0].terms, 0, groups, None)
     ga1[1].second()
-    out_sum[1].second()
-    grad_input = layer_out = None
-    for g in both:
-        layer_out = layer_out_rows(mid[g], out_sum[g].terms, g, groups, layer_out)
-        grad_input, sum1[g] = norm_back(g_mid[g], x[g], g1, ga1[g].terms, g, groups, grad_input)
-
-    def dp_sum(grad):
-        return lax.psum_scatter(grad, "dp", scatter_dimension=0, tiled=False).astype(F32)
+    layer_out = layer_out_rows(mid[1], out_sum[1].terms, 1, groups, layer_out)
+    grad_input, sum1[1] = norm_back(g_mid[1], x[1], g1, ga1[1].terms, 1, groups, grad_input)
 
     gain_sums = jnp.concatenate([sum1[0] + sum1[1], sum2[0] + sum2[1]], axis=0)
     gain_sums = lax.psum(gain_sums, ("dp", "tensor"))
     ds = gain1.shape[0]
     mine = lax.dynamic_slice_in_dim(gain_sums, lax.axis_index("dp") * ds, ds, 1)
-    grad_down, grad_gateup = dp_sum(grad_down), dp_sum(grad_gateup)
     return (
         layer_out.reshape(seqs, local, width),
         grad_input.reshape(seqs, local, width),
-        dp_sum(grad_qkv),
-        dp_sum(grad_wout)[:, :],
+        grad_qkvo[:3].astype(F32),
+        grad_qkvo[3].T.astype(F32),
         mine[0],
-        grad_gateup,
-        grad_down,
+        grad_gateup.astype(F32),
+        grad_down.astype(F32),
         mine[1],
     )
 

time: 1150 us -> 967 us (0.84)
  waiting for transfers between devices: 434 us -> 251 us
  local copies, waits for them, and re-layouts: 37 us -> 58.3 us
    reduce_scatter x4 -> x3, waiting for transfers between devices: 194 us -> 0.01 us  [dp_sum(): return lax.psum_scatter(grad, 'dp', scatter_dimension=0, tiled=False)]
    ppermute x8, waiting for transfers between devices: 17.6 us -> 105 us  [second(): lax.ppermute(to_x, 'tensor', swap_perm(4, 1))]
    ppermute x8, waiting for transfers between devices: 71.7 us -> 16.5 us  [__init__(): self.for_y = lax.ppermute(diag_x, 'tensor', swap_perm(4, 1))]
    unnamed x113 -> x129, local copies, waits for them, and re-layouts: 17.8 us -> 50.4 us
    ppermute x32, waiting for transfers between devices: 121 us -> 97 us  [the longest x8 35.4 us: second(): diag_y = lax.ppermute(right, 'tensor', swap_perm(4, 2))]
    ppermute x8, waiting for transfers between devices: 0.55 us -> 23.5 us  [__init__(): self.for_x = lax.ppermute(diag_y, 'tensor', swap_perm(4, 2))]
    ppermute x8, waiting for transfers between devices: 25.2 us -> 7.78 us  [second(): lax.ppermute(to_y, 'tensor', swap_perm(4, 2))]
    slice x17 -> x1, local copies, waits for them, and re-layouts: 13.3 us -> 0.21 us  [the longest x8 6.78 us: gather_pieces(): diag_x = lax.ppermute(from_y[:, :half], 'tensor', swap_perm(4, 1))]
  transfers between devices with their start and end apart: 72 -> 70, of which waited for: 22 -> 32; matrix products, arithmetic and copies ran while one was open for 3% -> 5% of each run, Pallas kernels for 33% -> 52%
where the time goes in v2:
time: 967 us; the launch traced here: 960 us
  Pallas kernels  501 us (52%)
  waiting for transfers between devices  251 us (26%)
  starting transfers between devices  64.1 us (7%)
  local copies, waits for them, and re-layouts  58.3 us (6%)
  blocking collectives  52.2 us (5%)
  other arithmetic  17.5 us (2%)
  between operations  15.1 us (2%)
    pallas_call x56, Pallas kernels, run(): pl.pallas_call(ordered_body, grid_spec=pltpu.PrefetchScalarGridSpec(num_s...  501 us
    ppermute x8, waiting for transfers between devices, second(): lax.ppermute(to_x, 'tensor', swap_perm(4, 1))  105 us
    unnamed x129, local copies, waits for them, and re-layouts  50.4 us
    psum x1, blocking collectives, per_device(): gain_sums = lax.psum(gain_sums, ('dp', 'tensor'))  39.8 us
    ppermute x8, waiting for transfers between devices, second(): diag_y = lax.ppermute(right, 'tensor', swap_perm(4, 2))  35.4 us
    ppermute x8, waiting for transfers between devices, __init__(): self.from_y = lax.ppermute(block, 'tensor', swap_perm(4, 2))  31.7 us
    ppermute x8, waiting for transfers between devices, __init__(): self.from_x = lax.ppermute(block, 'tensor', swap_perm(4, 1))  23.7 us
    ppermute x8, waiting for transfers between devices, __init__(): self.for_x = lax.ppermute(diag_y, 'tensor', swap_perm(4, 2))  23.5 us
  transfers between devices with their start and end apart: 70, of which 32 were waited for; matrix products, arithmetic and copies ran while one was open for 5% of the time, Pallas kernels for 52%

profile of v2, /device:TPU:0, one launch (start us, length us, event | category | flops | bytes accessed | tf_op | source)
XLA Modules:
  0.0 959.6 jit_solution(7876439646471081343)
XLA Ops:
  47.1 18.4 %collective-permute-done.1.refs_0_.refs_2_ = bf16[256,2048]{1,0:T(8,128)(2,1)} collective-permute-done((bf16[256,2048]{1,0:T(8,128)(2,1)S(1)}, bf16[256,2048]{1,0:T(8,128)(2,1)}, u32[]{:S(2)}, u32[]{:S(2)}) %collective-permute-start.1) | collective-permute-done | bytes 1048608 | tf_op jit(solution)/shard_map/ppermute | solution.py:121
  69.6 12.4 %all_gather.21 = bf16[2,2048]{1,0:T(2,128)(2,1)S(1)} all-gather(bf16[2,256]{1,0:T(2,128)(2,1)S(1)} %pad_maximum_fusion.4), channel_id=1, replica_groups=mesh['dp'=8,'tensor'=4] {'dp'}, dimensions={1}, use_global_device_ids=true | all-gather | bytes 9216 | tf_op jit(solution)/shard_map/all_gather | solution.py:802
  100.1 12.5 %shard_map.158.refs_1_.refs_2_.refs_3_.refs_5_ = bf16[3,4,256,512]{3,2,1,0:T(8,128)(2,1)} custom-call(bf16[4,256,2048]{2,1,0:T(8,128)(2,1)} %shard_map.154.refs_6_.refs_0_, bf16[8,4,256,512]{3,2,1,0:T(8,128)(2,1)} %bitcast.48, f32[4,256,128]{2,1,0:T(8,128)} %get-tuple-element.262.refs_2_.refs_7_, f32[4,256,128]{2,1,0:T(8,128)} %get-tuple-element.260.refs_3_.refs_8_, ...), custom_call_target="tpu_custom_call" | custom-call | flops 2147483648 | bytes 4543829 | tf_op jit(solution)/shard_map/pallas_call | solution.py:48
  112.7 16.2 %shard_map.159 = (bf16[4,256,512]{2,1,0:T(8,128)(2,1)}, f32[1,4,8,256]{3,2,1,0:T(8,128)}) custom-call(s32[4]{0:T(128)} %iota_xor_fusion.refs_0_, bf16[3,4,256,512]{3,2,1,0:T(8,128)(2,1)} %shard_map.158.refs_1_.refs_2_.refs_3_.refs_5_, bf16[3,4,256,512]{3,2,1,0:T(8,128)(2,1)} %shard_map.158.refs_1_.refs_2_.refs_3_.refs_5_, ...), custom_call_target="tpu_custom_call" | custom-call | flops 1431655808 | bytes 1398101 | tf_op jit(solution)/shard_map/pallas_call | solution.py:48
  138.1 12.5 %shard_map.161.refs_4_.refs_1_.refs_2_.refs_3_ = bf16[3,4,256,512]{3,2,1,0:T(8,128)(2,1)} custom-call(bf16[4,256,2048]{2,1,0:T(8,128)(2,1)} %shard_map.155.refs_1_.refs_2_.refs_0_, bf16[8,4,256,512]{3,2,1,0:T(8,128)(2,1)} %bitcast.50, f32[4,256,128]{2,1,0:T(8,128)} %get-tuple-element.263.refs_2_.refs_7_, f32[4,256,128]{2,1,0:T(8,128)} %get-tuple-element.261.refs_3_.refs_8_, ...), custom_call_target="tpu_custom_call" | custom-call | flops 2147483648 | bytes 4543829 | tf_op jit(solution)/shard_map/pallas_call | solution.py:48
  158.4 16.3 %shard_map.164 = (bf16[4,256,512]{2,1,0:T(8,128)(2,1)}, f32[1,4,8,256]{3,2,1,0:T(8,128)}) custom-call(s32[4]{0:T(128)} %iota_xor_fusion.refs_0_, bf16[3,4,256,512]{3,2,1,0:T(8,128)(2,1)} %shard_map.161.refs_4_.refs_1_.refs_2_.refs_3_, bf16[3,4,256,512]{3,2,1,0:T(8,128)(2,1)} %shard_map.161.refs_4_.refs_1_.refs_2_.refs_3_, ...), custom_call_target="tpu_custom_call" | custom-call | flops 1431655808 | bytes 1398101 | tf_op jit(solution)/shard_map/pallas_call | solution.py:48
  216.3 13.1 %collective-permute-done.21.refs_1_ = bf16[256,2048]{1,0:T(8,128)(2,1)S(1)} collective-permute-done((bf16[256,2048]{1,0:T(8,128)(2,1)}, bf16[256,2048]{1,0:T(8,128)(2,1)S(1)}, u32[]{:S(2)}, u32[]{:S(2)}) %collective-permute-start.21) | collective-permute-done | bytes 1048608 | tf_op jit(solution)/shard_map/ppermute | solution.py:120
  236.0 15.9 %collective-permute-done.18.refs_3_ = bf16[256,2048]{1,0:T(8,128)(2,1)S(1)} collective-permute-done((bf16[256,2048]{1,0:T(8,128)(2,1)}, bf16[256,2048]{1,0:T(8,128)(2,1)S(1)}, u32[]{:S(2)}, u32[]{:S(2)}) %collective-permute-start.18) | collective-permute-done | bytes 1048608 | tf_op jit(solution)/shard_map/ppermute | solution.py:173
  263.9 31.0 %collective-permute-done.27.refs_4_ = bf16[256,1024]{1,0:T(8,128)(2,1)S(1)} collective-permute-done((bf16[256,1024]{1,0:T(8,128)(2,1)S(1)}, bf16[256,1024]{1,0:T(8,128)(2,1)S(1)}, u32[]{:S(2)}, u32[]{:S(2)}) %collective-permute-start.27) | collective-permute-done | bytes 524320 | tf_op jit(solution)/shard_map/ppermute | solution.py:128
  316.5 23.4 %shard_map.174 = (bf16[4,256,2048]{2,1,0:T(8,128)(2,1)}, bf16[4,256,2048]{2,1,0:T(8,128)(2,1)}, bf16[4,256,2048]{2,1,0:T(8,128)(2,1)}, bf16[4,256,2048]{2,1,0:T(8,128)(2,1)}) custom-call(bf16[256,2048]{1,0:T(8,128)(2,1)} %get-tuple-element.142.refs_4_.refs_0_, bf16[256,2048]{1,0:T(8,128)(2,1)} %copy-done.19, bf16[256,2048]{1,0:T(8,128)(2,1)} %copy-done.20, ...), custom_call_target="tpu_custom_call" | custom-call | flops 5726623232 | bytes 12582912 | tf_op jit(solution)/shard_map/pallas_call | solution.py:48
  340.9 23.2 %shard_map.175 = (bf16[4,256,2048]{2,1,0:T(8,128)(2,1)}, bf16[4,256,2048]{2,1,0:T(8,128)(2,1)}, bf16[4,256,2048]{2,1,0:T(8,128)(2,1)}, bf16[4,256,2048]{2,1,0:T(8,128)(2,1)}) custom-call(bf16[256,2048]{1,0:T(8,128)(2,1)} %get-tuple-element.147.refs_5_.refs_0_, bf16[256,2048]{1,0:T(8,128)(2,1)} %copy-done.12, bf16[256,2048]{1,0:T(8,128)(2,1)} %copy-done.11, ...), custom_call_target="tpu_custom_call" | custom-call | flops 5726623232 | bytes 12582912 | tf_op jit(solution)/shard_map/pallas_call | solution.py:48
  364.1 23.9 %shard_map.176.refs_4_ = bf16[8,2048,256]{2,1,0:T(8,128)(2,1)} custom-call(bf16[4,256,2048]{2,1,0:T(8,128)(2,1)} %get-tuple-element.153.refs_6_.refs_0_, bf16[4,256,2048]{2,1,0:T(8,128)(2,1)} %get-tuple-element.154.refs_1_.refs_4_.refs_0_, bf16[4,256,2048]{2,1,0:T(8,128)(2,1)} %shard_map.171.refs_5_.refs_2_.refs_0_, ...), custom_call_target="tpu_custom_call" | custom-call | flops 5726623232 | bytes 8388608 | tf_op jit(solution)/shard_map/pallas_call | solution.py:48
  388.1 17.2 %shard_map.177 = (bf16[4,256,2048]{2,1,0:T(8,128)(2,1)}, bf16[4,256,2048]{2,1,0:T(8,128)(2,1)}) custom-call(bf16[4,256,2048]{2,1,0:T(8,128)(2,1)} %shard_map.171.refs_5_.refs_2_.refs_0_, bf16[8,2048,256]{2,1,0:T(8,128)(2,1)} %bitcast.66, bf16[4,256,2048]{2,1,0:T(8,128)(2,1)} %get-tuple-element.156.refs_2_, bf16[4,256,2048]{2,1,0:T(8,128)(2,1)} %get-tuple-element.157.refs_3_, ...), custom_call_target="tpu_custom_call" | custom-call | flops 2863311616 | bytes 9786709 | tf_op jit(solution)/shard_map/pallas_call | solution.py:48
  405.2 17.0 %shard_map.178 = (bf16[4,256,2048]{2,1,0:T(8,128)(2,1)}, bf16[4,256,2048]{2,1,0:T(8,128)(2,1)}) custom-call(bf16[4,256,2048]{2,1,0:T(8,128)(2,1)} %shard_map.172.refs_2_.refs_3_.refs_0_, bf16[8,2048,256]{2,1,0:T(8,128)(2,1)} %bitcast.67, bf16[4,256,2048]{2,1,0:T(8,128)(2,1)} %get-tuple-element.162.refs_2_, bf16[4,256,2048]{2,1,0:T(8,128)(2,1)} %get-tuple-element.163.refs_3_, ...), custom_call_target="tpu_custom_call" | custom-call | flops 2863311616 | bytes 9786709 | tf_op jit(solution)/shard_map/pallas_call | solution.py:48
  422.3 25.9 %shard_map.179.refs_7_ = bf16[8,2,256,2048]{3,2,1,0:T(8,128)(2,1)} custom-call(bf16[4,256,2048]{2,1,0:T(8,128)(2,1)} %get-tuple-element.160.refs_0_, bf16[4,256,2048]{2,1,0:T(8,128)(2,1)} %get-tuple-element.161.refs_1_, bf16[4,256,2048]{2,1,0:T(8,128)(2,1)} %get-tuple-element.158.refs_2_.refs_0_, bf16[4,256,2048]{2,1,0:T(8,128)(2,1)} %get-tuple-element.164.refs_3_.refs_0_, ...), custom_call_target="tpu_custom_call" | custom-call | flops 5726623232 | bytes 13981013 | tf_op jit(solution)/shard_map/pallas_call | solution.py:48
  448.1 14.2 %copy.55.refs_6_ = bf16[8,2,256,2048]{3,2,1,0:T(8,128)(2,1)} copy(bf16[8,2,256,2048]{3,2,1,0:T(8,128)(2,1)} %shard_map.179.refs_7_) | data formatting | bytes 33554432
  462.3 25.8 %shard_map.180.refs_2_ = bf16[8,2,256,2048]{3,2,1,0:T(8,128)(2,1)} custom-call(bf16[4,256,2048]{2,1,0:T(8,128)(2,1)} %get-tuple-element.160.refs_0_, bf16[4,256,2048]{2,1,0:T(8,128)(2,1)} %get-tuple-element.161.refs_1_, bf16[4,256,2048]{2,1,0:T(8,128)(2,1)} %get-tuple-element.158.refs_2_.refs_0_, ...), custom_call_target="tpu_custom_call", output_to_operand_aliasing={{}: (6, {})} | custom-call | flops 5726623232 | bytes 13981013 | tf_op jit(solution)/shard_map/pallas_call | solution.py:48
  488.1 14.1 %copy.56.refs_0_ = bf16[8,2,256,2048]{3,2,1,0:T(8,128)(2,1)} copy(bf16[8,2,256,2048]{3,2,1,0:T(8,128)(2,1)} %shard_map.180.refs_2_) | data formatting | bytes 33554432
  502.3 25.3 %shard_map.182 = (bf16[256,2048]{1,0:T(8,128)(2,1)}, bf16[256,2048]{1,0:T(8,128)(2,1)}, bf16[256,2048]{1,0:T(8,128)(2,1)}, bf16[256,1024]{1,0:T(8,128)(2,1)}, bf16[256,1024]{1,0:T(8,128)(2,1)}) custom-call(bf16[4,256,2048]{2,1,0:T(8,128)(2,1)} %get-tuple-element.158.refs_2_.refs_0_, bf16[4,256,2048]{2,1,0:T(8,128)(2,1)} %get-tuple-element.159.refs_4_.refs_1_, ...), custom_call_target="tpu_custom_call" | custom-call | flops 5726623232 | bytes 9786709 | tf_op jit(solution)/shard_map/pallas_call | solution.py:48
  530.5 24.3 %shard_map.183 = (bf16[256,2048]{1,0:T(8,128)(2,1)}, bf16[256,2048]{1,0:T(8,128)(2,1)}, bf16[256,2048]{1,0:T(8,128)(2,1)}, bf16[256,1024]{1,0:T(8,128)(2,1)}, bf16[256,1024]{1,0:T(8,128)(2,1)}) custom-call(bf16[4,256,2048]{2,1,0:T(8,128)(2,1)} %get-tuple-element.164.refs_3_.refs_0_, bf16[4,256,2048]{2,1,0:T(8,128)(2,1)} %get-tuple-element.165.refs_5_.refs_6_.refs_1_, ...), custom_call_target="tpu_custom_call" | custom-call | flops 5726623232 | bytes 9786709 | tf_op jit(solution)/shard_map/pallas_call | solution.py:48
  562.3 13.6 %shard_map.185 = (bf16[256,2048]{1,0:T(8,128)(2,1)}, bf16[256,2048]{1,0:T(8,128)(2,1)}, bf16[256,2048]{1,0:T(8,128)(2,1)}, bf16[256,1024]{1,0:T(8,128)(2,1)}, bf16[256,1024]{1,0:T(8,128)(2,1)}) custom-call(bf16[4,256,2048]{2,1,0:T(8,128)(2,1)} %get-tuple-element.153.refs_6_.refs_0_, bf16[8,2048,256]{2,1,0:T(8,128)(2,1)} %bitcast.68, ...), custom_call_target="tpu_custom_call" | custom-call | flops 2863311616 | bytes 5592405 | tf_op jit(solution)/shard_map/pallas_call | solution.py:48
  602.7 13.8 %shard_map.188 = (bf16[256,2048]{1,0:T(8,128)(2,1)}, bf16[256,2048]{1,0:T(8,128)(2,1)}, bf16[256,2048]{1,0:T(8,128)(2,1)}, bf16[256,1024]{1,0:T(8,128)(2,1)}, bf16[256,1024]{1,0:T(8,128)(2,1)}) custom-call(bf16[4,256,2048]{2,1,0:T(8,128)(2,1)} %get-tuple-element.154.refs_1_.refs_4_.refs_0_, bf16[8,2048,256]{2,1,0:T(8,128)(2,1)} %bitcast.69, ...), custom_call_target="tpu_custom_call" | custom-call | flops 2863311616 | bytes 5592405 | tf_op jit(solution)/shard_map/pallas_call | solution.py:48
  627.9 19.5 %collective-permute-done.46.refs_4_ = bf16[256,2048]{1,0:T(8,128)(2,1)} collective-permute-done((bf16[256,2048]{1,0:T(8,128)(2,1)}, bf16[256,2048]{1,0:T(8,128)(2,1)}, u32[]{:S(2)}, u32[]{:S(2)}) %collective-permute-start.46) | collective-permute-done | bytes 1048608 | tf_op jit(solution)/shard_map/ppermute | solution.py:173
  659.9 17.0 %collective-permute-done.44.refs_1_ = bf16[256,1024]{1,0:T(8,128)(2,1)S(1)} collective-permute-done((bf16[256,1024]{1,0:T(8,128)(2,1)S(1)}, bf16[256,1024]{1,0:T(8,128)(2,1)S(1)}, u32[]{:S(2)}, u32[]{:S(2)}) %collective-permute-start.44) | collective-permute-done | bytes 524320 | tf_op jit(solution)/shard_map/ppermute | solution.py:165
  689.7 23.6 %shard_map.193 = (bf16[4,256,512]{2,1,0:T(8,128)(2,1)}, bf16[4,256,512]{2,1,0:T(8,128)(2,1)}, bf16[4,256,512]{2,1,0:T(8,128)(2,1)}) custom-call(s32[4]{0:T(128)} %iota_xor_fusion.refs_0_, bf16[3,4,256,512]{3,2,1,0:T(8,128)(2,1)} %shard_map.158.refs_1_.refs_2_.refs_3_.refs_5_, bf16[3,4,256,512]{3,2,1,0:T(8,128)(2,1)} %shard_map.158.refs_1_.refs_2_.refs_3_.refs_5_, ...), custom_call_target="tpu_custom_call" | custom-call | flops 3579139328 | bytes 2446677 | tf_op jit(solution)/shard_map/pallas_call | solution.py:48
  718.4 11.7 %shard_map.195 = (bf16[256,2048]{1,0:T(8,128)(2,1)}, bf16[256,2048]{1,0:T(8,128)(2,1)}, bf16[256,2048]{1,0:T(8,128)(2,1)}, bf16[256,1024]{1,0:T(8,128)(2,1)}, bf16[256,1024]{1,0:T(8,128)(2,1)}) custom-call(bf16[4,256,512]{2,1,0:T(8,128)(2,1)} %get-tuple-element.201.refs_0_.refs_4_, bf16[4,256,512]{2,1,0:T(8,128)(2,1)} %get-tuple-element.202.refs_1_.refs_6_, ...), custom_call_target="tpu_custom_call" | custom-call | flops 2147483648 | bytes 4543829 | tf_op jit(solution)/shard_map/pallas_call | solution.py:48
  741.4 23.6 %shard_map.197 = (bf16[4,256,512]{2,1,0:T(8,128)(2,1)}, bf16[4,256,512]{2,1,0:T(8,128)(2,1)}, bf16[4,256,512]{2,1,0:T(8,128)(2,1)}) custom-call(s32[4]{0:T(128)} %iota_xor_fusion.refs_0_, bf16[3,4,256,512]{3,2,1,0:T(8,128)(2,1)} %shard_map.161.refs_4_.refs_1_.refs_2_.refs_3_, bf16[3,4,256,512]{3,2,1,0:T(8,128)(2,1)} %shard_map.161.refs_4_.refs_1_.refs_2_.refs_3_, ...), custom_call_target="tpu_custom_call" | custom-call | flops 3579139328 | bytes 2446677 | tf_op jit(solution)/shard_map/pallas_call | solution.py:48
  779.7 24.6 %shard_map.200.refs_4_.refs_0_ = bf16[8,4,256,512]{3,2,1,0:T(8,128)(2,1)} custom-call(bf16[4,256,2048]{2,1,0:T(8,128)(2,1)} %shard_map.154.refs_6_.refs_0_, bf16[4,256,2048]{2,1,0:T(8,128)(2,1)} %shard_map.155.refs_1_.refs_2_.refs_0_, bf16[4,256,2048]{2,1,0:T(8,128)(2,1)} %get-tuple-element.195.refs_2_, bf16[4,256,2048]{2,1,0:T(8,128)(2,1)} %get-tuple-element.204.refs_3_, ...), custom_call_target="tpu_custom_call" | custom-call | flops 5726623232 | bytes 8388608 | tf_op jit(solution)/shard_map/pallas_call | solution.py:48
  813.1 21.0 %collective-permute-done.56.refs_2_ = bf16[256,2048]{1,0:T(8,128)(2,1)S(1)} collective-permute-done((bf16[256,2048]{1,0:T(8,128)(2,1)}, bf16[256,2048]{1,0:T(8,128)(2,1)S(1)}, u32[]{:S(2)}, u32[]{:S(2)}) %collective-permute-start.56) | collective-permute-done | bytes 1048608 | tf_op jit(solution)/shard_map/ppermute | solution.py:173
  836.4 20.3 %collective-permute-done.60.refs_4_ = bf16[256,2048]{1,0:T(8,128)(2,1)} collective-permute-done((bf16[256,2048]{1,0:T(8,128)(2,1)}, bf16[256,2048]{1,0:T(8,128)(2,1)}, u32[]{:S(2)}, u32[]{:S(2)}) %collective-permute-start.60) | collective-permute-done | bytes 1048608 | tf_op jit(solution)/shard_map/ppermute | solution.py:173
  875.0 14.7 %collective-permute-done.54.refs_2_ = bf16[256,2048]{1,0:T(8,128)(2,1)S(1)} collective-permute-done((bf16[256,2048]{1,0:T(8,128)(2,1)}, bf16[256,2048]{1,0:T(8,128)(2,1)S(1)}, u32[]{:S(2)}, u32[]{:S(2)}) %collective-permute-start.54) | collective-permute-done | bytes 1048608 | tf_op jit(solution)/shard_map/ppermute | solution.py:173
  907.3 39.8 %psum.7 = f32[2,2048]{1,0:T(2,128)S(1)} all-reduce(f32[2,2048]{1,0:T(2,128)S(1)} %pad_maximum_fusion.3), channel_id=1, replica_groups=mesh['dp'=8,'tensor'=4] {'dp','tensor'}, use_global_device_ids=true, to_apply=%region_5.6 | all-reduce | flops 4096 | bytes 32768 | tf_op jit(solution)/shard_map/psum | solution.py:920
  (339 shorter events, 318.8 us)
Async XLA Ops:
  7.2 93.0 %all-gather.7.cloned.1.call-start = ((), (), s32[]{:S(2)}) async-start(), calls=%async_computation.6 | async-start | bytes 9437184 | tf_op jit(solution)/shard_map/all_gather | solution.py:805
  10.5 305.6 %all-gather.9.cloned.1.call-start = ((), (), s32[]{:S(2)}) async-start(), calls=%async_computation.7 | async-start | bytes 18874368 | tf_op jit(solution)/shard_map/all_gather | solution.py:806
  11.3 376.8 %all-gather.11.cloned.1.call-start = ((), (), s32[]{:S(2)}) async-start(), calls=%async_computation.8 | async-start | bytes 9437184 | tf_op jit(solution)/shard_map/all_gather | solution.py:807
  12.0 490.2 %reduce-scatter.4.cloned.1.call-start = ((), (), s32[]{:S(2)}) async-start(), calls=%async_computation.3 | async-start | bytes 9437184 | tf_op jit(solution)/shard_map/reduce_scatter | solution.py:833
  18.3 47.1 %collective-permute-start.1 = (bf16[256,2048]{1,0:T(8,128)(2,1)S(1)}, bf16[256,2048]{1,0:T(8,128)(2,1)}, u32[]{:S(2)}, u32[]{:S(2)}) collective-permute-start(bf16[256,2048]{1,0:T(8,128)(2,1)S(1)} %get-tuple-element.259.refs_0_.refs_1_), channel_id=1, source_target_pairs={{0,2},{1,3},{2,0},{3,1},{4,6},{5,7},{6,4},{7,5},{8,10},{9,11},{10,... | collective-permute-start | bytes 3145736 | tf_op jit(solution)/shard_map/ppermute | solution.py:121
  18.8 46.6 %collective-permute-start = (bf16[256,2048]{1,0:T(8,128)(2,1)S(1)}, bf16[256,2048]{1,0:T(8,128)(2,1)}, u32[]{:S(2)}, u32[]{:S(2)}) collective-permute-start(bf16[256,2048]{1,0:T(8,128)(2,1)S(1)} %get-tuple-element.259.refs_0_.refs_1_), channel_id=1, source_target_pairs={{0,1},{1,0},{2,3},{3,2},{4,5},{5,4},{6,7},{7,6},{8,9},{9,8},{10,11... | collective-permute-start | bytes 3145736 | tf_op jit(solution)/shard_map/ppermute | solution.py:120
  45.0 37.5 %collective-permute-start.6 = (bf16[256,1024]{1,0:T(8,128)(2,1)}, bf16[256,1024]{1,0:T(8,128)(2,1)S(1)}, u32[]{:S(2)}, u32[]{:S(2)}) collective-permute-start(bf16[256,1024]{1,0:T(8,128)(2,1)} %get-tuple-element.123), channel_id=1, source_target_pairs={{0,1},{1,0},{2,3},{3,2},{4,5},{5,4},{6,7},{7,6},{8,9},{9,8},{10,11... | collective-permute-start | bytes 1572872 | tf_op jit(solution)/shard_map/ppermute | solution.py:127
  45.0 37.5 %collective-permute-start.7 = (bf16[256,1024]{1,0:T(8,128)(2,1)}, bf16[256,1024]{1,0:T(8,128)(2,1)S(1)}, u32[]{:S(2)}, u32[]{:S(2)}) collective-permute-start(bf16[256,1024]{1,0:T(8,128)(2,1)} %get-tuple-element.120.refs_2_), channel_id=1, source_target_pairs={{0,2},{1,3},{2,0},{3,1},{4,6},{5,7},{6,4},{7,5},{8,10},{9,11},{10,... | collective-permute-start | bytes 1572872 | tf_op jit(solution)/shard_map/ppermute | solution.py:128
  96.1 58.0 %collective-permute-start.9 = (bf16[256,2048]{1,0:T(8,128)(2,1)}, bf16[256,2048]{1,0:T(8,128)(2,1)S(1)}, u32[]{:S(2)}, u32[]{:S(2)}) collective-permute-start(bf16[256,2048]{1,0:T(8,128)(2,1)} %shard_map.156.refs_2_.refs_0_), channel_id=1, source_target_pairs={{0,1},{1,0},{2,3},{3,2},{4,5},{5,4},{6,7},{7,6},{8,9},{9,8},{10,11... | collective-permute-start | bytes 3145736 | tf_op jit(solution)/shard_map/ppermute | solution.py:120
  99.6 55.8 %collective-permute-start.8 = (bf16[256,2048]{1,0:T(8,128)(2,1)}, bf16[256,2048]{1,0:T(8,128)(2,1)S(1)}, u32[]{:S(2)}, u32[]{:S(2)}) collective-permute-start(bf16[256,2048]{1,0:T(8,128)(2,1)} %shard_map.156.refs_2_.refs_0_), channel_id=1, source_target_pairs={{0,2},{1,3},{2,0},{3,1},{4,6},{5,7},{6,4},{7,5},{8,10},{9,11},{10,... | collective-permute-start | bytes 3145736 | tf_op jit(solution)/shard_map/ppermute | solution.py:121
  136.3 45.9 %collective-permute-start.17 = (bf16[256,2048]{1,0:T(8,128)(2,1)S(1)}, bf16[256,2048]{1,0:T(8,128)(2,1)}, u32[]{:S(2)}, u32[]{:S(2)}) collective-permute-start(bf16[256,2048]{1,0:T(8,128)(2,1)S(1)} %copy-done), channel_id=1, source_target_pairs={{0,1},{1,0},{2,3},{3,2},{4,5},{5,4},{6,7},{7,6},{8,9},{9,8},{10,11... | collective-permute-start | bytes 3145736 | tf_op jit(solution)/shard_map/ppermute | solution.py:120
  153.8 41.0 %collective-permute-start.14 = (bf16[256,2048]{1,0:T(8,128)(2,1)}, bf16[256,2048]{1,0:T(8,128)(2,1)}, u32[]{:S(2)}, u32[]{:S(2)}) collective-permute-start(bf16[256,2048]{1,0:T(8,128)(2,1)} %get-tuple-element.140), channel_id=1, source_target_pairs={{0,1},{1,0},{2,3},{3,2},{4,5},{5,4},{6,7},{7,6},{8,9},{9,8},{10,11... | collective-permute-start | bytes 3145736 | tf_op jit(solution)/shard_map/ppermute | solution.py:173
  154.1 45.3 %collective-permute-start.15 = (bf16[256,2048]{1,0:T(8,128)(2,1)}, bf16[256,2048]{1,0:T(8,128)(2,1)}, u32[]{:S(2)}, u32[]{:S(2)}) collective-permute-start(bf16[256,2048]{1,0:T(8,128)(2,1)} %get-tuple-element.130.refs_2_), channel_id=1, source_target_pairs={{0,2},{1,3},{2,0},{3,1},{4,6},{5,7},{6,4},{7,5},{8,10},{9,11},{10,... | collective-permute-start | bytes 3145736 | tf_op jit(solution)/shard_map/ppermute | solution.py:174
  213.7 38.2 %collective-permute-start.18 = (bf16[256,2048]{1,0:T(8,128)(2,1)}, bf16[256,2048]{1,0:T(8,128)(2,1)S(1)}, u32[]{:S(2)}, u32[]{:S(2)}) collective-permute-start(bf16[256,2048]{1,0:T(8,128)(2,1)} %get-tuple-element.143), channel_id=1, source_target_pairs={{0,1},{1,0},{2,3},{3,2},{4,5},{5,4},{6,7},{7,6},{8,9},{9,8},{10,11... | collective-permute-start | bytes 3145736 | tf_op jit(solution)/shard_map/ppermute | solution.py:173
  213.9 39.4 %collective-permute-start.19 = (bf16[256,2048]{1,0:T(8,128)(2,1)}, bf16[256,2048]{1,0:T(8,128)(2,1)}, u32[]{:S(2)}, u32[]{:S(2)}) collective-permute-start(bf16[256,2048]{1,0:T(8,128)(2,1)} %get-tuple-element.144.refs_2_), channel_id=1, source_target_pairs={{0,2},{1,3},{2,0},{3,1},{4,6},{5,7},{6,4},{7,5},{8,10},{9,11},{10,... | collective-permute-start | bytes 3145736 | tf_op jit(solution)/shard_map/ppermute | solution.py:174
  214.6 48.6 %collective-permute-start.26 = (bf16[256,1024]{1,0:T(8,128)(2,1)}, bf16[256,1024]{1,0:T(8,128)(2,1)}, u32[]{:S(2)}, u32[]{:S(2)}) collective-permute-start(bf16[256,1024]{1,0:T(8,128)(2,1)} %get-tuple-element.149), channel_id=1, source_target_pairs={{0,1},{1,0},{2,3},{3,2},{4,5},{5,4},{6,7},{7,6},{8,9},{9,8},{10,11... | collective-permute-start | bytes 1572872 | tf_op jit(solution)/shard_map/ppermute | solution.py:127
  257.4 53.6 %collective-permute-start.23 = (bf16[256,2048]{1,0:T(8,128)(2,1)}, bf16[256,2048]{1,0:T(8,128)(2,1)S(1)}, u32[]{:S(2)}, u32[]{:S(2)}) collective-permute-start(bf16[256,2048]{1,0:T(8,128)(2,1)} %get-tuple-element.147.refs_5_.refs_0_), channel_id=1, source_target_pairs={{0,2},{1,3},{2,0},{3,1},{4,6},{5,7},{6,4},{7,5},{8,10},{9,11},{10,... | collective-permute-start | bytes 3145736 | tf_op jit(solution)/shard_map/ppermute | solution.py:121
  258.0 53.0 %collective-permute-start.22 = (bf16[256,2048]{1,0:T(8,128)(2,1)}, bf16[256,2048]{1,0:T(8,128)(2,1)S(1)}, u32[]{:S(2)}, u32[]{:S(2)}) collective-permute-start(bf16[256,2048]{1,0:T(8,128)(2,1)} %get-tuple-element.147.refs_5_.refs_0_), channel_id=1, source_target_pairs={{0,1},{1,0},{2,3},{3,2},{4,5},{5,4},{6,7},{7,6},{8,9},{9,8},{10,11... | collective-permute-start | bytes 3145736 | tf_op jit(solution)/shard_map/ppermute | solution.py:120
  263.2 43.0 %collective-permute-start.25 = (bf16[256,1024]{1,0:T(8,128)(2,1)S(1)}, bf16[256,1024]{1,0:T(8,128)(2,1)}, u32[]{:S(2)}, u32[]{:S(2)}) collective-permute-start(bf16[256,1024]{1,0:T(8,128)(2,1)S(1)} %copy-done.29), channel_id=1, source_target_pairs={{0,2},{1,3},{2,0},{3,1},{4,6},{5,7},{6,4},{7,5},{8,10},{9,11},{10,... | collective-permute-start | bytes 1572872 | tf_op jit(solution)/shard_map/ppermute | solution.py:128
  388.0 419.7 %reduce-scatter.6.cloned.1.call-start = ((), (), s32[]{:S(2)}) async-start(), calls=%async_computation.4 | async-start | bytes 18874368 | tf_op jit(solution)/shard_map/reduce_scatter | solution.py:833
  502.2 445.6 %reduce-scatter.8.cloned.1.call-start = ((), (), s32[]{:S(2)}) async-start(), calls=%async_computation.5 | async-start | bytes 9437184 | tf_op jit(solution)/shard_map/reduce_scatter | solution.py:833
  600.0 47.4 %collective-permute-start.46 = (bf16[256,2048]{1,0:T(8,128)(2,1)}, bf16[256,2048]{1,0:T(8,128)(2,1)}, u32[]{:S(2)}, u32[]{:S(2)}) collective-permute-start(bf16[256,2048]{1,0:T(8,128)(2,1)} %get-tuple-element.192), channel_id=1, source_target_pairs={{0,1},{1,0},{2,3},{3,2},{4,5},{5,4},{6,7},{7,6},{8,9},{9,8},{10,11... | collective-permute-start | bytes 3145736 | tf_op jit(solution)/shard_map/ppermute | solution.py:173
  600.5 46.9 %collective-permute-start.47 = (bf16[256,2048]{1,0:T(8,128)(2,1)S(1)}, bf16[256,2048]{1,0:T(8,128)(2,1)}, u32[]{:S(2)}, u32[]{:S(2)}) collective-permute-start(bf16[256,2048]{1,0:T(8,128)(2,1)S(1)} %copy-done.14), channel_id=1, source_target_pairs={{0,2},{1,3},{2,0},{3,1},{4,6},{5,7},{6,4},{7,5},{8,10},{9,11},{10,... | collective-permute-start | bytes 3145736 | tf_op jit(solution)/shard_map/ppermute | solution.py:174
  601.8 56.8 %collective-permute-start.45 = (bf16[256,1024]{1,0:T(8,128)(2,1)}, bf16[256,1024]{1,0:T(8,128)(2,1)}, u32[]{:S(2)}, u32[]{:S(2)}) collective-permute-start(bf16[256,1024]{1,0:T(8,128)(2,1)} %get-tuple-element.190), channel_id=1, source_target_pairs={{0,1},{1,0},{2,3},{3,2},{4,5},{5,4},{6,7},{7,6},{8,9},{9,8},{10,11... | collective-permute-start | bytes 1572872 | tf_op jit(solution)/shard_map/ppermute | solution.py:164
  652.7 60.6 %collective-permute-start.49 = (bf16[256,2048]{1,0:T(8,128)(2,1)}, bf16[256,2048]{1,0:T(8,128)(2,1)S(1)}, u32[]{:S(2)}, u32[]{:S(2)}) collective-permute-start(bf16[256,2048]{1,0:T(8,128)(2,1)} %get-tuple-element.196.refs_0_), channel_id=1, source_target_pairs={{0,2},{1,3},{2,0},{3,1},{4,6},{5,7},{6,4},{7,5},{8,10},{9,11},{10,... | collective-permute-start | bytes 3145736 | tf_op jit(solution)/shard_map/ppermute | solution.py:121
  654.0 59.3 %collective-permute-start.48 = (bf16[256,2048]{1,0:T(8,128)(2,1)}, bf16[256,2048]{1,0:T(8,128)(2,1)S(1)}, u32[]{:S(2)}, u32[]{:S(2)}) collective-permute-start(bf16[256,2048]{1,0:T(8,128)(2,1)} %get-tuple-element.196.refs_0_), channel_id=1, source_target_pairs={{0,1},{1,0},{2,3},{3,2},{4,5},{5,4},{6,7},{7,6},{8,9},{9,8},{10,11... | collective-permute-start | bytes 3145736 | tf_op jit(solution)/shard_map/ppermute | solution.py:120
  732.4 72.0 %collective-permute-start.38 = (bf16[256,1024]{1,0:T(8,128)(2,1)S(1)}, bf16[256,1024]{1,0:T(8,128)(2,1)S(1)}, u32[]{:S(2)}, u32[]{:S(2)}) collective-permute-start(bf16[256,1024]{1,0:T(8,128)(2,1)S(1)} %copy-done.27), channel_id=1, source_target_pairs={{0,2},{1,3},{2,0},{3,1},{4,6},{5,7},{6,4},{7,5},{8,10},{9,11},{10,... | collective-permute-start | bytes 1572872 | tf_op jit(solution)/shard_map/ppermute | solution.py:165
  733.4 71.0 %collective-permute-start.39 = (bf16[256,1024]{1,0:T(8,128)(2,1)}, bf16[256,1024]{1,0:T(8,128)(2,1)S(1)}, u32[]{:S(2)}, u32[]{:S(2)}) collective-permute-start(bf16[256,1024]{1,0:T(8,128)(2,1)} %get-tuple-element.184), channel_id=1, source_target_pairs={{0,1},{1,0},{2,3},{3,2},{4,5},{5,4},{6,7},{7,6},{8,9},{9,8},{10,11... | collective-permute-start | bytes 1572872 | tf_op jit(solution)/shard_map/ppermute | solution.py:164
  810.3 46.4 %collective-permute-start.60 = (bf16[256,2048]{1,0:T(8,128)(2,1)}, bf16[256,2048]{1,0:T(8,128)(2,1)}, u32[]{:S(2)}, u32[]{:S(2)}) collective-permute-start(bf16[256,2048]{1,0:T(8,128)(2,1)} %get-tuple-element.223), channel_id=1, source_target_pairs={{0,1},{1,0},{2,3},{3,2},{4,5},{5,4},{6,7},{7,6},{8,9},{9,8},{10,11... | collective-permute-start | bytes 3145736 | tf_op jit(solution)/shard_map/ppermute | solution.py:173
  811.2 50.4 %collective-permute-start.61 = (bf16[256,2048]{1,0:T(8,128)(2,1)S(1)}, bf16[256,2048]{1,0:T(8,128)(2,1)}, u32[]{:S(2)}, u32[]{:S(2)}) collective-permute-start(bf16[256,2048]{1,0:T(8,128)(2,1)S(1)} %copy-done.13), channel_id=1, source_target_pairs={{0,2},{1,3},{2,0},{3,1},{4,6},{5,7},{6,4},{7,5},{8,10},{9,11},{10,... | collective-permute-start | bytes 3145736 | tf_op jit(solution)/shard_map/ppermute | solution.py:174
  812.2 55.7 %collective-permute-start.59 = (bf16[256,1024]{1,0:T(8,128)(2,1)}, bf16[256,1024]{1,0:T(8,128)(2,1)}, u32[]{:S(2)}, u32[]{:S(2)}) collective-permute-start(bf16[256,1024]{1,0:T(8,128)(2,1)} %get-tuple-element.220), channel_id=1, source_target_pairs={{0,1},{1,0},{2,3},{3,2},{4,5},{5,4},{6,7},{7,6},{8,9},{9,8},{10,11... | collective-permute-start | bytes 1572872 | tf_op jit(solution)/shard_map/ppermute | solution.py:164
  835.5 54.3 %collective-permute-start.54 = (bf16[256,2048]{1,0:T(8,128)(2,1)}, bf16[256,2048]{1,0:T(8,128)(2,1)S(1)}, u32[]{:S(2)}, u32[]{:S(2)}) collective-permute-start(bf16[256,2048]{1,0:T(8,128)(2,1)} %get-tuple-element.214), channel_id=1, source_target_pairs={{0,1},{1,0},{2,3},{3,2},{4,5},{5,4},{6,7},{7,6},{8,9},{9,8},{10,11... | collective-permute-start | bytes 3145736 | tf_op jit(solution)/shard_map/ppermute | solution.py:173
  (99 other events, 1528.2 us)
Sparse Core Ops, SparseCore 0:
  10.7 84.8 all-gather.6
  97.1 149.6 all-gather.8
  248.4 80.2 all-gather.10
  388.1 88.1 reduce-scatter.3
  502.3 166.5 reduce-scatter.5
  807.9 87.5 reduce-scatter.7

commit v3 on v2

--- a/solution.py
+++ b/solution.py
@@ -2,6 +2,7 @@
 
 import jax
 import jax.numpy as jnp
+import numpy as np
 from jax import lax
 from jax.experimental import pallas as pl
 from jax.experimental.pallas import tpu as pltpu
@@ -15,7 +16,10 @@
 MASKED_SCORE = -1e30
 BF = jnp.bfloat16
 F32 = jnp.float32
-VMEM_LIMIT = 60 * 1024 * 1024
+VMEM_SLACK = 8 * 1024 * 1024
+VMEM_SMALL = 24 * 1024 * 1024
+VMEM_LARGE = 44 * 1024 * 1024
+PIN_BYTES = 3 * 1024 * 1024
 SMALL = 3
 
 NT = (((1,), (1,)), ((), ()))
@@ -33,14 +37,44 @@
     last = None
 
 
+HBM = pl.BlockSpec(memory_space=pltpu.HBM)
 ANY = pl.BlockSpec(memory_space=pl.ANY)
+
+
+def is_large(array):
+    return array.size * array.dtype.itemsize >= PIN_BYTES
+
+
+def pin(array):
+    return pltpu.with_memory_space_constraint(array, pltpu.HBM) if is_large(array) else array
+
+
+def pinned(shape):
+    return pltpu.HBM(shape.shape, shape.dtype) if is_large(shape) else shape
+
+
+def block_bytes(spec, dtype):
+    if spec.block_shape is None:
+        return 0
+    count = 2 if spec.pipeline_mode is None else spec.pipeline_mode.buffer_count
+    return count * int(np.prod([d for d in spec.block_shape if d])) * np.dtype(dtype).itemsize
 
 
 def call(body, grid, in_specs, out_specs, out_shape, scratch=(), flops=0, nbytes=0, aliases=None, prefetch=0):
     first_extra = prefetch + len(in_specs)
+    many = isinstance(out_shape, (list, tuple))
+    out_blocks = list(zip(out_specs, out_shape)) if many else [(out_specs, out_shape)]
 
     def run(*args):
-        extra = [] if Order.last is None else [Order.last]
+        extra = [] if Order.last is None or any(a is Order.last for a in args) else [pin(Order.last)]
+
+        blocks = list(zip(in_specs, args[prefetch:])) + out_blocks
+        vmem = VMEM_SLACK + sum(block_bytes(spec, a.dtype) for spec, a in blocks)
+        vmem += sum(int(np.prod(m.shape)) * np.dtype(m.dtype).itemsize for m in scratch)
+        if vmem > VMEM_SMALL:
+            vmem = VMEM_LARGE
+
+        args = [pin(a) for a in args]
 
         def ordered_body(*refs):
             body(*refs[:first_extra], *refs[first_extra + len(extra) :])
@@ -54,10 +88,10 @@
                 out_specs=out_specs,
                 scratch_shapes=list(scratch),
             ),
-            out_shape=out_shape,
+            out_shape=[pinned(a) for a in out_shape] if many else pinned(out_shape),
             input_output_aliases=aliases or {},
             cost_estimate=pl.CostEstimate(flops=flops // SMALL, bytes_accessed=nbytes // SMALL, transcendentals=0),
-            compiler_params=pltpu.CompilerParams(vmem_limit_bytes=VMEM_LIMIT),
+            compiler_params=pltpu.CompilerParams(vmem_limit_bytes=vmem),
         )(*args, *extra)
         Order.last = outs[-1] if isinstance(outs, (list, tuple)) else outs
         return outs
@@ -70,7 +104,7 @@
 
 
 def link(value, done):
-    return call(link_kernel, (1,), [ANY, ANY], ANY, sds(value.shape, value.dtype), aliases={0: 0})(value, done)
+    return call(link_kernel, (1,), [HBM, HBM], HBM, sds(value.shape, value.dtype), aliases={0: 0})(value, done)
 
 
 def whole_spec(shape, buffers=1):
@@ -242,31 +276,34 @@
     return u * cos + turn(u * sin)
 
 
-def assemble_kernel(nt, normed, *refs):
-    pieces, full_ref = refs[: -1 - normed], refs[-1]
-    fill_from_pieces(pieces, full_ref, nt)
+def assemble_kernel(nt, count, normed, *refs):
+    full_ref = refs[-1]
+    fill_from_pieces(refs[:count], full_ref, nt)
     if normed:
-        gain = refs[-2][...]
+        gain = refs[count][...]
         for slot in range(nt):
             x = full_ref[slot].astype(F32)
             scale = lax.rsqrt(jnp.mean(x * x, axis=-1, keepdims=True) + NORM_EPS)
             full_ref[slot] = (x * scale * gain).astype(BF)
 
 
-def assemble(pieces, nt, gain=None):
+def assemble(pieces, nt, group, groups, gain=None, ready=()):
     rows, width = pieces[0][0].shape
+    rows //= groups
     tile = min(64, rows)
+    first = group * (rows // tile)
     items = flat(pieces)
     extra = [] if gain is None else [gain]
     return call(
-        functools.partial(assemble_kernel, nt, len(extra)),
+        functools.partial(assemble_kernel, nt, len(items), len(extra)),
         (rows // tile,),
-        [pl.BlockSpec((tile, a.shape[1]), lambda i: (i, 0)) for a in items]
-        + [whole_spec(a.shape) for a in extra],
+        [pl.BlockSpec((tile, a.shape[1]), lambda i: (i + first, 0)) for a in items]
+        + [whole_spec(a.shape) for a in extra]
+        + [ANY] * len(ready),
         pl.BlockSpec((nt, tile, width), lambda i: (0, i, 0)),
         sds((nt, rows, width), BF),
         nbytes=4 * nt * rows * width,
-    )(*items, *extra)
+    )(*items, *extra, *ready)
 
 
 def qkv_kernel(nt, a1_ref, w_ref, cos_ref, sin_ref, out_ref):
@@ -480,38 +517,48 @@
     return regroup(outs, nt)
 
 
-def cols_back_kernel(nt, steps, nlhs, *refs):
-    lhs, w_refs, outs = refs[:nlhs], refs[nlhs : 2 * nlhs], refs[2 * nlhs :]
+def cols_back_kernel(nt, steps, nlhs, nseen, *refs):
+    lhs, w_refs, outs = refs[:nlhs], refs[nlhs : 2 * nlhs], refs[2 * nlhs + nseen :]
     depth = w_refs[0].shape[3]
     weights = [w[:, 0].reshape(-1, depth) for w in w_refs]
+    sums = None
     for slot in range(nt):
         total = dot_nt(lhs[0][slot], weights[0])
         for c in range(1, nlhs):
             total += dot_nt(lhs[c][slot], weights[c])
-        store_piece(outs, nt, slot, steps, total)
-
-
-def mm_back(lhs, weight, channels, nt, group):
+        if nseen:
+            part = jnp.sum(total * refs[2 * nlhs][slot].astype(F32), axis=0, keepdims=True)
+            sums = part if sums is None else sums + part
+        store_piece(outs[: len(outs) - nseen], nt, slot, steps, total)
+    if nseen:
+        outs[-1][...] = sums
+
+
+def mm_back(lhs, weight, channels, nt, group, seen=None):
     nd, _, ds, depth = weight.shape
     count = len(lhs)
     group = shard_group(nd, group)
     rows = lhs[0].shape[1]
     width = nd * ds
     shapes = flat(piece_shapes(nt, rows, width))
+    step = group * ds
+    more = [] if seen is None else [seen]
 
     def spec(c):
         return pl.BlockSpec((group, 1, ds, depth), lambda j: (j, c, 0, 0))
 
     outs = call(
-        functools.partial(cols_back_kernel, nt, nd // group, count),
+        functools.partial(cols_back_kernel, nt, nd // group, count, len(more)),
         (nd // group,),
-        [whole_spec(a.shape) for a in lhs] + [spec(c) for c in channels],
-        out_piece_specs(nt, rows, width, group * ds),
-        [sds(s, BF) for s in shapes],
+        [whole_spec(a.shape) for a in lhs]
+        + [spec(c) for c in channels]
+        + [pl.BlockSpec((nt, rows, step), lambda j: (0, 0, j)) for _ in more],
+        out_piece_specs(nt, rows, width, step) + [pl.BlockSpec((1, step), lambda j: (0, j)) for _ in more],
+        [sds(s, BF) for s in shapes] + [sds((1, width), F32) for _ in more],
         flops=2 * nt * rows * depth * width * count,
         nbytes=2 * (nt * rows * (depth * count + width) + depth * width * count),
-    )(*lhs, *[weight] * count)
-    return regroup(outs, nt)
+    )(*lhs, *[weight] * count, *more)
+    return regroup(outs[: len(shapes)], nt), outs[len(shapes) :]
 
 
 def gateup_kernel(nt, *refs):
@@ -658,7 +705,7 @@
     return call(
         functools.partial(layer_out_kernel, len(terms)),
         (rows // tile,),
-        [blk] * (1 + len(terms)) + [ANY] * len(old),
+        [blk] * (1 + len(terms)) + [HBM] * len(old),
         spec,
         shape,
         nbytes=rows * width * (6 + 2 * len(terms)),
@@ -667,7 +714,9 @@
 
 
 def norm_back_kernel(nterms, nouts, first_ref, v_ref, gain_ref, *refs):
-    terms, outs, sum_ref = refs[:nterms], refs[-1 - nouts : -1], refs[-1]
+    terms, outs, sums = refs[:nterms], refs[len(refs) - nouts :], []
+    if nouts == 3:
+        outs, sums = outs[:2], outs[2:]
     u = sum_terms(terms)
     v = v_ref[...].astype(F32)
     q = lax.rsqrt(jnp.mean(v * v, axis=-1, keepdims=True) + NORM_EPS)
@@ -676,35 +725,46 @@
     grad = first_ref[...].astype(F32) + (q * ug - v * (q * q * q * inner))
     for out in outs:
         out[...] = grad.astype(out.dtype)
-
-    @pl.when(pl.program_id(0) == 0)
-    def _():
-        sum_ref[...] = jnp.zeros_like(sum_ref)
-
-    sum_ref[...] += jnp.sum(u * v * q, axis=0, keepdims=True)
-
-
-def norm_back(first, v, gain, terms, group=None, groups=None, into=None):
+    for sum_ref in sums:
+
+        @pl.when(pl.program_id(0) == 0)
+        def _():
+            sum_ref[...] = jnp.zeros_like(sum_ref)
+
+        sum_ref[...] += jnp.sum(u * v * q, axis=0, keepdims=True)
+
+
+def norm_back(first, v, gain, terms):
     rows, width = v.shape
     tile = min(128, rows)
     blk = pl.BlockSpec((tile, width), lambda i: (i, 0))
-    if group is None:
-        specs, shapes, old = [blk, blk], [sds((rows, width), F32), sds((rows, width), BF)], []
-    else:
-        spec, shape, old = place(group, groups, rows, tile, width, into)
-        specs, shapes = [spec], [shape]
-    return call(
-        functools.partial(norm_back_kernel, len(terms), len(specs)),
+    return call(
+        functools.partial(norm_back_kernel, len(terms), 3),
         (rows // tile,),
-        [blk, blk, whole_spec(gain.shape)] + [blk] * len(terms) + [ANY] * len(old),
-        specs + [pl.BlockSpec((1, width), lambda i: (0, 0))],
-        shapes + [sds((1, width), F32)],
+        [blk, blk, whole_spec(gain.shape)] + [blk] * len(terms),
+        [blk, blk, pl.BlockSpec((1, width), lambda i: (0, 0))],
+        [sds((rows, width), F32), sds((rows, width), BF), sds((1, width), F32)],
+        nbytes=rows * width * (12 + 2 * len(terms)),
+    )(first, v, gain, *terms)
+
+
+def norm_back_rows(first, v, gain, terms, group, groups, into):
+    rows, width = v.shape
+    tile = min(128, rows)
+    blk = pl.BlockSpec((tile, width), lambda i: (i, 0))
+    spec, shape, old = place(group, groups, rows, tile, width, into)
+    return call(
+        functools.partial(norm_back_kernel, len(terms), 1),
+        (rows // tile,),
+        [blk, blk, whole_spec(gain.shape)] + [blk] * len(terms) + [HBM] * len(old),
+        spec,
+        shape,
         nbytes=rows * width * (12 + 2 * len(terms)),
         aliases={3 + len(terms): 0} if old else None,
     )(first, v, gain, *terms, *old)
 
 
-def wgrad_rows_kernel(groups, which, *refs):
+def wgrad_rows_kernel(groups, which, nmore, *refs):
     nlhs = groups * (max(which) + 1)
     lhs, rhs, out_ref = refs[:nlhs], refs[nlhs : nlhs + groups * len(which)], refs[-1]
     tile = lhs[0].shape[2]
@@ -715,28 +775,29 @@
             a = left[w * groups + g]
             term = dot(a, rhs[c * groups + g][...].reshape(a.shape[1], -1))
             total = term if total is None else total + term
-        out_ref[0, c] = total.astype(BF)
-
-
-def wgrad_rows(lhs, rhs, which, nd, lo=0, hi=None, into=None):
-    hi = nd if hi is None else hi
+        out_ref[0, c * tile : (c + 1) * tile] = total.astype(BF)
+    if nmore:
+        out_ref[0, len(which) * tile :] = refs[-2][0]
+
+
+def wgrad_rows(lhs, rhs, which, nd, more=None):
     groups = len(lhs[0])
     nt, rows, width = lhs[0][0].shape
     ds = width // nd
     n = rhs[0][0].shape[2]
-    old = [] if into is None else [into]
-    return call(
-        functools.partial(wgrad_rows_kernel, groups, which),
-        (hi - lo,),
-        [pl.BlockSpec((nt, rows, ds), lambda j: (0, 0, j + lo))] * (groups * len(lhs))
+    more = [] if more is None else [more]
+    height = len(rhs) * ds + sum(a.shape[1] for a in more)
+    return call(
+        functools.partial(wgrad_rows_kernel, groups, which, len(more)),
+        (nd,),
+        [pl.BlockSpec((nt, rows, ds), lambda j: (0, 0, j))] * (groups * len(lhs))
         + [whole_spec(a.shape) for r in rhs for a in r]
-        + [ANY] * len(old),
-        pl.BlockSpec((1, len(rhs), ds, n), lambda j: (j + lo, 0, 0, 0)),
-        sds((nd, len(rhs), ds, n), BF),
-        flops=2 * groups * nt * rows * ds * (hi - lo) * n * len(rhs),
+        + [pl.BlockSpec((1,) + a.shape[1:], lambda j: (j, 0, 0)) for a in more],
+        pl.BlockSpec((1, height, n), lambda j: (j, 0, 0)),
+        sds((nd, height, n), BF),
+        flops=2 * groups * nt * rows * width * n * len(rhs),
         nbytes=2 * groups * nt * rows * (width + n * len(rhs)) + 2 * width * n * len(rhs),
-        aliases={groups * (len(lhs) + len(rhs)): 0} if old else None,
-    )(*[a for l in lhs for a in l], *[a for r in rhs for a in r], *old)
+    )(*[a for l in lhs for a in l], *[a for r in rhs for a in r], *more)
 
 
 def wgrad_cols_kernel(groups, nd, *refs):
@@ -778,6 +839,13 @@
     return lax.cummax(jnp.where(change, ids[None, :], 0), axis=1)
 
 
+def tensor_sum(value, nt):
+    if nt != 4:
+        return lax.psum(value, "tensor")
+    value = value + lax.ppermute(value, "tensor", swap_perm(4, 1))
+    return value + lax.ppermute(value, "tensor", swap_perm(4, 2))
+
+
 def slot_order(blocks, index, nt):
     if nt != 4:
         return blocks
@@ -797,7 +865,7 @@
     x = [layer_input[g * per : (g + 1) * per].reshape(per * local, width) for g in range(groups)]
     go = [grad_out[g * per : (g + 1) * per].reshape(per * local, width) for g in range(groups)]
     Order.last = None
-    x_all = [Gather(a, nt) for a in x]
+    x_all = Gather(layer_input.reshape(seqs * local, width), nt)
 
     gains = lax.all_gather(jnp.stack([gain1, gain2]), "dp", axis=1, tiled=True).astype(F32)
     g1, g2 = gains[:1], gains[1:]
@@ -837,14 +905,14 @@
 
     def attend(g):
         ctx[g], lse[g] = attention_forward(qkv[g], starts[g], slot_of, nt)
-        attn_sum[g] = Scatter(mm_back([ctx[g]], full_qkvo, [3], nt, 4), nt)
+        attn_sum[g] = Scatter(mm_back([ctx[g]], full_qkvo, [3], nt, 4)[0], nt)
 
     def middle(g):
         mid[g], low2[g] = make_middle(x[g], g2, attn_sum[g].terms)
         a2_all[g] = Gather(low2[g], nt)
 
     def second_back(g):
-        ga2[g] = Scatter(mm_back([gg[g], gu[g]], full_gateup, [0, 1], nt, 2), nt)
+        ga2[g] = Scatter(mm_back([gg[g], gu[g]], full_gateup, [0, 1], nt, 2)[0], nt)
 
     def project_out(g):
         out_sum[g] = Scatter(mm_cols(hid[g], full_down, nt, 2), nt)
@@ -860,75 +928,88 @@
         )
 
     def input_back(g):
-        ga1[g] = Scatter(mm_back(g_qkv[g], full_qkvo, [0, 1, 2], nt, 4), nt)
-
-    for g in both:
-        x_all[g].second()
-    a1 = [assemble(x_all[g].pieces, nt, g1) for g in both]
-    go_all = [Gather(link(go[g], a1[-1]), nt) for g in both]
+        parts, (sum1[g],) = mm_back(g_qkv[g], full_qkvo, [0, 1, 2], nt, 4, a1[g])
+        ga1[g] = Scatter(parts, nt)
+
+    def up_projection(g):
+        a2[g], gate[g], up[g], hid[g] = gate_up(a2_all[g].pieces, full_gateup, nt)
+
+    def hidden_back(g):
+        gg[g], gu[g] = gate_back(gof[g], full_down, gate[g], up[g], nt)
+
+    def finish(g, grad_input):
+        return norm_back_rows(g_mid[g], x[g], g1, ga1[g].terms, g, groups, grad_input)
+
+    def by_group(held):
+        return [held[g] for g in both]
+
+    a2, gate, up, hid, gg, gu = ({} for _ in range(6))
+    x_all.second()
+    a1 = [assemble(x_all.pieces, nt, 0, groups, g1, coss + sins)]
+    go_all = Gather(link(grad_out.reshape(seqs * local, width), a1[0]), nt)
     project(0)
     attend(0)
+    a1.append(assemble(x_all.pieces, nt, 1, groups, g1))
     project(1)
+    go_all.second()
     attn_sum[0].second()
-    go_all[0].second()
     attend(1)
-    go_all[1].second()
     middle(0)
     attn_sum[1].second()
     a2_all[0].second()
     middle(1)
-    gof = [assemble(go_all[g].pieces, nt) for g in both]
+    up_projection(0)
     a2_all[1].second()
-
-    a2, gate, up, hid = zip(*[gate_up(a2_all[g].pieces, full_gateup, nt) for g in both])
-    grad_down = dp_sum(wgrad_cols(hid, gof, nd))
-    gg, gu = zip(*[gate_back(gof[g], full_down, gate[g], up[g], nt) for g in both])
-    grad_gateup = wgrad_rows([a2], [gg, gu], [0, 0], nd, 0, nd // 2)
-    grad_gateup = wgrad_rows([a2], [gg, gu], [0, 0], nd, nd // 2, nd, grad_gateup)
+    gof = [assemble(go_all.pieces, nt, g, groups) for g in both]
+    up_projection(1)
+    hidden_back(0)
+    grad_down = dp_sum(wgrad_cols(by_group(hid), gof, nd))
+    second_back(0)
+    hidden_back(1)
+    ga2[0].second()
+    second_back(1)
+    residual_back(0)
+    grad_gateup = wgrad_rows([by_group(a2)], [by_group(gg), by_group(gu)], [0, 0], nd)
     grad_gateup = dp_sum(link(grad_gateup, grad_down))
-    second_back(0)
-    second_back(1)
-    ga2[0].second()
-    project_out(0)
     ga2[1].second()
-    residual_back(0)
     project_out(1)
     gm_all[0].second()
     residual_back(1)
-    out_sum[0].second()
+    project_out(0)
     attention_back(0)
     gm_all[1].second()
     input_back(0)
+    out_sum[1].second()
     attention_back(1)
     ga1[0].second()
     input_back(1)
+    ds = gain1.shape[0]
+    gains = tensor_sum(jnp.concatenate([(sum1[0] + sum1[1]) / g1, sum2[0] + sum2[1]]), nt)
+    gains = jnp.swapaxes(gains.reshape(2, nd, ds), 0, 1).astype(BF)
+    gains = jnp.pad(gains, ((0, 0), (0, 14), (0, qkv_w.shape[2] - ds)))
+    out_sum[0].second()
     grad_qkvo = wgrad_rows(
-        [a1, [gmf[g] for g in both]],
-        [[g_qkv[g][c] for g in both] for c in range(3)] + [[ctx[g] for g in both]],
+        [a1, by_group(gmf)],
+        [[g_qkv[g][c] for g in both] for c in range(3)] + [by_group(ctx)],
         [0, 0, 0, 1],
         nd,
+        gains,
     )
-    out_sum[1].second()
     grad_qkvo = dp_sum(link(grad_qkvo, grad_gateup))
-    layer_out = layer_out_rows(mid[0], out_sum[0].terms, 0, groups, None)
-    grad_input, sum1[0] = norm_back(g_mid[0], x[0], g1, ga1[0].terms, 0, groups, None)
+    layer_out = layer_out_rows(mid[1], out_sum[1].terms, 1, groups, None)
     ga1[1].second()
-    layer_out = layer_out_rows(mid[1], out_sum[1].terms, 1, groups, layer_out)
-    grad_input, sum1[1] = norm_back(g_mid[1], x[1], g1, ga1[1].terms, 1, groups, grad_input)
-
-    gain_sums = jnp.concatenate([sum1[0] + sum1[1], sum2[0] + sum2[1]], axis=0)
-    gain_sums = lax.psum(gain_sums, ("dp", "tensor"))
-    ds = gain1.shape[0]
-    mine = lax.dynamic_slice_in_dim(gain_sums, lax.axis_index("dp") * ds, ds, 1)
+    grad_input = finish(0, None)
+    layer_out = layer_out_rows(mid[0], out_sum[0].terms, 0, groups, layer_out)
+    grad_input = finish(1, grad_input)
     return (
         layer_out.reshape(seqs, local, width),
         grad_input.reshape(seqs, local, width),
-        grad_qkvo[:3].astype(F32),
-        grad_qkvo[3].T.astype(F32),
-        mine[0],
-        grad_gateup.astype(F32),
+        grad_qkvo[: 3 * ds].astype(F32).reshape(3, ds, -1),
+        grad_qkvo[3 * ds : 4 * ds].T.astype(F32),
+        grad_qkvo[4 * ds, :ds].astype(F32),
+        grad_gateup.astype(F32).reshape(2, ds, -1),
         grad_down.astype(F32),
-        mine[1],
+        grad_qkvo[4 * ds + 1, :ds].astype(F32),
     )
 
 

time: 967 us -> 833 us (0.86)
  Pallas kernels: 501 us -> 436 us
  blocking collectives: 52.2 us -> 13 us
  local copies, waits for them, and re-layouts: 58.3 us -> 38.8 us
    pallas_call x56 -> x52, Pallas kernels: 501 us -> 436 us  [run(): pl.pallas_call(ordered_body, grid_spec=pltpu.PrefetchScalarGridSpec(num_s...]
    psum x1 -> x0, blocking collectives: 39.8 us -> none  [per_device(): gain_sums = lax.psum(gain_sums, ('dp', 'tensor'))]
    ppermute x8, waiting for transfers between devices: 105 us -> 67.3 us  [second(): lax.ppermute(to_x, 'tensor', swap_perm(4, 1))]
    ppermute x8 -> x6, waiting for transfers between devices: 35.4 us -> 3.25 us  [second(): diag_y = lax.ppermute(right, 'tensor', swap_perm(4, 2))]
    ppermute x8 -> x6, waiting for transfers between devices: 6.13 us -> 36.9 us  [second(): diag_x = lax.ppermute(left, 'tensor', swap_perm(4, 1))]
    ppermute x8 -> x6, waiting for transfers between devices: 31.7 us -> 58.5 us  [__init__(): self.from_y = lax.ppermute(block, 'tensor', swap_perm(4, 2))]
    ppermute x8, waiting for transfers between devices: 16.5 us -> 39.5 us  [__init__(): self.for_y = lax.ppermute(diag_x, 'tensor', swap_perm(4, 1))]
    ppermute x8 -> x6, waiting for transfers between devices: 23.7 us -> 4 us  [__init__(): self.from_x = lax.ppermute(block, 'tensor', swap_perm(4, 1))]
  transfers between devices with their start and end apart: 70 -> 64, of which waited for: 32 -> 32; matrix products, arithmetic and copies ran while one was open for 5% -> 2% of each run, Pallas kernels for 52% -> 48%
where the time goes in v3:
time: 833 us; the launch traced here: 827 us
  Pallas kernels  436 us (52%)
  waiting for transfers between devices  246 us (30%)
  starting transfers between devices  61.4 us (7%)
  local copies, waits for them, and re-layouts  38.8 us (5%)
  other arithmetic  15.6 us (2%)
  between operations  15.5 us (2%)
  blocking collectives  13 us (2%)
    pallas_call x52, Pallas kernels, run(): pl.pallas_call(ordered_body, grid_spec=pltpu.PrefetchScalarGridSpec(num_s...  436 us
    ppermute x8, waiting for transfers between devices, second(): lax.ppermute(to_x, 'tensor', swap_perm(4, 1))  67.3 us
    ppermute x6, waiting for transfers between devices, __init__(): self.from_y = lax.ppermute(block, 'tensor', swap_perm(4, 2))  58.5 us
    ppermute x8, waiting for transfers between devices, __init__(): self.for_y = lax.ppermute(diag_x, 'tensor', swap_perm(4, 1))  39.5 us
    ppermute x6, waiting for transfers between devices, second(): diag_x = lax.ppermute(left, 'tensor', swap_perm(4, 1))  36.9 us
    unnamed x168, local copies, waits for them, and re-layouts  35.5 us
    ppermute x8, waiting for transfers between devices, second(): lax.ppermute(to_y, 'tensor', swap_perm(4, 2))  19.1 us
  transfers between devices with their start and end apart: 64, of which 32 were waited for; matrix products, arithmetic and copies ran while one was open for 2% of the time, Pallas kernels for 48%

profile of v3, /device:TPU:0, one launch (start us, length us, event | category | flops | bytes accessed | tf_op | source)
XLA Modules:
  0.0 826.5 jit_solution(2885312036122647211)
XLA Ops:
  23.3 37.4 %collective-permute-done.1.refs_0_.refs_2_ = bf16[512,2048]{1,0:T(8,128)(2,1)} collective-permute-done((bf16[512,2048]{1,0:T(8,128)(2,1)}, bf16[512,2048]{1,0:T(8,128)(2,1)}, u32[]{:S(2)}, u32[]{:S(2)}) %collective-permute-start.1) | collective-permute-done | bytes 2097184 | tf_op jit(solution)/shard_map/ppermute | solution.py:155
  66.6 13.0 %all_gather.21 = bf16[2,2048]{1,0:T(2,128)(2,1)S(1)} all-gather(bf16[2,256]{1,0:T(2,128)(2,1)S(1)} %pad_maximum_fusion.4), channel_id=1, replica_groups=mesh['dp'=8,'tensor'=4] {'dp'}, dimensions={1}, use_global_device_ids=true | all-gather | bytes 9216 | tf_op jit(solution)/shard_map/all_gather | solution.py:870
  98.2 11.8 %shard_map.155.refs_1_.refs_2_.refs_3_ = bf16[3,4,256,512]{3,2,1,0:T(8,128)(2,1)} custom-call(bf16[4,256,2048]{2,1,0:T(8,128)(2,1)} %shard_map.153.refs_1_.refs_0_.refs_6_, bf16[8,4,256,512]{3,2,1,0:T(8,128)(2,1)} %bitcast.62, f32[4,256,128]{2,1,0:T(8,128)S(1)} %copy-done.20, f32[4,256,128]{2,1,0:T(8,128)S(1)} %copy-done.17, ...), custom_call_target="tpu_custom_call" | custom-call | flops 2147483648 | bytes 4543829 | tf_op jit(solution)/shard_map/pallas_call | solution.py:82
  110.0 15.4 %shard_map.156 = (bf16[4,256,512]{2,1,0:T(8,128)(2,1)S(1)}, f32[1,4,8,256]{3,2,1,0:T(8,128)S(1)}) custom-call(s32[4]{0:T(128)S(1)} %iota_xor_fusion.refs_0_, bf16[3,4,256,512]{3,2,1,0:T(8,128)(2,1)} %shard_map.155.refs_1_.refs_2_.refs_3_, bf16[3,4,256,512]{3,2,1,0:T(8,128)(2,1)} %shard_map.155.refs_1_.refs_2_.refs_3_, ...), custom_call_target="tpu_custom_call" | custom-call | flops 1431655808 | bytes 1398101 | tf_op jit(solution)/shard_map/pallas_call | solution.py:82
  137.8 12.2 %shard_map.159.refs_2_.refs_1_.refs_3_ = bf16[3,4,256,512]{3,2,1,0:T(8,128)(2,1)} custom-call(bf16[4,256,2048]{2,1,0:T(8,128)(2,1)} %shard_map.158.refs_0_.refs_6_.refs_1_, bf16[8,4,256,512]{3,2,1,0:T(8,128)(2,1)} %bitcast.64, f32[4,256,128]{2,1,0:T(8,128)S(1)} %get-tuple-element.252.refs_7_.refs_2_, ...), custom_call_target="tpu_custom_call" | custom-call | flops 2147483648 | bytes 4543829 | tf_op jit(solution)/shard_map/pallas_call | solution.py:82
  155.7 15.4 %shard_map.162 = (bf16[4,256,512]{2,1,0:T(8,128)(2,1)S(1)}, f32[1,4,8,256]{3,2,1,0:T(8,128)S(1)}) custom-call(s32[4]{0:T(128)S(1)} %iota_xor_fusion.refs_0_, bf16[3,4,256,512]{3,2,1,0:T(8,128)(2,1)} %shard_map.159.refs_2_.refs_1_.refs_3_, bf16[3,4,256,512]{3,2,1,0:T(8,128)(2,1)} %shard_map.159.refs_2_.refs_1_.refs_3_, ...), custom_call_target="tpu_custom_call" | custom-call | flops 1431655808 | bytes 1398101 | tf_op jit(solution)/shard_map/pallas_call | solution.py:82
  183.0 8.2 collective-permute-done.13.refs_3_
  194.5 20.0 %collective-permute-done.11.refs_0_.refs_2_ = bf16[256,2048]{1,0:T(8,128)(2,1)S(1)} collective-permute-done((bf16[256,2048]{1,0:T(8,128)(2,1)S(1)}, bf16[256,2048]{1,0:T(8,128)(2,1)S(1)}, u32[]{:S(2)}, u32[]{:S(2)}) %collective-permute-start.11) | collective-permute-done | bytes 1048608 | tf_op jit(solution)/shard_map/ppermute | solution.py:155
  216.7 19.4 %collective-permute-done.16.refs_3_ = bf16[256,2048]{1,0:T(8,128)(2,1)S(1)} collective-permute-done((bf16[256,2048]{1,0:T(8,128)(2,1)S(1)}, bf16[256,2048]{1,0:T(8,128)(2,1)S(1)}, u32[]{:S(2)}, u32[]{:S(2)}) %collective-permute-start.16) | collective-permute-done | bytes 1048608 | tf_op jit(solution)/shard_map/ppermute | solution.py:207
  255.8 22.4 %shard_map.168 = (bf16[4,256,2048]{2,1,0:T(8,128)(2,1)}, bf16[4,256,2048]{2,1,0:T(8,128)(2,1)}, bf16[4,256,2048]{2,1,0:T(8,128)(2,1)}, bf16[4,256,2048]{2,1,0:T(8,128)(2,1)}) custom-call(bf16[256,2048]{1,0:T(8,128)(2,1)S(1)} %copy-done.45, bf16[256,2048]{1,0:T(8,128)(2,1)S(1)} %copy-done.43, bf16[256,2048]{1,0:T(8,128)(2,1)S(1)} %copy-done.41, ...), custom_call_target="tpu_custom_call" | custom-call | flops 5726623232 | bytes 12582912 | tf_op jit(solution)/shard_map/pallas_call | solution.py:82
  282.0 10.4 %collective-permute-done.18.refs_3_ = bf16[512,1024]{1,0:T(8,128)(2,1)} collective-permute-done((bf16[512,1024]{1,0:T(8,128)(2,1)}, bf16[512,1024]{1,0:T(8,128)(2,1)}, u32[]{:S(2)}, u32[]{:S(2)}) %collective-permute-start.18) | collective-permute-done | bytes 1048608 | tf_op jit(solution)/shard_map/ppermute | solution.py:161
  302.3 23.1 %shard_map.172 = (bf16[4,256,2048]{2,1,0:T(8,128)(2,1)}, bf16[4,256,2048]{2,1,0:T(8,128)(2,1)}, bf16[4,256,2048]{2,1,0:T(8,128)(2,1)}, bf16[4,256,2048]{2,1,0:T(8,128)(2,1)}) custom-call(bf16[256,2048]{1,0:T(8,128)(2,1)} %get-tuple-element.139.refs_6_.refs_0_, bf16[256,2048]{1,0:T(8,128)(2,1)} %collective-permute-done.21.refs_1_, ...), custom_call_target="tpu_custom_call" | custom-call | flops 5726623232 | bytes 12582912 | tf_op jit(solution)/shard_map/pallas_call | solution.py:82
  328.3 16.9 %shard_map.173 = (bf16[4,256,2048]{2,1,0:T(8,128)(2,1)}, bf16[4,256,2048]{2,1,0:T(8,128)(2,1)}) custom-call(bf16[4,256,2048]{2,1,0:T(8,128)(2,1)} %shard_map.170.refs_5_.refs_0_.refs_2_, bf16[8,2048,256]{2,1,0:T(8,128)(2,1)} %bitcast.80, bf16[4,256,2048]{2,1,0:T(8,128)(2,1)} %get-tuple-element.147.refs_2_, bf16[4,256,2048]{2,1,0:T(8,128)(2,1)} %get-tuple-element.148.refs_3_, ...), custom_call_target="tpu_custom_call" | custom-call | flops 2863311616 | bytes 9786709 | tf_op jit(solution)/shard_map/pallas_call | solution.py:82
  345.2 23.9 %shard_map.174.refs_4_ = bf16[8,2048,256]{2,1,0:T(8,128)(2,1)} custom-call(bf16[4,256,2048]{2,1,0:T(8,128)(2,1)} %get-tuple-element.140.refs_2_.refs_0_, bf16[4,256,2048]{2,1,0:T(8,128)(2,1)} %get-tuple-element.149.refs_4_.refs_1_.refs_0_, bf16[4,256,2048]{2,1,0:T(8,128)(2,1)} %shard_map.170.refs_5_.refs_0_.refs_2_, ...), custom_call_target="tpu_custom_call" | custom-call | flops 5726623232 | bytes 8388608 | tf_op jit(solution)/shard_map/pallas_call | solution.py:82
  369.2 24.3 %shard_map.175 = (bf16[256,2048]{1,0:T(8,128)(2,1)S(1)}, bf16[256,2048]{1,0:T(8,128)(2,1)S(1)}, bf16[256,2048]{1,0:T(8,128)(2,1)S(1)}, bf16[256,1024]{1,0:T(8,128)(2,1)S(1)}, bf16[256,1024]{1,0:T(8,128)(2,1)S(1)}) custom-call(bf16[4,256,2048]{2,1,0:T(8,128)(2,1)} %get-tuple-element.150.refs_0_.refs_2_, ...), custom_call_target="tpu_custom_call" | custom-call | flops 5726623232 | bytes 9786709 | tf_op jit(solution)/shard_map/pallas_call | solution.py:82
  396.1 17.1 %shard_map.176 = (bf16[4,256,2048]{2,1,0:T(8,128)(2,1)}, bf16[4,256,2048]{2,1,0:T(8,128)(2,1)}) custom-call(bf16[4,256,2048]{2,1,0:T(8,128)(2,1)} %shard_map.171.refs_6_.refs_3_.refs_0_, bf16[8,2048,256]{2,1,0:T(8,128)(2,1)} %bitcast.81, bf16[4,256,2048]{2,1,0:T(8,128)(2,1)} %get-tuple-element.145.refs_2_, bf16[4,256,2048]{2,1,0:T(8,128)(2,1)} %get-tuple-element.146.refs_3_, ...), custom_call_target="tpu_custom_call" | custom-call | flops 2863311616 | bytes 9786709 | tf_op jit(solution)/shard_map/pallas_call | solution.py:82
  415.0 24.2 %shard_map.178 = (bf16[256,2048]{1,0:T(8,128)(2,1)S(1)}, bf16[256,2048]{1,0:T(8,128)(2,1)}, bf16[256,2048]{1,0:T(8,128)(2,1)}, bf16[256,1024]{1,0:T(8,128)(2,1)S(1)}, bf16[256,1024]{1,0:T(8,128)(2,1)S(1)}) custom-call(bf16[4,256,2048]{2,1,0:T(8,128)(2,1)} %get-tuple-element.153.refs_0_.refs_3_, ...), custom_call_target="tpu_custom_call" | custom-call | flops 5726623232 | bytes 9786709 | tf_op jit(solution)/shard_map/pallas_call | solution.py:82
  443.1 44.0 %shard_map.180.refs_0_ = bf16[8,512,2048]{2,1,0:T(8,128)(2,1)} custom-call(bf16[4,256,2048]{2,1,0:T(8,128)(2,1)} %get-tuple-element.164.refs_0_, bf16[4,256,2048]{2,1,0:T(8,128)(2,1)} %get-tuple-element.165.refs_1_, bf16[4,256,2048]{2,1,0:T(8,128)(2,1)} %get-tuple-element.150.refs_0_.refs_2_, bf16[4,256,2048]{2,1,0:T(8,128)(2,1)} %get-tuple-element.153.refs_0_.refs_3_, ...), custom_call_target="tpu_custom_call" | custom-call | flops 11453246464 | bytes 13981013 | tf_op jit(solution)/shard_map/pallas_call | solution.py:82
  492.5 10.8 %collective-permute-done.27.refs_3_ = bf16[256,1024]{1,0:T(8,128)(2,1)S(1)} collective-permute-done((bf16[256,1024]{1,0:T(8,128)(2,1)S(1)}, bf16[256,1024]{1,0:T(8,128)(2,1)S(1)}, u32[]{:S(2)}, u32[]{:S(2)}) %collective-permute-start.27) | collective-permute-done | bytes 524320 | tf_op jit(solution)/shard_map/ppermute | solution.py:198
  508.7 13.6 %shard_map.183 = (bf16[256,2048]{1,0:T(8,128)(2,1)S(1)}, bf16[256,2048]{1,0:T(8,128)(2,1)S(1)}, bf16[256,2048]{1,0:T(8,128)(2,1)S(1)}, bf16[256,1024]{1,0:T(8,128)(2,1)}, bf16[256,1024]{1,0:T(8,128)(2,1)}) custom-call(bf16[4,256,2048]{2,1,0:T(8,128)(2,1)} %get-tuple-element.149.refs_4_.refs_1_.refs_0_, bf16[8,2048,256]{2,1,0:T(8,128)(2,1)} %bitcast.82, ...), custom_call_target="tpu_custom_call" | custom-call | flops 2863311616 | bytes 5592405 | tf_op jit(solution)/shard_map/pallas_call | solution.py:82
  527.1 19.1 %collective-permute-done.30.refs_4_ = bf16[256,2048]{1,0:T(8,128)(2,1)S(1)} collective-permute-done((bf16[256,2048]{1,0:T(8,128)(2,1)}, bf16[256,2048]{1,0:T(8,128)(2,1)S(1)}, u32[]{:S(2)}, u32[]{:S(2)}) %collective-permute-start.30) | collective-permute-done | bytes 1048608 | tf_op jit(solution)/shard_map/ppermute | solution.py:207
  556.2 12.7 %shard_map.186 = (bf16[256,2048]{1,0:T(8,128)(2,1)S(1)}, bf16[256,2048]{1,0:T(8,128)(2,1)S(1)}, bf16[256,2048]{1,0:T(8,128)(2,1)S(1)}, bf16[256,1024]{1,0:T(8,128)(2,1)S(1)}, bf16[256,1024]{1,0:T(8,128)(2,1)S(1)}) custom-call(bf16[4,256,2048]{2,1,0:T(8,128)(2,1)} %get-tuple-element.140.refs_2_.refs_0_, bf16[8,2048,256]{2,1,0:T(8,128)(2,1)} %bitcast.83, ...), custom_call_target="tpu_custom_call" | custom-call | flops 2863311616 | bytes 5592405 | tf_op jit(solution)/shard_map/pallas_call | solution.py:82
  570.7 15.7 %collective-permute-done.38.refs_3_ = bf16[256,1024]{1,0:T(8,128)(2,1)S(1)} collective-permute-done((bf16[256,1024]{1,0:T(8,128)(2,1)S(1)}, bf16[256,1024]{1,0:T(8,128)(2,1)S(1)}, u32[]{:S(2)}, u32[]{:S(2)}) %collective-permute-start.38) | collective-permute-done | bytes 524320 | tf_op jit(solution)/shard_map/ppermute | solution.py:161
  594.2 22.3 %shard_map.188 = (bf16[4,256,512]{2,1,0:T(8,128)(2,1)S(1)}, bf16[4,256,512]{2,1,0:T(8,128)(2,1)S(1)}, bf16[4,256,512]{2,1,0:T(8,128)(2,1)S(1)}) custom-call(s32[4]{0:T(128)S(1)} %iota_xor_fusion.refs_0_, bf16[3,4,256,512]{3,2,1,0:T(8,128)(2,1)} %shard_map.155.refs_1_.refs_2_.refs_3_, bf16[3,4,256,512]{3,2,1,0:T(8,128)(2,1)} %shard_map.155.refs_1_.refs_2_.refs_3_, ...), custom_call_target="tpu_custom_call" | custom-call | flops 3579139328 | bytes 2446677 | tf_op jit(solution)/shard_map/pallas_call | solution.py:82
  619.8 10.9 %shard_map.190 = (bf16[256,2048]{1,0:T(8,128)(2,1)S(1)}, bf16[256,2048]{1,0:T(8,128)(2,1)S(1)}, bf16[256,2048]{1,0:T(8,128)(2,1)S(1)}, bf16[256,1024]{1,0:T(8,12...) custom-call(bf16[4,256,512]{2,1,0:T(8,128)(2,1)S(1)} %get-tuple-element.189.refs_0_.refs_4_, ...), custom_call_target="tpu_custom_call" | custom-call | flops 2147483648 | bytes 4543829 | tf_op jit(solution)/shard_map/pallas_call | solution.py:82
  644.3 22.3 %shard_map.193 = (bf16[4,256,512]{2,1,0:T(8,128)(2,1)S(1)}, bf16[4,256,512]{2,1,0:T(8,128)(2,1)S(1)}, bf16[4,256,512]{2,1,0:T(8,128)(2,1)S(1)}) custom-call(s32[4]{0:T(128)S(1)} %iota_xor_fusion.refs_0_, bf16[3,4,256,512]{3,2,1,0:T(8,128)(2,1)} %shard_map.159.refs_2_.refs_1_.refs_3_, bf16[3,4,256,512]{3,2,1,0:T(8,128)(2,1)} %shard_map.159.refs_2_.refs_1_.refs_3_, ...), custom_call_target="tpu_custom_call" | custom-call | flops 3579139328 | bytes 2446677 | tf_op jit(solution)/shard_map/pallas_call | solution.py:82
  667.1 10.6 %shard_map.195 = (bf16[256,2048]{1,0:T(8,128)(2,1)S(1)}, bf16[256,2048]{1,0:T(8,128)(2,1)S(1)}, bf16[256,2048]{1,0:T(8,128)(2,1)S(1)}, bf16[256,1024]{1,0:T(8,12...) custom-call(bf16[4,256,512]{2,1,0:T(8,128)(2,1)S(1)} %get-tuple-element.194.refs_0_.refs_5_, ...), custom_call_target="tpu_custom_call" | custom-call | flops 2147483648 | bytes 4543829 | tf_op jit(solution)/shard_map/pallas_call | solution.py:82
  688.5 21.6 %shard_map.197.refs_0_ = bf16[8,1040,512]{2,1,0:T(8,128)(2,1)} custom-call(bf16[4,256,2048]{2,1,0:T(8,128)(2,1)} %shard_map.153.refs_1_.refs_0_.refs_6_, bf16[4,256,2048]{2,1,0:T(8,128)(2,1)} %shard_map.158.refs_0_.refs_6_.refs_1_, bf16[4,256,2048]{2,1,0:T(8,128)(2,1)} %get-tuple-element.207.refs_2_, bf16[4,256,2048]{2,1,0:T(8,128)(2,1)} %get-tuple-element.208.refs_3_, ...), custom_call_target="tpu_custom_call" | custom-call | flops 5726623232 | bytes 8388608 | tf_op jit(solution)/shard_map/pallas_call | solution.py:82
  718.1 20.9 %collective-permute-done.48.refs_2_ = bf16[256,2048]{1,0:T(8,128)(2,1)S(1)} collective-permute-done((bf16[256,2048]{1,0:T(8,128)(2,1)}, bf16[256,2048]{1,0:T(8,128)(2,1)S(1)}, u32[]{:S(2)}, u32[]{:S(2)}) %collective-permute-start.48) | collective-permute-done | bytes 1048608 | tf_op jit(solution)/shard_map/ppermute | solution.py:207
  743.6 8.0 collective-permute-done.54.refs_1_
  752.3 20.4 %collective-permute-done.55.refs_3_ = bf16[256,1024]{1,0:T(8,128)(2,1)S(1)} collective-permute-done((bf16[256,1024]{1,0:T(8,128)(2,1)}, bf16[256,1024]{1,0:T(8,128)(2,1)S(1)}, u32[]{:S(2)}, u32[]{:S(2)}) %collective-permute-start.55) | collective-permute-done | bytes 524320 | tf_op jit(solution)/shard_map/ppermute | solution.py:198
  781.0 15.5 %collective-permute-done.53.refs_5_ = bf16[256,2048]{1,0:T(8,128)(2,1)S(1)} collective-permute-done((bf16[256,2048]{1,0:T(8,128)(2,1)}, bf16[256,2048]{1,0:T(8,128)(2,1)S(1)}, u32[]{:S(2)}, u32[]{:S(2)}) %collective-permute-start.53) | collective-permute-done | bytes 1048608 | tf_op jit(solution)/shard_map/ppermute | solution.py:208
  (366 shorter events, 227.5 us)
Async XLA Ops:
  7.2 88.9 %all-gather.7.cloned.1.call-start = ((), (), s32[]{:S(2)}) async-start(), calls=%async_computation.6 | async-start | bytes 9437184 | tf_op jit(solution)/shard_map/all_gather | solution.py:873
  10.2 239.6 %all-gather.9.cloned.1.call-start = ((), (), s32[]{:S(2)}) async-start(), calls=%async_computation.7 | async-start | bytes 18874368 | tf_op jit(solution)/shard_map/all_gather | solution.py:874
  10.9 317.4 %all-gather.11.cloned.1.call-start = ((), (), s32[]{:S(2)}) async-start(), calls=%async_computation.8 | async-start | bytes 9437184 | tf_op jit(solution)/shard_map/all_gather | solution.py:875
  11.7 475.4 %reduce-scatter.4.cloned.1.call-start = ((), (), s32[]{:S(2)}) async-start(), calls=%async_computation.3 | async-start | bytes 9437184 | tf_op jit(solution)/shard_map/reduce_scatter | solution.py:901
  11.7 49.0 %collective-permute-start.1 = (bf16[512,2048]{1,0:T(8,128)(2,1)}, bf16[512,2048]{1,0:T(8,128)(2,1)}, u32[]{:S(2)}, u32[]{:S(2)}) collective-permute-start(bf16[512,2048]{1,0:T(8,128)(2,1)} %bitcast.54), channel_id=1, source_target_pairs={{0,2},{1,3},{2,0},{3,1},{4,6},{5,7},{6,4},{7,5},{8,10},{9,11},{10,... | collective-permute-start | bytes 6291464 | tf_op jit(solution)/shard_map/ppermute | solution.py:155
  14.8 47.4 %collective-permute-start = (bf16[512,2048]{1,0:T(8,128)(2,1)}, bf16[512,2048]{1,0:T(8,128)(2,1)}, u32[]{:S(2)}, u32[]{:S(2)}) collective-permute-start(bf16[512,2048]{1,0:T(8,128)(2,1)} %bitcast.55), channel_id=1, source_target_pairs={{0,1},{1,0},{2,3},{3,2},{4,5},{5,4},{6,7},{7,6},{8,9},{9,8},{10,11... | collective-permute-start | bytes 6291464 | tf_op jit(solution)/shard_map/ppermute | solution.py:154
  94.8 55.3 %collective-permute-start.7 = (bf16[512,2048]{1,0:T(8,128)(2,1)S(1)}, bf16[512,2048]{1,0:T(8,128)(2,1)}, u32[]{:S(2)}, u32[]{:S(2)}) collective-permute-start(bf16[512,2048]{1,0:T(8,128)(2,1)S(1)} %shard_map.154.refs_4_.refs_0_), channel_id=1, source_target_pairs={{0,1},{1,0},{2,3},{3,2},{4,5},{5,4},{6,7},{7,6},{8,9},{9,8},{10,11... | collective-permute-start | bytes 6291464 | tf_op jit(solution)/shard_map/ppermute | solution.py:154
  95.4 54.7 %collective-permute-start.6 = (bf16[512,2048]{1,0:T(8,128)(2,1)S(1)}, bf16[512,2048]{1,0:T(8,128)(2,1)}, u32[]{:S(2)}, u32[]{:S(2)}) collective-permute-start(bf16[512,2048]{1,0:T(8,128)(2,1)S(1)} %shard_map.154.refs_4_.refs_0_), channel_id=1, source_target_pairs={{0,2},{1,3},{2,0},{3,1},{4,6},{5,7},{6,4},{7,5},{8,10},{9,11},{10,... | collective-permute-start | bytes 6291464 | tf_op jit(solution)/shard_map/ppermute | solution.py:155
  192.5 43.7 %collective-permute-start.16 = (bf16[256,2048]{1,0:T(8,128)(2,1)S(1)}, bf16[256,2048]{1,0:T(8,128)(2,1)S(1)}, u32[]{:S(2)}, u32[]{:S(2)}) collective-permute-start(bf16[256,2048]{1,0:T(8,128)(2,1)S(1)} %get-tuple-element.138), channel_id=1, source_target_pairs={{0,1},{1,0},{2,3},{3,2},{4,5},{5,4},{6,7},{7,6},{8,9},{9,8},{10,11... | collective-permute-start | bytes 3145736 | tf_op jit(solution)/shard_map/ppermute | solution.py:207
  193.5 43.5 %collective-permute-start.17 = (bf16[256,2048]{1,0:T(8,128)(2,1)S(1)}, bf16[256,2048]{1,0:T(8,128)(2,1)S(1)}, u32[]{:S(2)}, u32[]{:S(2)}) collective-permute-start(bf16[256,2048]{1,0:T(8,128)(2,1)S(1)} %get-tuple-element.134.refs_2_), channel_id=1, source_target_pairs={{0,2},{1,3},{2,0},{3,1},{4,6},{5,7},{6,4},{7,5},{8,10},{9,11},{10,... | collective-permute-start | bytes 3145736 | tf_op jit(solution)/shard_map/ppermute | solution.py:208
  240.2 38.0 %collective-permute-start.21 = (bf16[256,2048]{1,0:T(8,128)(2,1)}, bf16[256,2048]{1,0:T(8,128)(2,1)}, u32[]{:S(2)}, u32[]{:S(2)}) collective-permute-start(bf16[256,2048]{1,0:T(8,128)(2,1)} %get-tuple-element.139.refs_6_.refs_0_), channel_id=1, source_target_pairs={{0,1},{1,0},{2,3},{3,2},{4,5},{5,4},{6,7},{7,6},{8,9},{9,8},{10,11... | collective-permute-start | bytes 3145736 | tf_op jit(solution)/shard_map/ppermute | solution.py:154
  241.1 37.1 %collective-permute-start.20 = (bf16[256,2048]{1,0:T(8,128)(2,1)}, bf16[256,2048]{1,0:T(8,128)(2,1)}, u32[]{:S(2)}, u32[]{:S(2)}) collective-permute-start(bf16[256,2048]{1,0:T(8,128)(2,1)} %get-tuple-element.139.refs_6_.refs_0_), channel_id=1, source_target_pairs={{0,2},{1,3},{2,0},{3,1},{4,6},{5,7},{6,4},{7,5},{8,10},{9,11},{10,... | collective-permute-start | bytes 3145736 | tf_op jit(solution)/shard_map/ppermute | solution.py:155
  242.1 51.1 %collective-permute-start.19 = (bf16[512,1024]{1,0:T(8,128)(2,1)}, bf16[512,1024]{1,0:T(8,128)(2,1)}, u32[]{:S(2)}, u32[]{:S(2)}) collective-permute-start(bf16[512,1024]{1,0:T(8,128)(2,1)} %get-tuple-element.123.refs_4_), channel_id=1, source_target_pairs={{0,2},{1,3},{2,0},{3,1},{4,6},{5,7},{6,4},{7,5},{8,10},{9,11},{10,... | collective-permute-start | bytes 3145736 | tf_op jit(solution)/shard_map/ppermute | solution.py:162
  248.1 44.3 %collective-permute-start.18 = (bf16[512,1024]{1,0:T(8,128)(2,1)}, bf16[512,1024]{1,0:T(8,128)(2,1)}, u32[]{:S(2)}, u32[]{:S(2)}) collective-permute-start(bf16[512,1024]{1,0:T(8,128)(2,1)} %get-tuple-element.142), channel_id=1, source_target_pairs={{0,1},{1,0},{2,3},{3,2},{4,5},{5,4},{6,7},{7,6},{8,9},{9,8},{10,11... | collective-permute-start | bytes 3145736 | tf_op jit(solution)/shard_map/ppermute | solution.py:161
  369.1 341.9 %reduce-scatter.6.cloned.1.call-start = ((), (), s32[]{:S(2)}) async-start(), calls=%async_computation.4 | async-start | bytes 18874368 | tf_op jit(solution)/shard_map/reduce_scatter | solution.py:901
  488.4 325.0 %reduce-scatter.8.cloned.1.call-start = ((), (), s32[]{:S(2)}) async-start(), calls=%async_computation.5 | async-start | bytes 9584640 | tf_op jit(solution)/shard_map/reduce_scatter | solution.py:901
  506.6 39.6 %collective-permute-start.30 = (bf16[256,2048]{1,0:T(8,128)(2,1)}, bf16[256,2048]{1,0:T(8,128)(2,1)S(1)}, u32[]{:S(2)}, u32[]{:S(2)}) collective-permute-start(bf16[256,2048]{1,0:T(8,128)(2,1)} %get-tuple-element.169), channel_id=1, source_target_pairs={{0,1},{1,0},{2,3},{3,2},{4,5},{5,4},{6,7},{7,6},{8,9},{9,8},{10,11... | collective-permute-start | bytes 3145736 | tf_op jit(solution)/shard_map/ppermute | solution.py:207
  507.6 39.8 %collective-permute-start.31 = (bf16[256,2048]{1,0:T(8,128)(2,1)}, bf16[256,2048]{1,0:T(8,128)(2,1)S(1)}, u32[]{:S(2)}, u32[]{:S(2)}) collective-permute-start(bf16[256,2048]{1,0:T(8,128)(2,1)} %get-tuple-element.170.refs_2_), channel_id=1, source_target_pairs={{0,2},{1,3},{2,0},{3,1},{4,6},{5,7},{6,4},{7,5},{8,10},{9,11},{10,... | collective-permute-start | bytes 3145736 | tf_op jit(solution)/shard_map/ppermute | solution.py:208
  550.6 65.9 %collective-permute-start.37 = (bf16[256,2048]{1,0:T(8,128)(2,1)S(1)}, bf16[256,2048]{1,0:T(8,128)(2,1)S(1)}, u32[]{:S(2)}, u32[]{:S(2)}) collective-permute-start(bf16[256,2048]{1,0:T(8,128)(2,1)S(1)} %get-tuple-element.180.refs_0_), channel_id=1, source_target_pairs={{0,2},{1,3},{2,0},{3,1},{4,6},{5,7},{6,4},{7,5},{8,10},{9,11},{10,... | collective-permute-start | bytes 3145736 | tf_op jit(solution)/shard_map/ppermute | solution.py:155
  552.1 64.5 %collective-permute-start.36 = (bf16[256,2048]{1,0:T(8,128)(2,1)S(1)}, bf16[256,2048]{1,0:T(8,128)(2,1)S(1)}, u32[]{:S(2)}, u32[]{:S(2)}) collective-permute-start(bf16[256,2048]{1,0:T(8,128)(2,1)S(1)} %get-tuple-element.180.refs_0_), channel_id=1, source_target_pairs={{0,1},{1,0},{2,3},{3,2},{4,5},{5,4},{6,7},{7,6},{8,9},{9,8},{10,11... | collective-permute-start | bytes 3145736 | tf_op jit(solution)/shard_map/ppermute | solution.py:154
  554.7 78.0 %collective-permute-start.42 = (bf16[256,1024]{1,0:T(8,128)(2,1)}, bf16[256,1024]{1,0:T(8,128)(2,1)S(1)}, u32[]{:S(2)}, u32[]{:S(2)}) collective-permute-start(bf16[256,1024]{1,0:T(8,128)(2,1)} %get-tuple-element.172.refs_2_), channel_id=1, source_target_pairs={{0,2},{1,3},{2,0},{3,1},{4,6},{5,7},{6,4},{7,5},{8,10},{9,11},{10,... | collective-permute-start | bytes 1572872 | tf_op jit(solution)/shard_map/ppermute | solution.py:199
  586.3 45.0 %collective-permute-start.43 = (bf16[256,1024]{1,0:T(8,128)(2,1)}, bf16[256,1024]{1,0:T(8,128)(2,1)}, u32[]{:S(2)}, u32[]{:S(2)}) collective-permute-start(bf16[256,1024]{1,0:T(8,128)(2,1)} %get-tuple-element.188), channel_id=1, source_target_pairs={{0,1},{1,0},{2,3},{3,2},{4,5},{5,4},{6,7},{7,6},{8,9},{9,8},{10,11... | collective-permute-start | bytes 1572872 | tf_op jit(solution)/shard_map/ppermute | solution.py:198
  630.8 35.9 %collective-permute-start.44 = (bf16[256,1024]{1,0:T(8,128)(2,1)}, bf16[256,1024]{1,0:T(8,128)(2,1)S(1)}, u32[]{:S(2)}, u32[]{:S(2)}) collective-permute-start(bf16[256,1024]{1,0:T(8,128)(2,1)} %get-tuple-element.198), channel_id=1, source_target_pairs={{0,2},{1,3},{2,0},{3,1},{4,6},{5,7},{6,4},{7,5},{8,10},{9,11},{10,... | collective-permute-start | bytes 1572872 | tf_op jit(solution)/shard_map/ppermute | solution.py:199
  631.3 35.3 %collective-permute-start.45 = (bf16[256,1024]{1,0:T(8,128)(2,1)}, bf16[256,1024]{1,0:T(8,128)(2,1)S(1)}, u32[]{:S(2)}, u32[]{:S(2)}) collective-permute-start(bf16[256,1024]{1,0:T(8,128)(2,1)} %get-tuple-element.200), channel_id=1, source_target_pairs={{0,1},{1,0},{2,3},{3,2},{4,5},{5,4},{6,7},{7,6},{8,9},{9,8},{10,11... | collective-permute-start | bytes 1572872 | tf_op jit(solution)/shard_map/ppermute | solution.py:198
  633.5 51.6 %collective-permute-start.34 = (bf16[256,1024]{1,0:T(8,128)(2,1)S(1)}, bf16[256,1024]{1,0:T(8,128)(2,1)S(1)}, u32[]{:S(2)}, u32[]{:S(2)}) collective-permute-start(bf16[256,1024]{1,0:T(8,128)(2,1)S(1)} %get-tuple-element.177.refs_6_), channel_id=1, source_target_pairs={{0,2},{1,3},{2,0},{3,1},{4,6},{5,7},{6,4},{7,5},{8,10},{9,11},{10,... | collective-permute-start | bytes 1572872 | tf_op jit(solution)/shard_map/ppermute | solution.py:199
  637.5 47.7 %collective-permute-start.35 = (bf16[256,1024]{1,0:T(8,128)(2,1)}, bf16[256,1024]{1,0:T(8,128)(2,1)}, u32[]{:S(2)}, u32[]{:S(2)}) collective-permute-start(bf16[256,1024]{1,0:T(8,128)(2,1)} %copy-done.72), channel_id=1, source_target_pairs={{0,1},{1,0},{2,3},{3,2},{4,5},{5,4},{6,7},{7,6},{8,9},{9,8},{10,11... | collective-permute-start | bytes 1572872 | tf_op jit(solution)/shard_map/ppermute | solution.py:198
  714.6 61.5 %collective-permute-start.52 = (bf16[256,2048]{1,0:T(8,128)(2,1)}, bf16[256,2048]{1,0:T(8,128)(2,1)S(1)}, u32[]{:S(2)}, u32[]{:S(2)}) collective-permute-start(bf16[256,2048]{1,0:T(8,128)(2,1)} %copy-done.57), channel_id=1, source_target_pairs={{0,1},{1,0},{2,3},{3,2},{4,5},{5,4},{6,7},{7,6},{8,9},{9,8},{10,11... | collective-permute-start | bytes 3145736 | tf_op jit(solution)/shard_map/ppermute | solution.py:207
  715.3 36.3 %collective-permute-start.54 = (bf16[256,1024]{1,0:T(8,128)(2,1)}, bf16[256,1024]{1,0:T(8,128)(2,1)S(1)}, u32[]{:S(2)}, u32[]{:S(2)}) collective-permute-start(bf16[256,1024]{1,0:T(8,128)(2,1)} %copy-done.74), channel_id=1, source_target_pairs={{0,2},{1,3},{2,0},{3,1},{4,6},{5,7},{6,4},{7,5},{8,10},{9,11},{10,... | collective-permute-start | bytes 1572872 | tf_op jit(solution)/shard_map/ppermute | solution.py:199
  716.7 56.0 %collective-permute-start.55 = (bf16[256,1024]{1,0:T(8,128)(2,1)}, bf16[256,1024]{1,0:T(8,128)(2,1)S(1)}, u32[]{:S(2)}, u32[]{:S(2)}) collective-permute-start(bf16[256,1024]{1,0:T(8,128)(2,1)} %copy-done.73), channel_id=1, source_target_pairs={{0,1},{1,0},{2,3},{3,2},{4,5},{5,4},{6,7},{7,6},{8,9},{9,8},{10,11... | collective-permute-start | bytes 1572872 | tf_op jit(solution)/shard_map/ppermute | solution.py:198
  739.0 60.0 %collective-permute-start.47 = (bf16[256,2048]{1,0:T(8,128)(2,1)S(1)}, bf16[256,2048]{1,0:T(8,128)(2,1)S(1)}, u32[]{:S(2)}, u32[]{:S(2)}) collective-permute-start(bf16[256,2048]{1,0:T(8,128)(2,1)S(1)} %copy-done.29), channel_id=1, source_target_pairs={{0,2},{1,3},{2,0},{3,1},{4,6},{5,7},{6,4},{7,5},{8,10},{9,11},{10,... | collective-permute-start | bytes 3145736 | tf_op jit(solution)/shard_map/ppermute | solution.py:208
  740.4 56.2 %collective-permute-start.53 = (bf16[256,2048]{1,0:T(8,128)(2,1)}, bf16[256,2048]{1,0:T(8,128)(2,1)S(1)}, u32[]{:S(2)}, u32[]{:S(2)}) collective-permute-start(bf16[256,2048]{1,0:T(8,128)(2,1)} %copy-done.30), channel_id=1, source_target_pairs={{0,2},{1,3},{2,0},{3,1},{4,6},{5,7},{6,4},{7,5},{8,10},{9,11},{10,... | collective-permute-start | bytes 3145736 | tf_op jit(solution)/shard_map/ppermute | solution.py:208
  751.6 47.4 %collective-permute-start.46 = (bf16[256,2048]{1,0:T(8,128)(2,1)S(1)}, bf16[256,2048]{1,0:T(8,128)(2,1)S(1)}, u32[]{:S(2)}, u32[]{:S(2)}) collective-permute-start(bf16[256,2048]{1,0:T(8,128)(2,1)S(1)} %copy-done.51), channel_id=1, source_target_pairs={{0,1},{1,0},{2,3},{3,2},{4,5},{5,4},{6,7},{7,6},{8,9},{9,8},{10,11... | collective-permute-start | bytes 3145736 | tf_op jit(solution)/shard_map/ppermute | solution.py:207
  (114 other events, 1688.1 us)
Sparse Core Ops, SparseCore 0:
  10.3 84.8 all-gather.6
  96.8 149.5 all-gather.8
  248.0 80.2 all-gather.10
  369.3 88.1 reduce-scatter.3
  488.5 166.3 reduce-scatter.5
  712.7 88.0 reduce-scatter.7

commit v4 on v3

--- a/solution.py
+++ b/solution.py
@@ -18,8 +18,9 @@
 F32 = jnp.float32
 VMEM_SLACK = 8 * 1024 * 1024
 VMEM_SMALL = 24 * 1024 * 1024
-VMEM_LARGE = 44 * 1024 * 1024
+VMEM_LARGE = 40 * 1024 * 1024
 PIN_BYTES = 3 * 1024 * 1024
+PIN_BYTES_LARGE = 1024 * 1024
 SMALL = 3
 
 NT = (((1,), (1,)), ((), ()))
@@ -41,12 +42,12 @@
 ANY = pl.BlockSpec(memory_space=pl.ANY)
 
 
-def is_large(array):
-    return array.size * array.dtype.itemsize >= PIN_BYTES
-
-
-def pin(array):
-    return pltpu.with_memory_space_constraint(array, pltpu.HBM) if is_large(array) else array
+def is_large(array, least=None):
+    return array.size * array.dtype.itemsize >= (least or PIN_BYTES)
+
+
+def pin(array, least=None):
+    return pltpu.with_memory_space_constraint(array, pltpu.HBM) if is_large(array, least) else array
 
 
 def pinned(shape):
@@ -71,10 +72,11 @@
         blocks = list(zip(in_specs, args[prefetch:])) + out_blocks
         vmem = VMEM_SLACK + sum(block_bytes(spec, a.dtype) for spec, a in blocks)
         vmem += sum(int(np.prod(m.shape)) * np.dtype(m.dtype).itemsize for m in scratch)
+        least = PIN_BYTES
         if vmem > VMEM_SMALL:
-            vmem = VMEM_LARGE
-
-        args = [pin(a) for a in args]
+            vmem, least = VMEM_LARGE, PIN_BYTES_LARGE
+
+        args = [pin(a, least) for a in args]
 
         def ordered_body(*refs):
             body(*refs[:first_extra], *refs[first_extra + len(extra) :])
@@ -144,7 +146,7 @@
 
 
 class Gather:
-    def __init__(self, block, nt):
+    def __init__(self, block, nt, direct=False):
         self.nt = nt
         if nt != 4:
             full = lax.all_gather(block, "tensor", axis=0, tiled=False)
@@ -153,6 +155,9 @@
         self.block = block
         self.from_x = lax.ppermute(block, "tensor", swap_perm(4, 1))
         self.from_y = lax.ppermute(block, "tensor", swap_perm(4, 2))
+        if direct:
+            diag = lax.ppermute(block, "tensor", swap_perm(4, 3))
+            self.pieces = [(block,), (self.from_x,), (self.from_y,), (diag,)]
 
     def second(self):
         if self.nt != 4:
@@ -220,7 +225,7 @@
 
 
 def regroup(items, nt):
-    if nt != 4:
+    if len(items) == nt:
         return [(a,) for a in items]
     return [(items[0],), (items[1],), (items[2],), (items[3], items[4])]
 
@@ -563,7 +568,7 @@
 
 def gateup_kernel(nt, *refs):
     count = len(flat(piece_shapes(nt, 8, 8)))
-    pieces, w_ref, (full_ref, gate_ref, up_ref, hid_ref) = (
+    pieces, w_ref, (full_ref, silu_ref, slope_ref, hid_ref) = (
         refs[:count],
         refs[count],
         refs[count + 1 :],
@@ -573,16 +578,18 @@
     def _():
         fill_from_pieces(pieces, full_ref, nt)
 
-    cols = gate_ref.shape[2]
+    cols = hid_ref.shape[2]
     w_gate = w_ref[:, 0].reshape(-1, cols)
     w_up = w_ref[:, 1].reshape(-1, cols)
     for slot in range(nt):
         a2 = full_ref[slot]
         gate = dot(a2, w_gate)
         up = dot(a2, w_up)
-        gate_ref[slot] = gate.astype(BF)
-        up_ref[slot] = up.astype(BF)
-        hid_ref[slot] = (gate * jax.nn.sigmoid(gate) * up).astype(BF)
+        sig = 0.5 + 0.5 * jnp.tanh(0.5 * gate)
+        silu = gate * sig
+        silu_ref[slot] = silu.astype(BF)
+        slope_ref[slot] = (up * (sig + silu - silu * sig)).astype(BF)
+        hid_ref[slot] = (silu * up).astype(BF)
 
 
 def gate_up(pieces, weight, nt):
@@ -602,18 +609,15 @@
     )(*flat(pieces), weight)
 
 
-def gate_back_kernel(nt, full_ref, w_ref, gate_ref, up_ref, gg_ref, gu_ref):
+def gate_back_kernel(nt, full_ref, w_ref, silu_ref, slope_ref, gg_ref, gu_ref):
     weight = jnp.concatenate([w_ref[j] for j in range(w_ref.shape[0])], axis=1)
     for slot in range(nt):
         gh = dot_nt(full_ref[slot], weight)
-        gate = gate_ref[slot].astype(F32)
-        up = up_ref[slot].astype(F32)
-        sig = jax.nn.sigmoid(gate)
-        gg_ref[slot] = (gh * up * sig * (1.0 + gate * (1.0 - sig))).astype(BF)
-        gu_ref[slot] = (gh * gate * sig).astype(BF)
-
-
-def gate_back(full, weight, gate, up, nt):
+        gg_ref[slot] = (gh * slope_ref[slot].astype(F32)).astype(BF)
+        gu_ref[slot] = (gh * silu_ref[slot].astype(F32)).astype(BF)
+
+
+def gate_back(full, weight, silu, slope, nt):
     nd, ff, ds = weight.shape
     _, rows, width = full.shape
     step = min(512, ff)
@@ -626,12 +630,11 @@
         [sds((nt, rows, ff), BF)] * 2,
         flops=2 * nt * rows * width * ff,
         nbytes=2 * (nt * rows * width + width * ff + 4 * nt * rows * ff),
-    )(full, weight, gate, up)
+    )(full, weight, silu, slope)
 
 
 def context_back_kernel(nt, *refs):
-    count = len(flat(piece_shapes(nt, 8, 8)))
-    pieces, w_ref, (full_ref, out_ref) = refs[:count], refs[count], refs[count + 1 :]
+    pieces, w_ref, (full_ref, out_ref) = refs[:-3], refs[-3], refs[-2:]
 
     @pl.when(pl.program_id(0) == 0)
     def _():
@@ -895,7 +898,7 @@
     both = range(groups)
     qkv, ctx, lse, mid, low2, g_mid, g_low = ({} for _ in range(7))
     attn_sum, a2_all, ga2, out_sum, ga1 = ({} for _ in range(5))
-    sum1, sum2, gm_all, gmf, g_qkv = ({} for _ in range(5))
+    sum1, sum2, gm_all, gmf, g_qkv, g_ctx = ({} for _ in range(6))
 
     def dp_sum(grad):
         return lax.psum_scatter(grad, "dp", scatter_dimension=0, tiled=False)
@@ -921,10 +924,12 @@
         g_mid[g], g_low[g], sum2[g] = norm_back(go[g], mid[g], g2, ga2[g].terms)
         gm_all[g] = Gather(g_low[g], nt)
 
+    def attention_back_start(g):
+        gmf[g], g_ctx[g] = context_back(gm_all[g].pieces, full_qkvo, 3, nt)
+
     def attention_back(g):
-        gmf[g], g_ctx = context_back(gm_all[g].pieces, full_qkvo, 3, nt)
         g_qkv[g] = attention_backward(
-            qkv[g], g_ctx, starts[g], lse[g], coss[g], sins[g], slot_of, nt
+            qkv[g], g_ctx[g], starts[g], lse[g], coss[g], sins[g], slot_of, nt
         )
 
     def input_back(g):
@@ -932,10 +937,10 @@
         ga1[g] = Scatter(parts, nt)
 
     def up_projection(g):
-        a2[g], gate[g], up[g], hid[g] = gate_up(a2_all[g].pieces, full_gateup, nt)
+        a2[g], silu[g], slope[g], hid[g] = gate_up(a2_all[g].pieces, full_gateup, nt)
 
     def hidden_back(g):
-        gg[g], gu[g] = gate_back(gof[g], full_down, gate[g], up[g], nt)
+        gg[g], gu[g] = gate_back(gof[g], full_down, silu[g], slope[g], nt)
 
     def finish(g, grad_input):
         return norm_back_rows(g_mid[g], x[g], g1, ga1[g].terms, g, groups, grad_input)
@@ -943,51 +948,59 @@
     def by_group(held):
         return [held[g] for g in both]
 
-    a2, gate, up, hid, gg, gu = ({} for _ in range(6))
+    def gather_cotangent(g):
+        go_all[g] = Gather(link(go[g], flat(x_all.pieces)[-1]), nt)
+
+    a2, silu, slope, hid, gg, gu, go_all, gof = ({} for _ in range(8))
     x_all.second()
+    gather_cotangent(0)
+    gather_cotangent(1)
     a1 = [assemble(x_all.pieces, nt, 0, groups, g1, coss + sins)]
-    go_all = Gather(link(grad_out.reshape(seqs * local, width), a1[0]), nt)
     project(0)
     attend(0)
+    go_all[0].second()
     a1.append(assemble(x_all.pieces, nt, 1, groups, g1))
     project(1)
-    go_all.second()
     attn_sum[0].second()
     attend(1)
     middle(0)
+    gof[0] = assemble(go_all[0].pieces, nt, 0, 1)
     attn_sum[1].second()
     a2_all[0].second()
     middle(1)
+    go_all[1].second()
     up_projection(0)
     a2_all[1].second()
-    gof = [assemble(go_all.pieces, nt, g, groups) for g in both]
+    gof[1] = assemble(go_all[1].pieces, nt, 0, 1)
     up_projection(1)
     hidden_back(0)
-    grad_down = dp_sum(wgrad_cols(by_group(hid), gof, nd))
+    grad_down = dp_sum(wgrad_cols(by_group(hid), by_group(gof), nd))
     second_back(0)
     hidden_back(1)
     ga2[0].second()
     second_back(1)
     residual_back(0)
     grad_gateup = wgrad_rows([by_group(a2)], [by_group(gg), by_group(gu)], [0, 0], nd)
+    ga2[1].second()
+    gm_all[0].second()
     grad_gateup = dp_sum(link(grad_gateup, grad_down))
-    ga2[1].second()
+    project_out(0)
+    residual_back(1)
     project_out(1)
-    gm_all[0].second()
-    residual_back(1)
-    project_out(0)
+    attention_back_start(0)
     attention_back(0)
     gm_all[1].second()
+    out_sum[0].second()
     input_back(0)
     out_sum[1].second()
+    attention_back_start(1)
     attention_back(1)
-    ga1[0].second()
     input_back(1)
     ds = gain1.shape[0]
     gains = tensor_sum(jnp.concatenate([(sum1[0] + sum1[1]) / g1, sum2[0] + sum2[1]]), nt)
     gains = jnp.swapaxes(gains.reshape(2, nd, ds), 0, 1).astype(BF)
     gains = jnp.pad(gains, ((0, 0), (0, 14), (0, qkv_w.shape[2] - ds)))
-    out_sum[0].second()
+    layer_out = layer_out_rows(mid[0], out_sum[0].terms, 0, groups, None)
     grad_qkvo = wgrad_rows(
         [a1, by_group(gmf)],
         [[g_qkv[g][c] for g in both] for c in range(3)] + [by_group(ctx)],
@@ -995,12 +1008,12 @@
         nd,
         gains,
     )
+    ga1[1].second()
     grad_qkvo = dp_sum(link(grad_qkvo, grad_gateup))
-    layer_out = layer_out_rows(mid[1], out_sum[1].terms, 1, groups, None)
-    ga1[1].second()
-    grad_input = finish(0, None)
-    layer_out = layer_out_rows(mid[0], out_sum[0].terms, 0, groups, layer_out)
-    grad_input = finish(1, grad_input)
+    layer_out = layer_out_rows(mid[1], out_sum[1].terms, 1, groups, layer_out)
+    ga1[0].second()
+    grad_input = finish(1, None)
+    grad_input = finish(0, grad_input)
     return (
         layer_out.reshape(seqs, local, width),
         grad_input.reshape(seqs, local, width),

time: 833 us -> 813 us (0.976)
  waiting for transfers between devices: 246 us -> 233 us
  Pallas kernels: 436 us -> 427 us
    ppermute x6 -> x7, waiting for transfers between devices: 58.5 us -> 23.9 us  [__init__(): self.from_y = lax.ppermute(block, 'tensor', swap_perm(4, 2))]
    ppermute x6 -> x7, waiting for transfers between devices: 4 us -> 37.9 us  [__init__(): self.from_x = lax.ppermute(block, 'tensor', swap_perm(4, 1))]
    ppermute x8, waiting for transfers between devices: 39.5 us -> 5.77 us  [__init__(): self.for_y = lax.ppermute(diag_x, 'tensor', swap_perm(4, 1))]
    reduce_scatter x3, waiting for transfers between devices: 0.01 us -> 22.6 us  [dp_sum(): return lax.psum_scatter(grad, 'dp', scatter_dimension=0, tiled=False)]
    ppermute x6 -> x7, waiting for transfers between devices: 3.25 us -> 24.9 us  [second(): diag_y = lax.ppermute(right, 'tensor', swap_perm(4, 2))]
    ppermute x8, waiting for transfers between devices: 19.1 us -> 4.73 us  [second(): lax.ppermute(to_y, 'tensor', swap_perm(4, 2))]
    pallas_call x52 -> x54, Pallas kernels: 436 us -> 427 us  [run(): pl.pallas_call(ordered_body, grid_spec=pltpu.PrefetchScalarGridSpec(num_s...]
    ppermute x6 -> x7, waiting for transfers between devices: 36.9 us -> 37.8 us  [second(): diag_x = lax.ppermute(left, 'tensor', swap_perm(4, 1))]
  transfers between devices with their start and end apart: 64 -> 68, of which waited for: 32 -> 32; matrix products, arithmetic and copies ran while one was open for 2% -> 2% of each run, Pallas kernels for 48% -> 48%
where the time goes in v4:
time: 813 us; the launch traced here: 807 us
  Pallas kernels  427 us (53%)
  waiting for transfers between devices  233 us (29%)
  starting transfers between devices  62.3 us (8%)
  local copies, waits for them, and re-layouts  39.6 us (5%)
  other arithmetic  16.6 us (2%)
  between operations  15.7 us (2%)
  blocking collectives  12.2 us (2%)
    pallas_call x54, Pallas kernels, run(): pl.pallas_call(ordered_body, grid_spec=pltpu.PrefetchScalarGridSpec(num_s...  427 us
    ppermute x8, waiting for transfers between devices, second(): lax.ppermute(to_x, 'tensor', swap_perm(4, 1))  59.9 us
    ppermute x7, waiting for transfers between devices, __init__(): self.from_x = lax.ppermute(block, 'tensor', swap_perm(4, 1))  37.9 us
    ppermute x7, waiting for transfers between devices, second(): diag_x = lax.ppermute(left, 'tensor', swap_perm(4, 1))  37.8 us
    unnamed x205, local copies, waits for them, and re-layouts  36.2 us
    ppermute x7, waiting for transfers between devices, second(): diag_y = lax.ppermute(right, 'tensor', swap_perm(4, 2))  24.9 us
    ppermute x7, waiting for transfers between devices, __init__(): self.from_y = lax.ppermute(block, 'tensor', swap_perm(4, 2))  23.9 us
    reduce_scatter x3, waiting for transfers between devices, dp_sum(): return lax.psum_scatter(grad, 'dp', scatter_dimension=0, tiled=False)  22.6 us
  transfers between devices with their start and end apart: 68, of which 32 were waited for; matrix products, arithmetic and copies ran while one was open for 2% of the time, Pallas kernels for 48%

profile of v4, /device:TPU:0, one launch (start us, length us, event | category | flops | bytes accessed | tf_op | source)
XLA Modules:
  0.0 807.1 jit_solution(8547689653714429331)
XLA Ops:
  20.9 12.2 %all_gather.21 = bf16[2,2048]{1,0:T(2,128)(2,1)S(1)} all-gather(bf16[2,256]{1,0:T(2,128)(2,1)S(1)} %pad_maximum_fusion.4), channel_id=1, replica_groups=mesh['dp'=8,'tensor'=4] {'dp'}, dimensions={1}, use_global_device_ids=true | all-gather | bytes 9216 | tf_op jit(solution)/shard_map/all_gather | solution.py:873
  37.9 23.1 %collective-permute-done.1.refs_0_.refs_2_ = bf16[512,2048]{1,0:T(8,128)(2,1)} collective-permute-done((bf16[512,2048]{1,0:T(8,128)(2,1)S(1)}, bf16[512,2048]{1,0:T(8,128)(2,1)}, u32[]{:S(2)}, u32[]{:S(2)}) %collective-permute-start.1) | collective-permute-done | bytes 2097184 | tf_op jit(solution)/shard_map/ppermute | solution.py:157
  68.2 20.6 %collective-permute-done.3.refs_1_.refs_4_ = bf16[512,1024]{1,0:T(8,128)(2,1)S(1)} collective-permute-done((bf16[512,1024]{1,0:T(8,128)(2,1)S(1)}, bf16[512,1024]{1,0:T(8,128)(2,1)S(1)}, u32[]{:S(2)}, u32[]{:S(2)}) %collective-permute-start.3) | collective-permute-done | bytes 1048608 | tf_op jit(solution)/shard_map/ppermute | solution.py:167
  100.0 12.1 %shard_map.156.refs_1_.refs_2_.refs_3_ = bf16[3,4,256,512]{3,2,1,0:T(8,128)(2,1)} custom-call(bf16[4,256,2048]{2,1,0:T(8,128)(2,1)} %shard_map.155.refs_0_.refs_6_, bf16[8,4,256,512]{3,2,1,0:T(8,128)(2,1)} %bitcast.59, f32[4,256,128]{2,1,0:T(8,128)S(1)} %copy-done.30, f32[4,256,128]{2,1,0:T(8,128)S(1)} %copy-done.27), custom_call_target="tpu_custom_call" | custom-call | flops 2147483648 | bytes 4543829 | tf_op jit(solution)/shard_map/pallas_call | solution.py:84
  112.1 15.4 %shard_map.157 = (bf16[4,256,512]{2,1,0:T(8,128)(2,1)S(1)}, f32[1,4,8,256]{3,2,1,0:T(8,128)S(1)}) custom-call(s32[4]{0:T(128)S(1)} %iota_xor_fusion.refs_0_, bf16[3,4,256,512]{3,2,1,0:T(8,128)(2,1)} %shard_map.156.refs_1_.refs_2_.refs_3_, bf16[3,4,256,512]{3,2,1,0:T(8,128)(2,1)} %shard_map.156.refs_1_.refs_2_.refs_3_, ...), custom_call_target="tpu_custom_call" | custom-call | flops 1431655808 | bytes 1398101 | tf_op jit(solution)/shard_map/pallas_call | solution.py:84
  140.6 12.2 %shard_map.161.refs_4_.refs_1_.refs_2_.refs_3_ = bf16[3,4,256,512]{3,2,1,0:T(8,128)(2,1)} custom-call(bf16[4,256,2048]{2,1,0:T(8,128)(2,1)} %shard_map.160.refs_0_.refs_6_.refs_1_, bf16[8,4,256,512]{3,2,1,0:T(8,128)(2,1)} %bitcast.61, f32[4,256,128]{2,1,0:T(8,128)S(1)} %copy-done.24, f32[4,256,128]{2,1,0:T(8,128)S(1)} %copy-done.21), custom_call_target="tpu_custom_call" | custom-call | flops 2147483648 | bytes 4543829 | tf_op jit(solution)/shard_map/pallas_call | solution.py:84
  157.7 15.4 %shard_map.163 = (bf16[4,256,512]{2,1,0:T(8,128)(2,1)S(1)}, f32[1,4,8,256]{3,2,1,0:T(8,128)S(1)}) custom-call(s32[4]{0:T(128)S(1)} %iota_xor_fusion.refs_0_, bf16[3,4,256,512]{3,2,1,0:T(8,128)(2,1)} %shard_map.161.refs_4_.refs_1_.refs_2_.refs_3_, bf16[3,4,256,512]{3,2,1,0:T(8,128)(2,1)} %shard_map.161.refs_4_.refs_1_.refs_2_.refs_3_, ...), custom_call_target="tpu_custom_call" | custom-call | flops 1431655808 | bytes 1398101 | tf_op jit(solution)/shard_map/pallas_call | solution.py:84
  183.1 7.6 collective-permute-done.10.refs_3_
  206.5 17.9 %collective-permute-done.17.refs_1_ = bf16[256,2048]{1,0:T(8,128)(2,1)S(1)} collective-permute-done((bf16[256,2048]{1,0:T(8,128)(2,1)S(1)}, bf16[256,2048]{1,0:T(8,128)(2,1)S(1)}, u32[]{:S(2)}, u32[]{:S(2)}) %collective-permute-start.17) | collective-permute-done | bytes 1048608 | tf_op jit(solution)/shard_map/ppermute | solution.py:156
  226.7 20.2 %collective-permute-done.14.refs_3_ = bf16[256,2048]{1,0:T(8,128)(2,1)S(1)} collective-permute-done((bf16[256,2048]{1,0:T(8,128)(2,1)S(1)}, bf16[256,2048]{1,0:T(8,128)(2,1)S(1)}, u32[]{:S(2)}, u32[]{:S(2)}) %collective-permute-start.14) | collective-permute-done | bytes 1048608 | tf_op jit(solution)/shard_map/ppermute | solution.py:212
  250.8 18.5 %collective-permute-done.23.refs_1_ = bf16[256,2048]{1,0:T(8,128)(2,1)S(1)} collective-permute-done((bf16[256,2048]{1,0:T(8,128)(2,1)S(1)}, bf16[256,2048]{1,0:T(8,128)(2,1)S(1)}, u32[]{:S(2)}, u32[]{:S(2)}) %collective-permute-start.23) | collective-permute-done | bytes 1048608 | tf_op jit(solution)/shard_map/ppermute | solution.py:156
  273.7 6.9 collective-permute-done.20.refs_3_
  284.7 24.0 %shard_map.171 = (bf16[4,256,2048]{2,1,0:T(8,128)(2,1)}, bf16[4,256,2048]{2,1,0:T(8,128)(2,1)}, bf16[4,256,2048]{2,1,0:T(8,128)(2,1)}, bf16[4,256,2048]{2,1,0:T(8,128)(2,1)}) custom-call(bf16[256,2048]{1,0:T(8,128)(2,1)} %copy-done.60, bf16[256,2048]{1,0:T(8,128)(2,1)} %copy-done.61, bf16[256,2048]{1,0:T(8,128)(2,1)} %copy-done.62, ...), custom_call_target="tpu_custom_call" | custom-call | flops 5726623232 | bytes 12582912 | tf_op jit(solution)/shard_map/pallas_call | solution.py:84
  322.8 23.9 %shard_map.174 = (bf16[4,256,2048]{2,1,0:T(8,128)(2,1)}, bf16[4,256,2048]{2,1,0:T(8,128)(2,1)}, bf16[4,256,2048]{2,1,0:T(8,128)(2,1)}, bf16[4,256,2048]{2,1,0:T(8,128)(2,1)}) custom-call(bf16[256,2048]{1,0:T(8,128)(2,1)} %get-tuple-element.141.refs_2_.refs_0_, bf16[256,2048]{1,0:T(8,128)(2,1)} %collective-permute-done.18.refs_1_, ...), custom_call_target="tpu_custom_call" | custom-call | flops 5726623232 | bytes 12582912 | tf_op jit(solution)/shard_map/pallas_call | solution.py:84
  346.7 15.4 %shard_map.175 = (bf16[4,256,2048]{2,1,0:T(8,128)(2,1)}, bf16[4,256,2048]{2,1,0:T(8,128)(2,1)}) custom-call(bf16[4,256,2048]{2,1,0:T(8,128)(2,1)} %shard_map.166.refs_4_.refs_0_.refs_2_, bf16[8,2048,256]{2,1,0:T(8,128)(2,1)} %bitcast.77, bf16[4,256,2048]{2,1,0:T(8,128)(2,1)} %get-tuple-element.151.refs_2_, bf16[4,256,2048]{2,1,0:T(8,128)(2,1)} %get-tuple-element.152.refs_3_, ...), custom_call_target="tpu_custom_call" | custom-call | flops 2863311616 | bytes 9786709 | tf_op jit(solution)/shard_map/pallas_call | solution.py:84
  362.1 23.9 %shard_map.176.refs_4_ = bf16[8,2048,256]{2,1,0:T(8,128)(2,1)} custom-call(bf16[4,256,2048]{2,1,0:T(8,128)(2,1)} %get-tuple-element.144.refs_2_.refs_0_, bf16[4,256,2048]{2,1,0:T(8,128)(2,1)} %get-tuple-element.148.refs_4_.refs_1_.refs_0_, bf16[4,256,2048]{2,1,0:T(8,128)(2,1)} %shard_map.166.refs_4_.refs_0_.refs_2_, ...), custom_call_target="tpu_custom_call" | custom-call | flops 5726623232 | bytes 8388608 | tf_op jit(solution)/shard_map/pallas_call | solution.py:84
  386.1 23.8 %shard_map.177 = (bf16[256,2048]{1,0:T(8,128)(2,1)S(1)}, bf16[256,2048]{1,0:T(8,128)(2,1)S(1)}, bf16[256,2048]{1,0:T(8,128)(2,1)S(1)}, bf16[256,1024]{1,0:T(8,128)(2,1)S(1)}, bf16[256,1024]{1,0:T(8,128)(2,1)S(1)}) custom-call(bf16[4,256,2048]{2,1,0:T(8,128)(2,1)} %get-tuple-element.153.refs_0_.refs_2_, ...), custom_call_target="tpu_custom_call" | custom-call | flops 5726623232 | bytes 9786709 | tf_op jit(solution)/shard_map/pallas_call | solution.py:84
  412.0 15.5 %shard_map.178 = (bf16[4,256,2048]{2,1,0:T(8,128)(2,1)}, bf16[4,256,2048]{2,1,0:T(8,128)(2,1)}) custom-call(bf16[4,256,2048]{2,1,0:T(8,128)(2,1)} %shard_map.173.refs_6_.refs_3_.refs_0_, bf16[8,2048,256]{2,1,0:T(8,128)(2,1)} %bitcast.78, bf16[4,256,2048]{2,1,0:T(8,128)(2,1)} %get-tuple-element.149.refs_2_, bf16[4,256,2048]{2,1,0:T(8,128)(2,1)} %get-tuple-element.150.refs_3_, ...), custom_call_target="tpu_custom_call" | custom-call | flops 2863311616 | bytes 9786709 | tf_op jit(solution)/shard_map/pallas_call | solution.py:84
  430.2 23.5 %shard_map.180 = (bf16[256,2048]{1,0:T(8,128)(2,1)S(1)}, bf16[256,2048]{1,0:T(8,128)(2,1)S(1)}, bf16[256,2048]{1,0:T(8,128)(2,1)S(1)}, bf16[256,1024]{1,0:T(8,128)(2,1)S(1)}, bf16[256,1024]{1,0:T(8,128)(2,1)S(1)}) custom-call(bf16[4,256,2048]{2,1,0:T(8,128)(2,1)} %get-tuple-element.156.refs_0_.refs_3_, ...), custom_call_target="tpu_custom_call" | custom-call | flops 5726623232 | bytes 9786709 | tf_op jit(solution)/shard_map/pallas_call | solution.py:84
  460.8 43.9 %shard_map.182.refs_4_.refs_0_ = bf16[8,512,2048]{2,1,0:T(8,128)(2,1)} custom-call(bf16[4,256,2048]{2,1,0:T(8,128)(2,1)} %get-tuple-element.167.refs_0_, bf16[4,256,2048]{2,1,0:T(8,128)(2,1)} %get-tuple-element.168.refs_1_, bf16[4,256,2048]{2,1,0:T(8,128)(2,1)} %get-tuple-element.153.refs_0_.refs_2_, ...), custom_call_target="tpu_custom_call" | custom-call | flops 11453246464 | bytes 13981013 | tf_op jit(solution)/shard_map/pallas_call | solution.py:84
  514.4 12.9 %shard_map.186 = (bf16[256,2048]{1,0:T(8,128)(2,1)S(1)}, bf16[256,2048]{1,0:T(8,128)(2,1)S(1)}, bf16[256,2048]{1,0:T(8,128)(2,1)S(1)}, bf16[256,1024]{1,0:T(8,128)(2,1)S(1)}, bf16[256,1024]{1,0:T(8,128)(2,1)S(1)}) custom-call(bf16[4,256,2048]{2,1,0:T(8,128)(2,1)} %get-tuple-element.144.refs_2_.refs_0_, bf16[8,2048,256]{2,1,0:T(8,128)(2,1)} %bitcast.79, ...), custom_call_target="tpu_custom_call" | custom-call | flops 2863311616 | bytes 5592405 | tf_op jit(solution)/shard_map/pallas_call | solution.py:84
  541.5 12.9 %shard_map.188 = (bf16[256,2048]{1,0:T(8,128)(2,1)S(1)}, bf16[256,2048]{1,0:T(8,128)(2,1)S(1)}, bf16[256,2048]{1,0:T(8,128)(2,1)S(1)}, bf16[256,1024]{1,0:T(8,128)(2,1)S(1)}, bf16[256,1024]{1,0:T(8,128)(2,1)S(1)}) custom-call(bf16[4,256,2048]{2,1,0:T(8,128)(2,1)} %get-tuple-element.148.refs_4_.refs_1_.refs_0_, bf16[8,2048,256]{2,1,0:T(8,128)(2,1)} %bitcast.80, ...), custom_call_target="tpu_custom_call" | custom-call | flops 2863311616 | bytes 5592405 | tf_op jit(solution)/shard_map/pallas_call | solution.py:84
  555.4 18.8 %collective-permute-done.40.refs_3_ = bf16[256,1024]{1,0:T(8,128)(2,1)S(1)} collective-permute-done((bf16[256,1024]{1,0:T(8,128)(2,1)S(1)}, bf16[256,1024]{1,0:T(8,128)(2,1)S(1)}, u32[]{:S(2)}, u32[]{:S(2)}) %collective-permute-start.40) | collective-permute-done | bytes 524320 | tf_op jit(solution)/shard_map/ppermute | solution.py:166
  581.7 22.3 %shard_map.190 = (bf16[4,256,512]{2,1,0:T(8,128)(2,1)S(1)}, bf16[4,256,512]{2,1,0:T(8,128)(2,1)S(1)}, bf16[4,256,512]{2,1,0:T(8,128)(2,1)S(1)}) custom-call(s32[4]{0:T(128)S(1)} %iota_xor_fusion.refs_0_, bf16[3,4,256,512]{3,2,1,0:T(8,128)(2,1)} %shard_map.156.refs_1_.refs_2_.refs_3_, bf16[3,4,256,512]{3,2,1,0:T(8,128)(2,1)} %shard_map.156.refs_1_.refs_2_.refs_3_, ...), custom_call_target="tpu_custom_call" | custom-call | flops 3579139328 | bytes 2446677 | tf_op jit(solution)/shard_map/pallas_call | solution.py:84
  610.6 10.8 %shard_map.193 = (bf16[256,2048]{1,0:T(8,128)(2,1)S(1)}, bf16[256,2048]{1,0:T(8,128)(2,1)S(1)}, bf16[256,2048]{1,0:T(8,128)(2,1)S(1)}, bf16[256,1024]{1,0:T(8,12...) custom-call(bf16[4,256,512]{2,1,0:T(8,128)(2,1)} %copy-done.38, bf16[4,256,512]{2,1,0:T(8,128)(2,1)} %copy-done.40, ...), custom_call_target="tpu_custom_call" | custom-call | flops 2147483648 | bytes 4543829 | tf_op jit(solution)/shard_map/pallas_call | solution.py:84
  632.7 22.3 %shard_map.196 = (bf16[4,256,512]{2,1,0:T(8,128)(2,1)S(1)}, bf16[4,256,512]{2,1,0:T(8,128)(2,1)S(1)}, bf16[4,256,512]{2,1,0:T(8,128)(2,1)S(1)}) custom-call(s32[4]{0:T(128)S(1)} %iota_xor_fusion.refs_0_, bf16[3,4,256,512]{3,2,1,0:T(8,128)(2,1)} %shard_map.161.refs_4_.refs_1_.refs_2_.refs_3_, ...), custom_call_target="tpu_custom_call" | custom-call | flops 3579139328 | bytes 2446677 | tf_op jit(solution)/shard_map/pallas_call | solution.py:84
  657.9 11.2 %shard_map.197 = (bf16[256,2048]{1,0:T(8,128)(2,1)S(1)}, bf16[256,2048]{1,0:T(8,128)(2,1)S(1)}, bf16[256,2048]{1,0:T(8,128)(2,1)S(1)}, bf16[256,1024]{1,0:T(8,12...) custom-call(bf16[4,256,512]{2,1,0:T(8,128)(2,1)} %copy-done.48, bf16[4,256,512]{2,1,0:T(8,128)(2,1)} %copy-done.50, ...), custom_call_target="tpu_custom_call" | custom-call | flops 2147483648 | bytes 4543829 | tf_op jit(solution)/shard_map/pallas_call | solution.py:84
  680.9 21.5 %shard_map.199.refs_4_.refs_0_ = bf16[8,1040,512]{2,1,0:T(8,128)(2,1)} custom-call(bf16[4,256,2048]{2,1,0:T(8,128)(2,1)} %shard_map.155.refs_0_.refs_6_, bf16[4,256,2048]{2,1,0:T(8,128)(2,1)} %shard_map.160.refs_0_.refs_6_.refs_1_, bf16[4,256,2048]{2,1,0:T(8,128)(2,1)} %get-tuple-element.206.refs_2_, bf16[4,256,2048]{2,1,0:T(8,128)(2,1)} %get-tuple-element.207.refs_3_, ...), custom_call_target="tpu_custom_call" | custom-call | flops 5726623232 | bytes 8388608 | tf_op jit(solution)/shard_map/pallas_call | solution.py:84
  710.5 21.5 %collective-permute-done.46.refs_2_ = bf16[256,2048]{1,0:T(8,128)(2,1)S(1)} collective-permute-done((bf16[256,2048]{1,0:T(8,128)(2,1)}, bf16[256,2048]{1,0:T(8,128)(2,1)S(1)}, u32[]{:S(2)}, u32[]{:S(2)}) %collective-permute-start.46) | collective-permute-done | bytes 1048608 | tf_op jit(solution)/shard_map/ppermute | solution.py:212
  734.9 8.7 %collective-permute-done.56.refs_1_ = bf16[256,1024]{1,0:T(8,128)(2,1)S(1)} collective-permute-done((bf16[256,1024]{1,0:T(8,128)(2,1)}, bf16[256,1024]{1,0:T(8,128)(2,1)S(1)}, u32[]{:S(2)}, u32[]{:S(2)}) %collective-permute-start.56) | collective-permute-done | bytes 524320 | tf_op jit(solution)/shard_map/ppermute | solution.py:204
  760.1 7.8 collective-permute-done.58.refs_4_
  771.3 22.6 %reduce-scatter.8.cloned.1.call-done = bf16[1,1040,512]{2,1,0:T(8,128)(2,1)} async-done(((bf16[8,1040,512]{2,1,0:T(8,128)(2,1)}), bf16[1,1040,512]{2,1,0:T(8,128)(2,1)}) %reduce-scatter.8.cloned.1.call-update) | async-done | bytes 1064976 | tf_op jit(solution)/shard_map/reduce_scatter | solution.py:904
  (413 shorter events, 221.7 us)
Async XLA Ops:
  7.2 90.7 %all-gather.7.cloned.1.call-start = ((), (), s32[]{:S(2)}) async-start(), calls=%async_computation.6 | async-start | bytes 9437184 | tf_op jit(solution)/shard_map/all_gather | solution.py:876
  10.7 271.9 %all-gather.9.cloned.1.call-start = ((), (), s32[]{:S(2)}) async-start(), calls=%async_computation.7 | async-start | bytes 18874368 | tf_op jit(solution)/shard_map/all_gather | solution.py:877
  11.5 335.3 %all-gather.11.cloned.1.call-start = ((), (), s32[]{:S(2)}) async-start(), calls=%async_computation.8 | async-start | bytes 9437184 | tf_op jit(solution)/shard_map/all_gather | solution.py:878
  12.2 497.8 %reduce-scatter.4.cloned.1.call-start = ((), (), s32[]{:S(2)}) async-start(), calls=%async_computation.3 | async-start | bytes 9437184 | tf_op jit(solution)/shard_map/reduce_scatter | solution.py:904
  12.2 48.8 %collective-permute-start.1 = (bf16[512,2048]{1,0:T(8,128)(2,1)S(1)}, bf16[512,2048]{1,0:T(8,128)(2,1)}, u32[]{:S(2)}, u32[]{:S(2)}) collective-permute-start(bf16[512,2048]{1,0:T(8,128)(2,1)S(1)} %bitcast.52), channel_id=1, source_target_pairs={{0,2},{1,3},{2,0},{3,1},{4,6},{5,7},{6,4},{7,5},{8,10},{9,11},{10,... | collective-permute-start | bytes 6291464 | tf_op jit(solution)/shard_map/ppermute | solution.py:157
  15.3 47.2 %collective-permute-start = (bf16[512,2048]{1,0:T(8,128)(2,1)S(1)}, bf16[512,2048]{1,0:T(8,128)(2,1)}, u32[]{:S(2)}, u32[]{:S(2)}) collective-permute-start(bf16[512,2048]{1,0:T(8,128)(2,1)S(1)} %bitcast.53), channel_id=1, source_target_pairs={{0,1},{1,0},{2,3},{3,2},{4,5},{5,4},{6,7},{7,6},{8,9},{9,8},{10,11... | collective-permute-start | bytes 6291464 | tf_op jit(solution)/shard_map/ppermute | solution.py:156
  88.8 45.5 %collective-permute-start.5 = (bf16[256,2048]{1,0:T(8,128)(2,1)}, bf16[256,2048]{1,0:T(8,128)(2,1)}, u32[]{:S(2)}, u32[]{:S(2)}) collective-permute-start(bf16[256,2048]{1,0:T(8,128)(2,1)} %shard_map.153.refs_2_.refs_0_), channel_id=1, source_target_pairs={{0,1},{1,0},{2,3},{3,2},{4,5},{5,4},{6,7},{7,6},{8,9},{9,8},{10,11... | collective-permute-start | bytes 3145736 | tf_op jit(solution)/shard_map/ppermute | solution.py:156
  90.3 44.0 %collective-permute-start.4 = (bf16[256,2048]{1,0:T(8,128)(2,1)}, bf16[256,2048]{1,0:T(8,128)(2,1)}, u32[]{:S(2)}, u32[]{:S(2)}) collective-permute-start(bf16[256,2048]{1,0:T(8,128)(2,1)} %shard_map.153.refs_2_.refs_0_), channel_id=1, source_target_pairs={{0,2},{1,3},{2,0},{3,1},{4,6},{5,7},{6,4},{7,5},{8,10},{9,11},{10,... | collective-permute-start | bytes 3145736 | tf_op jit(solution)/shard_map/ppermute | solution.py:157
  155.5 36.2 %collective-permute-start.11 = (bf16[256,1024]{1,0:T(8,128)(2,1)S(1)}, bf16[256,1024]{1,0:T(8,128)(2,1)S(1)}, u32[]{:S(2)}, u32[]{:S(2)}) collective-permute-start(bf16[256,1024]{1,0:T(8,128)(2,1)S(1)} %get-tuple-element.121.refs_6_), channel_id=1, source_target_pairs={{0,2},{1,3},{2,0},{3,1},{4,6},{5,7},{6,4},{7,5},{8,10},{9,11},{10,... | collective-permute-start | bytes 1572872 | tf_op jit(solution)/shard_map/ppermute | solution.py:167
  181.7 42.8 %collective-permute-start.17 = (bf16[256,2048]{1,0:T(8,128)(2,1)S(1)}, bf16[256,2048]{1,0:T(8,128)(2,1)S(1)}, u32[]{:S(2)}, u32[]{:S(2)}) collective-permute-start(bf16[256,2048]{1,0:T(8,128)(2,1)S(1)} %get-tuple-element.136.refs_5_.refs_0_), channel_id=1, source_target_pairs={{0,1},{1,0},{2,3},{3,2},{4,5},{5,4},{6,7},{7,6},{8,9},{9,8},{10,11... | collective-permute-start | bytes 3145736 | tf_op jit(solution)/shard_map/ppermute | solution.py:156
  203.4 43.4 %collective-permute-start.14 = (bf16[256,2048]{1,0:T(8,128)(2,1)S(1)}, bf16[256,2048]{1,0:T(8,128)(2,1)S(1)}, u32[]{:S(2)}, u32[]{:S(2)}) collective-permute-start(bf16[256,2048]{1,0:T(8,128)(2,1)S(1)} %get-tuple-element.137), channel_id=1, source_target_pairs={{0,1},{1,0},{2,3},{3,2},{4,5},{5,4},{6,7},{7,6},{8,9},{9,8},{10,11... | collective-permute-start | bytes 3145736 | tf_op jit(solution)/shard_map/ppermute | solution.py:212
  204.5 43.5 %collective-permute-start.15 = (bf16[256,2048]{1,0:T(8,128)(2,1)S(1)}, bf16[256,2048]{1,0:T(8,128)(2,1)S(1)}, u32[]{:S(2)}, u32[]{:S(2)}) collective-permute-start(bf16[256,2048]{1,0:T(8,128)(2,1)S(1)} %get-tuple-element.138.refs_2_), channel_id=1, source_target_pairs={{0,2},{1,3},{2,0},{3,1},{4,6},{5,7},{6,4},{7,5},{8,10},{9,11},{10,... | collective-permute-start | bytes 3145736 | tf_op jit(solution)/shard_map/ppermute | solution.py:213
  204.8 64.5 %collective-permute-start.23 = (bf16[256,2048]{1,0:T(8,128)(2,1)S(1)}, bf16[256,2048]{1,0:T(8,128)(2,1)S(1)}, u32[]{:S(2)}, u32[]{:S(2)}) collective-permute-start(bf16[256,2048]{1,0:T(8,128)(2,1)S(1)} %shard_map.154.refs_10_.refs_0_), channel_id=1, source_target_pairs={{0,1},{1,0},{2,3},{3,2},{4,5},{5,4},{6,7},{7,6},{8,9},{9,8},{10,11... | collective-permute-start | bytes 3145736 | tf_op jit(solution)/shard_map/ppermute | solution.py:156
  224.4 46.0 %collective-permute-start.22 = (bf16[256,2048]{1,0:T(8,128)(2,1)S(1)}, bf16[256,2048]{1,0:T(8,128)(2,1)S(1)}, u32[]{:S(2)}, u32[]{:S(2)}) collective-permute-start(bf16[256,2048]{1,0:T(8,128)(2,1)S(1)} %shard_map.154.refs_10_.refs_0_), channel_id=1, source_target_pairs={{0,2},{1,3},{2,0},{3,1},{4,6},{5,7},{6,4},{7,5},{8,10},{9,11},{10,... | collective-permute-start | bytes 3145736 | tf_op jit(solution)/shard_map/ppermute | solution.py:157
  225.7 54.9 %collective-permute-start.20 = (bf16[256,1024]{1,0:T(8,128)(2,1)S(1)}, bf16[256,1024]{1,0:T(8,128)(2,1)S(1)}, u32[]{:S(2)}, u32[]{:S(2)}) collective-permute-start(bf16[256,1024]{1,0:T(8,128)(2,1)S(1)} %get-tuple-element.142), channel_id=1, source_target_pairs={{0,1},{1,0},{2,3},{3,2},{4,5},{5,4},{6,7},{7,6},{8,9},{9,8},{10,11... | collective-permute-start | bytes 1572872 | tf_op jit(solution)/shard_map/ppermute | solution.py:166
  249.9 58.9 %collective-permute-start.19 = (bf16[256,2048]{1,0:T(8,128)(2,1)}, bf16[256,2048]{1,0:T(8,128)(2,1)}, u32[]{:S(2)}, u32[]{:S(2)}) collective-permute-start(bf16[256,2048]{1,0:T(8,128)(2,1)} %get-tuple-element.141.refs_2_.refs_0_), channel_id=1, source_target_pairs={{0,2},{1,3},{2,0},{3,1},{4,6},{5,7},{6,4},{7,5},{8,10},{9,11},{10,... | collective-permute-start | bytes 3145736 | tf_op jit(solution)/shard_map/ppermute | solution.py:157
  269.3 39.4 %collective-permute-start.18 = (bf16[256,2048]{1,0:T(8,128)(2,1)}, bf16[256,2048]{1,0:T(8,128)(2,1)}, u32[]{:S(2)}, u32[]{:S(2)}) collective-permute-start(bf16[256,2048]{1,0:T(8,128)(2,1)} %get-tuple-element.141.refs_2_.refs_0_), channel_id=1, source_target_pairs={{0,1},{1,0},{2,3},{3,2},{4,5},{5,4},{6,7},{7,6},{8,9},{9,8},{10,11... | collective-permute-start | bytes 3145736 | tf_op jit(solution)/shard_map/ppermute | solution.py:156
  272.8 41.6 %collective-permute-start.26 = (bf16[256,1024]{1,0:T(8,128)(2,1)}, bf16[256,1024]{1,0:T(8,128)(2,1)}, u32[]{:S(2)}, u32[]{:S(2)}) collective-permute-start(bf16[256,1024]{1,0:T(8,128)(2,1)} %get-tuple-element.147), channel_id=1, source_target_pairs={{0,1},{1,0},{2,3},{3,2},{4,5},{5,4},{6,7},{7,6},{8,9},{9,8},{10,11... | collective-permute-start | bytes 1572872 | tf_op jit(solution)/shard_map/ppermute | solution.py:166
  386.1 317.9 %reduce-scatter.6.cloned.1.call-start = ((), (), s32[]{:S(2)}) async-start(), calls=%async_computation.4 | async-start | bytes 18874368 | tf_op jit(solution)/shard_map/reduce_scatter | solution.py:904
  454.7 50.1 %collective-permute-start.31 = (bf16[256,1024]{1,0:T(8,128)(2,1)S(1)}, bf16[256,1024]{1,0:T(8,128)(2,1)S(1)}, u32[]{:S(2)}, u32[]{:S(2)}) collective-permute-start(bf16[256,1024]{1,0:T(8,128)(2,1)S(1)} %get-tuple-element.166), channel_id=1, source_target_pairs={{0,1},{1,0},{2,3},{3,2},{4,5},{5,4},{6,7},{7,6},{8,9},{9,8},{10,11... | collective-permute-start | bytes 1572872 | tf_op jit(solution)/shard_map/ppermute | solution.py:203
  456.1 48.7 %collective-permute-start.30 = (bf16[256,1024]{1,0:T(8,128)(2,1)S(1)}, bf16[256,1024]{1,0:T(8,128)(2,1)S(1)}, u32[]{:S(2)}, u32[]{:S(2)}) collective-permute-start(bf16[256,1024]{1,0:T(8,128)(2,1)S(1)} %get-tuple-element.164.refs_6_), channel_id=1, source_target_pairs={{0,2},{1,3},{2,0},{3,1},{4,6},{5,7},{6,4},{7,5},{8,10},{9,11},{10,... | collective-permute-start | bytes 1572872 | tf_op jit(solution)/shard_map/ppermute | solution.py:204
  458.7 47.5 %collective-permute-start.37 = (bf16[256,2048]{1,0:T(8,128)(2,1)S(1)}, bf16[256,2048]{1,0:T(8,128)(2,1)S(1)}, u32[]{:S(2)}, u32[]{:S(2)}) collective-permute-start(bf16[256,2048]{1,0:T(8,128)(2,1)S(1)} %get-tuple-element.175.refs_0_), channel_id=1, source_target_pairs={{0,1},{1,0},{2,3},{3,2},{4,5},{5,4},{6,7},{7,6},{8,9},{9,8},{10,11... | collective-permute-start | bytes 3145736 | tf_op jit(solution)/shard_map/ppermute | solution.py:156
  459.4 46.8 %collective-permute-start.36 = (bf16[256,2048]{1,0:T(8,128)(2,1)S(1)}, bf16[256,2048]{1,0:T(8,128)(2,1)S(1)}, u32[]{:S(2)}, u32[]{:S(2)}) collective-permute-start(bf16[256,2048]{1,0:T(8,128)(2,1)S(1)} %get-tuple-element.175.refs_0_), channel_id=1, source_target_pairs={{0,2},{1,3},{2,0},{3,1},{4,6},{5,7},{6,4},{7,5},{8,10},{9,11},{10,... | collective-permute-start | bytes 3145736 | tf_op jit(solution)/shard_map/ppermute | solution.py:157
  512.2 281.7 %reduce-scatter.8.cloned.1.call-start = ((), (), s32[]{:S(2)}) async-start(), calls=%async_computation.5 | async-start | bytes 9584640 | tf_op jit(solution)/shard_map/reduce_scatter | solution.py:904
  536.8 68.1 %collective-permute-start.45 = (bf16[256,2048]{1,0:T(8,128)(2,1)S(1)}, bf16[256,2048]{1,0:T(8,128)(2,1)S(1)}, u32[]{:S(2)}, u32[]{:S(2)}) collective-permute-start(bf16[256,2048]{1,0:T(8,128)(2,1)S(1)} %get-tuple-element.192.refs_0_), channel_id=1, source_target_pairs={{0,1},{1,0},{2,3},{3,2},{4,5},{5,4},{6,7},{7,6},{8,9},{9,8},{10,11... | collective-permute-start | bytes 3145736 | tf_op jit(solution)/shard_map/ppermute | solution.py:156
  537.5 68.6 %collective-permute-start.44 = (bf16[256,2048]{1,0:T(8,128)(2,1)S(1)}, bf16[256,2048]{1,0:T(8,128)(2,1)S(1)}, u32[]{:S(2)}, u32[]{:S(2)}) collective-permute-start(bf16[256,2048]{1,0:T(8,128)(2,1)S(1)} %get-tuple-element.192.refs_0_), channel_id=1, source_target_pairs={{0,2},{1,3},{2,0},{3,1},{4,6},{5,7},{6,4},{7,5},{8,10},{9,11},{10,... | collective-permute-start | bytes 3145736 | tf_op jit(solution)/shard_map/ppermute | solution.py:157
  540.9 66.9 %collective-permute-start.43 = (bf16[256,1024]{1,0:T(8,128)(2,1)S(1)}, bf16[256,1024]{1,0:T(8,128)(2,1)S(1)}, u32[]{:S(2)}, u32[]{:S(2)}) collective-permute-start(bf16[256,1024]{1,0:T(8,128)(2,1)S(1)} %get-tuple-element.191), channel_id=1, source_target_pairs={{0,1},{1,0},{2,3},{3,2},{4,5},{5,4},{6,7},{7,6},{8,9},{9,8},{10,11... | collective-permute-start | bytes 1572872 | tf_op jit(solution)/shard_map/ppermute | solution.py:203
  574.6 48.8 %collective-permute-start.39 = (bf16[256,1024]{1,0:T(8,128)(2,1)S(1)}, bf16[256,1024]{1,0:T(8,128)(2,1)S(1)}, u32[]{:S(2)}, u32[]{:S(2)}) collective-permute-start(bf16[256,1024]{1,0:T(8,128)(2,1)S(1)} %get-tuple-element.183), channel_id=1, source_target_pairs={{0,1},{1,0},{2,3},{3,2},{4,5},{5,4},{6,7},{7,6},{8,9},{9,8},{10,11... | collective-permute-start | bytes 1572872 | tf_op jit(solution)/shard_map/ppermute | solution.py:203
  608.9 69.0 %collective-permute-start.49 = (bf16[256,2048]{1,0:T(8,128)(2,1)S(1)}, bf16[256,2048]{1,0:T(8,128)(2,1)S(1)}, u32[]{:S(2)}, u32[]{:S(2)}) collective-permute-start(bf16[256,2048]{1,0:T(8,128)(2,1)S(1)} %get-tuple-element.194.refs_7_), channel_id=1, source_target_pairs={{0,2},{1,3},{2,0},{3,1},{4,6},{5,7},{6,4},{7,5},{8,10},{9,11},{10,... | collective-permute-start | bytes 3145736 | tf_op jit(solution)/shard_map/ppermute | solution.py:213
  623.4 54.6 %collective-permute-start.48 = (bf16[256,2048]{1,0:T(8,128)(2,1)S(1)}, bf16[256,2048]{1,0:T(8,128)(2,1)S(1)}, u32[]{:S(2)}, u32[]{:S(2)}) collective-permute-start(bf16[256,2048]{1,0:T(8,128)(2,1)S(1)} %get-tuple-element.199), channel_id=1, source_target_pairs={{0,1},{1,0},{2,3},{3,2},{4,5},{5,4},{6,7},{7,6},{8,9},{9,8},{10,11... | collective-permute-start | bytes 3145736 | tf_op jit(solution)/shard_map/ppermute | solution.py:212
  707.7 36.0 %collective-permute-start.56 = (bf16[256,1024]{1,0:T(8,128)(2,1)}, bf16[256,1024]{1,0:T(8,128)(2,1)S(1)}, u32[]{:S(2)}, u32[]{:S(2)}) collective-permute-start(bf16[256,1024]{1,0:T(8,128)(2,1)} %copy-done.92), channel_id=1, source_target_pairs={{0,2},{1,3},{2,0},{3,1},{4,6},{5,7},{6,4},{7,5},{8,10},{9,11},{10,... | collective-permute-start | bytes 1572872 | tf_op jit(solution)/shard_map/ppermute | solution.py:204
  709.7 48.0 %collective-permute-start.61 = (bf16[256,2048]{1,0:T(8,128)(2,1)S(1)}, bf16[256,2048]{1,0:T(8,128)(2,1)S(1)}, u32[]{:S(2)}, u32[]{:S(2)}) collective-permute-start(bf16[256,2048]{1,0:T(8,128)(2,1)S(1)} %get-tuple-element.212.refs_2_), channel_id=1, source_target_pairs={{0,2},{1,3},{2,0},{3,1},{4,6},{5,7},{6,4},{7,5},{8,10},{9,11},{10,... | collective-permute-start | bytes 3145736 | tf_op jit(solution)/shard_map/ppermute | solution.py:213
  (136 other events, 1928.3 us)
Sparse Core Ops, SparseCore 0:
  10.8 84.8 all-gather.6
  97.3 149.5 all-gather.8
  248.5 80.2 all-gather.10
  386.2 88.5 reduce-scatter.3
  512.4 167.2 reduce-scatter.5
  705.7 88.1 reduce-scatter.7

commit v5 on v4

--- a/solution.py
+++ b/solution.py
@@ -127,21 +127,20 @@
     right_ref[...] = x_ref[...]
 
 
-def halves(from_y, from_x):
+def halves(from_y, from_x, axis=1):
     rows, width = from_y.shape
-    half = width // 2
-    tile = min(128, rows)
-
-    def spec(which):
-        return pl.BlockSpec((tile, half), lambda i: (i, which))
-
+    shape = (rows, width // 2) if axis else (rows // 2, width)
+    tile = min(128, shape[0])
+    steps = shape[0] // tile
+    first = pl.BlockSpec((tile, shape[1]), lambda i: (i, 0))
+    second = pl.BlockSpec((tile, shape[1]), (lambda i: (i, 1)) if axis else (lambda i: (i + steps, 0)))
     return call(
         halves_kernel,
-        (rows // tile,),
-        [spec(0), spec(1)],
-        [spec(0), spec(0)],
-        [sds((rows, half), BF)] * 2,
-        nbytes=rows * half * 8,
+        (steps,),
+        [first, second],
+        [first, first],
+        [sds(shape, BF)] * 2,
+        nbytes=rows * width * 4,
     )(from_y, from_x)
 
 
@@ -212,6 +211,41 @@
             lax.ppermute(to_x, "tensor", swap_perm(4, 1)),
             lax.ppermute(to_y, "tensor", swap_perm(4, 2)),
         ]
+
+
+class HeadWeights:
+    def __init__(self, full, channel, nd):
+        _, _, ds, hc = full.shape
+        half = nd // 2
+        core = (lax.axis_index("dp") % 2).astype(jnp.int32)
+        self.full, self.channel, self.nd, self.core = full, channel, nd, core.reshape(1)
+        part = lax.dynamic_slice(full, (core * half, channel, 0, 0), (half, 1, ds, hc)).reshape(half * ds, hc)
+        self.from_x = lax.ppermute(part, "tensor", swap_perm(4, 1))
+        self.from_y = lax.ppermute(part, "tensor", swap_perm(4, 2))
+
+    def second(self):
+        top, bottom = halves(self.from_y, self.from_x, axis=0)
+        diag = [
+            lax.ppermute(top, "tensor", swap_perm(4, 1)),
+            lax.ppermute(bottom, "tensor", swap_perm(4, 2)),
+        ]
+        self.mine = [self.from_x, self.from_y] + diag
+        self.other = [lax.ppermute(a, "dp", swap_perm(self.nd, 1)) for a in self.mine]
+
+    def specs(self):
+        _, _, ds, hc = self.full.shape
+        block = (self.nd // 2, 1, ds, hc)
+        return [
+            pl.BlockSpec(block, lambda i, core: (core[0], self.channel, 0, 0), pipeline_mode=pl.Buffered(1)),
+            pl.BlockSpec(block, lambda i, core: (1 - core[0], self.channel, 0, 0), pipeline_mode=pl.Buffered(1)),
+        ] + [whole_spec(a.shape) for a in self.mine + self.other]
+
+    def arrays(self):
+        return [self.full, self.full] + self.mine + self.other
+
+
+def exchange_slots(blocks):
+    return [lax.ppermute(blocks[r], "tensor", swap_perm(4, r)) for r in range(1, 4)]
 
 
 def piece_shapes(nt, rows, width):
@@ -716,6 +750,44 @@
     )(mid, *terms, *old)
 
 
+def out_middle_kernel(core_ref, own_ref, *refs):
+    others, weights, (x_ref, gain_ref, mid_ref, low_ref) = refs[:3], refs[3:13], refs[13:]
+    hc = own_ref.shape[2]
+    half = x_ref.shape[1] // 2
+    for part, own, (wx, wy, wd0, wd1) in (
+        (core_ref[0], weights[0], weights[2:6]),
+        (1 - core_ref[0], weights[1], weights[6:10]),
+    ):
+        total = dot_nt(own_ref[0], own[:, 0].reshape(-1, hc))
+        total += dot_nt(others[0][...], wx[...])
+        total += dot_nt(others[1][...], wy[...])
+        diag = others[2][...]
+        total += jnp.concatenate([dot_nt(diag, wd0[...]), dot_nt(diag, wd1[...])], axis=1)
+        mid_ref[:, pl.ds(pl.multiple_of(part * half, half), half)] = total
+    mid = x_ref[...].astype(F32) + mid_ref[...]
+    mid_ref[...] = mid
+    scale = lax.rsqrt(jnp.mean(mid * mid, axis=-1, keepdims=True) + NORM_EPS)
+    low_ref[...] = (mid * scale * gain_ref[...]).astype(BF)
+
+
+def out_middle(ctx, received, weights, x, gain):
+    rows, width = x.shape
+    hc = ctx.shape[2]
+    return call(
+        out_middle_kernel,
+        (1,),
+        [pl.BlockSpec((1, rows, hc), lambda i, core: (0, 0, 0))]
+        + [whole_spec(a.shape) for a in received]
+        + weights.specs()
+        + [whole_spec(x.shape), whole_spec(gain.shape)],
+        [whole_spec((rows, width))] * 2,
+        [sds((rows, width), F32), sds((rows, width), BF)],
+        flops=8 * rows * width * hc,
+        nbytes=rows * (8 * width + 8 * hc) + 8 * width * hc,
+        prefetch=1,
+    )(weights.core, ctx, *received, *weights.arrays(), x, gain)
+
+
 def norm_back_kernel(nterms, nouts, first_ref, v_ref, gain_ref, *refs):
     terms, outs, sums = refs[:nterms], refs[len(refs) - nouts :], []
     if nouts == 3:
@@ -896,6 +968,8 @@
     starts = [start_slot[g * per : (g + 1) * per] for g in range(groups)]
 
     both = range(groups)
+    swap_heads = nt == 4 and nd % 4 == 0
+    received = {}
     qkv, ctx, lse, mid, low2, g_mid, g_low = ({} for _ in range(7))
     attn_sum, a2_all, ga2, out_sum, ga1 = ({} for _ in range(5))
     sum1, sum2, gm_all, gmf, g_qkv, g_ctx = ({} for _ in range(6))
@@ -908,10 +982,17 @@
 
     def attend(g):
         ctx[g], lse[g] = attention_forward(qkv[g], starts[g], slot_of, nt)
+        if swap_heads:
+            received[g] = exchange_slots(ctx[g])
+            return
         attn_sum[g] = Scatter(mm_back([ctx[g]], full_qkvo, [3], nt, 4)[0], nt)
 
     def middle(g):
-        mid[g], low2[g] = make_middle(x[g], g2, attn_sum[g].terms)
+        if swap_heads:
+            mid[g], low2[g] = out_middle(ctx[g], received[g], head_weights, x[g], g2)
+        else:
+            attn_sum[g].second()
+            mid[g], low2[g] = make_middle(x[g], g2, attn_sum[g].terms)
         a2_all[g] = Gather(low2[g], nt)
 
     def second_back(g):
@@ -953,28 +1034,30 @@
 
     a2, silu, slope, hid, gg, gu, go_all, gof = ({} for _ in range(8))
     x_all.second()
-    gather_cotangent(0)
     gather_cotangent(1)
     a1 = [assemble(x_all.pieces, nt, 0, groups, g1, coss + sins)]
+    if swap_heads:
+        head_weights = HeadWeights(full_qkvo, 3, nd)
+    gather_cotangent(0)
     project(0)
+    a1.append(assemble(x_all.pieces, nt, 1, groups, g1))
+    if swap_heads:
+        head_weights.second()
     attend(0)
+    go_all[1].second()
+    project(1)
+    middle(0)
+    attend(1)
+    a2_all[0].second()
+    gof[1] = assemble(go_all[1].pieces, nt, 0, 1)
+    middle(1)
     go_all[0].second()
-    a1.append(assemble(x_all.pieces, nt, 1, groups, g1))
-    project(1)
-    attn_sum[0].second()
-    attend(1)
-    middle(0)
-    gof[0] = assemble(go_all[0].pieces, nt, 0, 1)
-    attn_sum[1].second()
-    a2_all[0].second()
-    middle(1)
-    go_all[1].second()
     up_projection(0)
     a2_all[1].second()
-    gof[1] = assemble(go_all[1].pieces, nt, 0, 1)
+    gof[0] = assemble(go_all[0].pieces, nt, 0, 1)
     up_projection(1)
+    grad_down = dp_sum(wgrad_cols(by_group(hid), by_group(gof), nd))
     hidden_back(0)
-    grad_down = dp_sum(wgrad_cols(by_group(hid), by_group(gof), nd))
     second_back(0)
     hidden_back(1)
     ga2[0].second()
@@ -992,15 +1075,15 @@
     gm_all[1].second()
     out_sum[0].second()
     input_back(0)
-    out_sum[1].second()
     attention_back_start(1)
     attention_back(1)
+    layer_out = layer_out_rows(mid[0], out_sum[0].terms, 0, groups, None)
     input_back(1)
     ds = gain1.shape[0]
     gains = tensor_sum(jnp.concatenate([(sum1[0] + sum1[1]) / g1, sum2[0] + sum2[1]]), nt)
     gains = jnp.swapaxes(gains.reshape(2, nd, ds), 0, 1).astype(BF)
     gains = jnp.pad(gains, ((0, 0), (0, 14), (0, qkv_w.shape[2] - ds)))
-    layer_out = layer_out_rows(mid[0], out_sum[0].terms, 0, groups, None)
+    out_sum[1].second()
     grad_qkvo = wgrad_rows(
         [a1, by_group(gmf)],
         [[g_qkv[g][c] for g in both] for c in range(3)] + [by_group(ctx)],
@@ -1008,12 +1091,12 @@
         nd,
         gains,
     )
+    ga1[0].second()
     ga1[1].second()
     grad_qkvo = dp_sum(link(grad_qkvo, grad_gateup))
+    grad_input = finish(0, None)
     layer_out = layer_out_rows(mid[1], out_sum[1].terms, 1, groups, layer_out)
-    ga1[0].second()
-    grad_input = finish(1, None)
-    grad_input = finish(0, grad_input)
+    grad_input = finish(1, grad_input)
     return (
         layer_out.reshape(seqs, local, width),
         grad_input.reshape(seqs, local, width),

time: 813 us -> 820 us (level)
  waiting for transfers between devices: 233 us -> 221 us
  starting transfers between devices: 62.3 us -> 74.1 us
    all_gather x1, waiting for transfers between devices: 0.01 us -> 27.3 us  [per_device(): full_qkvo = lax.all_gather(qkvo_w, 'dp', axis=0, tiled=False)]
    ppermute x7, waiting for transfers between devices: 23.9 us -> 1.47 us  [__init__(): self.from_y = lax.ppermute(block, 'tensor', swap_perm(4, 2))]
    ppermute x7, waiting for transfers between devices: 37.9 us -> 18.1 us  [__init__(): self.from_x = lax.ppermute(block, 'tensor', swap_perm(4, 1))]
    ppermute x0 -> x14, waiting for transfers between devices: none -> 17.8 us  [the longest x6 17.7 us: exchange_slots(): lax.ppermute(blocks[r], 'tensor', swap_perm(4, r))]
    ppermute x8 -> x6, waiting for transfers between devices: 59.9 us -> 45.1 us  [second(): lax.ppermute(to_x, 'tensor', swap_perm(4, 1))]
    reduce_scatter x3, waiting for transfers between devices: 22.6 us -> 37.1 us  [dp_sum(): return lax.psum_scatter(grad, 'dp', scatter_dimension=0, tiled=False)]
    ppermute x0 -> x14, starting transfers between devices: none -> 14.4 us  [the longest x6 8.68 us: exchange_slots(): lax.ppermute(blocks[r], 'tensor', swap_perm(4, r))]
    ppermute x8 -> x6, waiting for transfers between devices: 9.83 us -> 0.02 us  [__init__(): self.for_x = lax.ppermute(diag_y, 'tensor', swap_perm(4, 2))]
  transfers between devices with their start and end apart: 68 -> 74, of which waited for: 32 -> 22; matrix products, arithmetic and copies ran while one was open for 2% -> 3% of each run, Pallas kernels for 48% -> 53%
where the time goes in v5:
time: 820 us; the launch traced here: 809 us
  Pallas kernels  426 us (52%)
  waiting for transfers between devices  221 us (27%)
  starting transfers between devices  74.1 us (9%)
  local copies, waits for them, and re-layouts  40 us (5%)
  other arithmetic  20.7 us (3%)
  between operations  15.8 us (2%)
  blocking collectives  12.1 us (1%)
    pallas_call x51, Pallas kernels, run(): pl.pallas_call(ordered_body, grid_spec=pltpu.PrefetchScalarGridSpec(num_s...  426 us
    ppermute x6, waiting for transfers between devices, second(): lax.ppermute(to_x, 'tensor', swap_perm(4, 1))  45.1 us
    ppermute x7, waiting for transfers between devices, second(): diag_x = lax.ppermute(left, 'tensor', swap_perm(4, 1))  37.2 us
    reduce_scatter x3, waiting for transfers between devices, dp_sum(): return lax.psum_scatter(grad, 'dp', scatter_dimension=0, tiled=False)  37.1 us
    unnamed x187, local copies, waits for them, and re-layouts  33.1 us
    ppermute x7, waiting for transfers between devices, second(): diag_y = lax.ppermute(right, 'tensor', swap_perm(4, 2))  32.2 us
    all_gather x1, waiting for transfers between devices, per_device(): full_qkvo = lax.all_gather(qkvo_w, 'dp', axis=0, tiled=False)  27.3 us
    ppermute x7, waiting for transfers between devices, __init__(): self.from_x = lax.ppermute(block, 'tensor', swap_perm(4, 1))  18.1 us
  transfers between devices with their start and end apart: 74, of which 22 were waited for; matrix products, arithmetic and copies ran while one was open for 3% of the time, Pallas kernels for 53%

profile of v5, /device:TPU:0, one launch (start us, length us, event | category | flops | bytes accessed | tf_op | source)
XLA Modules:
  0.0 809.1 jit_solution(7559852002732163520)
XLA Ops:
  23.8 12.1 %all_gather.21 = bf16[2,2048]{1,0:T(2,128)(2,1)S(1)} all-gather(bf16[2,256]{1,0:T(2,128)(2,1)S(1)} %pad_maximum_fusion.4), channel_id=1, replica_groups=mesh['dp'=8,'tensor'=4] {'dp'}, dimensions={1}, use_global_device_ids=true | all-gather | bytes 9216 | tf_op jit(solution)/shard_map/all_gather | solution.py:945
  43.4 17.6 %collective-permute-done.refs_1_ = bf16[512,2048]{1,0:T(8,128)(2,1)} collective-permute-done((bf16[512,2048]{1,0:T(8,128)(2,1)S(1)}, bf16[512,2048]{1,0:T(8,128)(2,1)}, u32[]{:S(2)}, u32[]{:S(2)}) %collective-permute-start) | collective-permute-done | bytes 2097184 | tf_op jit(solution)/shard_map/ppermute | solution.py:155
  68.3 27.3 %all-gather.7.cloned.1.call-done = bf16[32,256,512]{2,1,0:T(8,128)(2,1)} async-done(((bf16[4,256,512]{2,1,0:T(8,128)(2,1)}), bf16[32,256,512]{2,1,0:T(8,128)(2,1)}) %all-gather.7.cloned.1.call-update) | async-done | bytes 8388624 | tf_op jit(solution)/shard_map/all_gather | solution.py:948
  110.3 11.8 %shard_map.156.refs_6_.refs_1_.refs_2_.refs_3_ = bf16[3,4,256,512]{3,2,1,0:T(8,128)(2,1)} custom-call(bf16[4,256,2048]{2,1,0:T(8,128)(2,1)} %shard_map.154.refs_2_.refs_0_.refs_6_, bf16[8,4,256,512]{3,2,1,0:T(8,128)(2,1)} %bitcast.75, f32[4,256,128]{2,1,0:T(8,128)S(1)} %copy-done.31, f32[4,256,128]{2,1,0:T(8,128)S(1)} %get-tuple-element.237.refs_8_.refs_3_, ...), custom_call_target="tpu_custom_call" | custom-call | flops 2147483648 | bytes 4543829 | tf_op jit(solution)/shard_map/pallas_call | solution.py:84
  127.4 15.5 %shard_map.159 = (bf16[4,256,512]{2,1,0:T(8,128)(2,1)S(1)}, f32[1,4,8,256]{3,2,1,0:T(8,128)S(1)}) custom-call(s32[4]{0:T(128)S(1)} %iota_xor_fusion.refs_0_, bf16[3,4,256,512]{3,2,1,0:T(8,128)(2,1)} %shard_map.156.refs_6_.refs_1_.refs_2_.refs_3_, bf16[3,4,256,512]{3,2,1,0:T(8,128)(2,1)} %shard_map.156.refs_6_.refs_1_.refs_2_.refs_3_, ...), custom_call_target="tpu_custom_call" | custom-call | flops 1431655808 | bytes 1398101 | tf_op jit(solution)/shard_map/pallas_call | solution.py:84
  153.8 9.3 %collective-permute-done.9.refs_3_ = bf16[256,512]{1,0:T(8,128)(2,1)S(1)} collective-permute-done((bf16[256,512]{1,0:T(8,128)(2,1)S(1)}, bf16[256,512]{1,0:T(8,128)(2,1)S(1)}, u32[]{:S(2)}, u32[]{:S(2)}) %collective-permute-start.9) | collective-permute-done | bytes 262176 | tf_op jit(solution)/shard_map/ppermute | solution.py:248
  166.5 12.4 %shard_map.161.refs_17_.refs_1_.refs_2_.refs_3_ = bf16[3,4,256,512]{3,2,1,0:T(8,128)(2,1)} custom-call(bf16[4,256,2048]{2,1,0:T(8,128)(2,1)} %shard_map.157.refs_2_.refs_0_.refs_6_.refs_1_, bf16[8,4,256,512]{3,2,1,0:T(8,128)(2,1)} %bitcast.76, f32[4,256,128]{2,1,0:T(8,128)S(1)} %copy-done.27, f32[4,256,128]{2,1,0:T(8,128)S(1)} %get-tuple-element.236.refs_9_.refs_3_.refs_8_, ...), custom_call_target="tpu_custom_call" | custom-call | flops 2147483648 | bytes 4543829 | tf_op jit(solution)/shard_map/pallas_call | solution.py:84
  188.2 15.4 %shard_map.163 = (bf16[4,256,512]{2,1,0:T(8,128)(2,1)S(1)}, f32[1,4,8,256]{3,2,1,0:T(8,128)S(1)}) custom-call(s32[4]{0:T(128)S(1)} %iota_xor_fusion.refs_0_, bf16[3,4,256,512]{3,2,1,0:T(8,128)(2,1)} %shard_map.161.refs_17_.refs_1_.refs_2_.refs_3_, bf16[3,4,256,512]{3,2,1,0:T(8,128)(2,1)} %shard_map.161.refs_17_.refs_1_.refs_2_.refs_3_, ...), custom_call_target="tpu_custom_call" | custom-call | flops 1431655808 | bytes 1398101 | tf_op jit(solution)/shard_map/pallas_call | solution.py:84
  203.6 16.6 %collective-permute-done.20.refs_3_ = bf16[256,1024]{1,0:T(8,128)(2,1)S(1)} collective-permute-done((bf16[256,1024]{1,0:T(8,128)(2,1)S(1)}, bf16[256,1024]{1,0:T(8,128)(2,1)S(1)}, u32[]{:S(2)}, u32[]{:S(2)}) %collective-permute-start.20) | collective-permute-done | bytes 524320 | tf_op jit(solution)/shard_map/ppermute | solution.py:165
  220.6 21.8 %collective-permute-done.21.refs_4_ = bf16[256,1024]{1,0:T(8,128)(2,1)S(1)} collective-permute-done((bf16[256,1024]{1,0:T(8,128)(2,1)S(1)}, bf16[256,1024]{1,0:T(8,128)(2,1)S(1)}, u32[]{:S(2)}, u32[]{:S(2)}) %collective-permute-start.21) | collective-permute-done | bytes 524320 | tf_op jit(solution)/shard_map/ppermute | solution.py:166
  273.5 23.8 %shard_map.168 = (bf16[4,256,2048]{2,1,0:T(8,128)(2,1)}, bf16[4,256,2048]{2,1,0:T(8,128)(2,1)}, bf16[4,256,2048]{2,1,0:T(8,128)(2,1)}, bf16[4,256,2048]{2,1,0:T(8,128)(2,1)}) custom-call(bf16[256,2048]{1,0:T(8,128)(2,1)} %copy-done.55, bf16[256,2048]{1,0:T(8,128)(2,1)} %copy-done.57, bf16[256,2048]{1,0:T(8,128)(2,1)} %copy-done.56, ...), custom_call_target="tpu_custom_call" | custom-call | flops 5726623232 | bytes 12582912 | tf_op jit(solution)/shard_map/pallas_call | solution.py:84
  312.6 23.8 %shard_map.171 = (bf16[4,256,2048]{2,1,0:T(8,128)(2,1)}, bf16[4,256,2048]{2,1,0:T(8,128)(2,1)}, bf16[4,256,2048]{2,1,0:T(8,128)(2,1)}, bf16[4,256,2048]{2,1,0:T(8,128)(2,1)}) custom-call(bf16[256,2048]{1,0:T(8,128)(2,1)} %get-tuple-element.117.refs_2_.refs_0_, bf16[256,2048]{1,0:T(8,128)(2,1)} %collective-permute-done.24.refs_1_, ...), custom_call_target="tpu_custom_call" | custom-call | flops 5726623232 | bytes 12582912 | tf_op jit(solution)/shard_map/pallas_call | solution.py:84
  336.3 23.9 %shard_map.172.refs_4_ = bf16[8,2048,256]{2,1,0:T(8,128)(2,1)} custom-call(bf16[4,256,2048]{2,1,0:T(8,128)(2,1)} %get-tuple-element.120.refs_2_.refs_0_, bf16[4,256,2048]{2,1,0:T(8,128)(2,1)} %get-tuple-element.124.refs_1_.refs_0_, bf16[4,256,2048]{2,1,0:T(8,128)(2,1)} %shard_map.170.refs_6_.refs_2_.refs_0_, ...), custom_call_target="tpu_custom_call" | custom-call | flops 5726623232 | bytes 8388608 | tf_op jit(solution)/shard_map/pallas_call | solution.py:84
  360.3 15.9 %shard_map.173 = (bf16[4,256,2048]{2,1,0:T(8,128)(2,1)}, bf16[4,256,2048]{2,1,0:T(8,128)(2,1)}) custom-call(bf16[4,256,2048]{2,1,0:T(8,128)(2,1)} %shard_map.170.refs_6_.refs_2_.refs_0_, bf16[8,2048,256]{2,1,0:T(8,128)(2,1)} %bitcast.95, bf16[4,256,2048]{2,1,0:T(8,128)(2,1)} %get-tuple-element.127.refs_2_, bf16[4,256,2048]{2,1,0:T(8,128)(2,1)} %get-tuple-element.128.refs_3_, ...), custom_call_target="tpu_custom_call" | custom-call | flops 2863311616 | bytes 9786709 | tf_op jit(solution)/shard_map/pallas_call | solution.py:84
  376.3 23.4 %shard_map.174 = (bf16[256,2048]{1,0:T(8,128)(2,1)S(1)}, bf16[256,2048]{1,0:T(8,128)(2,1)S(1)}, bf16[256,2048]{1,0:T(8,128)(2,1)S(1)}, bf16[256,1024]{1,0:T(8,128)(2,1)S(1)}, bf16[256,1024]{1,0:T(8,128)(2,1)S(1)}) custom-call(bf16[4,256,2048]{2,1,0:T(8,128)(2,1)} %get-tuple-element.129.refs_0_.refs_2_, ...), custom_call_target="tpu_custom_call" | custom-call | flops 5726623232 | bytes 9786709 | tf_op jit(solution)/shard_map/pallas_call | solution.py:84
  401.3 15.6 %shard_map.175 = (bf16[4,256,2048]{2,1,0:T(8,128)(2,1)}, bf16[4,256,2048]{2,1,0:T(8,128)(2,1)}) custom-call(bf16[4,256,2048]{2,1,0:T(8,128)(2,1)} %shard_map.165.refs_17_.refs_3_.refs_0_, bf16[8,2048,256]{2,1,0:T(8,128)(2,1)} %bitcast.96, bf16[4,256,2048]{2,1,0:T(8,128)(2,1)} %get-tuple-element.125.refs_2_, ...), custom_call_target="tpu_custom_call" | custom-call | flops 2863311616 | bytes 9786709 | tf_op jit(solution)/shard_map/pallas_call | solution.py:84
  420.0 23.5 %shard_map.177 = (bf16[256,2048]{1,0:T(8,128)(2,1)S(1)}, bf16[256,2048]{1,0:T(8,128)(2,1)S(1)}, bf16[256,2048]{1,0:T(8,128)(2,1)S(1)}, bf16[256,1024]{1,0:T(8,128)(2,1)S(1)}, bf16[256,1024]{1,0:T(8,128)(2,1)S(1)}) custom-call(bf16[4,256,2048]{2,1,0:T(8,128)(2,1)} %get-tuple-element.132.refs_0_.refs_3_, ...), custom_call_target="tpu_custom_call" | custom-call | flops 5726623232 | bytes 9786709 | tf_op jit(solution)/shard_map/pallas_call | solution.py:84
  450.8 43.9 %shard_map.179.refs_4_.refs_0_ = bf16[8,512,2048]{2,1,0:T(8,128)(2,1)} custom-call(bf16[4,256,2048]{2,1,0:T(8,128)(2,1)} %get-tuple-element.143.refs_0_, bf16[4,256,2048]{2,1,0:T(8,128)(2,1)} %get-tuple-element.144.refs_1_, bf16[4,256,2048]{2,1,0:T(8,128)(2,1)} %get-tuple-element.129.refs_0_.refs_2_, ...), custom_call_target="tpu_custom_call" | custom-call | flops 11453246464 | bytes 13981013 | tf_op jit(solution)/shard_map/pallas_call | solution.py:84
  505.1 13.5 %shard_map.183 = (bf16[256,2048]{1,0:T(8,128)(2,1)S(1)}, bf16[256,2048]{1,0:T(8,128)(2,1)S(1)}, bf16[256,2048]{1,0:T(8,128)(2,1)S(1)}, bf16[256,1024]{1,0:T(8,128)(2,1)S(1)}, bf16[256,1024]{1,0:T(8,128)(2,1)S(1)}) custom-call(bf16[4,256,2048]{2,1,0:T(8,128)(2,1)} %get-tuple-element.120.refs_2_.refs_0_, bf16[8,2048,256]{2,1,0:T(8,128)(2,1)} %bitcast.97, ...), custom_call_target="tpu_custom_call" | custom-call | flops 2863311616 | bytes 5592405 | tf_op jit(solution)/shard_map/pallas_call | solution.py:84
  518.6 10.1 %collective-permute-done.40.refs_4_ = bf16[256,2048]{1,0:T(8,128)(2,1)S(1)} collective-permute-done((bf16[256,2048]{1,0:T(8,128)(2,1)}, bf16[256,2048]{1,0:T(8,128)(2,1)S(1)}, u32[]{:S(2)}, u32[]{:S(2)}) %collective-permute-start.40) | collective-permute-done | bytes 1048608 | tf_op jit(solution)/shard_map/ppermute | solution.py:211
  540.8 12.9 %shard_map.185 = (bf16[256,2048]{1,0:T(8,128)(2,1)S(1)}, bf16[256,2048]{1,0:T(8,128)(2,1)S(1)}, bf16[256,2048]{1,0:T(8,128)(2,1)S(1)}, bf16[256,1024]{1,0:T(8,128)(2,1)S(1)}, bf16[256,1024]{1,0:T(8,128)(2,1)S(1)}) custom-call(bf16[4,256,2048]{2,1,0:T(8,128)(2,1)} %get-tuple-element.124.refs_1_.refs_0_, bf16[8,2048,256]{2,1,0:T(8,128)(2,1)} %bitcast.98, ...), custom_call_target="tpu_custom_call" | custom-call | flops 2863311616 | bytes 5592405 | tf_op jit(solution)/shard_map/pallas_call | solution.py:84
  554.7 9.6 %collective-permute-done.49.refs_4_ = bf16[256,1024]{1,0:T(8,128)(2,1)S(1)} collective-permute-done((bf16[256,1024]{1,0:T(8,128)(2,1)S(1)}, bf16[256,1024]{1,0:T(8,128)(2,1)S(1)}, u32[]{:S(2)}, u32[]{:S(2)}) %collective-permute-start.49) | collective-permute-done | bytes 524320 | tf_op jit(solution)/shard_map/ppermute | solution.py:166
  564.4 6.0 shard_map.186
  570.4 22.3 %shard_map.187 = (bf16[4,256,512]{2,1,0:T(8,128)(2,1)S(1)}, bf16[4,256,512]{2,1,0:T(8,128)(2,1)S(1)}, bf16[4,256,512]{2,1,0:T(8,128)(2,1)S(1)}) custom-call(s32[4]{0:T(128)S(1)} %iota_xor_fusion.refs_0_, bf16[3,4,256,512]{3,2,1,0:T(8,128)(2,1)} %shard_map.156.refs_6_.refs_1_.refs_2_.refs_3_, ...), custom_call_target="tpu_custom_call" | custom-call | flops 3579139328 | bytes 2446677 | tf_op jit(solution)/shard_map/pallas_call | solution.py:84
  601.5 10.8 %shard_map.190 = (bf16[256,2048]{1,0:T(8,128)(2,1)S(1)}, bf16[256,2048]{1,0:T(8,128)(2,1)S(1)}, bf16[256,2048]{1,0:T(8,128)(2,1)S(1)}, bf16[256,1024]{1,0:T(8,12...) custom-call(bf16[4,256,512]{2,1,0:T(8,128)(2,1)} %copy-done.37, bf16[4,256,512]{2,1,0:T(8,128)(2,1)} %copy-done.39, ...), custom_call_target="tpu_custom_call" | custom-call | flops 2147483648 | bytes 4543829 | tf_op jit(solution)/shard_map/pallas_call | solution.py:84
  612.4 9.3 %collective-permute-done.50.refs_3_ = bf16[256,1024]{1,0:T(8,128)(2,1)S(1)} collective-permute-done((bf16[256,1024]{1,0:T(8,128)(2,1)S(1)}, bf16[256,1024]{1,0:T(8,128)(2,1)S(1)}, u32[]{:S(2)}, u32[]{:S(2)}) %collective-permute-start.50) | collective-permute-done | bytes 524320 | tf_op jit(solution)/shard_map/ppermute | solution.py:165
  628.8 22.4 %shard_map.192 = (bf16[4,256,512]{2,1,0:T(8,128)(2,1)S(1)}, bf16[4,256,512]{2,1,0:T(8,128)(2,1)S(1)}, bf16[4,256,512]{2,1,0:T(8,128)(2,1)S(1)}) custom-call(s32[4]{0:T(128)S(1)} %iota_xor_fusion.refs_0_, bf16[3,4,256,512]{3,2,1,0:T(8,128)(2,1)} %shard_map.161.refs_17_.refs_1_.refs_2_.refs_3_, ...), custom_call_target="tpu_custom_call" | custom-call | flops 3579139328 | bytes 2446677 | tf_op jit(solution)/shard_map/pallas_call | solution.py:84
  655.5 11.1 %shard_map.194 = (bf16[256,2048]{1,0:T(8,128)(2,1)S(1)}, bf16[256,2048]{1,0:T(8,128)(2,1)S(1)}, bf16[256,2048]{1,0:T(8,128)(2,1)S(1)}, bf16[256,1024]{1,0:T(8,12...) custom-call(bf16[4,256,512]{2,1,0:T(8,128)(2,1)} %copy-done.48, bf16[4,256,512]{2,1,0:T(8,128)(2,1)} %copy-done.50, ...), custom_call_target="tpu_custom_call" | custom-call | flops 2147483648 | bytes 4543829 | tf_op jit(solution)/shard_map/pallas_call | solution.py:84
  677.1 22.1 %shard_map.196.refs_4_.refs_0_ = bf16[8,1040,512]{2,1,0:T(8,128)(2,1)} custom-call(bf16[4,256,2048]{2,1,0:T(8,128)(2,1)} %shard_map.154.refs_2_.refs_0_.refs_6_, bf16[4,256,2048]{2,1,0:T(8,128)(2,1)} %shard_map.157.refs_2_.refs_0_.refs_6_.refs_1_, bf16[4,256,2048]{2,1,0:T(8,128)(2,1)} %get-tuple-element.188.refs_2_, ...), custom_call_target="tpu_custom_call" | custom-call | flops 5726623232 | bytes 8388608 | tf_op jit(solution)/shard_map/pallas_call | solution.py:84
  710.3 21.2 %collective-permute-done.62.refs_4_ = bf16[256,2048]{1,0:T(8,128)(2,1)S(1)} collective-permute-done((bf16[256,2048]{1,0:T(8,128)(2,1)}, bf16[256,2048]{1,0:T(8,128)(2,1)S(1)}, u32[]{:S(2)}, u32[]{:S(2)}) %collective-permute-start.62) | collective-permute-done | bytes 1048608 | tf_op jit(solution)/shard_map/ppermute | solution.py:211
  746.6 8.3 %collective-permute-done.66.refs_4_ = bf16[256,2048]{1,0:T(8,128)(2,1)S(1)} collective-permute-done((bf16[256,2048]{1,0:T(8,128)(2,1)}, bf16[256,2048]{1,0:T(8,128)(2,1)S(1)}, u32[]{:S(2)}, u32[]{:S(2)}) %collective-permute-start.66) | collective-permute-done | bytes 1048608 | tf_op jit(solution)/shard_map/ppermute | solution.py:211
  758.9 37.1 %reduce-scatter.8.cloned.1.call-done = bf16[1,1040,512]{2,1,0:T(8,128)(2,1)} async-done(((bf16[8,1040,512]{2,1,0:T(8,128)(2,1)}), bf16[1,1040,512]{2,1,0:T(8,128)(2,1)}) %reduce-scatter.8.cloned.1.call-update) | async-done | bytes 1064976 | tf_op jit(solution)/shard_map/reduce_scatter | solution.py:978
  (407 shorter events, 222.7 us)
Async XLA Ops:
  7.2 88.4 %all-gather.7.cloned.1.call-start = ((), (), s32[]{:S(2)}) async-start(), calls=%async_computation.6 | async-start | bytes 9437184 | tf_op jit(solution)/shard_map/all_gather | solution.py:948
  10.7 260.7 %all-gather.9.cloned.1.call-start = ((), (), s32[]{:S(2)}) async-start(), calls=%async_computation.7 | async-start | bytes 18874368 | tf_op jit(solution)/shard_map/all_gather | solution.py:949
  11.5 348.9 %all-gather.11.cloned.1.call-start = ((), (), s32[]{:S(2)}) async-start(), calls=%async_computation.8 | async-start | bytes 9437184 | tf_op jit(solution)/shard_map/all_gather | solution.py:950
  12.2 487.8 %reduce-scatter.4.cloned.1.call-start = ((), (), s32[]{:S(2)}) async-start(), calls=%async_computation.3 | async-start | bytes 9437184 | tf_op jit(solution)/shard_map/reduce_scatter | solution.py:978
  12.2 48.7 %collective-permute-start = (bf16[512,2048]{1,0:T(8,128)(2,1)S(1)}, bf16[512,2048]{1,0:T(8,128)(2,1)}, u32[]{:S(2)}, u32[]{:S(2)}) collective-permute-start(bf16[512,2048]{1,0:T(8,128)(2,1)S(1)} %bitcast.66), channel_id=1, source_target_pairs={{0,1},{1,0},{2,3},{3,2},{4,5},{5,4},{6,7},{7,6},{8,9},{9,8},{10,11... | collective-permute-start | bytes 6291464 | tf_op jit(solution)/shard_map/ppermute | solution.py:155
  15.3 47.2 %collective-permute-start.1 = (bf16[512,2048]{1,0:T(8,128)(2,1)S(1)}, bf16[512,2048]{1,0:T(8,128)(2,1)}, u32[]{:S(2)}, u32[]{:S(2)}) collective-permute-start(bf16[512,2048]{1,0:T(8,128)(2,1)S(1)} %bitcast.67), channel_id=1, source_target_pairs={{0,2},{1,3},{2,0},{3,1},{4,6},{5,7},{6,4},{7,5},{8,10},{9,11},{10,... | collective-permute-start | bytes 6291464 | tf_op jit(solution)/shard_map/ppermute | solution.py:156
  66.2 37.2 %collective-permute-start.3 = (bf16[512,1024]{1,0:T(8,128)(2,1)}, bf16[512,1024]{1,0:T(8,128)(2,1)}, u32[]{:S(2)}, u32[]{:S(2)}) collective-permute-start(bf16[512,1024]{1,0:T(8,128)(2,1)} %get-tuple-element.105.refs_2_), channel_id=1, source_target_pairs={{0,2},{1,3},{2,0},{3,1},{4,6},{5,7},{6,4},{7,5},{8,10},{9,11},{10,... | collective-permute-start | bytes 3145736 | tf_op jit(solution)/shard_map/ppermute | solution.py:166
  67.7 36.8 %collective-permute-start.2 = (bf16[512,1024]{1,0:T(8,128)(2,1)}, bf16[512,1024]{1,0:T(8,128)(2,1)}, u32[]{:S(2)}, u32[]{:S(2)}) collective-permute-start(bf16[512,1024]{1,0:T(8,128)(2,1)} %get-tuple-element.104), channel_id=1, source_target_pairs={{0,1},{1,0},{2,3},{3,2},{4,5},{5,4},{6,7},{7,6},{8,9},{9,8},{10,11... | collective-permute-start | bytes 3145736 | tf_op jit(solution)/shard_map/ppermute | solution.py:165
  103.5 43.1 %collective-permute-start.4 = (bf16[256,2048]{1,0:T(8,128)(2,1)S(1)}, bf16[256,2048]{1,0:T(8,128)(2,1)S(1)}, u32[]{:S(2)}, u32[]{:S(2)}) collective-permute-start(bf16[256,2048]{1,0:T(8,128)(2,1)S(1)} %shard_map.153.refs_10_.refs_0_), channel_id=1, source_target_pairs={{0,2},{1,3},{2,0},{3,1},{4,6},{5,7},{6,4},{7,5},{8,10},{9,11},{10,... | collective-permute-start | bytes 3145736 | tf_op jit(solution)/shard_map/ppermute | solution.py:156
  103.9 43.2 %collective-permute-start.5 = (bf16[256,2048]{1,0:T(8,128)(2,1)S(1)}, bf16[256,2048]{1,0:T(8,128)(2,1)S(1)}, u32[]{:S(2)}, u32[]{:S(2)}) collective-permute-start(bf16[256,2048]{1,0:T(8,128)(2,1)S(1)} %shard_map.153.refs_10_.refs_0_), channel_id=1, source_target_pairs={{0,1},{1,0},{2,3},{3,2},{4,5},{5,4},{6,7},{7,6},{8,9},{9,8},{10,11... | collective-permute-start | bytes 3145736 | tf_op jit(solution)/shard_map/ppermute | solution.py:155
  183.5 59.5 %collective-permute-start.22 = (bf16[256,2048]{1,0:T(8,128)(2,1)S(1)}, bf16[256,2048]{1,0:T(8,128)(2,1)S(1)}, u32[]{:S(2)}, u32[]{:S(2)}) collective-permute-start(bf16[256,2048]{1,0:T(8,128)(2,1)S(1)} %get-tuple-element.111.refs_5_.refs_0_), channel_id=1, source_target_pairs={{0,2},{1,3},{2,0},{3,1},{4,6},{5,7},{6,4},{7,5},{8,10},{9,11},{10,... | collective-permute-start | bytes 3145736 | tf_op jit(solution)/shard_map/ppermute | solution.py:156
  184.1 59.1 %collective-permute-start.23 = (bf16[256,2048]{1,0:T(8,128)(2,1)S(1)}, bf16[256,2048]{1,0:T(8,128)(2,1)S(1)}, u32[]{:S(2)}, u32[]{:S(2)}) collective-permute-start(bf16[256,2048]{1,0:T(8,128)(2,1)S(1)} %get-tuple-element.111.refs_5_.refs_0_), channel_id=1, source_target_pairs={{0,1},{1,0},{2,3},{3,2},{4,5},{5,4},{6,7},{7,6},{8,9},{9,8},{10,11... | collective-permute-start | bytes 3145736 | tf_op jit(solution)/shard_map/ppermute | solution.py:155
  186.1 77.5 %collective-permute-start.28 = (bf16[256,2048]{1,0:T(8,128)(2,1)S(1)}, bf16[256,2048]{1,0:T(8,128)(2,1)S(1)}, u32[]{:S(2)}, u32[]{:S(2)}) collective-permute-start(bf16[256,2048]{1,0:T(8,128)(2,1)S(1)} %shard_map.155.refs_4_.refs_0_), channel_id=1, source_target_pairs={{0,2},{1,3},{2,0},{3,1},{4,6},{5,7},{6,4},{7,5},{8,10},{9,11},{10,... | collective-permute-start | bytes 3145736 | tf_op jit(solution)/shard_map/ppermute | solution.py:156
  187.6 54.8 %collective-permute-start.21 = (bf16[256,1024]{1,0:T(8,128)(2,1)S(1)}, bf16[256,1024]{1,0:T(8,128)(2,1)S(1)}, u32[]{:S(2)}, u32[]{:S(2)}) collective-permute-start(bf16[256,1024]{1,0:T(8,128)(2,1)S(1)} %get-tuple-element.108.refs_4_), channel_id=1, source_target_pairs={{0,2},{1,3},{2,0},{3,1},{4,6},{5,7},{6,4},{7,5},{8,10},{9,11},{10,... | collective-permute-start | bytes 1572872 | tf_op jit(solution)/shard_map/ppermute | solution.py:166
  220.2 44.7 %collective-permute-start.29 = (bf16[256,2048]{1,0:T(8,128)(2,1)S(1)}, bf16[256,2048]{1,0:T(8,128)(2,1)S(1)}, u32[]{:S(2)}, u32[]{:S(2)}) collective-permute-start(bf16[256,2048]{1,0:T(8,128)(2,1)S(1)} %shard_map.155.refs_4_.refs_0_), channel_id=1, source_target_pairs={{0,1},{1,0},{2,3},{3,2},{4,5},{5,4},{6,7},{7,6},{8,9},{9,8},{10,11... | collective-permute-start | bytes 3145736 | tf_op jit(solution)/shard_map/ppermute | solution.py:155
  360.2 342.9 %reduce-scatter.6.cloned.1.call-start = ((), (), s32[]{:S(2)}) async-start(), calls=%async_computation.4 | async-start | bytes 18874368 | tf_op jit(solution)/shard_map/reduce_scatter | solution.py:978
  444.5 50.2 %collective-permute-start.36 = (bf16[256,1024]{1,0:T(8,128)(2,1)S(1)}, bf16[256,1024]{1,0:T(8,128)(2,1)S(1)}, u32[]{:S(2)}, u32[]{:S(2)}) collective-permute-start(bf16[256,1024]{1,0:T(8,128)(2,1)S(1)} %get-tuple-element.140.refs_6_), channel_id=1, source_target_pairs={{0,2},{1,3},{2,0},{3,1},{4,6},{5,7},{6,4},{7,5},{8,10},{9,11},{10,... | collective-permute-start | bytes 1572872 | tf_op jit(solution)/shard_map/ppermute | solution.py:203
  445.2 49.5 %collective-permute-start.37 = (bf16[256,1024]{1,0:T(8,128)(2,1)S(1)}, bf16[256,1024]{1,0:T(8,128)(2,1)S(1)}, u32[]{:S(2)}, u32[]{:S(2)}) collective-permute-start(bf16[256,1024]{1,0:T(8,128)(2,1)S(1)} %get-tuple-element.142), channel_id=1, source_target_pairs={{0,1},{1,0},{2,3},{3,2},{4,5},{5,4},{6,7},{7,6},{8,9},{9,8},{10,11... | collective-permute-start | bytes 1572872 | tf_op jit(solution)/shard_map/ppermute | solution.py:202
  448.3 47.9 %collective-permute-start.42 = (bf16[256,2048]{1,0:T(8,128)(2,1)S(1)}, bf16[256,2048]{1,0:T(8,128)(2,1)S(1)}, u32[]{:S(2)}, u32[]{:S(2)}) collective-permute-start(bf16[256,2048]{1,0:T(8,128)(2,1)S(1)} %get-tuple-element.151.refs_0_), channel_id=1, source_target_pairs={{0,2},{1,3},{2,0},{3,1},{4,6},{5,7},{6,4},{7,5},{8,10},{9,11},{10,... | collective-permute-start | bytes 3145736 | tf_op jit(solution)/shard_map/ppermute | solution.py:156
  449.7 46.5 %collective-permute-start.43 = (bf16[256,2048]{1,0:T(8,128)(2,1)S(1)}, bf16[256,2048]{1,0:T(8,128)(2,1)S(1)}, u32[]{:S(2)}, u32[]{:S(2)}) collective-permute-start(bf16[256,2048]{1,0:T(8,128)(2,1)S(1)} %get-tuple-element.151.refs_0_), channel_id=1, source_target_pairs={{0,1},{1,0},{2,3},{3,2},{4,5},{5,4},{6,7},{7,6},{8,9},{9,8},{10,11... | collective-permute-start | bytes 3145736 | tf_op jit(solution)/shard_map/ppermute | solution.py:155
  502.3 293.7 %reduce-scatter.8.cloned.1.call-start = ((), (), s32[]{:S(2)}) async-start(), calls=%async_computation.5 | async-start | bytes 9584640 | tf_op jit(solution)/shard_map/reduce_scatter | solution.py:978
  532.0 62.7 %collective-permute-start.46 = (bf16[256,2048]{1,0:T(8,128)(2,1)S(1)}, bf16[256,2048]{1,0:T(8,128)(2,1)S(1)}, u32[]{:S(2)}, u32[]{:S(2)}) collective-permute-start(bf16[256,2048]{1,0:T(8,128)(2,1)S(1)} %get-tuple-element.160.refs_0_), channel_id=1, source_target_pairs={{0,1},{1,0},{2,3},{3,2},{4,5},{5,4},{6,7},{7,6},{8,9},{9,8},{10,11... | collective-permute-start | bytes 3145736 | tf_op jit(solution)/shard_map/ppermute | solution.py:155
  532.9 61.8 %collective-permute-start.47 = (bf16[256,2048]{1,0:T(8,128)(2,1)S(1)}, bf16[256,2048]{1,0:T(8,128)(2,1)S(1)}, u32[]{:S(2)}, u32[]{:S(2)}) collective-permute-start(bf16[256,2048]{1,0:T(8,128)(2,1)S(1)} %get-tuple-element.160.refs_0_), channel_id=1, source_target_pairs={{0,2},{1,3},{2,0},{3,1},{4,6},{5,7},{6,4},{7,5},{8,10},{9,11},{10,... | collective-permute-start | bytes 3145736 | tf_op jit(solution)/shard_map/ppermute | solution.py:156
  534.9 60.0 %collective-permute-start.52 = (bf16[256,1024]{1,0:T(8,128)(2,1)S(1)}, bf16[256,1024]{1,0:T(8,128)(2,1)S(1)}, u32[]{:S(2)}, u32[]{:S(2)}) collective-permute-start(bf16[256,1024]{1,0:T(8,128)(2,1)S(1)} %get-tuple-element.153.refs_6_), channel_id=1, source_target_pairs={{0,2},{1,3},{2,0},{3,1},{4,6},{5,7},{6,4},{7,5},{8,10},{9,11},{10,... | collective-permute-start | bytes 1572872 | tf_op jit(solution)/shard_map/ppermute | solution.py:203
  539.9 55.0 %collective-permute-start.53 = (bf16[256,1024]{1,0:T(8,128)(2,1)S(1)}, bf16[256,1024]{1,0:T(8,128)(2,1)S(1)}, u32[]{:S(2)}, u32[]{:S(2)}) collective-permute-start(bf16[256,1024]{1,0:T(8,128)(2,1)S(1)} %get-tuple-element.170), channel_id=1, source_target_pairs={{0,1},{1,0},{2,3},{3,2},{4,5},{5,4},{6,7},{7,6},{8,9},{9,8},{10,11... | collective-permute-start | bytes 1572872 | tf_op jit(solution)/shard_map/ppermute | solution.py:202
  595.6 56.6 %collective-permute-start.54 = (bf16[256,2048]{1,0:T(8,128)(2,1)S(1)}, bf16[256,2048]{1,0:T(8,128)(2,1)S(1)}, u32[]{:S(2)}, u32[]{:S(2)}) collective-permute-start(bf16[256,2048]{1,0:T(8,128)(2,1)S(1)} %get-tuple-element.178), channel_id=1, source_target_pairs={{0,1},{1,0},{2,3},{3,2},{4,5},{5,4},{6,7},{7,6},{8,9},{9,8},{10,11... | collective-permute-start | bytes 3145736 | tf_op jit(solution)/shard_map/ppermute | solution.py:211
  596.8 55.4 %collective-permute-start.55 = (bf16[256,2048]{1,0:T(8,128)(2,1)S(1)}, bf16[256,2048]{1,0:T(8,128)(2,1)S(1)}, u32[]{:S(2)}, u32[]{:S(2)}) collective-permute-start(bf16[256,2048]{1,0:T(8,128)(2,1)S(1)} %get-tuple-element.171.refs_7_), channel_id=1, source_target_pairs={{0,2},{1,3},{2,0},{3,1},{4,6},{5,7},{6,4},{7,5},{8,10},{9,11},{10,... | collective-permute-start | bytes 3145736 | tf_op jit(solution)/shard_map/ppermute | solution.py:212
  599.7 73.8 %collective-permute-start.44 = (bf16[256,1024]{1,0:T(8,128)(2,1)S(1)}, bf16[256,1024]{1,0:T(8,128)(2,1)S(1)}, u32[]{:S(2)}, u32[]{:S(2)}) collective-permute-start(bf16[256,1024]{1,0:T(8,128)(2,1)S(1)} %get-tuple-element.157.refs_6_), channel_id=1, source_target_pairs={{0,2},{1,3},{2,0},{3,1},{4,6},{5,7},{6,4},{7,5},{8,10},{9,11},{10,... | collective-permute-start | bytes 1572872 | tf_op jit(solution)/shard_map/ppermute | solution.py:203
  621.7 53.7 %collective-permute-start.45 = (bf16[256,1024]{1,0:T(8,128)(2,1)S(1)}, bf16[256,1024]{1,0:T(8,128)(2,1)S(1)}, u32[]{:S(2)}, u32[]{:S(2)}) collective-permute-start(bf16[256,1024]{1,0:T(8,128)(2,1)S(1)} %get-tuple-element.159), channel_id=1, source_target_pairs={{0,1},{1,0},{2,3},{3,2},{4,5},{5,4},{6,7},{7,6},{8,9},{9,8},{10,11... | collective-permute-start | bytes 1572872 | tf_op jit(solution)/shard_map/ppermute | solution.py:202
  706.3 37.4 %collective-permute-start.56 = (bf16[256,2048]{1,0:T(8,128)(2,1)}, bf16[256,2048]{1,0:T(8,128)(2,1)S(1)}, u32[]{:S(2)}, u32[]{:S(2)}) collective-permute-start(bf16[256,2048]{1,0:T(8,128)(2,1)} %copy-done.62), channel_id=1, source_target_pairs={{0,1},{1,0},{2,3},{3,2},{4,5},{5,4},{6,7},{7,6},{8,9},{9,8},{10,11... | collective-permute-start | bytes 3145736 | tf_op jit(solution)/shard_map/ppermute | solution.py:211
  707.5 36.2 %collective-permute-start.57 = (bf16[256,2048]{1,0:T(8,128)(2,1)}, bf16[256,2048]{1,0:T(8,128)(2,1)S(1)}, u32[]{:S(2)}, u32[]{:S(2)}) collective-permute-start(bf16[256,2048]{1,0:T(8,128)(2,1)} %copy-done.41), channel_id=1, source_target_pairs={{0,2},{1,3},{2,0},{3,1},{4,6},{5,7},{6,4},{7,5},{8,10},{9,11},{10,... | collective-permute-start | bytes 3145736 | tf_op jit(solution)/shard_map/ppermute | solution.py:212
  709.3 45.6 %collective-permute-start.66 = (bf16[256,2048]{1,0:T(8,128)(2,1)}, bf16[256,2048]{1,0:T(8,128)(2,1)S(1)}, u32[]{:S(2)}, u32[]{:S(2)}) collective-permute-start(bf16[256,2048]{1,0:T(8,128)(2,1)} %copy-done.69), channel_id=1, source_target_pairs={{0,1},{1,0},{2,3},{3,2},{4,5},{5,4},{6,7},{7,6},{8,9},{9,8},{10,11... | collective-permute-start | bytes 3145736 | tf_op jit(solution)/shard_map/ppermute | solution.py:211
  (133 other events, 2457.9 us)
Sparse Core Ops, SparseCore 0:
  10.8 84.7 all-gather.6
  97.2 149.7 all-gather.8
  248.5 80.2 all-gather.10
  360.4 87.5 reduce-scatter.3
  502.4 166.2 reduce-scatter.5
  705.3 90.6 reduce-scatter.7

commit v6 on v4

--- a/solution.py
+++ b/solution.py
@@ -978,21 +978,20 @@
     second_back(0)
     hidden_back(1)
     ga2[0].second()
+    grad_gateup = wgrad_rows([by_group(a2)], [by_group(gg), by_group(gu)], [0, 0], nd)
+    residual_back(0)
+    grad_gateup = dp_sum(link(grad_gateup, grad_down))
     second_back(1)
-    residual_back(0)
-    grad_gateup = wgrad_rows([by_group(a2)], [by_group(gg), by_group(gu)], [0, 0], nd)
+    gm_all[0].second()
+    project_out(0)
+    attention_back_start(0)
     ga2[1].second()
-    gm_all[0].second()
-    grad_gateup = dp_sum(link(grad_gateup, grad_down))
-    project_out(0)
+    attention_back(0)
     residual_back(1)
+    input_back(0)
     project_out(1)
-    attention_back_start(0)
-    attention_back(0)
     gm_all[1].second()
     out_sum[0].second()
-    input_back(0)
-    out_sum[1].second()
     attention_back_start(1)
     attention_back(1)
     input_back(1)
@@ -1000,6 +999,7 @@
     gains = tensor_sum(jnp.concatenate([(sum1[0] + sum1[1]) / g1, sum2[0] + sum2[1]]), nt)
     gains = jnp.swapaxes(gains.reshape(2, nd, ds), 0, 1).astype(BF)
     gains = jnp.pad(gains, ((0, 0), (0, 14), (0, qkv_w.shape[2] - ds)))
+    out_sum[1].second()
     layer_out = layer_out_rows(mid[0], out_sum[0].terms, 0, groups, None)
     grad_qkvo = wgrad_rows(
         [a1, by_group(gmf)],

time: 813 us -> 798 us (0.982)
  waiting for transfers between devices: 233 us -> 215 us
    ppermute x7, waiting for transfers between devices: 37.8 us -> 27.1 us  [second(): diag_x = lax.ppermute(left, 'tensor', swap_perm(4, 1))]
    unnamed x205 -> x179, local copies, waits for them, and re-layouts: 36.2 us -> 34.6 us
  transfers between devices with their start and end apart: 68 -> 68, of which waited for: 32 -> 29; matrix products, arithmetic and copies ran while one was open for 2% -> 2% of each run, Pallas kernels for 48% -> 49%
where the time goes in v6:
time: 798 us; the launch traced here: 792 us
  Pallas kernels  431 us (54%)
  waiting for transfers between devices  215 us (27%)
  starting transfers between devices  63.7 us (8%)
  local copies, waits for them, and re-layouts  38 us (5%)
  other arithmetic  16.6 us (2%)
  between operations  15.7 us (2%)
  blocking collectives  12.1 us (2%)
    pallas_call x54, Pallas kernels, run(): pl.pallas_call(ordered_body, grid_spec=pltpu.PrefetchScalarGridSpec(num_s...  431 us
    ppermute x8, waiting for transfers between devices, second(): lax.ppermute(to_x, 'tensor', swap_perm(4, 1))  60.5 us
    ppermute x7, waiting for transfers between devices, __init__(): self.from_x = lax.ppermute(block, 'tensor', swap_perm(4, 1))  38.3 us
    unnamed x179, local copies, waits for them, and re-layouts  34.6 us
    ppermute x7, waiting for transfers between devices, second(): diag_x = lax.ppermute(left, 'tensor', swap_perm(4, 1))  27.1 us
    ppermute x7, waiting for transfers between devices, __init__(): self.from_y = lax.ppermute(block, 'tensor', swap_perm(4, 2))  24 us
    ppermute x7, waiting for transfers between devices, second(): diag_y = lax.ppermute(right, 'tensor', swap_perm(4, 2))  23.7 us
    reduce_scatter x3, waiting for transfers between devices, dp_sum(): return lax.psum_scatter(grad, 'dp', scatter_dimension=0, tiled=False)  18.1 us
  transfers between devices with their start and end apart: 68, of which 29 were waited for; matrix products, arithmetic and copies ran while one was open for 2% of the time, Pallas kernels for 49%

profile of v6, /device:TPU:0, one launch (start us, length us, event | category | flops | bytes accessed | tf_op | source)
XLA Modules:
  0.0 791.7 jit_solution(16657463220186975234)
XLA Ops:
  21.0 12.1 %all_gather.21 = bf16[2,2048]{1,0:T(2,128)(2,1)S(1)} all-gather(bf16[2,256]{1,0:T(2,128)(2,1)S(1)} %pad_maximum_fusion.4), channel_id=1, replica_groups=mesh['dp'=8,'tensor'=4] {'dp'}, dimensions={1}, use_global_device_ids=true | all-gather | bytes 9216 | tf_op jit(solution)/shard_map/all_gather | solution.py:873
  37.9 23.2 %collective-permute-done.1.refs_0_.refs_2_ = bf16[512,2048]{1,0:T(8,128)(2,1)} collective-permute-done((bf16[512,2048]{1,0:T(8,128)(2,1)S(1)}, bf16[512,2048]{1,0:T(8,128)(2,1)}, u32[]{:S(2)}, u32[]{:S(2)}) %collective-permute-start.1) | collective-permute-done | bytes 2097184 | tf_op jit(solution)/shard_map/ppermute | solution.py:157
  68.5 20.6 %collective-permute-done.3.refs_1_.refs_4_ = bf16[512,1024]{1,0:T(8,128)(2,1)S(1)} collective-permute-done((bf16[512,1024]{1,0:T(8,128)(2,1)S(1)}, bf16[512,1024]{1,0:T(8,128)(2,1)S(1)}, u32[]{:S(2)}, u32[]{:S(2)}) %collective-permute-start.3) | collective-permute-done | bytes 1048608 | tf_op jit(solution)/shard_map/ppermute | solution.py:167
  100.2 12.2 %shard_map.156.refs_1_.refs_2_.refs_3_ = bf16[3,4,256,512]{3,2,1,0:T(8,128)(2,1)} custom-call(bf16[4,256,2048]{2,1,0:T(8,128)(2,1)} %shard_map.155.refs_0_.refs_6_, bf16[8,4,256,512]{3,2,1,0:T(8,128)(2,1)} %bitcast.59, f32[4,256,128]{2,1,0:T(8,128)S(1)} %copy-done.30, f32[4,256,128]{2,1,0:T(8,128)S(1)} %copy-done.27), custom_call_target="tpu_custom_call" | custom-call | flops 2147483648 | bytes 4543829 | tf_op jit(solution)/shard_map/pallas_call | solution.py:84
  112.4 15.5 %shard_map.157 = (bf16[4,256,512]{2,1,0:T(8,128)(2,1)S(1)}, f32[1,4,8,256]{3,2,1,0:T(8,128)S(1)}) custom-call(s32[4]{0:T(128)S(1)} %iota_xor_fusion.refs_0_, bf16[3,4,256,512]{3,2,1,0:T(8,128)(2,1)} %shard_map.156.refs_1_.refs_2_.refs_3_, bf16[3,4,256,512]{3,2,1,0:T(8,128)(2,1)} %shard_map.156.refs_1_.refs_2_.refs_3_, ...), custom_call_target="tpu_custom_call" | custom-call | flops 1431655808 | bytes 1398101 | tf_op jit(solution)/shard_map/pallas_call | solution.py:84
  141.4 12.0 %shard_map.161.refs_4_.refs_1_.refs_2_.refs_3_ = bf16[3,4,256,512]{3,2,1,0:T(8,128)(2,1)} custom-call(bf16[4,256,2048]{2,1,0:T(8,128)(2,1)} %shard_map.160.refs_0_.refs_6_.refs_1_, bf16[8,4,256,512]{3,2,1,0:T(8,128)(2,1)} %bitcast.61, f32[4,256,128]{2,1,0:T(8,128)S(1)} %copy-done.24, f32[4,256,128]{2,1,0:T(8,128)S(1)} %copy-done.21), custom_call_target="tpu_custom_call" | custom-call | flops 2147483648 | bytes 4543829 | tf_op jit(solution)/shard_map/pallas_call | solution.py:84
  158.3 15.5 %shard_map.163 = (bf16[4,256,512]{2,1,0:T(8,128)(2,1)S(1)}, f32[1,4,8,256]{3,2,1,0:T(8,128)S(1)}) custom-call(s32[4]{0:T(128)S(1)} %iota_xor_fusion.refs_0_, bf16[3,4,256,512]{3,2,1,0:T(8,128)(2,1)} %shard_map.161.refs_4_.refs_1_.refs_2_.refs_3_, bf16[3,4,256,512]{3,2,1,0:T(8,128)(2,1)} %shard_map.161.refs_4_.refs_1_.refs_2_.refs_3_, ...), custom_call_target="tpu_custom_call" | custom-call | flops 1431655808 | bytes 1398101 | tf_op jit(solution)/shard_map/pallas_call | solution.py:84
  183.3 8.0 %collective-permute-done.10.refs_3_ = bf16[256,1024]{1,0:T(8,128)(2,1)S(1)} collective-permute-done((bf16[256,1024]{1,0:T(8,128)(2,1)S(1)}, bf16[256,1024]{1,0:T(8,128)(2,1)S(1)}, u32[]{:S(2)}, u32[]{:S(2)}) %collective-permute-start.10) | collective-permute-done | bytes 524320 | tf_op jit(solution)/shard_map/ppermute | solution.py:166
  206.7 18.3 %collective-permute-done.17.refs_1_ = bf16[256,2048]{1,0:T(8,128)(2,1)S(1)} collective-permute-done((bf16[256,2048]{1,0:T(8,128)(2,1)S(1)}, bf16[256,2048]{1,0:T(8,128)(2,1)S(1)}, u32[]{:S(2)}, u32[]{:S(2)}) %collective-permute-start.17) | collective-permute-done | bytes 1048608 | tf_op jit(solution)/shard_map/ppermute | solution.py:156
  227.3 20.2 %collective-permute-done.14.refs_3_ = bf16[256,2048]{1,0:T(8,128)(2,1)S(1)} collective-permute-done((bf16[256,2048]{1,0:T(8,128)(2,1)S(1)}, bf16[256,2048]{1,0:T(8,128)(2,1)S(1)}, u32[]{:S(2)}, u32[]{:S(2)}) %collective-permute-start.14) | collective-permute-done | bytes 1048608 | tf_op jit(solution)/shard_map/ppermute | solution.py:212
  251.5 18.5 %collective-permute-done.23.refs_1_ = bf16[256,2048]{1,0:T(8,128)(2,1)S(1)} collective-permute-done((bf16[256,2048]{1,0:T(8,128)(2,1)S(1)}, bf16[256,2048]{1,0:T(8,128)(2,1)S(1)}, u32[]{:S(2)}, u32[]{:S(2)}) %collective-permute-start.23) | collective-permute-done | bytes 1048608 | tf_op jit(solution)/shard_map/ppermute | solution.py:156
  285.1 24.1 %shard_map.171 = (bf16[4,256,2048]{2,1,0:T(8,128)(2,1)}, bf16[4,256,2048]{2,1,0:T(8,128)(2,1)}, bf16[4,256,2048]{2,1,0:T(8,128)(2,1)}, bf16[4,256,2048]{2,1,0:T(8,128)(2,1)}) custom-call(bf16[256,2048]{1,0:T(8,128)(2,1)} %copy-done.57, bf16[256,2048]{1,0:T(8,128)(2,1)} %copy-done.58, bf16[256,2048]{1,0:T(8,128)(2,1)} %copy-done.59, ...), custom_call_target="tpu_custom_call" | custom-call | flops 5726623232 | bytes 12582912 | tf_op jit(solution)/shard_map/pallas_call | solution.py:84
  322.8 23.9 %shard_map.174 = (bf16[4,256,2048]{2,1,0:T(8,128)(2,1)}, bf16[4,256,2048]{2,1,0:T(8,128)(2,1)}, bf16[4,256,2048]{2,1,0:T(8,128)(2,1)}, bf16[4,256,2048]{2,1,0:T(8,128)(2,1)}) custom-call(bf16[256,2048]{1,0:T(8,128)(2,1)} %get-tuple-element.141.refs_2_.refs_0_, bf16[256,2048]{1,0:T(8,128)(2,1)} %collective-permute-done.18.refs_1_, ...), custom_call_target="tpu_custom_call" | custom-call | flops 5726623232 | bytes 12582912 | tf_op jit(solution)/shard_map/pallas_call | solution.py:84
  346.6 15.4 %shard_map.175 = (bf16[4,256,2048]{2,1,0:T(8,128)(2,1)}, bf16[4,256,2048]{2,1,0:T(8,128)(2,1)}) custom-call(bf16[4,256,2048]{2,1,0:T(8,128)(2,1)} %shard_map.166.refs_4_.refs_0_.refs_2_, bf16[8,2048,256]{2,1,0:T(8,128)(2,1)} %bitcast.77, bf16[4,256,2048]{2,1,0:T(8,128)(2,1)} %get-tuple-element.150.refs_2_, bf16[4,256,2048]{2,1,0:T(8,128)(2,1)} %get-tuple-element.151.refs_3_, ...), custom_call_target="tpu_custom_call" | custom-call | flops 2863311616 | bytes 9786709 | tf_op jit(solution)/shard_map/pallas_call | solution.py:84
  362.1 23.9 %shard_map.176.refs_4_ = bf16[8,2048,256]{2,1,0:T(8,128)(2,1)} custom-call(bf16[4,256,2048]{2,1,0:T(8,128)(2,1)} %get-tuple-element.144.refs_2_.refs_0_, bf16[4,256,2048]{2,1,0:T(8,128)(2,1)} %get-tuple-element.148.refs_4_.refs_1_.refs_0_, bf16[4,256,2048]{2,1,0:T(8,128)(2,1)} %shard_map.166.refs_4_.refs_0_.refs_2_, ...), custom_call_target="tpu_custom_call" | custom-call | flops 5726623232 | bytes 8388608 | tf_op jit(solution)/shard_map/pallas_call | solution.py:84
  386.0 23.7 %shard_map.177 = (bf16[256,2048]{1,0:T(8,128)(2,1)S(1)}, bf16[256,2048]{1,0:T(8,128)(2,1)S(1)}, bf16[256,2048]{1,0:T(8,128)(2,1)S(1)}, bf16[256,1024]{1,0:T(8,128)(2,1)S(1)}, bf16[256,1024]{1,0:T(8,128)(2,1)S(1)}) custom-call(bf16[4,256,2048]{2,1,0:T(8,128)(2,1)} %get-tuple-element.152.refs_0_.refs_2_, ...), custom_call_target="tpu_custom_call" | custom-call | flops 5726623232 | bytes 9786709 | tf_op jit(solution)/shard_map/pallas_call | solution.py:84
  411.9 15.6 %shard_map.178 = (bf16[4,256,2048]{2,1,0:T(8,128)(2,1)}, bf16[4,256,2048]{2,1,0:T(8,128)(2,1)}) custom-call(bf16[4,256,2048]{2,1,0:T(8,128)(2,1)} %shard_map.173.refs_6_.refs_3_.refs_0_, bf16[8,2048,256]{2,1,0:T(8,128)(2,1)} %bitcast.78, bf16[4,256,2048]{2,1,0:T(8,128)(2,1)} %get-tuple-element.159.refs_2_, bf16[4,256,2048]{2,1,0:T(8,128)(2,1)} %get-tuple-element.160.refs_3_, ...), custom_call_target="tpu_custom_call" | custom-call | flops 2863311616 | bytes 9786709 | tf_op jit(solution)/shard_map/pallas_call | solution.py:84
  430.1 44.2 %shard_map.180.refs_6_.refs_0_ = bf16[8,512,2048]{2,1,0:T(8,128)(2,1)} custom-call(bf16[4,256,2048]{2,1,0:T(8,128)(2,1)} %get-tuple-element.164.refs_0_, bf16[4,256,2048]{2,1,0:T(8,128)(2,1)} %get-tuple-element.165.refs_1_, bf16[4,256,2048]{2,1,0:T(8,128)(2,1)} %get-tuple-element.152.refs_0_.refs_2_, ...), custom_call_target="tpu_custom_call" | custom-call | flops 11453246464 | bytes 13981013 | tf_op jit(solution)/shard_map/pallas_call | solution.py:84
  481.1 24.3 %shard_map.183 = (bf16[256,2048]{1,0:T(8,128)(2,1)S(1)}, bf16[256,2048]{1,0:T(8,128)(2,1)S(1)}, bf16[256,2048]{1,0:T(8,128)(2,1)S(1)}, bf16[256,1024]{1,0:T(8,128)(2,1)S(1)}, bf16[256,1024]{1,0:T(8,128)(2,1)S(1)}) custom-call(bf16[4,256,2048]{2,1,0:T(8,128)(2,1)} %get-tuple-element.166.refs_3_.refs_0_, ...), custom_call_target="tpu_custom_call" | custom-call | flops 5726623232 | bytes 9786709 | tf_op jit(solution)/shard_map/pallas_call | solution.py:84
  509.7 12.8 %shard_map.185 = (bf16[256,2048]{1,0:T(8,128)(2,1)S(1)}, bf16[256,2048]{1,0:T(8,128)(2,1)S(1)}, bf16[256,2048]{1,0:T(8,128)(2,1)S(1)}, bf16[256,1024]{1,0:T(8,128)(2,1)S(1)}, bf16[256,1024]{1,0:T(8,128)(2,1)S(1)}) custom-call(bf16[4,256,2048]{2,1,0:T(8,128)(2,1)} %get-tuple-element.144.refs_2_.refs_0_, bf16[8,2048,256]{2,1,0:T(8,128)(2,1)} %bitcast.79, ...), custom_call_target="tpu_custom_call" | custom-call | flops 2863311616 | bytes 5592405 | tf_op jit(solution)/shard_map/pallas_call | solution.py:84
  530.5 22.9 %shard_map.188 = (bf16[4,256,512]{2,1,0:T(8,128)(2,1)S(1)}, bf16[4,256,512]{2,1,0:T(8,128)(2,1)S(1)}, bf16[4,256,512]{2,1,0:T(8,128)(2,1)S(1)}) custom-call(s32[4]{0:T(128)S(1)} %iota_xor_fusion.refs_0_, bf16[3,4,256,512]{3,2,1,0:T(8,128)(2,1)} %shard_map.156.refs_1_.refs_2_.refs_3_, bf16[3,4,256,512]{3,2,1,0:T(8,128)(2,1)} %shard_map.156.refs_1_.refs_2_.refs_3_, ...), custom_call_target="tpu_custom_call" | custom-call | flops 3579139328 | bytes 2446677 | tf_op jit(solution)/shard_map/pallas_call | solution.py:84
  561.7 10.9 %shard_map.190 = (bf16[256,2048]{1,0:T(8,128)(2,1)S(1)}, bf16[256,2048]{1,0:T(8,128)(2,1)S(1)}, bf16[256,2048]{1,0:T(8,128)(2,1)S(1)}, bf16[256,1024]{1,0:T(8,12...) custom-call(bf16[4,256,512]{2,1,0:T(8,128)(2,1)} %copy-done.38, bf16[4,256,512]{2,1,0:T(8,128)(2,1)} %copy-done.40, ...), custom_call_target="tpu_custom_call" | custom-call | flops 2147483648 | bytes 4543829 | tf_op jit(solution)/shard_map/pallas_call | solution.py:84
  575.3 13.5 %shard_map.191 = (bf16[256,2048]{1,0:T(8,128)(2,1)S(1)}, bf16[256,2048]{1,0:T(8,128)(2,1)S(1)}, bf16[256,2048]{1,0:T(8,128)(2,1)S(1)}, bf16[256,1024]{1,0:T(8,128)(2,1)S(1)}, bf16[256,1024]{1,0:T(8,128)(2,1)S(1)}) custom-call(bf16[4,256,2048]{2,1,0:T(8,128)(2,1)} %get-tuple-element.148.refs_4_.refs_1_.refs_0_, bf16[8,2048,256]{2,1,0:T(8,128)(2,1)} %bitcast.80, ...), custom_call_target="tpu_custom_call" | custom-call | flops 2863311616 | bytes 5592405 | tf_op jit(solution)/shard_map/pallas_call | solution.py:84
  595.7 8.2 %collective-permute-done.44.refs_3_ = bf16[256,1024]{1,0:T(8,128)(2,1)S(1)} collective-permute-done((bf16[256,1024]{1,0:T(8,128)(2,1)S(1)}, bf16[256,1024]{1,0:T(8,128)(2,1)S(1)}, u32[]{:S(2)}, u32[]{:S(2)}) %collective-permute-start.44) | collective-permute-done | bytes 524320 | tf_op jit(solution)/shard_map/ppermute | solution.py:166
  611.9 22.7 %shard_map.195 = (bf16[4,256,512]{2,1,0:T(8,128)(2,1)S(1)}, bf16[4,256,512]{2,1,0:T(8,128)(2,1)S(1)}, bf16[4,256,512]{2,1,0:T(8,128)(2,1)S(1)}) custom-call(s32[4]{0:T(128)S(1)} %iota_xor_fusion.refs_0_, bf16[3,4,256,512]{3,2,1,0:T(8,128)(2,1)} %shard_map.161.refs_4_.refs_1_.refs_2_.refs_3_, ...), custom_call_target="tpu_custom_call" | custom-call | flops 3579139328 | bytes 2446677 | tf_op jit(solution)/shard_map/pallas_call | solution.py:84
  637.6 10.7 %shard_map.196 = (bf16[256,2048]{1,0:T(8,128)(2,1)S(1)}, bf16[256,2048]{1,0:T(8,128)(2,1)S(1)}, bf16[256,2048]{1,0:T(8,128)(2,1)S(1)}, bf16[256,1024]{1,0:T(8,12...) custom-call(bf16[4,256,512]{2,1,0:T(8,128)(2,1)} %copy-done.46, bf16[4,256,512]{2,1,0:T(8,128)(2,1)} %copy-done.48, ...), custom_call_target="tpu_custom_call" | custom-call | flops 2147483648 | bytes 4543829 | tf_op jit(solution)/shard_map/pallas_call | solution.py:84
  663.4 21.8 %shard_map.199.refs_4_.refs_0_ = bf16[8,1040,512]{2,1,0:T(8,128)(2,1)} custom-call(bf16[4,256,2048]{2,1,0:T(8,128)(2,1)} %shard_map.155.refs_0_.refs_6_, bf16[4,256,2048]{2,1,0:T(8,128)(2,1)} %shard_map.160.refs_0_.refs_6_.refs_1_, bf16[4,256,2048]{2,1,0:T(8,128)(2,1)} %get-tuple-element.206.refs_2_, bf16[4,256,2048]{2,1,0:T(8,128)(2,1)} %get-tuple-element.207.refs_3_, ...), custom_call_target="tpu_custom_call" | custom-call | flops 5726623232 | bytes 8388608 | tf_op jit(solution)/shard_map/pallas_call | solution.py:84
  693.9 21.0 %collective-permute-done.48.refs_2_ = bf16[256,2048]{1,0:T(8,128)(2,1)S(1)} collective-permute-done((bf16[256,2048]{1,0:T(8,128)(2,1)}, bf16[256,2048]{1,0:T(8,128)(2,1)S(1)}, u32[]{:S(2)}, u32[]{:S(2)}) %collective-permute-start.48) | collective-permute-done | bytes 1048608 | tf_op jit(solution)/shard_map/ppermute | solution.py:212
  718.7 8.7 %collective-permute-done.56.refs_1_ = bf16[256,1024]{1,0:T(8,128)(2,1)S(1)} collective-permute-done((bf16[256,1024]{1,0:T(8,128)(2,1)}, bf16[256,1024]{1,0:T(8,128)(2,1)S(1)}, u32[]{:S(2)}, u32[]{:S(2)}) %collective-permute-start.56) | collective-permute-done | bytes 524320 | tf_op jit(solution)/shard_map/ppermute | solution.py:204
  735.8 10.3 %collective-permute-done.60.refs_4_ = bf16[256,2048]{1,0:T(8,128)(2,1)S(1)} collective-permute-done((bf16[256,2048]{1,0:T(8,128)(2,1)}, bf16[256,2048]{1,0:T(8,128)(2,1)S(1)}, u32[]{:S(2)}, u32[]{:S(2)}) %collective-permute-start.60) | collective-permute-done | bytes 1048608 | tf_op jit(solution)/shard_map/ppermute | solution.py:212
  749.1 8.1 %collective-permute-done.58.refs_4_ = bf16[256,2048]{1,0:T(8,128)(2,1)S(1)} collective-permute-done((bf16[256,2048]{1,0:T(8,128)(2,1)S(1)}, bf16[256,2048]{1,0:T(8,128)(2,1)S(1)}, u32[]{:S(2)}, u32[]{:S(2)}) %collective-permute-start.58) | collective-permute-done | bytes 1048608 | tf_op jit(solution)/shard_map/ppermute | solution.py:212
  760.4 18.1 %reduce-scatter.8.cloned.1.call-done = bf16[1,1040,512]{2,1,0:T(8,128)(2,1)} async-done(((bf16[8,1040,512]{2,1,0:T(8,128)(2,1)}), bf16[1,1040,512]{2,1,0:T(8,128)(2,1)}) %reduce-scatter.8.cloned.1.call-update) | async-done | bytes 1064976 | tf_op jit(solution)/shard_map/reduce_scatter | solution.py:904
  (387 shorter events, 215.1 us)
Async XLA Ops:
  7.2 90.9 %all-gather.7.cloned.1.call-start = ((), (), s32[]{:S(2)}) async-start(), calls=%async_computation.6 | async-start | bytes 9437184 | tf_op jit(solution)/shard_map/all_gather | solution.py:876
  10.7 272.2 %all-gather.9.cloned.1.call-start = ((), (), s32[]{:S(2)}) async-start(), calls=%async_computation.7 | async-start | bytes 18874368 | tf_op jit(solution)/shard_map/all_gather | solution.py:877
  11.5 335.2 %all-gather.11.cloned.1.call-start = ((), (), s32[]{:S(2)}) async-start(), calls=%async_computation.8 | async-start | bytes 9437184 | tf_op jit(solution)/shard_map/all_gather | solution.py:878
  12.2 465.5 %reduce-scatter.4.cloned.1.call-start = ((), (), s32[]{:S(2)}) async-start(), calls=%async_computation.3 | async-start | bytes 9437184 | tf_op jit(solution)/shard_map/reduce_scatter | solution.py:904
  12.2 48.8 %collective-permute-start.1 = (bf16[512,2048]{1,0:T(8,128)(2,1)S(1)}, bf16[512,2048]{1,0:T(8,128)(2,1)}, u32[]{:S(2)}, u32[]{:S(2)}) collective-permute-start(bf16[512,2048]{1,0:T(8,128)(2,1)S(1)} %bitcast.52), channel_id=1, source_target_pairs={{0,2},{1,3},{2,0},{3,1},{4,6},{5,7},{6,4},{7,5},{8,10},{9,11},{10,... | collective-permute-start | bytes 6291464 | tf_op jit(solution)/shard_map/ppermute | solution.py:157
  15.3 47.2 %collective-permute-start = (bf16[512,2048]{1,0:T(8,128)(2,1)S(1)}, bf16[512,2048]{1,0:T(8,128)(2,1)}, u32[]{:S(2)}, u32[]{:S(2)}) collective-permute-start(bf16[512,2048]{1,0:T(8,128)(2,1)S(1)} %bitcast.53), channel_id=1, source_target_pairs={{0,1},{1,0},{2,3},{3,2},{4,5},{5,4},{6,7},{7,6},{8,9},{9,8},{10,11... | collective-permute-start | bytes 6291464 | tf_op jit(solution)/shard_map/ppermute | solution.py:156
  89.2 45.9 %collective-permute-start.5 = (bf16[256,2048]{1,0:T(8,128)(2,1)}, bf16[256,2048]{1,0:T(8,128)(2,1)}, u32[]{:S(2)}, u32[]{:S(2)}) collective-permute-start(bf16[256,2048]{1,0:T(8,128)(2,1)} %shard_map.153.refs_2_.refs_0_), channel_id=1, source_target_pairs={{0,1},{1,0},{2,3},{3,2},{4,5},{5,4},{6,7},{7,6},{8,9},{9,8},{10,11... | collective-permute-start | bytes 3145736 | tf_op jit(solution)/shard_map/ppermute | solution.py:156
  90.7 44.4 %collective-permute-start.4 = (bf16[256,2048]{1,0:T(8,128)(2,1)}, bf16[256,2048]{1,0:T(8,128)(2,1)}, u32[]{:S(2)}, u32[]{:S(2)}) collective-permute-start(bf16[256,2048]{1,0:T(8,128)(2,1)} %shard_map.153.refs_2_.refs_0_), channel_id=1, source_target_pairs={{0,2},{1,3},{2,0},{3,1},{4,6},{5,7},{6,4},{7,5},{8,10},{9,11},{10,... | collective-permute-start | bytes 3145736 | tf_op jit(solution)/shard_map/ppermute | solution.py:157
  155.8 36.4 %collective-permute-start.11 = (bf16[256,1024]{1,0:T(8,128)(2,1)S(1)}, bf16[256,1024]{1,0:T(8,128)(2,1)S(1)}, u32[]{:S(2)}, u32[]{:S(2)}) collective-permute-start(bf16[256,1024]{1,0:T(8,128)(2,1)S(1)} %get-tuple-element.121.refs_6_), channel_id=1, source_target_pairs={{0,2},{1,3},{2,0},{3,1},{4,6},{5,7},{6,4},{7,5},{8,10},{9,11},{10,... | collective-permute-start | bytes 1572872 | tf_op jit(solution)/shard_map/ppermute | solution.py:167
  157.1 34.2 %collective-permute-start.10 = (bf16[256,1024]{1,0:T(8,128)(2,1)S(1)}, bf16[256,1024]{1,0:T(8,128)(2,1)S(1)}, u32[]{:S(2)}, u32[]{:S(2)}) collective-permute-start(bf16[256,1024]{1,0:T(8,128)(2,1)S(1)} %get-tuple-element.133), channel_id=1, source_target_pairs={{0,1},{1,0},{2,3},{3,2},{4,5},{5,4},{6,7},{7,6},{8,9},{9,8},{10,11... | collective-permute-start | bytes 1572872 | tf_op jit(solution)/shard_map/ppermute | solution.py:166
  182.1 43.0 %collective-permute-start.17 = (bf16[256,2048]{1,0:T(8,128)(2,1)S(1)}, bf16[256,2048]{1,0:T(8,128)(2,1)S(1)}, u32[]{:S(2)}, u32[]{:S(2)}) collective-permute-start(bf16[256,2048]{1,0:T(8,128)(2,1)S(1)} %get-tuple-element.136.refs_5_.refs_0_), channel_id=1, source_target_pairs={{0,1},{1,0},{2,3},{3,2},{4,5},{5,4},{6,7},{7,6},{8,9},{9,8},{10,11... | collective-permute-start | bytes 3145736 | tf_op jit(solution)/shard_map/ppermute | solution.py:156
  191.3 34.6 %collective-permute-start.16 = (bf16[256,2048]{1,0:T(8,128)(2,1)S(1)}, bf16[256,2048]{1,0:T(8,128)(2,1)S(1)}, u32[]{:S(2)}, u32[]{:S(2)}) collective-permute-start(bf16[256,2048]{1,0:T(8,128)(2,1)S(1)} %get-tuple-element.136.refs_5_.refs_0_), channel_id=1, source_target_pairs={{0,2},{1,3},{2,0},{3,1},{4,6},{5,7},{6,4},{7,5},{8,10},{9,11},{10,... | collective-permute-start | bytes 3145736 | tf_op jit(solution)/shard_map/ppermute | solution.py:157
  203.9 43.7 %collective-permute-start.14 = (bf16[256,2048]{1,0:T(8,128)(2,1)S(1)}, bf16[256,2048]{1,0:T(8,128)(2,1)S(1)}, u32[]{:S(2)}, u32[]{:S(2)}) collective-permute-start(bf16[256,2048]{1,0:T(8,128)(2,1)S(1)} %get-tuple-element.137), channel_id=1, source_target_pairs={{0,1},{1,0},{2,3},{3,2},{4,5},{5,4},{6,7},{7,6},{8,9},{9,8},{10,11... | collective-permute-start | bytes 3145736 | tf_op jit(solution)/shard_map/ppermute | solution.py:212
  205.1 43.3 %collective-permute-start.15 = (bf16[256,2048]{1,0:T(8,128)(2,1)S(1)}, bf16[256,2048]{1,0:T(8,128)(2,1)S(1)}, u32[]{:S(2)}, u32[]{:S(2)}) collective-permute-start(bf16[256,2048]{1,0:T(8,128)(2,1)S(1)} %get-tuple-element.138.refs_2_), channel_id=1, source_target_pairs={{0,2},{1,3},{2,0},{3,1},{4,6},{5,7},{6,4},{7,5},{8,10},{9,11},{10,... | collective-permute-start | bytes 3145736 | tf_op jit(solution)/shard_map/ppermute | solution.py:213
  205.1 64.9 %collective-permute-start.23 = (bf16[256,2048]{1,0:T(8,128)(2,1)S(1)}, bf16[256,2048]{1,0:T(8,128)(2,1)S(1)}, u32[]{:S(2)}, u32[]{:S(2)}) collective-permute-start(bf16[256,2048]{1,0:T(8,128)(2,1)S(1)} %shard_map.154.refs_10_.refs_0_), channel_id=1, source_target_pairs={{0,1},{1,0},{2,3},{3,2},{4,5},{5,4},{6,7},{7,6},{8,9},{9,8},{10,11... | collective-permute-start | bytes 3145736 | tf_op jit(solution)/shard_map/ppermute | solution.py:156
  225.0 45.8 %collective-permute-start.22 = (bf16[256,2048]{1,0:T(8,128)(2,1)S(1)}, bf16[256,2048]{1,0:T(8,128)(2,1)S(1)}, u32[]{:S(2)}, u32[]{:S(2)}) collective-permute-start(bf16[256,2048]{1,0:T(8,128)(2,1)S(1)} %shard_map.154.refs_10_.refs_0_), channel_id=1, source_target_pairs={{0,2},{1,3},{2,0},{3,1},{4,6},{5,7},{6,4},{7,5},{8,10},{9,11},{10,... | collective-permute-start | bytes 3145736 | tf_op jit(solution)/shard_map/ppermute | solution.py:157
  226.1 55.1 %collective-permute-start.20 = (bf16[256,1024]{1,0:T(8,128)(2,1)S(1)}, bf16[256,1024]{1,0:T(8,128)(2,1)S(1)}, u32[]{:S(2)}, u32[]{:S(2)}) collective-permute-start(bf16[256,1024]{1,0:T(8,128)(2,1)S(1)} %get-tuple-element.142), channel_id=1, source_target_pairs={{0,1},{1,0},{2,3},{3,2},{4,5},{5,4},{6,7},{7,6},{8,9},{9,8},{10,11... | collective-permute-start | bytes 1572872 | tf_op jit(solution)/shard_map/ppermute | solution.py:166
  247.5 34.6 %collective-permute-start.21 = (bf16[256,1024]{1,0:T(8,128)(2,1)S(1)}, bf16[256,1024]{1,0:T(8,128)(2,1)S(1)}, u32[]{:S(2)}, u32[]{:S(2)}) collective-permute-start(bf16[256,1024]{1,0:T(8,128)(2,1)S(1)} %get-tuple-element.139.refs_5_), channel_id=1, source_target_pairs={{0,2},{1,3},{2,0},{3,1},{4,6},{5,7},{6,4},{7,5},{8,10},{9,11},{10,... | collective-permute-start | bytes 1572872 | tf_op jit(solution)/shard_map/ppermute | solution.py:167
  250.3 58.9 %collective-permute-start.19 = (bf16[256,2048]{1,0:T(8,128)(2,1)}, bf16[256,2048]{1,0:T(8,128)(2,1)}, u32[]{:S(2)}, u32[]{:S(2)}) collective-permute-start(bf16[256,2048]{1,0:T(8,128)(2,1)} %get-tuple-element.141.refs_2_.refs_0_), channel_id=1, source_target_pairs={{0,2},{1,3},{2,0},{3,1},{4,6},{5,7},{6,4},{7,5},{8,10},{9,11},{10,... | collective-permute-start | bytes 3145736 | tf_op jit(solution)/shard_map/ppermute | solution.py:157
  270.0 39.2 %collective-permute-start.18 = (bf16[256,2048]{1,0:T(8,128)(2,1)}, bf16[256,2048]{1,0:T(8,128)(2,1)}, u32[]{:S(2)}, u32[]{:S(2)}) collective-permute-start(bf16[256,2048]{1,0:T(8,128)(2,1)} %get-tuple-element.141.refs_2_.refs_0_), channel_id=1, source_target_pairs={{0,1},{1,0},{2,3},{3,2},{4,5},{5,4},{6,7},{7,6},{8,9},{9,8},{10,11... | collective-permute-start | bytes 3145736 | tf_op jit(solution)/shard_map/ppermute | solution.py:156
  273.2 41.8 %collective-permute-start.26 = (bf16[256,1024]{1,0:T(8,128)(2,1)}, bf16[256,1024]{1,0:T(8,128)(2,1)}, u32[]{:S(2)}, u32[]{:S(2)}) collective-permute-start(bf16[256,1024]{1,0:T(8,128)(2,1)} %get-tuple-element.147), channel_id=1, source_target_pairs={{0,1},{1,0},{2,3},{3,2},{4,5},{5,4},{6,7},{7,6},{8,9},{9,8},{10,11... | collective-permute-start | bytes 1572872 | tf_op jit(solution)/shard_map/ppermute | solution.py:166
  386.0 301.0 %reduce-scatter.6.cloned.1.call-start = ((), (), s32[]{:S(2)}) async-start(), calls=%async_computation.4 | async-start | bytes 18874368 | tf_op jit(solution)/shard_map/reduce_scatter | solution.py:904
  428.0 46.3 %collective-permute-start.30 = (bf16[256,2048]{1,0:T(8,128)(2,1)S(1)}, bf16[256,2048]{1,0:T(8,128)(2,1)S(1)}, u32[]{:S(2)}, u32[]{:S(2)}) collective-permute-start(bf16[256,2048]{1,0:T(8,128)(2,1)S(1)} %get-tuple-element.162), channel_id=1, source_target_pairs={{0,1},{1,0},{2,3},{3,2},{4,5},{5,4},{6,7},{7,6},{8,9},{9,8},{10,11... | collective-permute-start | bytes 3145736 | tf_op jit(solution)/shard_map/ppermute | solution.py:212
  428.7 45.6 %collective-permute-start.31 = (bf16[256,2048]{1,0:T(8,128)(2,1)S(1)}, bf16[256,2048]{1,0:T(8,128)(2,1)S(1)}, u32[]{:S(2)}, u32[]{:S(2)}) collective-permute-start(bf16[256,2048]{1,0:T(8,128)(2,1)S(1)} %get-tuple-element.163.refs_6_), channel_id=1, source_target_pairs={{0,2},{1,3},{2,0},{3,1},{4,6},{5,7},{6,4},{7,5},{8,10},{9,11},{10,... | collective-permute-start | bytes 3145736 | tf_op jit(solution)/shard_map/ppermute | solution.py:213
  478.9 299.5 %reduce-scatter.8.cloned.1.call-start = ((), (), s32[]{:S(2)}) async-start(), calls=%async_computation.5 | async-start | bytes 9584640 | tf_op jit(solution)/shard_map/reduce_scatter | solution.py:904
  591.8 63.6 %collective-permute-start.40 = (bf16[256,1024]{1,0:T(8,128)(2,1)S(1)}, bf16[256,1024]{1,0:T(8,128)(2,1)S(1)}, u32[]{:S(2)}, u32[]{:S(2)}) collective-permute-start(bf16[256,1024]{1,0:T(8,128)(2,1)S(1)} %get-tuple-element.187.refs_2_), channel_id=1, source_target_pairs={{0,2},{1,3},{2,0},{3,1},{4,6},{5,7},{6,4},{7,5},{8,10},{9,11},{10,... | collective-permute-start | bytes 1572872 | tf_op jit(solution)/shard_map/ppermute | solution.py:204
  593.1 61.0 %collective-permute-start.41 = (bf16[256,1024]{1,0:T(8,128)(2,1)S(1)}, bf16[256,1024]{1,0:T(8,128)(2,1)S(1)}, u32[]{:S(2)}, u32[]{:S(2)}) collective-permute-start(bf16[256,1024]{1,0:T(8,128)(2,1)S(1)} %get-tuple-element.189), channel_id=1, source_target_pairs={{0,1},{1,0},{2,3},{3,2},{4,5},{5,4},{6,7},{7,6},{8,9},{9,8},{10,11... | collective-permute-start | bytes 1572872 | tf_op jit(solution)/shard_map/ppermute | solution.py:203
  594.5 63.2 %collective-permute-start.50 = (bf16[256,2048]{1,0:T(8,128)(2,1)S(1)}, bf16[256,2048]{1,0:T(8,128)(2,1)S(1)}, u32[]{:S(2)}, u32[]{:S(2)}) collective-permute-start(bf16[256,2048]{1,0:T(8,128)(2,1)S(1)} %get-tuple-element.205), channel_id=1, source_target_pairs={{0,1},{1,0},{2,3},{3,2},{4,5},{5,4},{6,7},{7,6},{8,9},{9,8},{10,11... | collective-permute-start | bytes 3145736 | tf_op jit(solution)/shard_map/ppermute | solution.py:212
  604.0 53.7 %collective-permute-start.51 = (bf16[256,2048]{1,0:T(8,128)(2,1)S(1)}, bf16[256,2048]{1,0:T(8,128)(2,1)S(1)}, u32[]{:S(2)}, u32[]{:S(2)}) collective-permute-start(bf16[256,2048]{1,0:T(8,128)(2,1)S(1)} %get-tuple-element.196.refs_6_), channel_id=1, source_target_pairs={{0,2},{1,3},{2,0},{3,1},{4,6},{5,7},{6,4},{7,5},{8,10},{9,11},{10,... | collective-permute-start | bytes 3145736 | tf_op jit(solution)/shard_map/ppermute | solution.py:213
  690.7 36.7 %collective-permute-start.56 = (bf16[256,1024]{1,0:T(8,128)(2,1)}, bf16[256,1024]{1,0:T(8,128)(2,1)S(1)}, u32[]{:S(2)}, u32[]{:S(2)}) collective-permute-start(bf16[256,1024]{1,0:T(8,128)(2,1)} %copy-done.81), channel_id=1, source_target_pairs={{0,2},{1,3},{2,0},{3,1},{4,6},{5,7},{6,4},{7,5},{8,10},{9,11},{10,... | collective-permute-start | bytes 1572872 | tf_op jit(solution)/shard_map/ppermute | solution.py:204
  691.9 35.5 %collective-permute-start.57 = (bf16[256,1024]{1,0:T(8,128)(2,1)}, bf16[256,1024]{1,0:T(8,128)(2,1)S(1)}, u32[]{:S(2)}, u32[]{:S(2)}) collective-permute-start(bf16[256,1024]{1,0:T(8,128)(2,1)} %copy-done.80), channel_id=1, source_target_pairs={{0,1},{1,0},{2,3},{3,2},{4,5},{5,4},{6,7},{7,6},{8,9},{9,8},{10,11... | collective-permute-start | bytes 1572872 | tf_op jit(solution)/shard_map/ppermute | solution.py:203
  692.7 54.0 %collective-permute-start.61 = (bf16[256,2048]{1,0:T(8,128)(2,1)S(1)}, bf16[256,2048]{1,0:T(8,128)(2,1)S(1)}, u32[]{:S(2)}, u32[]{:S(2)}) collective-permute-start(bf16[256,2048]{1,0:T(8,128)(2,1)S(1)} %get-tuple-element.212.refs_2_), channel_id=1, source_target_pairs={{0,2},{1,3},{2,0},{3,1},{4,6},{5,7},{6,4},{7,5},{8,10},{9,11},{10,... | collective-permute-start | bytes 3145736 | tf_op jit(solution)/shard_map/ppermute | solution.py:213
  (123 other events, 1691.2 us)
Sparse Core Ops, SparseCore 0:
  10.8 84.8 all-gather.6
  97.3 149.5 all-gather.8
  248.5 80.2 all-gather.10
  386.1 88.9 reduce-scatter.3
  479.1 167.5 reduce-scatter.5
  688.7 89.7 reduce-scatter.7

commit v7 on v6

--- a/solution.py
+++ b/solution.py
@@ -19,7 +19,7 @@
 VMEM_SLACK = 8 * 1024 * 1024
 VMEM_SMALL = 24 * 1024 * 1024
 VMEM_LARGE = 40 * 1024 * 1024
-PIN_BYTES = 3 * 1024 * 1024
+PIN_BYTES = 2 * 1024 * 1024
 PIN_BYTES_LARGE = 1024 * 1024
 SMALL = 3
 
@@ -989,7 +989,6 @@
     attention_back(0)
     residual_back(1)
     input_back(0)
-    project_out(1)
     gm_all[1].second()
     out_sum[0].second()
     attention_back_start(1)
@@ -999,7 +998,7 @@
     gains = tensor_sum(jnp.concatenate([(sum1[0] + sum1[1]) / g1, sum2[0] + sum2[1]]), nt)
     gains = jnp.swapaxes(gains.reshape(2, nd, ds), 0, 1).astype(BF)
     gains = jnp.pad(gains, ((0, 0), (0, 14), (0, qkv_w.shape[2] - ds)))
-    out_sum[1].second()
+    project_out(1)
     layer_out = layer_out_rows(mid[0], out_sum[0].terms, 0, groups, None)
     grad_qkvo = wgrad_rows(
         [a1, by_group(gmf)],
@@ -1009,6 +1008,7 @@
         gains,
     )
     ga1[1].second()
+    out_sum[1].second()
     grad_qkvo = dp_sum(link(grad_qkvo, grad_gateup))
     layer_out = layer_out_rows(mid[1], out_sum[1].terms, 1, groups, layer_out)
     ga1[0].second()

time: 798 us -> 810 us (1.015)
  waiting for transfers between devices: 215 us -> 233 us
  local copies, waits for them, and re-layouts: 38 us -> 23.7 us
  Pallas kernels: 431 us -> 440 us
    unnamed x179 -> x137, local copies, waits for them, and re-layouts: 34.6 us -> 20.3 us
    ppermute x7, waiting for transfers between devices: 24 us -> 36.8 us  [__init__(): self.from_y = lax.ppermute(block, 'tensor', swap_perm(4, 2))]
    pallas_call x54, Pallas kernels: 431 us -> 440 us  [run(): pl.pallas_call(ordered_body, grid_spec=pltpu.PrefetchScalarGridSpec(num_s...]
  transfers between devices with their start and end apart: 68 -> 68, of which waited for: 29 -> 32; matrix products, arithmetic and copies ran while one was open for 2% -> 2% of each run, Pallas kernels for 49% -> 50%
where the time goes in v7:
time: 810 us; the launch traced here: 805 us
  Pallas kernels  440 us (54%)
  waiting for transfers between devices  233 us (29%)
  starting transfers between devices  63.8 us (8%)
  local copies, waits for them, and re-layouts  23.7 us (3%)
  other arithmetic  16.6 us (2%)
  between operations  15.6 us (2%)
  blocking collectives  12.2 us (2%)
    pallas_call x54, Pallas kernels, run(): pl.pallas_call(ordered_body, grid_spec=pltpu.PrefetchScalarGridSpec(num_s...  440 us
    ppermute x8, waiting for transfers between devices, second(): lax.ppermute(to_x, 'tensor', swap_perm(4, 1))  57.5 us
    ppermute x7, waiting for transfers between devices, __init__(): self.from_x = lax.ppermute(block, 'tensor', swap_perm(4, 1))  38.9 us
    ppermute x7, waiting for transfers between devices, __init__(): self.from_y = lax.ppermute(block, 'tensor', swap_perm(4, 2))  36.8 us
    ppermute x7, waiting for transfers between devices, second(): diag_x = lax.ppermute(left, 'tensor', swap_perm(4, 1))  24.7 us
    reduce_scatter x3, waiting for transfers between devices, dp_sum(): return lax.psum_scatter(grad, 'dp', scatter_dimension=0, tiled=False)  22.5 us
    ppermute x7, waiting for transfers between devices, second(): diag_y = lax.ppermute(right, 'tensor', swap_perm(4, 2))  22.3 us
    unnamed x137, local copies, waits for them, and re-layouts  20.3 us
  transfers between devices with their start and end apart: 68, of which 32 were waited for; matrix products, arithmetic and copies ran while one was open for 2% of the time, Pallas kernels for 50%

profile of v7, /device:TPU:0, one launch (start us, length us, event | category | flops | bytes accessed | tf_op | source)
XLA Modules:
  0.0 804.5 jit_solution(18233755439081979269)
XLA Ops:
  18.5 12.2 %all_gather.21 = bf16[2,2048]{1,0:T(2,128)(2,1)S(1)} all-gather(bf16[2,256]{1,0:T(2,128)(2,1)S(1)} %pad_maximum_fusion.4), channel_id=1, replica_groups=mesh['dp'=8,'tensor'=4] {'dp'}, dimensions={1}, use_global_device_ids=true | all-gather | bytes 9216 | tf_op jit(solution)/shard_map/all_gather | solution.py:873
  35.4 25.8 %collective-permute-done.1.refs_0_.refs_2_ = bf16[512,2048]{1,0:T(8,128)(2,1)} collective-permute-done((bf16[512,2048]{1,0:T(8,128)(2,1)}, bf16[512,2048]{1,0:T(8,128)(2,1)}, u32[]{:S(2)}, u32[]{:S(2)}) %collective-permute-start.1) | collective-permute-done | bytes 2097184 | tf_op jit(solution)/shard_map/ppermute | solution.py:157
  68.7 20.7 %collective-permute-done.3.refs_1_.refs_4_ = bf16[512,1024]{1,0:T(8,128)(2,1)S(1)} collective-permute-done((bf16[512,1024]{1,0:T(8,128)(2,1)S(1)}, bf16[512,1024]{1,0:T(8,128)(2,1)S(1)}, u32[]{:S(2)}, u32[]{:S(2)}) %collective-permute-start.3) | collective-permute-done | bytes 1048608 | tf_op jit(solution)/shard_map/ppermute | solution.py:167
  100.6 12.3 %shard_map.156.refs_1_.refs_2_.refs_3_ = bf16[3,4,256,512]{3,2,1,0:T(8,128)(2,1)} custom-call(bf16[4,256,2048]{2,1,0:T(8,128)(2,1)} %shard_map.155.refs_0_.refs_6_, bf16[8,4,256,512]{3,2,1,0:T(8,128)(2,1)} %bitcast.52, f32[4,256,128]{2,1,0:T(8,128)S(1)} %copy-done.20, f32[4,256,128]{2,1,0:T(8,128)S(1)} %copy-done.17), custom_call_target="tpu_custom_call" | custom-call | flops 2147483648 | bytes 4543829 | tf_op jit(solution)/shard_map/pallas_call | solution.py:84
  112.9 15.4 %shard_map.157 = (bf16[4,256,512]{2,1,0:T(8,128)(2,1)S(1)}, f32[1,4,8,256]{3,2,1,0:T(8,128)S(1)}) custom-call(s32[4]{0:T(128)S(1)} %iota_xor_fusion.refs_0_, bf16[3,4,256,512]{3,2,1,0:T(8,128)(2,1)} %shard_map.156.refs_1_.refs_2_.refs_3_, bf16[3,4,256,512]{3,2,1,0:T(8,128)(2,1)} %shard_map.156.refs_1_.refs_2_.refs_3_, ...), custom_call_target="tpu_custom_call" | custom-call | flops 1431655808 | bytes 1398101 | tf_op jit(solution)/shard_map/pallas_call | solution.py:84
  142.2 12.0 %shard_map.161.refs_4_.refs_1_.refs_2_.refs_3_ = bf16[3,4,256,512]{3,2,1,0:T(8,128)(2,1)} custom-call(bf16[4,256,2048]{2,1,0:T(8,128)(2,1)} %shard_map.160.refs_0_.refs_6_.refs_1_, bf16[8,4,256,512]{3,2,1,0:T(8,128)(2,1)} %bitcast.54, f32[4,256,128]{2,1,0:T(8,128)S(1)} %copy-done.14, f32[4,256,128]{2,1,0:T(8,128)S(1)} %copy-done.11), custom_call_target="tpu_custom_call" | custom-call | flops 2147483648 | bytes 4543829 | tf_op jit(solution)/shard_map/pallas_call | solution.py:84
  160.6 15.4 %shard_map.163 = (bf16[4,256,512]{2,1,0:T(8,128)(2,1)S(1)}, f32[1,4,8,256]{3,2,1,0:T(8,128)S(1)}) custom-call(s32[4]{0:T(128)S(1)} %iota_xor_fusion.refs_0_, bf16[3,4,256,512]{3,2,1,0:T(8,128)(2,1)} %shard_map.161.refs_4_.refs_1_.refs_2_.refs_3_, bf16[3,4,256,512]{3,2,1,0:T(8,128)(2,1)} %shard_map.161.refs_4_.refs_1_.refs_2_.refs_3_, ...), custom_call_target="tpu_custom_call" | custom-call | flops 1431655808 | bytes 1398101 | tf_op jit(solution)/shard_map/pallas_call | solution.py:84
  184.8 7.3 collective-permute-done.10.refs_3_
  207.3 18.5 %collective-permute-done.17.refs_1_ = bf16[256,2048]{1,0:T(8,128)(2,1)S(1)} collective-permute-done((bf16[256,2048]{1,0:T(8,128)(2,1)S(1)}, bf16[256,2048]{1,0:T(8,128)(2,1)S(1)}, u32[]{:S(2)}, u32[]{:S(2)}) %collective-permute-start.17) | collective-permute-done | bytes 1048608 | tf_op jit(solution)/shard_map/ppermute | solution.py:156
  228.1 20.2 %collective-permute-done.14.refs_3_ = bf16[256,2048]{1,0:T(8,128)(2,1)S(1)} collective-permute-done((bf16[256,2048]{1,0:T(8,128)(2,1)S(1)}, bf16[256,2048]{1,0:T(8,128)(2,1)S(1)}, u32[]{:S(2)}, u32[]{:S(2)}) %collective-permute-start.14) | collective-permute-done | bytes 1048608 | tf_op jit(solution)/shard_map/ppermute | solution.py:212
  252.4 18.3 %collective-permute-done.23.refs_1_ = bf16[256,2048]{1,0:T(8,128)(2,1)S(1)} collective-permute-done((bf16[256,2048]{1,0:T(8,128)(2,1)S(1)}, bf16[256,2048]{1,0:T(8,128)(2,1)S(1)}, u32[]{:S(2)}, u32[]{:S(2)}) %collective-permute-start.23) | collective-permute-done | bytes 1048608 | tf_op jit(solution)/shard_map/ppermute | solution.py:156
  273.9 8.1 %collective-permute-done.20.refs_3_ = bf16[256,1024]{1,0:T(8,128)(2,1)S(1)} collective-permute-done((bf16[256,1024]{1,0:T(8,128)(2,1)S(1)}, bf16[256,1024]{1,0:T(8,128)(2,1)S(1)}, u32[]{:S(2)}, u32[]{:S(2)}) %collective-permute-start.20) | collective-permute-done | bytes 524320 | tf_op jit(solution)/shard_map/ppermute | solution.py:166
  285.7 24.0 %shard_map.171 = (bf16[4,256,2048]{2,1,0:T(8,128)(2,1)}, bf16[4,256,2048]{2,1,0:T(8,128)(2,1)}, bf16[4,256,2048]{2,1,0:T(8,128)(2,1)}, bf16[4,256,2048]{2,1,0:T(8,128)(2,1)}) custom-call(bf16[256,2048]{1,0:T(8,128)(2,1)} %copy-done.40, bf16[256,2048]{1,0:T(8,128)(2,1)} %copy-done.41, bf16[256,2048]{1,0:T(8,128)(2,1)} %copy-done.42, ...), custom_call_target="tpu_custom_call" | custom-call | flops 5726623232 | bytes 12582912 | tf_op jit(solution)/shard_map/pallas_call | solution.py:84
  322.8 23.9 %shard_map.174 = (bf16[4,256,2048]{2,1,0:T(8,128)(2,1)}, bf16[4,256,2048]{2,1,0:T(8,128)(2,1)}, bf16[4,256,2048]{2,1,0:T(8,128)(2,1)}, bf16[4,256,2048]{2,1,0:T(8,128)(2,1)}) custom-call(bf16[256,2048]{1,0:T(8,128)(2,1)} %get-tuple-element.141.refs_2_.refs_0_, bf16[256,2048]{1,0:T(8,128)(2,1)} %collective-permute-done.18.refs_1_, ...), custom_call_target="tpu_custom_call" | custom-call | flops 5726623232 | bytes 12582912 | tf_op jit(solution)/shard_map/pallas_call | solution.py:84
  346.7 15.4 %shard_map.175 = (bf16[4,256,2048]{2,1,0:T(8,128)(2,1)}, bf16[4,256,2048]{2,1,0:T(8,128)(2,1)}) custom-call(bf16[4,256,2048]{2,1,0:T(8,128)(2,1)} %shard_map.166.refs_4_.refs_0_.refs_2_, bf16[8,2048,256]{2,1,0:T(8,128)(2,1)} %bitcast.70, bf16[4,256,2048]{2,1,0:T(8,128)(2,1)} %get-tuple-element.151.refs_2_, bf16[4,256,2048]{2,1,0:T(8,128)(2,1)} %get-tuple-element.152.refs_3_, ...), custom_call_target="tpu_custom_call" | custom-call | flops 2863311616 | bytes 9786709 | tf_op jit(solution)/shard_map/pallas_call | solution.py:84
  362.1 23.9 %shard_map.176.refs_4_ = bf16[8,2048,256]{2,1,0:T(8,128)(2,1)} custom-call(bf16[4,256,2048]{2,1,0:T(8,128)(2,1)} %get-tuple-element.144.refs_2_.refs_0_, bf16[4,256,2048]{2,1,0:T(8,128)(2,1)} %get-tuple-element.148.refs_4_.refs_1_.refs_0_, bf16[4,256,2048]{2,1,0:T(8,128)(2,1)} %shard_map.166.refs_4_.refs_0_.refs_2_, ...), custom_call_target="tpu_custom_call" | custom-call | flops 5726623232 | bytes 8388608 | tf_op jit(solution)/shard_map/pallas_call | solution.py:84
  386.1 23.8 %shard_map.177 = (bf16[256,2048]{1,0:T(8,128)(2,1)S(1)}, bf16[256,2048]{1,0:T(8,128)(2,1)S(1)}, bf16[256,2048]{1,0:T(8,128)(2,1)S(1)}, bf16[256,1024]{1,0:T(8,128)(2,1)S(1)}, bf16[256,1024]{1,0:T(8,128)(2,1)S(1)}) custom-call(bf16[4,256,2048]{2,1,0:T(8,128)(2,1)} %get-tuple-element.153.refs_0_.refs_2_, ...), custom_call_target="tpu_custom_call" | custom-call | flops 5726623232 | bytes 9786709 | tf_op jit(solution)/shard_map/pallas_call | solution.py:84
  411.9 15.6 %shard_map.178 = (bf16[4,256,2048]{2,1,0:T(8,128)(2,1)}, bf16[4,256,2048]{2,1,0:T(8,128)(2,1)}) custom-call(bf16[4,256,2048]{2,1,0:T(8,128)(2,1)} %shard_map.173.refs_6_.refs_3_.refs_0_, bf16[8,2048,256]{2,1,0:T(8,128)(2,1)} %bitcast.71, bf16[4,256,2048]{2,1,0:T(8,128)(2,1)} %get-tuple-element.149.refs_2_, bf16[4,256,2048]{2,1,0:T(8,128)(2,1)} %get-tuple-element.150.refs_3_, ...), custom_call_target="tpu_custom_call" | custom-call | flops 2863311616 | bytes 9786709 | tf_op jit(solution)/shard_map/pallas_call | solution.py:84
  430.0 44.1 %shard_map.180.refs_6_.refs_0_ = bf16[8,512,2048]{2,1,0:T(8,128)(2,1)} custom-call(bf16[4,256,2048]{2,1,0:T(8,128)(2,1)} %get-tuple-element.158.refs_0_, bf16[4,256,2048]{2,1,0:T(8,128)(2,1)} %get-tuple-element.159.refs_1_, bf16[4,256,2048]{2,1,0:T(8,128)(2,1)} %get-tuple-element.153.refs_0_.refs_2_, ...), custom_call_target="tpu_custom_call" | custom-call | flops 11453246464 | bytes 13981013 | tf_op jit(solution)/shard_map/pallas_call | solution.py:84
  481.7 24.3 %shard_map.183 = (bf16[256,2048]{1,0:T(8,128)(2,1)S(1)}, bf16[256,2048]{1,0:T(8,128)(2,1)S(1)}, bf16[256,2048]{1,0:T(8,128)(2,1)S(1)}, bf16[256,1024]{1,0:T(8,128)(2,1)S(1)}, bf16[256,1024]{1,0:T(8,128)(2,1)S(1)}) custom-call(bf16[4,256,2048]{2,1,0:T(8,128)(2,1)} %get-tuple-element.156.refs_3_.refs_0_, ...), custom_call_target="tpu_custom_call" | custom-call | flops 5726623232 | bytes 9786709 | tf_op jit(solution)/shard_map/pallas_call | solution.py:84
  510.3 12.7 %shard_map.185 = (bf16[256,2048]{1,0:T(8,128)(2,1)S(1)}, bf16[256,2048]{1,0:T(8,128)(2,1)S(1)}, bf16[256,2048]{1,0:T(8,128)(2,1)S(1)}, bf16[256,1024]{1,0:T(8,128)(2,1)S(1)}, bf16[256,1024]{1,0:T(8,128)(2,1)S(1)}) custom-call(bf16[4,256,2048]{2,1,0:T(8,128)(2,1)} %get-tuple-element.144.refs_2_.refs_0_, bf16[8,2048,256]{2,1,0:T(8,128)(2,1)} %bitcast.72, ...), custom_call_target="tpu_custom_call" | custom-call | flops 2863311616 | bytes 5592405 | tf_op jit(solution)/shard_map/pallas_call | solution.py:84
  530.9 22.6 %shard_map.188 = (bf16[4,256,512]{2,1,0:T(8,128)(2,1)S(1)}, bf16[4,256,512]{2,1,0:T(8,128)(2,1)S(1)}, bf16[4,256,512]{2,1,0:T(8,128)(2,1)S(1)}) custom-call(s32[4]{0:T(128)S(1)} %iota_xor_fusion.refs_0_, bf16[3,4,256,512]{3,2,1,0:T(8,128)(2,1)} %shard_map.156.refs_1_.refs_2_.refs_3_, bf16[3,4,256,512]{3,2,1,0:T(8,128)(2,1)} %shard_map.156.refs_1_.refs_2_.refs_3_, ...), custom_call_target="tpu_custom_call" | custom-call | flops 3579139328 | bytes 2446677 | tf_op jit(solution)/shard_map/pallas_call | solution.py:84
  563.3 11.0 %shard_map.190 = (bf16[256,2048]{1,0:T(8,128)(2,1)S(1)}, bf16[256,2048]{1,0:T(8,128)(2,1)S(1)}, bf16[256,2048]{1,0:T(8,128)(2,1)S(1)}, bf16[256,1024]{1,0:T(8,12...) custom-call(bf16[4,256,512]{2,1,0:T(8,128)(2,1)} %copy-done.28, bf16[4,256,512]{2,1,0:T(8,128)(2,1)} %copy-done.30, ...), custom_call_target="tpu_custom_call" | custom-call | flops 2147483648 | bytes 4543829 | tf_op jit(solution)/shard_map/pallas_call | solution.py:84
  575.0 10.3 %collective-permute-done.41.refs_0_.refs_2_ = bf16[256,2048]{1,0:T(8,128)(2,1)S(1)} collective-permute-done((bf16[256,2048]{1,0:T(8,128)(2,1)S(1)}, bf16[256,2048]{1,0:T(8,128)(2,1)S(1)}, u32[]{:S(2)}, u32[]{:S(2)}) %collective-permute-start.41) | collective-permute-done | bytes 1048608 | tf_op jit(solution)/shard_map/ppermute | solution.py:157
  606.5 22.7 %shard_map.194 = (bf16[4,256,512]{2,1,0:T(8,128)(2,1)S(1)}, bf16[4,256,512]{2,1,0:T(8,128)(2,1)S(1)}, bf16[4,256,512]{2,1,0:T(8,128)(2,1)S(1)}) custom-call(s32[4]{0:T(128)S(1)} %iota_xor_fusion.refs_0_, bf16[3,4,256,512]{3,2,1,0:T(8,128)(2,1)} %shard_map.161.refs_4_.refs_1_.refs_2_.refs_3_, ...), custom_call_target="tpu_custom_call" | custom-call | flops 3579139328 | bytes 2446677 | tf_op jit(solution)/shard_map/pallas_call | solution.py:84
  632.1 10.8 %shard_map.195 = (bf16[256,2048]{1,0:T(8,128)(2,1)S(1)}, bf16[256,2048]{1,0:T(8,128)(2,1)S(1)}, bf16[256,2048]{1,0:T(8,128)(2,1)S(1)}, bf16[256,1024]{1,0:T(8,12...) custom-call(bf16[4,256,512]{2,1,0:T(8,128)(2,1)} %copy-done.32, bf16[4,256,512]{2,1,0:T(8,128)(2,1)} %copy-done.34, ...), custom_call_target="tpu_custom_call" | custom-call | flops 2147483648 | bytes 4543829 | tf_op jit(solution)/shard_map/pallas_call | solution.py:84
  648.8 12.8 %shard_map.196 = (bf16[256,2048]{1,0:T(8,128)(2,1)S(1)}, bf16[256,2048]{1,0:T(8,128)(2,1)S(1)}, bf16[256,2048]{1,0:T(8,128)(2,1)S(1)}, bf16[256,1024]{1,0:T(8,128)(2,1)S(1)}, bf16[256,1024]{1,0:T(8,128)(2,1)S(1)}) custom-call(bf16[4,256,2048]{2,1,0:T(8,128)(2,1)} %get-tuple-element.148.refs_4_.refs_1_.refs_0_, bf16[8,2048,256]{2,1,0:T(8,128)(2,1)} %bitcast.73, ...), custom_call_target="tpu_custom_call" | custom-call | flops 2863311616 | bytes 5592405 | tf_op jit(solution)/shard_map/pallas_call | solution.py:84
  674.1 21.9 %shard_map.198.refs_4_.refs_0_ = bf16[8,1040,512]{2,1,0:T(8,128)(2,1)} custom-call(bf16[4,256,2048]{2,1,0:T(8,128)(2,1)} %shard_map.155.refs_0_.refs_6_, bf16[4,256,2048]{2,1,0:T(8,128)(2,1)} %shard_map.160.refs_0_.refs_6_.refs_1_, bf16[4,256,2048]{2,1,0:T(8,128)(2,1)} %get-tuple-element.206.refs_2_, bf16[4,256,2048]{2,1,0:T(8,128)(2,1)} %get-tuple-element.207.refs_3_, ...), custom_call_target="tpu_custom_call" | custom-call | flops 5726623232 | bytes 8388608 | tf_op jit(solution)/shard_map/pallas_call | solution.py:84
  704.1 21.2 %collective-permute-done.54.refs_2_ = bf16[256,2048]{1,0:T(8,128)(2,1)S(1)} collective-permute-done((bf16[256,2048]{1,0:T(8,128)(2,1)}, bf16[256,2048]{1,0:T(8,128)(2,1)S(1)}, u32[]{:S(2)}, u32[]{:S(2)}) %collective-permute-start.54) | collective-permute-done | bytes 1048608 | tf_op jit(solution)/shard_map/ppermute | solution.py:212
  730.0 7.1 collective-permute-done.56.refs_1_
  743.9 9.3 %collective-permute-done.60.refs_4_ = bf16[256,2048]{1,0:T(8,128)(2,1)S(1)} collective-permute-done((bf16[256,2048]{1,0:T(8,128)(2,1)}, bf16[256,2048]{1,0:T(8,128)(2,1)S(1)}, u32[]{:S(2)}, u32[]{:S(2)}) %collective-permute-start.60) | collective-permute-done | bytes 1048608 | tf_op jit(solution)/shard_map/ppermute | solution.py:212
  768.8 22.5 %reduce-scatter.8.cloned.1.call-done = bf16[1,1040,512]{2,1,0:T(8,128)(2,1)} async-done(((bf16[8,1040,512]{2,1,0:T(8,128)(2,1)}), bf16[1,1040,512]{2,1,0:T(8,128)(2,1)}) %reduce-scatter.8.cloned.1.call-update) | async-done | bytes 1064976 | tf_op jit(solution)/shard_map/reduce_scatter | solution.py:904
  (345 shorter events, 223.1 us)
Async XLA Ops:
  7.2 91.3 %all-gather.7.cloned.1.call-start = ((), (), s32[]{:S(2)}) async-start(), calls=%async_computation.6 | async-start | bytes 9437184 | tf_op jit(solution)/shard_map/all_gather | solution.py:876
  10.7 272.9 %all-gather.9.cloned.1.call-start = ((), (), s32[]{:S(2)}) async-start(), calls=%async_computation.7 | async-start | bytes 18874368 | tf_op jit(solution)/shard_map/all_gather | solution.py:877
  11.5 335.2 %all-gather.11.cloned.1.call-start = ((), (), s32[]{:S(2)}) async-start(), calls=%async_computation.8 | async-start | bytes 9437184 | tf_op jit(solution)/shard_map/all_gather | solution.py:878
  12.2 465.9 %reduce-scatter.4.cloned.1.call-start = ((), (), s32[]{:S(2)}) async-start(), calls=%async_computation.3 | async-start | bytes 9437184 | tf_op jit(solution)/shard_map/reduce_scatter | solution.py:904
  12.2 49.0 %collective-permute-start.1 = (bf16[512,2048]{1,0:T(8,128)(2,1)}, bf16[512,2048]{1,0:T(8,128)(2,1)}, u32[]{:S(2)}, u32[]{:S(2)}) collective-permute-start(bf16[512,2048]{1,0:T(8,128)(2,1)} %bitcast.1.refs_0_), channel_id=1, source_target_pairs={{0,2},{1,3},{2,0},{3,1},{4,6},{5,7},{6,4},{7,5},{8,10},{9,11},{10,... | collective-permute-start | bytes 6291464 | tf_op jit(solution)/shard_map/ppermute | solution.py:157
  15.3 47.4 %collective-permute-start = (bf16[512,2048]{1,0:T(8,128)(2,1)}, bf16[512,2048]{1,0:T(8,128)(2,1)}, u32[]{:S(2)}, u32[]{:S(2)}) collective-permute-start(bf16[512,2048]{1,0:T(8,128)(2,1)} %bitcast.1.refs_0_), channel_id=1, source_target_pairs={{0,1},{1,0},{2,3},{3,2},{4,5},{5,4},{6,7},{7,6},{8,9},{9,8},{10,11... | collective-permute-start | bytes 6291464 | tf_op jit(solution)/shard_map/ppermute | solution.py:156
  89.4 46.2 %collective-permute-start.5 = (bf16[256,2048]{1,0:T(8,128)(2,1)S(1)}, bf16[256,2048]{1,0:T(8,128)(2,1)}, u32[]{:S(2)}, u32[]{:S(2)}) collective-permute-start(bf16[256,2048]{1,0:T(8,128)(2,1)S(1)} %shard_map.153.refs_2_.refs_0_), channel_id=1, source_target_pairs={{0,1},{1,0},{2,3},{3,2},{4,5},{5,4},{6,7},{7,6},{8,9},{9,8},{10,11... | collective-permute-start | bytes 3145736 | tf_op jit(solution)/shard_map/ppermute | solution.py:156
  90.8 44.8 %collective-permute-start.4 = (bf16[256,2048]{1,0:T(8,128)(2,1)S(1)}, bf16[256,2048]{1,0:T(8,128)(2,1)}, u32[]{:S(2)}, u32[]{:S(2)}) collective-permute-start(bf16[256,2048]{1,0:T(8,128)(2,1)S(1)} %shard_map.153.refs_2_.refs_0_), channel_id=1, source_target_pairs={{0,2},{1,3},{2,0},{3,1},{4,6},{5,7},{6,4},{7,5},{8,10},{9,11},{10,... | collective-permute-start | bytes 3145736 | tf_op jit(solution)/shard_map/ppermute | solution.py:157
  157.9 34.8 %collective-permute-start.11 = (bf16[256,1024]{1,0:T(8,128)(2,1)S(1)}, bf16[256,1024]{1,0:T(8,128)(2,1)S(1)}, u32[]{:S(2)}, u32[]{:S(2)}) collective-permute-start(bf16[256,1024]{1,0:T(8,128)(2,1)S(1)} %get-tuple-element.121.refs_6_), channel_id=1, source_target_pairs={{0,2},{1,3},{2,0},{3,1},{4,6},{5,7},{6,4},{7,5},{8,10},{9,11},{10,... | collective-permute-start | bytes 1572872 | tf_op jit(solution)/shard_map/ppermute | solution.py:167
  159.2 32.8 %collective-permute-start.10 = (bf16[256,1024]{1,0:T(8,128)(2,1)S(1)}, bf16[256,1024]{1,0:T(8,128)(2,1)S(1)}, u32[]{:S(2)}, u32[]{:S(2)}) collective-permute-start(bf16[256,1024]{1,0:T(8,128)(2,1)S(1)} %get-tuple-element.133), channel_id=1, source_target_pairs={{0,1},{1,0},{2,3},{3,2},{4,5},{5,4},{6,7},{7,6},{8,9},{9,8},{10,11... | collective-permute-start | bytes 1572872 | tf_op jit(solution)/shard_map/ppermute | solution.py:166
  183.4 42.3 %collective-permute-start.17 = (bf16[256,2048]{1,0:T(8,128)(2,1)S(1)}, bf16[256,2048]{1,0:T(8,128)(2,1)S(1)}, u32[]{:S(2)}, u32[]{:S(2)}) collective-permute-start(bf16[256,2048]{1,0:T(8,128)(2,1)S(1)} %get-tuple-element.136.refs_5_.refs_0_), channel_id=1, source_target_pairs={{0,1},{1,0},{2,3},{3,2},{4,5},{5,4},{6,7},{7,6},{8,9},{9,8},{10,11... | collective-permute-start | bytes 3145736 | tf_op jit(solution)/shard_map/ppermute | solution.py:156
  192.1 34.4 %collective-permute-start.16 = (bf16[256,2048]{1,0:T(8,128)(2,1)S(1)}, bf16[256,2048]{1,0:T(8,128)(2,1)S(1)}, u32[]{:S(2)}, u32[]{:S(2)}) collective-permute-start(bf16[256,2048]{1,0:T(8,128)(2,1)S(1)} %get-tuple-element.136.refs_5_.refs_0_), channel_id=1, source_target_pairs={{0,2},{1,3},{2,0},{3,1},{4,6},{5,7},{6,4},{7,5},{8,10},{9,11},{10,... | collective-permute-start | bytes 3145736 | tf_op jit(solution)/shard_map/ppermute | solution.py:157
  204.4 43.8 %collective-permute-start.14 = (bf16[256,2048]{1,0:T(8,128)(2,1)S(1)}, bf16[256,2048]{1,0:T(8,128)(2,1)S(1)}, u32[]{:S(2)}, u32[]{:S(2)}) collective-permute-start(bf16[256,2048]{1,0:T(8,128)(2,1)S(1)} %get-tuple-element.137), channel_id=1, source_target_pairs={{0,1},{1,0},{2,3},{3,2},{4,5},{5,4},{6,7},{7,6},{8,9},{9,8},{10,11... | collective-permute-start | bytes 3145736 | tf_op jit(solution)/shard_map/ppermute | solution.py:212
  205.8 43.1 %collective-permute-start.15 = (bf16[256,2048]{1,0:T(8,128)(2,1)S(1)}, bf16[256,2048]{1,0:T(8,128)(2,1)S(1)}, u32[]{:S(2)}, u32[]{:S(2)}) collective-permute-start(bf16[256,2048]{1,0:T(8,128)(2,1)S(1)} %get-tuple-element.138.refs_2_), channel_id=1, source_target_pairs={{0,2},{1,3},{2,0},{3,1},{4,6},{5,7},{6,4},{7,5},{8,10},{9,11},{10,... | collective-permute-start | bytes 3145736 | tf_op jit(solution)/shard_map/ppermute | solution.py:213
  205.8 64.9 %collective-permute-start.23 = (bf16[256,2048]{1,0:T(8,128)(2,1)S(1)}, bf16[256,2048]{1,0:T(8,128)(2,1)S(1)}, u32[]{:S(2)}, u32[]{:S(2)}) collective-permute-start(bf16[256,2048]{1,0:T(8,128)(2,1)S(1)} %shard_map.154.refs_10_.refs_0_), channel_id=1, source_target_pairs={{0,1},{1,0},{2,3},{3,2},{4,5},{5,4},{6,7},{7,6},{8,9},{9,8},{10,11... | collective-permute-start | bytes 3145736 | tf_op jit(solution)/shard_map/ppermute | solution.py:156
  225.8 45.6 %collective-permute-start.22 = (bf16[256,2048]{1,0:T(8,128)(2,1)S(1)}, bf16[256,2048]{1,0:T(8,128)(2,1)S(1)}, u32[]{:S(2)}, u32[]{:S(2)}) collective-permute-start(bf16[256,2048]{1,0:T(8,128)(2,1)S(1)} %shard_map.154.refs_10_.refs_0_), channel_id=1, source_target_pairs={{0,2},{1,3},{2,0},{3,1},{4,6},{5,7},{6,4},{7,5},{8,10},{9,11},{10,... | collective-permute-start | bytes 3145736 | tf_op jit(solution)/shard_map/ppermute | solution.py:157
  226.7 55.3 %collective-permute-start.20 = (bf16[256,1024]{1,0:T(8,128)(2,1)S(1)}, bf16[256,1024]{1,0:T(8,128)(2,1)S(1)}, u32[]{:S(2)}, u32[]{:S(2)}) collective-permute-start(bf16[256,1024]{1,0:T(8,128)(2,1)S(1)} %get-tuple-element.142), channel_id=1, source_target_pairs={{0,1},{1,0},{2,3},{3,2},{4,5},{5,4},{6,7},{7,6},{8,9},{9,8},{10,11... | collective-permute-start | bytes 1572872 | tf_op jit(solution)/shard_map/ppermute | solution.py:166
  248.3 34.5 %collective-permute-start.21 = (bf16[256,1024]{1,0:T(8,128)(2,1)S(1)}, bf16[256,1024]{1,0:T(8,128)(2,1)S(1)}, u32[]{:S(2)}, u32[]{:S(2)}) collective-permute-start(bf16[256,1024]{1,0:T(8,128)(2,1)S(1)} %get-tuple-element.139.refs_5_), channel_id=1, source_target_pairs={{0,2},{1,3},{2,0},{3,1},{4,6},{5,7},{6,4},{7,5},{8,10},{9,11},{10,... | collective-permute-start | bytes 1572872 | tf_op jit(solution)/shard_map/ppermute | solution.py:167
  251.1 58.6 %collective-permute-start.19 = (bf16[256,2048]{1,0:T(8,128)(2,1)}, bf16[256,2048]{1,0:T(8,128)(2,1)}, u32[]{:S(2)}, u32[]{:S(2)}) collective-permute-start(bf16[256,2048]{1,0:T(8,128)(2,1)} %get-tuple-element.141.refs_2_.refs_0_), channel_id=1, source_target_pairs={{0,2},{1,3},{2,0},{3,1},{4,6},{5,7},{6,4},{7,5},{8,10},{9,11},{10,... | collective-permute-start | bytes 3145736 | tf_op jit(solution)/shard_map/ppermute | solution.py:157
  270.7 39.0 %collective-permute-start.18 = (bf16[256,2048]{1,0:T(8,128)(2,1)}, bf16[256,2048]{1,0:T(8,128)(2,1)}, u32[]{:S(2)}, u32[]{:S(2)}) collective-permute-start(bf16[256,2048]{1,0:T(8,128)(2,1)} %get-tuple-element.141.refs_2_.refs_0_), channel_id=1, source_target_pairs={{0,1},{1,0},{2,3},{3,2},{4,5},{5,4},{6,7},{7,6},{8,9},{9,8},{10,11... | collective-permute-start | bytes 3145736 | tf_op jit(solution)/shard_map/ppermute | solution.py:156
  272.6 43.2 %collective-permute-start.26 = (bf16[256,1024]{1,0:T(8,128)(2,1)}, bf16[256,1024]{1,0:T(8,128)(2,1)}, u32[]{:S(2)}, u32[]{:S(2)}) collective-permute-start(bf16[256,1024]{1,0:T(8,128)(2,1)} %get-tuple-element.147), channel_id=1, source_target_pairs={{0,1},{1,0},{2,3},{3,2},{4,5},{5,4},{6,7},{7,6},{8,9},{9,8},{10,11... | collective-permute-start | bytes 1572872 | tf_op jit(solution)/shard_map/ppermute | solution.py:166
  282.8 33.7 %collective-permute-start.27 = (bf16[256,1024]{1,0:T(8,128)(2,1)}, bf16[256,1024]{1,0:T(8,128)(2,1)}, u32[]{:S(2)}, u32[]{:S(2)}) collective-permute-start(bf16[256,1024]{1,0:T(8,128)(2,1)} %get-tuple-element.143.refs_6_), channel_id=1, source_target_pairs={{0,2},{1,3},{2,0},{3,1},{4,6},{5,7},{6,4},{7,5},{8,10},{9,11},{10,... | collective-permute-start | bytes 1572872 | tf_op jit(solution)/shard_map/ppermute | solution.py:167
  386.0 312.8 %reduce-scatter.6.cloned.1.call-start = ((), (), s32[]{:S(2)}) async-start(), calls=%async_computation.4 | async-start | bytes 18874368 | tf_op jit(solution)/shard_map/reduce_scatter | solution.py:904
  428.0 46.1 %collective-permute-start.30 = (bf16[256,2048]{1,0:T(8,128)(2,1)S(1)}, bf16[256,2048]{1,0:T(8,128)(2,1)S(1)}, u32[]{:S(2)}, u32[]{:S(2)}) collective-permute-start(bf16[256,2048]{1,0:T(8,128)(2,1)S(1)} %get-tuple-element.166), channel_id=1, source_target_pairs={{0,1},{1,0},{2,3},{3,2},{4,5},{5,4},{6,7},{7,6},{8,9},{9,8},{10,11... | collective-permute-start | bytes 3145736 | tf_op jit(solution)/shard_map/ppermute | solution.py:212
  428.6 45.5 %collective-permute-start.31 = (bf16[256,2048]{1,0:T(8,128)(2,1)S(1)}, bf16[256,2048]{1,0:T(8,128)(2,1)S(1)}, u32[]{:S(2)}, u32[]{:S(2)}) collective-permute-start(bf16[256,2048]{1,0:T(8,128)(2,1)S(1)} %get-tuple-element.163.refs_6_), channel_id=1, source_target_pairs={{0,2},{1,3},{2,0},{3,1},{4,6},{5,7},{6,4},{7,5},{8,10},{9,11},{10,... | collective-permute-start | bytes 3145736 | tf_op jit(solution)/shard_map/ppermute | solution.py:213
  479.4 311.9 %reduce-scatter.8.cloned.1.call-start = ((), (), s32[]{:S(2)}) async-start(), calls=%async_computation.5 | async-start | bytes 9584640 | tf_op jit(solution)/shard_map/reduce_scatter | solution.py:904
  561.8 33.1 %collective-permute-start.44 = (bf16[256,1024]{1,0:T(8,128)(2,1)S(1)}, bf16[256,1024]{1,0:T(8,128)(2,1)S(1)}, u32[]{:S(2)}, u32[]{:S(2)}) collective-permute-start(bf16[256,1024]{1,0:T(8,128)(2,1)S(1)} %get-tuple-element.176.refs_6_), channel_id=1, source_target_pairs={{0,2},{1,3},{2,0},{3,1},{4,6},{5,7},{6,4},{7,5},{8,10},{9,11},{10,... | collective-permute-start | bytes 1572872 | tf_op jit(solution)/shard_map/ppermute | solution.py:204
  661.7 34.3 %collective-permute-start.48 = (bf16[256,1024]{1,0:T(8,128)(2,1)S(1)}, bf16[256,1024]{1,0:T(8,128)(2,1)S(1)}, u32[]{:S(2)}, u32[]{:S(2)}) collective-permute-start(bf16[256,1024]{1,0:T(8,128)(2,1)S(1)} %get-tuple-element.203), channel_id=1, source_target_pairs={{0,2},{1,3},{2,0},{3,1},{4,6},{5,7},{6,4},{7,5},{8,10},{9,11},{10,... | collective-permute-start | bytes 1572872 | tf_op jit(solution)/shard_map/ppermute | solution.py:204
  663.0 33.0 %collective-permute-start.49 = (bf16[256,1024]{1,0:T(8,128)(2,1)S(1)}, bf16[256,1024]{1,0:T(8,128)(2,1)S(1)}, u32[]{:S(2)}, u32[]{:S(2)}) collective-permute-start(bf16[256,1024]{1,0:T(8,128)(2,1)S(1)} %get-tuple-element.205), channel_id=1, source_target_pairs={{0,1},{1,0},{2,3},{3,2},{4,5},{5,4},{6,7},{7,6},{8,9},{9,8},{10,11... | collective-permute-start | bytes 1572872 | tf_op jit(solution)/shard_map/ppermute | solution.py:203
  701.7 35.3 %collective-permute-start.56 = (bf16[256,1024]{1,0:T(8,128)(2,1)}, bf16[256,1024]{1,0:T(8,128)(2,1)S(1)}, u32[]{:S(2)}, u32[]{:S(2)}) collective-permute-start(bf16[256,1024]{1,0:T(8,128)(2,1)} %copy-done.58), channel_id=1, source_target_pairs={{0,2},{1,3},{2,0},{3,1},{4,6},{5,7},{6,4},{7,5},{8,10},{9,11},{10,... | collective-permute-start | bytes 1572872 | tf_op jit(solution)/shard_map/ppermute | solution.py:204
  701.8 35.3 %collective-permute-start.57 = (bf16[256,1024]{1,0:T(8,128)(2,1)}, bf16[256,1024]{1,0:T(8,128)(2,1)S(1)}, u32[]{:S(2)}, u32[]{:S(2)}) collective-permute-start(bf16[256,1024]{1,0:T(8,128)(2,1)} %copy-done.57), channel_id=1, source_target_pairs={{0,1},{1,0},{2,3},{3,2},{4,5},{5,4},{6,7},{7,6},{8,9},{9,8},{10,11... | collective-permute-start | bytes 1572872 | tf_op jit(solution)/shard_map/ppermute | solution.py:203
  703.0 51.0 %collective-permute-start.61 = (bf16[256,2048]{1,0:T(8,128)(2,1)S(1)}, bf16[256,2048]{1,0:T(8,128)(2,1)S(1)}, u32[]{:S(2)}, u32[]{:S(2)}) collective-permute-start(bf16[256,2048]{1,0:T(8,128)(2,1)S(1)} %get-tuple-element.210.refs_4_), channel_id=1, source_target_pairs={{0,2},{1,3},{2,0},{3,1},{4,6},{5,7},{6,4},{7,5},{8,10},{9,11},{10,... | collective-permute-start | bytes 3145736 | tf_op jit(solution)/shard_map/ppermute | solution.py:213
  (102 other events, 1595.4 us)
Sparse Core Ops, SparseCore 0:
  10.8 84.7 all-gather.6
  97.2 149.6 all-gather.8
  248.5 80.2 all-gather.10
  386.1 89.4 reduce-scatter.3
  479.5 168.0 reduce-scatter.5
  699.0 92.2 reduce-scatter.7

commit v8 on v6

--- a/solution.py
+++ b/solution.py
@@ -19,7 +19,7 @@
 VMEM_SLACK = 8 * 1024 * 1024
 VMEM_SMALL = 24 * 1024 * 1024
 VMEM_LARGE = 40 * 1024 * 1024
-PIN_BYTES = 3 * 1024 * 1024
+PIN_BYTES = 2 * 1024 * 1024
 PIN_BYTES_LARGE = 1024 * 1024
 SMALL = 3
 

time: 798 us -> 796 us (level)
  local copies, waits for them, and re-layouts: 38 us -> 25.2 us
  Pallas kernels: 431 us -> 441 us
    unnamed x179 -> x137, local copies, waits for them, and re-layouts: 34.6 us -> 21.7 us
    pallas_call x54, Pallas kernels: 431 us -> 441 us  [run(): pl.pallas_call(ordered_body, grid_spec=pltpu.PrefetchScalarGridSpec(num_s...]
  transfers between devices with their start and end apart: 68 -> 68, of which waited for: 29 -> 29; matrix products, arithmetic and copies ran while one was open for 2% -> 2% of each run, Pallas kernels for 49% -> 51%
where the time goes in v8:
time: 796 us; the launch traced here: 791 us
  Pallas kernels  441 us (55%)
  waiting for transfers between devices  214 us (27%)
  starting transfers between devices  66.3 us (8%)
  local copies, waits for them, and re-layouts  25.2 us (3%)
  other arithmetic  16.6 us (2%)
  between operations  15.6 us (2%)
  blocking collectives  12.2 us (2%)
    pallas_call x54, Pallas kernels, run(): pl.pallas_call(ordered_body, grid_spec=pltpu.PrefetchScalarGridSpec(num_s...  441 us
    ppermute x8, waiting for transfers between devices, second(): lax.ppermute(to_x, 'tensor', swap_perm(4, 1))  60 us
    ppermute x7, waiting for transfers between devices, __init__(): self.from_x = lax.ppermute(block, 'tensor', swap_perm(4, 1))  38.2 us
    ppermute x7, waiting for transfers between devices, second(): diag_x = lax.ppermute(left, 'tensor', swap_perm(4, 1))  28.2 us
    ppermute x7, waiting for transfers between devices, __init__(): self.from_y = lax.ppermute(block, 'tensor', swap_perm(4, 2))  26.5 us
    ppermute x7, waiting for transfers between devices, second(): diag_y = lax.ppermute(right, 'tensor', swap_perm(4, 2))  22.3 us
    unnamed x137, local copies, waits for them, and re-layouts  21.7 us
    reduce_scatter x3, waiting for transfers between devices, dp_sum(): return lax.psum_scatter(grad, 'dp', scatter_dimension=0, tiled=False)  17.6 us
  transfers between devices with their start and end apart: 68, of which 29 were waited for; matrix products, arithmetic and copies ran while one was open for 2% of the time, Pallas kernels for 51%

profile of v8, /device:TPU:0, one launch (start us, length us, event | category | flops | bytes accessed | tf_op | source)
XLA Modules:
  0.0 790.6 jit_solution(6474980828010547322)
XLA Ops:
  18.5 12.2 %all_gather.21 = bf16[2,2048]{1,0:T(2,128)(2,1)S(1)} all-gather(bf16[2,256]{1,0:T(2,128)(2,1)S(1)} %pad_maximum_fusion.4), channel_id=1, replica_groups=mesh['dp'=8,'tensor'=4] {'dp'}, dimensions={1}, use_global_device_ids=true | all-gather | bytes 9216 | tf_op jit(solution)/shard_map/all_gather | solution.py:873
  35.4 25.8 %collective-permute-done.1.refs_0_.refs_2_ = bf16[512,2048]{1,0:T(8,128)(2,1)} collective-permute-done((bf16[512,2048]{1,0:T(8,128)(2,1)}, bf16[512,2048]{1,0:T(8,128)(2,1)}, u32[]{:S(2)}, u32[]{:S(2)}) %collective-permute-start.1) | collective-permute-done | bytes 2097184 | tf_op jit(solution)/shard_map/ppermute | solution.py:157
  68.7 20.7 %collective-permute-done.3.refs_1_.refs_4_ = bf16[512,1024]{1,0:T(8,128)(2,1)S(1)} collective-permute-done((bf16[512,1024]{1,0:T(8,128)(2,1)S(1)}, bf16[512,1024]{1,0:T(8,128)(2,1)S(1)}, u32[]{:S(2)}, u32[]{:S(2)}) %collective-permute-start.3) | collective-permute-done | bytes 1048608 | tf_op jit(solution)/shard_map/ppermute | solution.py:167
  100.6 12.3 %shard_map.156.refs_1_.refs_2_.refs_3_ = bf16[3,4,256,512]{3,2,1,0:T(8,128)(2,1)} custom-call(bf16[4,256,2048]{2,1,0:T(8,128)(2,1)} %shard_map.155.refs_0_.refs_6_, bf16[8,4,256,512]{3,2,1,0:T(8,128)(2,1)} %bitcast.52, f32[4,256,128]{2,1,0:T(8,128)S(1)} %copy-done.20, f32[4,256,128]{2,1,0:T(8,128)S(1)} %copy-done.17), custom_call_target="tpu_custom_call" | custom-call | flops 2147483648 | bytes 4543829 | tf_op jit(solution)/shard_map/pallas_call | solution.py:84
  112.9 15.4 %shard_map.157 = (bf16[4,256,512]{2,1,0:T(8,128)(2,1)S(1)}, f32[1,4,8,256]{3,2,1,0:T(8,128)S(1)}) custom-call(s32[4]{0:T(128)S(1)} %iota_xor_fusion.refs_0_, bf16[3,4,256,512]{3,2,1,0:T(8,128)(2,1)} %shard_map.156.refs_1_.refs_2_.refs_3_, bf16[3,4,256,512]{3,2,1,0:T(8,128)(2,1)} %shard_map.156.refs_1_.refs_2_.refs_3_, ...), custom_call_target="tpu_custom_call" | custom-call | flops 1431655808 | bytes 1398101 | tf_op jit(solution)/shard_map/pallas_call | solution.py:84
  142.2 12.0 %shard_map.161.refs_4_.refs_1_.refs_2_.refs_3_ = bf16[3,4,256,512]{3,2,1,0:T(8,128)(2,1)} custom-call(bf16[4,256,2048]{2,1,0:T(8,128)(2,1)} %shard_map.160.refs_0_.refs_6_.refs_1_, bf16[8,4,256,512]{3,2,1,0:T(8,128)(2,1)} %bitcast.54, f32[4,256,128]{2,1,0:T(8,128)S(1)} %copy-done.14, f32[4,256,128]{2,1,0:T(8,128)S(1)} %copy-done.11), custom_call_target="tpu_custom_call" | custom-call | flops 2147483648 | bytes 4543829 | tf_op jit(solution)/shard_map/pallas_call | solution.py:84
  160.6 15.4 %shard_map.163 = (bf16[4,256,512]{2,1,0:T(8,128)(2,1)S(1)}, f32[1,4,8,256]{3,2,1,0:T(8,128)S(1)}) custom-call(s32[4]{0:T(128)S(1)} %iota_xor_fusion.refs_0_, bf16[3,4,256,512]{3,2,1,0:T(8,128)(2,1)} %shard_map.161.refs_4_.refs_1_.refs_2_.refs_3_, bf16[3,4,256,512]{3,2,1,0:T(8,128)(2,1)} %shard_map.161.refs_4_.refs_1_.refs_2_.refs_3_, ...), custom_call_target="tpu_custom_call" | custom-call | flops 1431655808 | bytes 1398101 | tf_op jit(solution)/shard_map/pallas_call | solution.py:84
  184.8 7.3 collective-permute-done.10.refs_3_
  207.3 18.5 %collective-permute-done.17.refs_1_ = bf16[256,2048]{1,0:T(8,128)(2,1)S(1)} collective-permute-done((bf16[256,2048]{1,0:T(8,128)(2,1)S(1)}, bf16[256,2048]{1,0:T(8,128)(2,1)S(1)}, u32[]{:S(2)}, u32[]{:S(2)}) %collective-permute-start.17) | collective-permute-done | bytes 1048608 | tf_op jit(solution)/shard_map/ppermute | solution.py:156
  228.1 20.2 %collective-permute-done.14.refs_3_ = bf16[256,2048]{1,0:T(8,128)(2,1)S(1)} collective-permute-done((bf16[256,2048]{1,0:T(8,128)(2,1)S(1)}, bf16[256,2048]{1,0:T(8,128)(2,1)S(1)}, u32[]{:S(2)}, u32[]{:S(2)}) %collective-permute-start.14) | collective-permute-done | bytes 1048608 | tf_op jit(solution)/shard_map/ppermute | solution.py:212
  252.4 18.3 %collective-permute-done.23.refs_1_ = bf16[256,2048]{1,0:T(8,128)(2,1)S(1)} collective-permute-done((bf16[256,2048]{1,0:T(8,128)(2,1)S(1)}, bf16[256,2048]{1,0:T(8,128)(2,1)S(1)}, u32[]{:S(2)}, u32[]{:S(2)}) %collective-permute-start.23) | collective-permute-done | bytes 1048608 | tf_op jit(solution)/shard_map/ppermute | solution.py:156
  273.9 8.1 %collective-permute-done.20.refs_3_ = bf16[256,1024]{1,0:T(8,128)(2,1)S(1)} collective-permute-done((bf16[256,1024]{1,0:T(8,128)(2,1)S(1)}, bf16[256,1024]{1,0:T(8,128)(2,1)S(1)}, u32[]{:S(2)}, u32[]{:S(2)}) %collective-permute-start.20) | collective-permute-done | bytes 524320 | tf_op jit(solution)/shard_map/ppermute | solution.py:166
  285.7 24.0 %shard_map.171 = (bf16[4,256,2048]{2,1,0:T(8,128)(2,1)}, bf16[4,256,2048]{2,1,0:T(8,128)(2,1)}, bf16[4,256,2048]{2,1,0:T(8,128)(2,1)}, bf16[4,256,2048]{2,1,0:T(8,128)(2,1)}) custom-call(bf16[256,2048]{1,0:T(8,128)(2,1)} %copy-done.40, bf16[256,2048]{1,0:T(8,128)(2,1)} %copy-done.41, bf16[256,2048]{1,0:T(8,128)(2,1)} %copy-done.42, ...), custom_call_target="tpu_custom_call" | custom-call | flops 5726623232 | bytes 12582912 | tf_op jit(solution)/shard_map/pallas_call | solution.py:84
  322.8 23.9 %shard_map.174 = (bf16[4,256,2048]{2,1,0:T(8,128)(2,1)}, bf16[4,256,2048]{2,1,0:T(8,128)(2,1)}, bf16[4,256,2048]{2,1,0:T(8,128)(2,1)}, bf16[4,256,2048]{2,1,0:T(8,128)(2,1)}) custom-call(bf16[256,2048]{1,0:T(8,128)(2,1)} %get-tuple-element.141.refs_2_.refs_0_, bf16[256,2048]{1,0:T(8,128)(2,1)} %collective-permute-done.18.refs_1_, ...), custom_call_target="tpu_custom_call" | custom-call | flops 5726623232 | bytes 12582912 | tf_op jit(solution)/shard_map/pallas_call | solution.py:84
  346.7 15.4 %shard_map.175 = (bf16[4,256,2048]{2,1,0:T(8,128)(2,1)}, bf16[4,256,2048]{2,1,0:T(8,128)(2,1)}) custom-call(bf16[4,256,2048]{2,1,0:T(8,128)(2,1)} %shard_map.166.refs_4_.refs_0_.refs_2_, bf16[8,2048,256]{2,1,0:T(8,128)(2,1)} %bitcast.70, bf16[4,256,2048]{2,1,0:T(8,128)(2,1)} %get-tuple-element.150.refs_2_, bf16[4,256,2048]{2,1,0:T(8,128)(2,1)} %get-tuple-element.151.refs_3_, ...), custom_call_target="tpu_custom_call" | custom-call | flops 2863311616 | bytes 9786709 | tf_op jit(solution)/shard_map/pallas_call | solution.py:84
  362.1 23.9 %shard_map.176.refs_4_ = bf16[8,2048,256]{2,1,0:T(8,128)(2,1)} custom-call(bf16[4,256,2048]{2,1,0:T(8,128)(2,1)} %get-tuple-element.144.refs_2_.refs_0_, bf16[4,256,2048]{2,1,0:T(8,128)(2,1)} %get-tuple-element.148.refs_4_.refs_1_.refs_0_, bf16[4,256,2048]{2,1,0:T(8,128)(2,1)} %shard_map.166.refs_4_.refs_0_.refs_2_, ...), custom_call_target="tpu_custom_call" | custom-call | flops 5726623232 | bytes 8388608 | tf_op jit(solution)/shard_map/pallas_call | solution.py:84
  386.1 23.8 %shard_map.177 = (bf16[256,2048]{1,0:T(8,128)(2,1)S(1)}, bf16[256,2048]{1,0:T(8,128)(2,1)S(1)}, bf16[256,2048]{1,0:T(8,128)(2,1)S(1)}, bf16[256,1024]{1,0:T(8,128)(2,1)S(1)}, bf16[256,1024]{1,0:T(8,128)(2,1)S(1)}) custom-call(bf16[4,256,2048]{2,1,0:T(8,128)(2,1)} %get-tuple-element.152.refs_0_.refs_2_, ...), custom_call_target="tpu_custom_call" | custom-call | flops 5726623232 | bytes 9786709 | tf_op jit(solution)/shard_map/pallas_call | solution.py:84
  411.9 15.6 %shard_map.178 = (bf16[4,256,2048]{2,1,0:T(8,128)(2,1)}, bf16[4,256,2048]{2,1,0:T(8,128)(2,1)}) custom-call(bf16[4,256,2048]{2,1,0:T(8,128)(2,1)} %shard_map.173.refs_6_.refs_3_.refs_0_, bf16[8,2048,256]{2,1,0:T(8,128)(2,1)} %bitcast.71, bf16[4,256,2048]{2,1,0:T(8,128)(2,1)} %get-tuple-element.159.refs_2_, bf16[4,256,2048]{2,1,0:T(8,128)(2,1)} %get-tuple-element.160.refs_3_, ...), custom_call_target="tpu_custom_call" | custom-call | flops 2863311616 | bytes 9786709 | tf_op jit(solution)/shard_map/pallas_call | solution.py:84
  430.0 44.1 %shard_map.180.refs_6_.refs_0_ = bf16[8,512,2048]{2,1,0:T(8,128)(2,1)} custom-call(bf16[4,256,2048]{2,1,0:T(8,128)(2,1)} %get-tuple-element.164.refs_0_, bf16[4,256,2048]{2,1,0:T(8,128)(2,1)} %get-tuple-element.165.refs_1_, bf16[4,256,2048]{2,1,0:T(8,128)(2,1)} %get-tuple-element.152.refs_0_.refs_2_, ...), custom_call_target="tpu_custom_call" | custom-call | flops 11453246464 | bytes 13981013 | tf_op jit(solution)/shard_map/pallas_call | solution.py:84
  481.7 24.3 %shard_map.183 = (bf16[256,2048]{1,0:T(8,128)(2,1)S(1)}, bf16[256,2048]{1,0:T(8,128)(2,1)S(1)}, bf16[256,2048]{1,0:T(8,128)(2,1)S(1)}, bf16[256,1024]{1,0:T(8,128)(2,1)S(1)}, bf16[256,1024]{1,0:T(8,128)(2,1)S(1)}) custom-call(bf16[4,256,2048]{2,1,0:T(8,128)(2,1)} %get-tuple-element.166.refs_3_.refs_0_, ...), custom_call_target="tpu_custom_call" | custom-call | flops 5726623232 | bytes 9786709 | tf_op jit(solution)/shard_map/pallas_call | solution.py:84
  510.3 12.7 %shard_map.185 = (bf16[256,2048]{1,0:T(8,128)(2,1)S(1)}, bf16[256,2048]{1,0:T(8,128)(2,1)S(1)}, bf16[256,2048]{1,0:T(8,128)(2,1)S(1)}, bf16[256,1024]{1,0:T(8,128)(2,1)S(1)}, bf16[256,1024]{1,0:T(8,128)(2,1)S(1)}) custom-call(bf16[4,256,2048]{2,1,0:T(8,128)(2,1)} %get-tuple-element.144.refs_2_.refs_0_, bf16[8,2048,256]{2,1,0:T(8,128)(2,1)} %bitcast.72, ...), custom_call_target="tpu_custom_call" | custom-call | flops 2863311616 | bytes 5592405 | tf_op jit(solution)/shard_map/pallas_call | solution.py:84
  530.9 22.6 %shard_map.188 = (bf16[4,256,512]{2,1,0:T(8,128)(2,1)S(1)}, bf16[4,256,512]{2,1,0:T(8,128)(2,1)S(1)}, bf16[4,256,512]{2,1,0:T(8,128)(2,1)S(1)}) custom-call(s32[4]{0:T(128)S(1)} %iota_xor_fusion.refs_0_, bf16[3,4,256,512]{3,2,1,0:T(8,128)(2,1)} %shard_map.156.refs_1_.refs_2_.refs_3_, bf16[3,4,256,512]{3,2,1,0:T(8,128)(2,1)} %shard_map.156.refs_1_.refs_2_.refs_3_, ...), custom_call_target="tpu_custom_call" | custom-call | flops 3579139328 | bytes 2446677 | tf_op jit(solution)/shard_map/pallas_call | solution.py:84
  563.4 11.0 %shard_map.190 = (bf16[256,2048]{1,0:T(8,128)(2,1)S(1)}, bf16[256,2048]{1,0:T(8,128)(2,1)S(1)}, bf16[256,2048]{1,0:T(8,128)(2,1)S(1)}, bf16[256,1024]{1,0:T(8,12...) custom-call(bf16[4,256,512]{2,1,0:T(8,128)(2,1)} %copy-done.28, bf16[4,256,512]{2,1,0:T(8,128)(2,1)} %copy-done.30, ...), custom_call_target="tpu_custom_call" | custom-call | flops 2147483648 | bytes 4543829 | tf_op jit(solution)/shard_map/pallas_call | solution.py:84
  575.9 13.5 %shard_map.191 = (bf16[256,2048]{1,0:T(8,128)(2,1)S(1)}, bf16[256,2048]{1,0:T(8,128)(2,1)S(1)}, bf16[256,2048]{1,0:T(8,128)(2,1)S(1)}, bf16[256,1024]{1,0:T(8,128)(2,1)S(1)}, bf16[256,1024]{1,0:T(8,128)(2,1)S(1)}) custom-call(bf16[4,256,2048]{2,1,0:T(8,128)(2,1)} %get-tuple-element.148.refs_4_.refs_1_.refs_0_, bf16[8,2048,256]{2,1,0:T(8,128)(2,1)} %bitcast.73, ...), custom_call_target="tpu_custom_call" | custom-call | flops 2863311616 | bytes 5592405 | tf_op jit(solution)/shard_map/pallas_call | solution.py:84
  597.3 8.7 %collective-permute-done.44.refs_3_ = bf16[256,1024]{1,0:T(8,128)(2,1)S(1)} collective-permute-done((bf16[256,1024]{1,0:T(8,128)(2,1)S(1)}, bf16[256,1024]{1,0:T(8,128)(2,1)S(1)}, u32[]{:S(2)}, u32[]{:S(2)}) %collective-permute-start.44) | collective-permute-done | bytes 524320 | tf_op jit(solution)/shard_map/ppermute | solution.py:166
  612.6 22.4 %shard_map.195 = (bf16[4,256,512]{2,1,0:T(8,128)(2,1)S(1)}, bf16[4,256,512]{2,1,0:T(8,128)(2,1)S(1)}, bf16[4,256,512]{2,1,0:T(8,128)(2,1)S(1)}) custom-call(s32[4]{0:T(128)S(1)} %iota_xor_fusion.refs_0_, bf16[3,4,256,512]{3,2,1,0:T(8,128)(2,1)} %shard_map.161.refs_4_.refs_1_.refs_2_.refs_3_, ...), custom_call_target="tpu_custom_call" | custom-call | flops 3579139328 | bytes 2446677 | tf_op jit(solution)/shard_map/pallas_call | solution.py:84
  638.0 10.8 %shard_map.196 = (bf16[256,2048]{1,0:T(8,128)(2,1)S(1)}, bf16[256,2048]{1,0:T(8,128)(2,1)S(1)}, bf16[256,2048]{1,0:T(8,128)(2,1)S(1)}, bf16[256,1024]{1,0:T(8,12...) custom-call(bf16[4,256,512]{2,1,0:T(8,128)(2,1)} %copy-done.32, bf16[4,256,512]{2,1,0:T(8,128)(2,1)} %copy-done.34, ...), custom_call_target="tpu_custom_call" | custom-call | flops 2147483648 | bytes 4543829 | tf_op jit(solution)/shard_map/pallas_call | solution.py:84
  662.7 21.5 %shard_map.199.refs_4_.refs_0_ = bf16[8,1040,512]{2,1,0:T(8,128)(2,1)} custom-call(bf16[4,256,2048]{2,1,0:T(8,128)(2,1)} %shard_map.155.refs_0_.refs_6_, bf16[4,256,2048]{2,1,0:T(8,128)(2,1)} %shard_map.160.refs_0_.refs_6_.refs_1_, bf16[4,256,2048]{2,1,0:T(8,128)(2,1)} %get-tuple-element.206.refs_2_, bf16[4,256,2048]{2,1,0:T(8,128)(2,1)} %get-tuple-element.207.refs_3_, ...), custom_call_target="tpu_custom_call" | custom-call | flops 5726623232 | bytes 8388608 | tf_op jit(solution)/shard_map/pallas_call | solution.py:84
  692.0 20.3 %collective-permute-done.48.refs_2_ = bf16[256,2048]{1,0:T(8,128)(2,1)S(1)} collective-permute-done((bf16[256,2048]{1,0:T(8,128)(2,1)}, bf16[256,2048]{1,0:T(8,128)(2,1)S(1)}, u32[]{:S(2)}, u32[]{:S(2)}) %collective-permute-start.48) | collective-permute-done | bytes 1048608 | tf_op jit(solution)/shard_map/ppermute | solution.py:212
  717.2 7.1 collective-permute-done.56.refs_1_
  731.9 12.6 %collective-permute-done.60.refs_4_ = bf16[256,2048]{1,0:T(8,128)(2,1)S(1)} collective-permute-done((bf16[256,2048]{1,0:T(8,128)(2,1)}, bf16[256,2048]{1,0:T(8,128)(2,1)S(1)}, u32[]{:S(2)}, u32[]{:S(2)}) %collective-permute-start.60) | collective-permute-done | bytes 1048608 | tf_op jit(solution)/shard_map/ppermute | solution.py:212
  759.8 17.6 %reduce-scatter.8.cloned.1.call-done = bf16[1,1040,512]{2,1,0:T(8,128)(2,1)} async-done(((bf16[8,1040,512]{2,1,0:T(8,128)(2,1)}), bf16[1,1040,512]{2,1,0:T(8,128)(2,1)}) %reduce-scatter.8.cloned.1.call-update) | async-done | bytes 1064976 | tf_op jit(solution)/shard_map/reduce_scatter | solution.py:904
  (345 shorter events, 213.0 us)
Async XLA Ops:
  7.2 91.3 %all-gather.7.cloned.1.call-start = ((), (), s32[]{:S(2)}) async-start(), calls=%async_computation.6 | async-start | bytes 9437184 | tf_op jit(solution)/shard_map/all_gather | solution.py:876
  10.7 272.9 %all-gather.9.cloned.1.call-start = ((), (), s32[]{:S(2)}) async-start(), calls=%async_computation.7 | async-start | bytes 18874368 | tf_op jit(solution)/shard_map/all_gather | solution.py:877
  11.5 335.2 %all-gather.11.cloned.1.call-start = ((), (), s32[]{:S(2)}) async-start(), calls=%async_computation.8 | async-start | bytes 9437184 | tf_op jit(solution)/shard_map/all_gather | solution.py:878
  12.2 465.9 %reduce-scatter.4.cloned.1.call-start = ((), (), s32[]{:S(2)}) async-start(), calls=%async_computation.3 | async-start | bytes 9437184 | tf_op jit(solution)/shard_map/reduce_scatter | solution.py:904
  12.2 49.0 %collective-permute-start.1 = (bf16[512,2048]{1,0:T(8,128)(2,1)}, bf16[512,2048]{1,0:T(8,128)(2,1)}, u32[]{:S(2)}, u32[]{:S(2)}) collective-permute-start(bf16[512,2048]{1,0:T(8,128)(2,1)} %bitcast.1.refs_0_), channel_id=1, source_target_pairs={{0,2},{1,3},{2,0},{3,1},{4,6},{5,7},{6,4},{7,5},{8,10},{9,11},{10,... | collective-permute-start | bytes 6291464 | tf_op jit(solution)/shard_map/ppermute | solution.py:157
  15.3 47.4 %collective-permute-start = (bf16[512,2048]{1,0:T(8,128)(2,1)}, bf16[512,2048]{1,0:T(8,128)(2,1)}, u32[]{:S(2)}, u32[]{:S(2)}) collective-permute-start(bf16[512,2048]{1,0:T(8,128)(2,1)} %bitcast.1.refs_0_), channel_id=1, source_target_pairs={{0,1},{1,0},{2,3},{3,2},{4,5},{5,4},{6,7},{7,6},{8,9},{9,8},{10,11... | collective-permute-start | bytes 6291464 | tf_op jit(solution)/shard_map/ppermute | solution.py:156
  89.4 46.2 %collective-permute-start.5 = (bf16[256,2048]{1,0:T(8,128)(2,1)S(1)}, bf16[256,2048]{1,0:T(8,128)(2,1)}, u32[]{:S(2)}, u32[]{:S(2)}) collective-permute-start(bf16[256,2048]{1,0:T(8,128)(2,1)S(1)} %shard_map.153.refs_2_.refs_0_), channel_id=1, source_target_pairs={{0,1},{1,0},{2,3},{3,2},{4,5},{5,4},{6,7},{7,6},{8,9},{9,8},{10,11... | collective-permute-start | bytes 3145736 | tf_op jit(solution)/shard_map/ppermute | solution.py:156
  90.8 44.8 %collective-permute-start.4 = (bf16[256,2048]{1,0:T(8,128)(2,1)S(1)}, bf16[256,2048]{1,0:T(8,128)(2,1)}, u32[]{:S(2)}, u32[]{:S(2)}) collective-permute-start(bf16[256,2048]{1,0:T(8,128)(2,1)S(1)} %shard_map.153.refs_2_.refs_0_), channel_id=1, source_target_pairs={{0,2},{1,3},{2,0},{3,1},{4,6},{5,7},{6,4},{7,5},{8,10},{9,11},{10,... | collective-permute-start | bytes 3145736 | tf_op jit(solution)/shard_map/ppermute | solution.py:157
  157.9 34.8 %collective-permute-start.11 = (bf16[256,1024]{1,0:T(8,128)(2,1)S(1)}, bf16[256,1024]{1,0:T(8,128)(2,1)S(1)}, u32[]{:S(2)}, u32[]{:S(2)}) collective-permute-start(bf16[256,1024]{1,0:T(8,128)(2,1)S(1)} %get-tuple-element.121.refs_6_), channel_id=1, source_target_pairs={{0,2},{1,3},{2,0},{3,1},{4,6},{5,7},{6,4},{7,5},{8,10},{9,11},{10,... | collective-permute-start | bytes 1572872 | tf_op jit(solution)/shard_map/ppermute | solution.py:167
  183.4 42.3 %collective-permute-start.17 = (bf16[256,2048]{1,0:T(8,128)(2,1)S(1)}, bf16[256,2048]{1,0:T(8,128)(2,1)S(1)}, u32[]{:S(2)}, u32[]{:S(2)}) collective-permute-start(bf16[256,2048]{1,0:T(8,128)(2,1)S(1)} %get-tuple-element.136.refs_5_.refs_0_), channel_id=1, source_target_pairs={{0,1},{1,0},{2,3},{3,2},{4,5},{5,4},{6,7},{7,6},{8,9},{9,8},{10,11... | collective-permute-start | bytes 3145736 | tf_op jit(solution)/shard_map/ppermute | solution.py:156
  192.1 34.4 %collective-permute-start.16 = (bf16[256,2048]{1,0:T(8,128)(2,1)S(1)}, bf16[256,2048]{1,0:T(8,128)(2,1)S(1)}, u32[]{:S(2)}, u32[]{:S(2)}) collective-permute-start(bf16[256,2048]{1,0:T(8,128)(2,1)S(1)} %get-tuple-element.136.refs_5_.refs_0_), channel_id=1, source_target_pairs={{0,2},{1,3},{2,0},{3,1},{4,6},{5,7},{6,4},{7,5},{8,10},{9,11},{10,... | collective-permute-start | bytes 3145736 | tf_op jit(solution)/shard_map/ppermute | solution.py:157
  204.4 43.8 %collective-permute-start.14 = (bf16[256,2048]{1,0:T(8,128)(2,1)S(1)}, bf16[256,2048]{1,0:T(8,128)(2,1)S(1)}, u32[]{:S(2)}, u32[]{:S(2)}) collective-permute-start(bf16[256,2048]{1,0:T(8,128)(2,1)S(1)} %get-tuple-element.137), channel_id=1, source_target_pairs={{0,1},{1,0},{2,3},{3,2},{4,5},{5,4},{6,7},{7,6},{8,9},{9,8},{10,11... | collective-permute-start | bytes 3145736 | tf_op jit(solution)/shard_map/ppermute | solution.py:212
  205.8 43.1 %collective-permute-start.15 = (bf16[256,2048]{1,0:T(8,128)(2,1)S(1)}, bf16[256,2048]{1,0:T(8,128)(2,1)S(1)}, u32[]{:S(2)}, u32[]{:S(2)}) collective-permute-start(bf16[256,2048]{1,0:T(8,128)(2,1)S(1)} %get-tuple-element.138.refs_2_), channel_id=1, source_target_pairs={{0,2},{1,3},{2,0},{3,1},{4,6},{5,7},{6,4},{7,5},{8,10},{9,11},{10,... | collective-permute-start | bytes 3145736 | tf_op jit(solution)/shard_map/ppermute | solution.py:213
  205.8 64.9 %collective-permute-start.23 = (bf16[256,2048]{1,0:T(8,128)(2,1)S(1)}, bf16[256,2048]{1,0:T(8,128)(2,1)S(1)}, u32[]{:S(2)}, u32[]{:S(2)}) collective-permute-start(bf16[256,2048]{1,0:T(8,128)(2,1)S(1)} %shard_map.154.refs_10_.refs_0_), channel_id=1, source_target_pairs={{0,1},{1,0},{2,3},{3,2},{4,5},{5,4},{6,7},{7,6},{8,9},{9,8},{10,11... | collective-permute-start | bytes 3145736 | tf_op jit(solution)/shard_map/ppermute | solution.py:156
  225.8 45.6 %collective-permute-start.22 = (bf16[256,2048]{1,0:T(8,128)(2,1)S(1)}, bf16[256,2048]{1,0:T(8,128)(2,1)S(1)}, u32[]{:S(2)}, u32[]{:S(2)}) collective-permute-start(bf16[256,2048]{1,0:T(8,128)(2,1)S(1)} %shard_map.154.refs_10_.refs_0_), channel_id=1, source_target_pairs={{0,2},{1,3},{2,0},{3,1},{4,6},{5,7},{6,4},{7,5},{8,10},{9,11},{10,... | collective-permute-start | bytes 3145736 | tf_op jit(solution)/shard_map/ppermute | solution.py:157
  226.7 55.3 %collective-permute-start.20 = (bf16[256,1024]{1,0:T(8,128)(2,1)S(1)}, bf16[256,1024]{1,0:T(8,128)(2,1)S(1)}, u32[]{:S(2)}, u32[]{:S(2)}) collective-permute-start(bf16[256,1024]{1,0:T(8,128)(2,1)S(1)} %get-tuple-element.142), channel_id=1, source_target_pairs={{0,1},{1,0},{2,3},{3,2},{4,5},{5,4},{6,7},{7,6},{8,9},{9,8},{10,11... | collective-permute-start | bytes 1572872 | tf_op jit(solution)/shard_map/ppermute | solution.py:166
  248.3 34.5 %collective-permute-start.21 = (bf16[256,1024]{1,0:T(8,128)(2,1)S(1)}, bf16[256,1024]{1,0:T(8,128)(2,1)S(1)}, u32[]{:S(2)}, u32[]{:S(2)}) collective-permute-start(bf16[256,1024]{1,0:T(8,128)(2,1)S(1)} %get-tuple-element.139.refs_5_), channel_id=1, source_target_pairs={{0,2},{1,3},{2,0},{3,1},{4,6},{5,7},{6,4},{7,5},{8,10},{9,11},{10,... | collective-permute-start | bytes 1572872 | tf_op jit(solution)/shard_map/ppermute | solution.py:167
  251.1 58.6 %collective-permute-start.19 = (bf16[256,2048]{1,0:T(8,128)(2,1)}, bf16[256,2048]{1,0:T(8,128)(2,1)}, u32[]{:S(2)}, u32[]{:S(2)}) collective-permute-start(bf16[256,2048]{1,0:T(8,128)(2,1)} %get-tuple-element.141.refs_2_.refs_0_), channel_id=1, source_target_pairs={{0,2},{1,3},{2,0},{3,1},{4,6},{5,7},{6,4},{7,5},{8,10},{9,11},{10,... | collective-permute-start | bytes 3145736 | tf_op jit(solution)/shard_map/ppermute | solution.py:157
  270.7 39.0 %collective-permute-start.18 = (bf16[256,2048]{1,0:T(8,128)(2,1)}, bf16[256,2048]{1,0:T(8,128)(2,1)}, u32[]{:S(2)}, u32[]{:S(2)}) collective-permute-start(bf16[256,2048]{1,0:T(8,128)(2,1)} %get-tuple-element.141.refs_2_.refs_0_), channel_id=1, source_target_pairs={{0,1},{1,0},{2,3},{3,2},{4,5},{5,4},{6,7},{7,6},{8,9},{9,8},{10,11... | collective-permute-start | bytes 3145736 | tf_op jit(solution)/shard_map/ppermute | solution.py:156
  272.6 43.2 %collective-permute-start.26 = (bf16[256,1024]{1,0:T(8,128)(2,1)}, bf16[256,1024]{1,0:T(8,128)(2,1)}, u32[]{:S(2)}, u32[]{:S(2)}) collective-permute-start(bf16[256,1024]{1,0:T(8,128)(2,1)} %get-tuple-element.147), channel_id=1, source_target_pairs={{0,1},{1,0},{2,3},{3,2},{4,5},{5,4},{6,7},{7,6},{8,9},{9,8},{10,11... | collective-permute-start | bytes 1572872 | tf_op jit(solution)/shard_map/ppermute | solution.py:166
  386.0 299.9 %reduce-scatter.6.cloned.1.call-start = ((), (), s32[]{:S(2)}) async-start(), calls=%async_computation.4 | async-start | bytes 18874368 | tf_op jit(solution)/shard_map/reduce_scatter | solution.py:904
  428.0 46.1 %collective-permute-start.30 = (bf16[256,2048]{1,0:T(8,128)(2,1)S(1)}, bf16[256,2048]{1,0:T(8,128)(2,1)S(1)}, u32[]{:S(2)}, u32[]{:S(2)}) collective-permute-start(bf16[256,2048]{1,0:T(8,128)(2,1)S(1)} %get-tuple-element.162), channel_id=1, source_target_pairs={{0,1},{1,0},{2,3},{3,2},{4,5},{5,4},{6,7},{7,6},{8,9},{9,8},{10,11... | collective-permute-start | bytes 3145736 | tf_op jit(solution)/shard_map/ppermute | solution.py:212
  428.6 45.5 %collective-permute-start.31 = (bf16[256,2048]{1,0:T(8,128)(2,1)S(1)}, bf16[256,2048]{1,0:T(8,128)(2,1)S(1)}, u32[]{:S(2)}, u32[]{:S(2)}) collective-permute-start(bf16[256,2048]{1,0:T(8,128)(2,1)S(1)} %get-tuple-element.163.refs_6_), channel_id=1, source_target_pairs={{0,2},{1,3},{2,0},{3,1},{4,6},{5,7},{6,4},{7,5},{8,10},{9,11},{10,... | collective-permute-start | bytes 3145736 | tf_op jit(solution)/shard_map/ppermute | solution.py:213
  479.4 298.0 %reduce-scatter.8.cloned.1.call-start = ((), (), s32[]{:S(2)}) async-start(), calls=%async_computation.5 | async-start | bytes 9584640 | tf_op jit(solution)/shard_map/reduce_scatter | solution.py:904
  561.9 34.9 %collective-permute-start.46 = (bf16[256,1024]{1,0:T(8,128)(2,1)S(1)}, bf16[256,1024]{1,0:T(8,128)(2,1)S(1)}, u32[]{:S(2)}, u32[]{:S(2)}) collective-permute-start(bf16[256,1024]{1,0:T(8,128)(2,1)S(1)} %get-tuple-element.172.refs_6_), channel_id=1, source_target_pairs={{0,2},{1,3},{2,0},{3,1},{4,6},{5,7},{6,4},{7,5},{8,10},{9,11},{10,... | collective-permute-start | bytes 1572872 | tf_op jit(solution)/shard_map/ppermute | solution.py:204
  592.4 63.4 %collective-permute-start.40 = (bf16[256,1024]{1,0:T(8,128)(2,1)S(1)}, bf16[256,1024]{1,0:T(8,128)(2,1)S(1)}, u32[]{:S(2)}, u32[]{:S(2)}) collective-permute-start(bf16[256,1024]{1,0:T(8,128)(2,1)S(1)} %get-tuple-element.187.refs_2_), channel_id=1, source_target_pairs={{0,2},{1,3},{2,0},{3,1},{4,6},{5,7},{6,4},{7,5},{8,10},{9,11},{10,... | collective-permute-start | bytes 1572872 | tf_op jit(solution)/shard_map/ppermute | solution.py:204
  594.8 60.6 %collective-permute-start.41 = (bf16[256,1024]{1,0:T(8,128)(2,1)S(1)}, bf16[256,1024]{1,0:T(8,128)(2,1)S(1)}, u32[]{:S(2)}, u32[]{:S(2)}) collective-permute-start(bf16[256,1024]{1,0:T(8,128)(2,1)S(1)} %get-tuple-element.189), channel_id=1, source_target_pairs={{0,1},{1,0},{2,3},{3,2},{4,5},{5,4},{6,7},{7,6},{8,9},{9,8},{10,11... | collective-permute-start | bytes 1572872 | tf_op jit(solution)/shard_map/ppermute | solution.py:203
  597.2 60.7 %collective-permute-start.50 = (bf16[256,2048]{1,0:T(8,128)(2,1)S(1)}, bf16[256,2048]{1,0:T(8,128)(2,1)S(1)}, u32[]{:S(2)}, u32[]{:S(2)}) collective-permute-start(bf16[256,2048]{1,0:T(8,128)(2,1)S(1)} %get-tuple-element.205), channel_id=1, source_target_pairs={{0,1},{1,0},{2,3},{3,2},{4,5},{5,4},{6,7},{7,6},{8,9},{9,8},{10,11... | collective-permute-start | bytes 3145736 | tf_op jit(solution)/shard_map/ppermute | solution.py:212
  606.0 51.9 %collective-permute-start.51 = (bf16[256,2048]{1,0:T(8,128)(2,1)S(1)}, bf16[256,2048]{1,0:T(8,128)(2,1)S(1)}, u32[]{:S(2)}, u32[]{:S(2)}) collective-permute-start(bf16[256,2048]{1,0:T(8,128)(2,1)S(1)} %get-tuple-element.196.refs_6_), channel_id=1, source_target_pairs={{0,2},{1,3},{2,0},{3,1},{4,6},{5,7},{6,4},{7,5},{8,10},{9,11},{10,... | collective-permute-start | bytes 3145736 | tf_op jit(solution)/shard_map/ppermute | solution.py:213
  688.9 35.4 %collective-permute-start.56 = (bf16[256,1024]{1,0:T(8,128)(2,1)}, bf16[256,1024]{1,0:T(8,128)(2,1)S(1)}, u32[]{:S(2)}, u32[]{:S(2)}) collective-permute-start(bf16[256,1024]{1,0:T(8,128)(2,1)} %copy-done.58), channel_id=1, source_target_pairs={{0,2},{1,3},{2,0},{3,1},{4,6},{5,7},{6,4},{7,5},{8,10},{9,11},{10,... | collective-permute-start | bytes 1572872 | tf_op jit(solution)/shard_map/ppermute | solution.py:204
  689.0 35.3 %collective-permute-start.57 = (bf16[256,1024]{1,0:T(8,128)(2,1)}, bf16[256,1024]{1,0:T(8,128)(2,1)S(1)}, u32[]{:S(2)}, u32[]{:S(2)}) collective-permute-start(bf16[256,1024]{1,0:T(8,128)(2,1)} %copy-done.57), channel_id=1, source_target_pairs={{0,1},{1,0},{2,3},{3,2},{4,5},{5,4},{6,7},{7,6},{8,9},{9,8},{10,11... | collective-permute-start | bytes 1572872 | tf_op jit(solution)/shard_map/ppermute | solution.py:203
  690.1 54.9 %collective-permute-start.61 = (bf16[256,2048]{1,0:T(8,128)(2,1)S(1)}, bf16[256,2048]{1,0:T(8,128)(2,1)S(1)}, u32[]{:S(2)}, u32[]{:S(2)}) collective-permute-start(bf16[256,2048]{1,0:T(8,128)(2,1)S(1)} %get-tuple-element.212.refs_2_), channel_id=1, source_target_pairs={{0,2},{1,3},{2,0},{3,1},{4,6},{5,7},{6,4},{7,5},{8,10},{9,11},{10,... | collective-permute-start | bytes 3145736 | tf_op jit(solution)/shard_map/ppermute | solution.py:213
  (102 other events, 1478.2 us)
Sparse Core Ops, SparseCore 0:
  10.8 84.7 all-gather.6
  97.2 149.6 all-gather.8
  248.5 80.2 all-gather.10
  386.1 89.4 reduce-scatter.3
  479.5 168.0 reduce-scatter.5
  686.1 91.2 reduce-scatter.7

commit v9 on v8

--- a/solution.py
+++ b/solution.py
@@ -842,6 +842,14 @@
     return lax.cummax(jnp.where(change, ids[None, :], 0), axis=1)
 
 
+def sum_all(value, axis, count):
+    bit = 1
+    while bit < count:
+        value = value + lax.ppermute(value, axis, swap_perm(count, bit))
+        bit *= 2
+    return value
+
+
 def tensor_sum(value, nt):
     if nt != 4:
         return lax.psum(value, "tensor")
@@ -994,35 +1002,36 @@
     out_sum[0].second()
     attention_back_start(1)
     attention_back(1)
-    input_back(1)
-    ds = gain1.shape[0]
-    gains = tensor_sum(jnp.concatenate([(sum1[0] + sum1[1]) / g1, sum2[0] + sum2[1]]), nt)
-    gains = jnp.swapaxes(gains.reshape(2, nd, ds), 0, 1).astype(BF)
-    gains = jnp.pad(gains, ((0, 0), (0, 14), (0, qkv_w.shape[2] - ds)))
-    out_sum[1].second()
     layer_out = layer_out_rows(mid[0], out_sum[0].terms, 0, groups, None)
     grad_qkvo = wgrad_rows(
         [a1, by_group(gmf)],
         [[g_qkv[g][c] for g in both] for c in range(3)] + [by_group(ctx)],
         [0, 0, 0, 1],
         nd,
-        gains,
     )
+    grad_qkvo = dp_sum(link(grad_qkvo, grad_gateup))
+    input_back(1)
+    ga1[0].second()
+    out_sum[1].second()
     ga1[1].second()
-    grad_qkvo = dp_sum(link(grad_qkvo, grad_gateup))
+    grad_input = finish(0, None)
     layer_out = layer_out_rows(mid[1], out_sum[1].terms, 1, groups, layer_out)
-    ga1[0].second()
-    grad_input = finish(1, None)
-    grad_input = finish(0, grad_input)
+    gains = jnp.concatenate([(sum1[0] + sum1[1]) / g1, sum2[0] + sum2[1]])
+    gains = link(gains, Order.last)
+    grad_input = finish(1, grad_input)
+    ds = gain1.shape[0]
+    gains = lax.psum(gains, "dp") if nd & (nd - 1) else sum_all(gains, "dp", nd)
+    gains = tensor_sum(gains, nt)
+    gains = lax.dynamic_slice_in_dim(gains, lax.axis_index("dp") * ds, ds, 1)
     return (
         layer_out.reshape(seqs, local, width),
         grad_input.reshape(seqs, local, width),
         grad_qkvo[: 3 * ds].astype(F32).reshape(3, ds, -1),
         grad_qkvo[3 * ds : 4 * ds].T.astype(F32),
-        grad_qkvo[4 * ds, :ds].astype(F32),
+        gains[0],
         grad_gateup.astype(F32).reshape(2, ds, -1),
         grad_down.astype(F32),
-        grad_qkvo[4 * ds + 1, :ds].astype(F32),
+        gains[1],
     )
 
 

time: 796 us -> 808 us (1.015)
  waiting for transfers between devices: 214 us -> 224 us
  local copies, waits for them, and re-layouts: 25.2 us -> 17.1 us
    ppermute x8, waiting for transfers between devices: 7.42 us -> 53.8 us  [__init__(): self.for_y = lax.ppermute(diag_x, 'tensor', swap_perm(4, 1))]
    ppermute x8, waiting for transfers between devices: 60 us -> 20.2 us  [second(): lax.ppermute(to_x, 'tensor', swap_perm(4, 1))]
    reduce_scatter x3, waiting for transfers between devices: 17.6 us -> 0.01 us  [dp_sum(): return lax.psum_scatter(grad, 'dp', scatter_dimension=0, tiled=False)]
    ppermute x7, waiting for transfers between devices: 28.2 us -> 44.1 us  [second(): diag_x = lax.ppermute(left, 'tensor', swap_perm(4, 1))]
    unnamed x137 -> x139, local copies, waits for them, and re-layouts: 21.7 us -> 13.1 us
    pallas_call x54 -> x55, Pallas kernels: 441 us -> 448 us  [run(): pl.pallas_call(ordered_body, grid_spec=pltpu.PrefetchScalarGridSpec(num_s...]
  transfers between devices with their start and end apart: 68 -> 71, of which waited for: 29 -> 28; matrix products, arithmetic and copies ran while one was open for 2% -> 2% of each run, Pallas kernels for 51% -> 51%
where the time goes in v9:
time: 808 us; the launch traced here: 802 us
  Pallas kernels  448 us (55%)
  waiting for transfers between devices  224 us (28%)
  starting transfers between devices  69.5 us (9%)
  local copies, waits for them, and re-layouts  17.1 us (2%)
  between operations  15.7 us (2%)
  other arithmetic  15.2 us (2%)
  blocking collectives  12.1 us (1%)
    pallas_call x55, Pallas kernels, run(): pl.pallas_call(ordered_body, grid_spec=pltpu.PrefetchScalarGridSpec(num_s...  448 us
    ppermute x8, waiting for transfers between devices, __init__(): self.for_y = lax.ppermute(diag_x, 'tensor', swap_perm(4, 1))  53.8 us
    ppermute x7, waiting for transfers between devices, second(): diag_x = lax.ppermute(left, 'tensor', swap_perm(4, 1))  44.1 us
    ppermute x7, waiting for transfers between devices, __init__(): self.from_x = lax.ppermute(block, 'tensor', swap_perm(4, 1))  38.2 us
    ppermute x7, waiting for transfers between devices, __init__(): self.from_y = lax.ppermute(block, 'tensor', swap_perm(4, 2))  26.6 us
    ppermute x7, waiting for transfers between devices, second(): diag_y = lax.ppermute(right, 'tensor', swap_perm(4, 2))  22.3 us
    ppermute x8, waiting for transfers between devices, second(): lax.ppermute(to_x, 'tensor', swap_perm(4, 1))  20.2 us
  transfers between devices with their start and end apart: 71, of which 28 were waited for; matrix products, arithmetic and copies ran while one was open for 2% of the time, Pallas kernels for 51%

profile of v9, /device:TPU:0, one launch (start us, length us, event | category | flops | bytes accessed | tf_op | source)
XLA Modules:
  0.0 802.1 jit_solution(9718661066826148590)
XLA Ops:
  18.4 12.1 %all_gather.21 = bf16[2,2048]{1,0:T(2,128)(2,1)S(1)} all-gather(bf16[2,256]{1,0:T(2,128)(2,1)S(1)} %pad_maximum_fusion.4), channel_id=1, replica_groups=mesh['dp'=8,'tensor'=4] {'dp'}, dimensions={1}, use_global_device_ids=true | all-gather | bytes 9216 | tf_op jit(solution)/shard_map/all_gather | solution.py:881
  35.3 25.9 %collective-permute-done.1.refs_0_.refs_2_ = bf16[512,2048]{1,0:T(8,128)(2,1)} collective-permute-done((bf16[512,2048]{1,0:T(8,128)(2,1)}, bf16[512,2048]{1,0:T(8,128)(2,1)}, u32[]{:S(2)}, u32[]{:S(2)}) %collective-permute-start.1) | collective-permute-done | bytes 2097184 | tf_op jit(solution)/shard_map/ppermute | solution.py:157
  68.7 20.6 %collective-permute-done.3.refs_1_.refs_4_ = bf16[512,1024]{1,0:T(8,128)(2,1)S(1)} collective-permute-done((bf16[512,1024]{1,0:T(8,128)(2,1)S(1)}, bf16[512,1024]{1,0:T(8,128)(2,1)S(1)}, u32[]{:S(2)}, u32[]{:S(2)}) %collective-permute-start.3) | collective-permute-done | bytes 1048608 | tf_op jit(solution)/shard_map/ppermute | solution.py:167
  100.6 12.4 %shard_map.156.refs_1_.refs_2_.refs_3_ = bf16[3,4,256,512]{3,2,1,0:T(8,128)(2,1)} custom-call(bf16[4,256,2048]{2,1,0:T(8,128)(2,1)} %shard_map.155.refs_0_.refs_6_, bf16[8,4,256,512]{3,2,1,0:T(8,128)(2,1)} %bitcast.48, f32[4,256,128]{2,1,0:T(8,128)S(1)} %copy-done.21, f32[4,256,128]{2,1,0:T(8,128)S(1)} %copy-done.18), custom_call_target="tpu_custom_call" | custom-call | flops 2147483648 | bytes 4543829 | tf_op jit(solution)/shard_map/pallas_call | solution.py:84
  113.0 15.5 %shard_map.157 = (bf16[4,256,512]{2,1,0:T(8,128)(2,1)S(1)}, f32[1,4,8,256]{3,2,1,0:T(8,128)S(1)}) custom-call(s32[4]{0:T(128)S(1)} %iota_xor_fusion.refs_0_, bf16[3,4,256,512]{3,2,1,0:T(8,128)(2,1)} %shard_map.156.refs_1_.refs_2_.refs_3_, bf16[3,4,256,512]{3,2,1,0:T(8,128)(2,1)} %shard_map.156.refs_1_.refs_2_.refs_3_, ...), custom_call_target="tpu_custom_call" | custom-call | flops 1431655808 | bytes 1398101 | tf_op jit(solution)/shard_map/pallas_call | solution.py:84
  142.2 12.0 %shard_map.161.refs_4_.refs_1_.refs_2_.refs_3_ = bf16[3,4,256,512]{3,2,1,0:T(8,128)(2,1)} custom-call(bf16[4,256,2048]{2,1,0:T(8,128)(2,1)} %shard_map.160.refs_0_.refs_1_.refs_6_, bf16[8,4,256,512]{3,2,1,0:T(8,128)(2,1)} %bitcast.50, f32[4,256,128]{2,1,0:T(8,128)S(1)} %copy-done.15, f32[4,256,128]{2,1,0:T(8,128)S(1)} %copy-done.12), custom_call_target="tpu_custom_call" | custom-call | flops 2147483648 | bytes 4543829 | tf_op jit(solution)/shard_map/pallas_call | solution.py:84
  160.7 15.5 %shard_map.163 = (bf16[4,256,512]{2,1,0:T(8,128)(2,1)S(1)}, f32[1,4,8,256]{3,2,1,0:T(8,128)S(1)}) custom-call(s32[4]{0:T(128)S(1)} %iota_xor_fusion.refs_0_, bf16[3,4,256,512]{3,2,1,0:T(8,128)(2,1)} %shard_map.161.refs_4_.refs_1_.refs_2_.refs_3_, bf16[3,4,256,512]{3,2,1,0:T(8,128)(2,1)} %shard_map.161.refs_4_.refs_1_.refs_2_.refs_3_, ...), custom_call_target="tpu_custom_call" | custom-call | flops 1431655808 | bytes 1398101 | tf_op jit(solution)/shard_map/pallas_call | solution.py:84
  184.9 7.3 collective-permute-done.10.refs_3_
  197.1 6.3 collective-permute-done.9.refs_3_
  207.5 18.4 %collective-permute-done.17.refs_1_ = bf16[256,2048]{1,0:T(8,128)(2,1)S(1)} collective-permute-done((bf16[256,2048]{1,0:T(8,128)(2,1)S(1)}, bf16[256,2048]{1,0:T(8,128)(2,1)S(1)}, u32[]{:S(2)}, u32[]{:S(2)}) %collective-permute-start.17) | collective-permute-done | bytes 1048608 | tf_op jit(solution)/shard_map/ppermute | solution.py:156
  228.2 20.2 %collective-permute-done.14.refs_3_ = bf16[256,2048]{1,0:T(8,128)(2,1)S(1)} collective-permute-done((bf16[256,2048]{1,0:T(8,128)(2,1)S(1)}, bf16[256,2048]{1,0:T(8,128)(2,1)S(1)}, u32[]{:S(2)}, u32[]{:S(2)}) %collective-permute-start.14) | collective-permute-done | bytes 1048608 | tf_op jit(solution)/shard_map/ppermute | solution.py:212
  252.5 18.3 %collective-permute-done.23.refs_1_ = bf16[256,2048]{1,0:T(8,128)(2,1)S(1)} collective-permute-done((bf16[256,2048]{1,0:T(8,128)(2,1)S(1)}, bf16[256,2048]{1,0:T(8,128)(2,1)S(1)}, u32[]{:S(2)}, u32[]{:S(2)}) %collective-permute-start.23) | collective-permute-done | bytes 1048608 | tf_op jit(solution)/shard_map/ppermute | solution.py:156
  274.0 8.1 %collective-permute-done.20.refs_3_ = bf16[256,1024]{1,0:T(8,128)(2,1)S(1)} collective-permute-done((bf16[256,1024]{1,0:T(8,128)(2,1)S(1)}, bf16[256,1024]{1,0:T(8,128)(2,1)S(1)}, u32[]{:S(2)}, u32[]{:S(2)}) %collective-permute-start.20) | collective-permute-done | bytes 524320 | tf_op jit(solution)/shard_map/ppermute | solution.py:166
  285.8 24.0 %shard_map.171 = (bf16[4,256,2048]{2,1,0:T(8,128)(2,1)}, bf16[4,256,2048]{2,1,0:T(8,128)(2,1)}, bf16[4,256,2048]{2,1,0:T(8,128)(2,1)}, bf16[4,256,2048]{2,1,0:T(8,128)(2,1)}) custom-call(bf16[256,2048]{1,0:T(8,128)(2,1)} %copy-done.41, bf16[256,2048]{1,0:T(8,128)(2,1)} %copy-done.42, bf16[256,2048]{1,0:T(8,128)(2,1)} %copy-done.43, ...), custom_call_target="tpu_custom_call" | custom-call | flops 5726623232 | bytes 12582912 | tf_op jit(solution)/shard_map/pallas_call | solution.py:84
  322.9 23.9 %shard_map.174 = (bf16[4,256,2048]{2,1,0:T(8,128)(2,1)}, bf16[4,256,2048]{2,1,0:T(8,128)(2,1)}, bf16[4,256,2048]{2,1,0:T(8,128)(2,1)}, bf16[4,256,2048]{2,1,0:T(8,128)(2,1)}) custom-call(bf16[256,2048]{1,0:T(8,128)(2,1)} %get-tuple-element.141.refs_2_.refs_0_, bf16[256,2048]{1,0:T(8,128)(2,1)} %collective-permute-done.18.refs_1_, ...), custom_call_target="tpu_custom_call" | custom-call | flops 5726623232 | bytes 12582912 | tf_op jit(solution)/shard_map/pallas_call | solution.py:84
  346.8 15.4 %shard_map.175 = (bf16[4,256,2048]{2,1,0:T(8,128)(2,1)}, bf16[4,256,2048]{2,1,0:T(8,128)(2,1)}) custom-call(bf16[4,256,2048]{2,1,0:T(8,128)(2,1)} %shard_map.166.refs_4_.refs_0_.refs_2_, bf16[8,2048,256]{2,1,0:T(8,128)(2,1)} %bitcast.66, bf16[4,256,2048]{2,1,0:T(8,128)(2,1)} %get-tuple-element.150.refs_2_, bf16[4,256,2048]{2,1,0:T(8,128)(2,1)} %get-tuple-element.151.refs_3_, ...), custom_call_target="tpu_custom_call" | custom-call | flops 2863311616 | bytes 9786709 | tf_op jit(solution)/shard_map/pallas_call | solution.py:84
  362.2 23.9 %shard_map.176.refs_4_ = bf16[8,2048,256]{2,1,0:T(8,128)(2,1)} custom-call(bf16[4,256,2048]{2,1,0:T(8,128)(2,1)} %get-tuple-element.144.refs_2_.refs_0_, bf16[4,256,2048]{2,1,0:T(8,128)(2,1)} %get-tuple-element.148.refs_4_.refs_1_.refs_0_, bf16[4,256,2048]{2,1,0:T(8,128)(2,1)} %shard_map.166.refs_4_.refs_0_.refs_2_, ...), custom_call_target="tpu_custom_call" | custom-call | flops 5726623232 | bytes 8388608 | tf_op jit(solution)/shard_map/pallas_call | solution.py:84
  386.2 23.8 %shard_map.177 = (bf16[256,2048]{1,0:T(8,128)(2,1)S(1)}, bf16[256,2048]{1,0:T(8,128)(2,1)S(1)}, bf16[256,2048]{1,0:T(8,128)(2,1)S(1)}, bf16[256,1024]{1,0:T(8,128)(2,1)S(1)}, bf16[256,1024]{1,0:T(8,128)(2,1)S(1)}) custom-call(bf16[4,256,2048]{2,1,0:T(8,128)(2,1)} %get-tuple-element.152.refs_0_.refs_2_, ...), custom_call_target="tpu_custom_call" | custom-call | flops 5726623232 | bytes 9786709 | tf_op jit(solution)/shard_map/pallas_call | solution.py:84
  412.1 15.6 %shard_map.178 = (bf16[4,256,2048]{2,1,0:T(8,128)(2,1)}, bf16[4,256,2048]{2,1,0:T(8,128)(2,1)}) custom-call(bf16[4,256,2048]{2,1,0:T(8,128)(2,1)} %shard_map.173.refs_6_.refs_3_.refs_0_, bf16[8,2048,256]{2,1,0:T(8,128)(2,1)} %bitcast.67, bf16[4,256,2048]{2,1,0:T(8,128)(2,1)} %get-tuple-element.159.refs_2_, bf16[4,256,2048]{2,1,0:T(8,128)(2,1)} %get-tuple-element.160.refs_3_, ...), custom_call_target="tpu_custom_call" | custom-call | flops 2863311616 | bytes 9786709 | tf_op jit(solution)/shard_map/pallas_call | solution.py:84
  430.2 44.1 %shard_map.180.refs_6_.refs_0_ = bf16[8,512,2048]{2,1,0:T(8,128)(2,1)} custom-call(bf16[4,256,2048]{2,1,0:T(8,128)(2,1)} %get-tuple-element.164.refs_0_, bf16[4,256,2048]{2,1,0:T(8,128)(2,1)} %get-tuple-element.165.refs_1_, bf16[4,256,2048]{2,1,0:T(8,128)(2,1)} %get-tuple-element.152.refs_0_.refs_2_, ...), custom_call_target="tpu_custom_call" | custom-call | flops 11453246464 | bytes 13981013 | tf_op jit(solution)/shard_map/pallas_call | solution.py:84
  482.0 24.3 %shard_map.183 = (bf16[256,2048]{1,0:T(8,128)(2,1)S(1)}, bf16[256,2048]{1,0:T(8,128)(2,1)S(1)}, bf16[256,2048]{1,0:T(8,128)(2,1)S(1)}, bf16[256,1024]{1,0:T(8,128)(2,1)S(1)}, bf16[256,1024]{1,0:T(8,128)(2,1)S(1)}) custom-call(bf16[4,256,2048]{2,1,0:T(8,128)(2,1)} %get-tuple-element.166.refs_3_.refs_0_, ...), custom_call_target="tpu_custom_call" | custom-call | flops 5726623232 | bytes 9786709 | tf_op jit(solution)/shard_map/pallas_call | solution.py:84
  510.6 12.7 %shard_map.185 = (bf16[256,2048]{1,0:T(8,128)(2,1)S(1)}, bf16[256,2048]{1,0:T(8,128)(2,1)S(1)}, bf16[256,2048]{1,0:T(8,128)(2,1)S(1)}, bf16[256,1024]{1,0:T(8,128)(2,1)S(1)}, bf16[256,1024]{1,0:T(8,128)(2,1)S(1)}) custom-call(bf16[4,256,2048]{2,1,0:T(8,128)(2,1)} %get-tuple-element.144.refs_2_.refs_0_, bf16[8,2048,256]{2,1,0:T(8,128)(2,1)} %bitcast.68, ...), custom_call_target="tpu_custom_call" | custom-call | flops 2863311616 | bytes 5592405 | tf_op jit(solution)/shard_map/pallas_call | solution.py:84
  531.3 22.8 %shard_map.188 = (bf16[4,256,512]{2,1,0:T(8,128)(2,1)S(1)}, bf16[4,256,512]{2,1,0:T(8,128)(2,1)S(1)}, bf16[4,256,512]{2,1,0:T(8,128)(2,1)S(1)}) custom-call(s32[4]{0:T(128)S(1)} %iota_xor_fusion.refs_0_, bf16[3,4,256,512]{3,2,1,0:T(8,128)(2,1)} %shard_map.156.refs_1_.refs_2_.refs_3_, bf16[3,4,256,512]{3,2,1,0:T(8,128)(2,1)} %shard_map.156.refs_1_.refs_2_.refs_3_, ...), custom_call_target="tpu_custom_call" | custom-call | flops 3579139328 | bytes 2446677 | tf_op jit(solution)/shard_map/pallas_call | solution.py:84
  563.9 12.0 %shard_map.190 = (bf16[256,2048]{1,0:T(8,128)(2,1)S(1)}, bf16[256,2048]{1,0:T(8,128)(2,1)S(1)}, bf16[256,2048]{1,0:T(8,128)(2,1)S(1)}, bf16[256,1024]{1,0:T(8,12...) custom-call(bf16[4,256,512]{2,1,0:T(8,128)(2,1)} %copy-done.29, bf16[4,256,512]{2,1,0:T(8,128)(2,1)} %copy-done.31, ...), custom_call_target="tpu_custom_call" | custom-call | flops 2147483648 | bytes 4543829 | tf_op jit(solution)/shard_map/pallas_call | solution.py:84
  575.9 14.5 %shard_map.191 = (bf16[256,2048]{1,0:T(8,128)(2,1)S(1)}, bf16[256,2048]{1,0:T(8,128)(2,1)S(1)}, bf16[256,2048]{1,0:T(8,128)(2,1)S(1)}, bf16[256,1024]{1,0:T(8,128)(2,1)}, bf16[256,1024]{1,0:T(8,128)(2,1)S(1)}) custom-call(bf16[4,256,2048]{2,1,0:T(8,128)(2,1)} %get-tuple-element.148.refs_4_.refs_1_.refs_0_, bf16[8,2048,256]{2,1,0:T(8,128)(2,1)} %bitcast.69, ...), custom_call_target="tpu_custom_call" | custom-call | flops 2863311616 | bytes 5592405 | tf_op jit(solution)/shard_map/pallas_call | solution.py:84
  599.0 24.5 %collective-permute-done.46.refs_3_ = bf16[256,1024]{1,0:T(8,128)(2,1)S(1)} collective-permute-done((bf16[256,1024]{1,0:T(8,128)(2,1)S(1)}, bf16[256,1024]{1,0:T(8,128)(2,1)S(1)}, u32[]{:S(2)}, u32[]{:S(2)}) %collective-permute-start.46) | collective-permute-done | bytes 524320 | tf_op jit(solution)/shard_map/ppermute | solution.py:166
  623.5 6.0 shard_map.194
  629.6 22.6 %shard_map.195 = (bf16[4,256,512]{2,1,0:T(8,128)(2,1)S(1)}, bf16[4,256,512]{2,1,0:T(8,128)(2,1)S(1)}, bf16[4,256,512]{2,1,0:T(8,128)(2,1)S(1)}) custom-call(s32[4]{0:T(128)S(1)} %iota_xor_fusion.refs_0_, bf16[3,4,256,512]{3,2,1,0:T(8,128)(2,1)} %shard_map.161.refs_4_.refs_1_.refs_2_.refs_3_, ...), custom_call_target="tpu_custom_call" | custom-call | flops 3579139328 | bytes 2446677 | tf_op jit(solution)/shard_map/pallas_call | solution.py:84
  656.8 21.8 %shard_map.197.refs_0_ = bf16[8,1024,512]{2,1,0:T(8,128)(2,1)} custom-call(bf16[4,256,2048]{2,1,0:T(8,128)(2,1)} %shard_map.155.refs_0_.refs_6_, bf16[4,256,2048]{2,1,0:T(8,128)(2,1)} %shard_map.160.refs_0_.refs_1_.refs_6_, bf16[4,256,2048]{2,1,0:T(8,128)(2,1)} %get-tuple-element.205.refs_2_, bf16[4,256,2048]{2,1,0:T(8,128)(2,1)} %get-tuple-element.206.refs_3_, ...), custom_call_target="tpu_custom_call" | custom-call | flops 5726623232 | bytes 8388608 | tf_op jit(solution)/shard_map/pallas_call | solution.py:84
  682.8 12.1 %shard_map.199 = (bf16[256,2048]{1,0:T(8,128)(2,1)S(1)}, bf16[256,2048]{1,0:T(8,128)(2,1)}, bf16[256,2048]{1,0:T(8,128)(2,1)S(1)}, bf16[256,1024]{1,0:T(8,128)(2...) custom-call(bf16[4,256,512]{2,1,0:T(8,128)(2,1)} %copy-done.33, bf16[4,256,512]{2,1,0:T(8,128)(2,1)} %copy-done.34, ...), custom_call_target="tpu_custom_call" | custom-call | flops 2147483648 | bytes 4543829 | tf_op jit(solution)/shard_map/pallas_call | solution.py:84
  707.5 7.1 collective-permute-done.56.refs_1_
  716.4 38.9 %collective-permute-done.57.refs_3_ = bf16[256,1024]{1,0:T(8,128)(2,1)S(1)} collective-permute-done((bf16[256,1024]{1,0:T(8,128)(2,1)S(1)}, bf16[256,1024]{1,0:T(8,128)(2,1)S(1)}, u32[]{:S(2)}, u32[]{:S(2)}) %collective-permute-start.57) | collective-permute-done | bytes 524320 | tf_op jit(solution)/shard_map/ppermute | solution.py:203
  (356 shorter events, 203.8 us)
Async XLA Ops:
  7.2 91.3 %all-gather.7.cloned.1.call-start = ((), (), s32[]{:S(2)}) async-start(), calls=%async_computation.6 | async-start | bytes 9437184 | tf_op jit(solution)/shard_map/all_gather | solution.py:884
  10.7 273.0 %all-gather.9.cloned.1.call-start = ((), (), s32[]{:S(2)}) async-start(), calls=%async_computation.7 | async-start | bytes 18874368 | tf_op jit(solution)/shard_map/all_gather | solution.py:885
  11.5 335.4 %all-gather.11.cloned.1.call-start = ((), (), s32[]{:S(2)}) async-start(), calls=%async_computation.8 | async-start | bytes 9437184 | tf_op jit(solution)/shard_map/all_gather | solution.py:886
  12.2 466.2 %reduce-scatter.4.cloned.1.call-start = ((), (), s32[]{:S(2)}) async-start(), calls=%async_computation.3 | async-start | bytes 9437184 | tf_op jit(solution)/shard_map/reduce_scatter | solution.py:912
  12.2 49.0 %collective-permute-start.1 = (bf16[512,2048]{1,0:T(8,128)(2,1)}, bf16[512,2048]{1,0:T(8,128)(2,1)}, u32[]{:S(2)}, u32[]{:S(2)}) collective-permute-start(bf16[512,2048]{1,0:T(8,128)(2,1)} %bitcast.1.refs_0_), channel_id=1, source_target_pairs={{0,2},{1,3},{2,0},{3,1},{4,6},{5,7},{6,4},{7,5},{8,10},{9,11},{10,... | collective-permute-start | bytes 6291464 | tf_op jit(solution)/shard_map/ppermute | solution.py:157
  15.3 47.4 %collective-permute-start = (bf16[512,2048]{1,0:T(8,128)(2,1)}, bf16[512,2048]{1,0:T(8,128)(2,1)}, u32[]{:S(2)}, u32[]{:S(2)}) collective-permute-start(bf16[512,2048]{1,0:T(8,128)(2,1)} %bitcast.1.refs_0_), channel_id=1, source_target_pairs={{0,1},{1,0},{2,3},{3,2},{4,5},{5,4},{6,7},{7,6},{8,9},{9,8},{10,11... | collective-permute-start | bytes 6291464 | tf_op jit(solution)/shard_map/ppermute | solution.py:156
  89.4 46.3 %collective-permute-start.5 = (bf16[256,2048]{1,0:T(8,128)(2,1)S(1)}, bf16[256,2048]{1,0:T(8,128)(2,1)}, u32[]{:S(2)}, u32[]{:S(2)}) collective-permute-start(bf16[256,2048]{1,0:T(8,128)(2,1)S(1)} %shard_map.153.refs_2_.refs_0_), channel_id=1, source_target_pairs={{0,1},{1,0},{2,3},{3,2},{4,5},{5,4},{6,7},{7,6},{8,9},{9,8},{10,11... | collective-permute-start | bytes 3145736 | tf_op jit(solution)/shard_map/ppermute | solution.py:156
  90.8 44.9 %collective-permute-start.4 = (bf16[256,2048]{1,0:T(8,128)(2,1)S(1)}, bf16[256,2048]{1,0:T(8,128)(2,1)}, u32[]{:S(2)}, u32[]{:S(2)}) collective-permute-start(bf16[256,2048]{1,0:T(8,128)(2,1)S(1)} %shard_map.153.refs_2_.refs_0_), channel_id=1, source_target_pairs={{0,2},{1,3},{2,0},{3,1},{4,6},{5,7},{6,4},{7,5},{8,10},{9,11},{10,... | collective-permute-start | bytes 3145736 | tf_op jit(solution)/shard_map/ppermute | solution.py:157
  158.1 34.8 %collective-permute-start.11 = (bf16[256,1024]{1,0:T(8,128)(2,1)S(1)}, bf16[256,1024]{1,0:T(8,128)(2,1)S(1)}, u32[]{:S(2)}, u32[]{:S(2)}) collective-permute-start(bf16[256,1024]{1,0:T(8,128)(2,1)S(1)} %get-tuple-element.121.refs_6_), channel_id=1, source_target_pairs={{0,2},{1,3},{2,0},{3,1},{4,6},{5,7},{6,4},{7,5},{8,10},{9,11},{10,... | collective-permute-start | bytes 1572872 | tf_op jit(solution)/shard_map/ppermute | solution.py:167
  183.5 42.3 %collective-permute-start.17 = (bf16[256,2048]{1,0:T(8,128)(2,1)S(1)}, bf16[256,2048]{1,0:T(8,128)(2,1)S(1)}, u32[]{:S(2)}, u32[]{:S(2)}) collective-permute-start(bf16[256,2048]{1,0:T(8,128)(2,1)S(1)} %get-tuple-element.136.refs_5_.refs_0_), channel_id=1, source_target_pairs={{0,1},{1,0},{2,3},{3,2},{4,5},{5,4},{6,7},{7,6},{8,9},{9,8},{10,11... | collective-permute-start | bytes 3145736 | tf_op jit(solution)/shard_map/ppermute | solution.py:156
  192.2 34.4 %collective-permute-start.16 = (bf16[256,2048]{1,0:T(8,128)(2,1)S(1)}, bf16[256,2048]{1,0:T(8,128)(2,1)S(1)}, u32[]{:S(2)}, u32[]{:S(2)}) collective-permute-start(bf16[256,2048]{1,0:T(8,128)(2,1)S(1)} %get-tuple-element.136.refs_5_.refs_0_), channel_id=1, source_target_pairs={{0,2},{1,3},{2,0},{3,1},{4,6},{5,7},{6,4},{7,5},{8,10},{9,11},{10,... | collective-permute-start | bytes 3145736 | tf_op jit(solution)/shard_map/ppermute | solution.py:157
  204.6 43.8 %collective-permute-start.14 = (bf16[256,2048]{1,0:T(8,128)(2,1)S(1)}, bf16[256,2048]{1,0:T(8,128)(2,1)S(1)}, u32[]{:S(2)}, u32[]{:S(2)}) collective-permute-start(bf16[256,2048]{1,0:T(8,128)(2,1)S(1)} %get-tuple-element.137), channel_id=1, source_target_pairs={{0,1},{1,0},{2,3},{3,2},{4,5},{5,4},{6,7},{7,6},{8,9},{9,8},{10,11... | collective-permute-start | bytes 3145736 | tf_op jit(solution)/shard_map/ppermute | solution.py:212
  205.9 43.1 %collective-permute-start.15 = (bf16[256,2048]{1,0:T(8,128)(2,1)S(1)}, bf16[256,2048]{1,0:T(8,128)(2,1)S(1)}, u32[]{:S(2)}, u32[]{:S(2)}) collective-permute-start(bf16[256,2048]{1,0:T(8,128)(2,1)S(1)} %get-tuple-element.138.refs_2_), channel_id=1, source_target_pairs={{0,2},{1,3},{2,0},{3,1},{4,6},{5,7},{6,4},{7,5},{8,10},{9,11},{10,... | collective-permute-start | bytes 3145736 | tf_op jit(solution)/shard_map/ppermute | solution.py:213
  206.0 64.9 %collective-permute-start.23 = (bf16[256,2048]{1,0:T(8,128)(2,1)S(1)}, bf16[256,2048]{1,0:T(8,128)(2,1)S(1)}, u32[]{:S(2)}, u32[]{:S(2)}) collective-permute-start(bf16[256,2048]{1,0:T(8,128)(2,1)S(1)} %shard_map.154.refs_10_.refs_0_), channel_id=1, source_target_pairs={{0,1},{1,0},{2,3},{3,2},{4,5},{5,4},{6,7},{7,6},{8,9},{9,8},{10,11... | collective-permute-start | bytes 3145736 | tf_op jit(solution)/shard_map/ppermute | solution.py:156
  225.9 45.6 %collective-permute-start.22 = (bf16[256,2048]{1,0:T(8,128)(2,1)S(1)}, bf16[256,2048]{1,0:T(8,128)(2,1)S(1)}, u32[]{:S(2)}, u32[]{:S(2)}) collective-permute-start(bf16[256,2048]{1,0:T(8,128)(2,1)S(1)} %shard_map.154.refs_10_.refs_0_), channel_id=1, source_target_pairs={{0,2},{1,3},{2,0},{3,1},{4,6},{5,7},{6,4},{7,5},{8,10},{9,11},{10,... | collective-permute-start | bytes 3145736 | tf_op jit(solution)/shard_map/ppermute | solution.py:157
  226.8 55.3 %collective-permute-start.20 = (bf16[256,1024]{1,0:T(8,128)(2,1)S(1)}, bf16[256,1024]{1,0:T(8,128)(2,1)S(1)}, u32[]{:S(2)}, u32[]{:S(2)}) collective-permute-start(bf16[256,1024]{1,0:T(8,128)(2,1)S(1)} %get-tuple-element.142), channel_id=1, source_target_pairs={{0,1},{1,0},{2,3},{3,2},{4,5},{5,4},{6,7},{7,6},{8,9},{9,8},{10,11... | collective-permute-start | bytes 1572872 | tf_op jit(solution)/shard_map/ppermute | solution.py:166
  248.4 34.5 %collective-permute-start.21 = (bf16[256,1024]{1,0:T(8,128)(2,1)S(1)}, bf16[256,1024]{1,0:T(8,128)(2,1)S(1)}, u32[]{:S(2)}, u32[]{:S(2)}) collective-permute-start(bf16[256,1024]{1,0:T(8,128)(2,1)S(1)} %get-tuple-element.139.refs_5_), channel_id=1, source_target_pairs={{0,2},{1,3},{2,0},{3,1},{4,6},{5,7},{6,4},{7,5},{8,10},{9,11},{10,... | collective-permute-start | bytes 1572872 | tf_op jit(solution)/shard_map/ppermute | solution.py:167
  251.2 58.6 %collective-permute-start.19 = (bf16[256,2048]{1,0:T(8,128)(2,1)}, bf16[256,2048]{1,0:T(8,128)(2,1)}, u32[]{:S(2)}, u32[]{:S(2)}) collective-permute-start(bf16[256,2048]{1,0:T(8,128)(2,1)} %get-tuple-element.141.refs_2_.refs_0_), channel_id=1, source_target_pairs={{0,2},{1,3},{2,0},{3,1},{4,6},{5,7},{6,4},{7,5},{8,10},{9,11},{10,... | collective-permute-start | bytes 3145736 | tf_op jit(solution)/shard_map/ppermute | solution.py:157
  270.8 39.0 %collective-permute-start.18 = (bf16[256,2048]{1,0:T(8,128)(2,1)}, bf16[256,2048]{1,0:T(8,128)(2,1)}, u32[]{:S(2)}, u32[]{:S(2)}) collective-permute-start(bf16[256,2048]{1,0:T(8,128)(2,1)} %get-tuple-element.141.refs_2_.refs_0_), channel_id=1, source_target_pairs={{0,1},{1,0},{2,3},{3,2},{4,5},{5,4},{6,7},{7,6},{8,9},{9,8},{10,11... | collective-permute-start | bytes 3145736 | tf_op jit(solution)/shard_map/ppermute | solution.py:156
  272.7 43.2 %collective-permute-start.26 = (bf16[256,1024]{1,0:T(8,128)(2,1)}, bf16[256,1024]{1,0:T(8,128)(2,1)}, u32[]{:S(2)}, u32[]{:S(2)}) collective-permute-start(bf16[256,1024]{1,0:T(8,128)(2,1)} %get-tuple-element.147), channel_id=1, source_target_pairs={{0,1},{1,0},{2,3},{3,2},{4,5},{5,4},{6,7},{7,6},{8,9},{9,8},{10,11... | collective-permute-start | bytes 1572872 | tf_op jit(solution)/shard_map/ppermute | solution.py:166
  282.9 33.7 %collective-permute-start.27 = (bf16[256,1024]{1,0:T(8,128)(2,1)}, bf16[256,1024]{1,0:T(8,128)(2,1)}, u32[]{:S(2)}, u32[]{:S(2)}) collective-permute-start(bf16[256,1024]{1,0:T(8,128)(2,1)} %get-tuple-element.143.refs_6_), channel_id=1, source_target_pairs={{0,2},{1,3},{2,0},{3,1},{4,6},{5,7},{6,4},{7,5},{8,10},{9,11},{10,... | collective-permute-start | bytes 1572872 | tf_op jit(solution)/shard_map/ppermute | solution.py:167
  386.2 292.4 %reduce-scatter.6.cloned.1.call-start = ((), (), s32[]{:S(2)}) async-start(), calls=%async_computation.4 | async-start | bytes 18874368 | tf_op jit(solution)/shard_map/reduce_scatter | solution.py:912
  428.3 46.1 %collective-permute-start.30 = (bf16[256,2048]{1,0:T(8,128)(2,1)S(1)}, bf16[256,2048]{1,0:T(8,128)(2,1)S(1)}, u32[]{:S(2)}, u32[]{:S(2)}) collective-permute-start(bf16[256,2048]{1,0:T(8,128)(2,1)S(1)} %get-tuple-element.162), channel_id=1, source_target_pairs={{0,1},{1,0},{2,3},{3,2},{4,5},{5,4},{6,7},{7,6},{8,9},{9,8},{10,11... | collective-permute-start | bytes 3145736 | tf_op jit(solution)/shard_map/ppermute | solution.py:212
  428.8 45.5 %collective-permute-start.31 = (bf16[256,2048]{1,0:T(8,128)(2,1)S(1)}, bf16[256,2048]{1,0:T(8,128)(2,1)S(1)}, u32[]{:S(2)}, u32[]{:S(2)}) collective-permute-start(bf16[256,2048]{1,0:T(8,128)(2,1)S(1)} %get-tuple-element.163.refs_6_), channel_id=1, source_target_pairs={{0,2},{1,3},{2,0},{3,1},{4,6},{5,7},{6,4},{7,5},{8,10},{9,11},{10,... | collective-permute-start | bytes 3145736 | tf_op jit(solution)/shard_map/ppermute | solution.py:213
  479.6 310.5 %reduce-scatter.8.cloned.1.call-start = ((), (), s32[]{:S(2)}) async-start(), calls=%async_computation.5 | async-start | bytes 9437184 | tf_op jit(solution)/shard_map/reduce_scatter | solution.py:912
  594.8 57.4 %collective-permute-start.50 = (bf16[256,2048]{1,0:T(8,128)(2,1)S(1)}, bf16[256,2048]{1,0:T(8,128)(2,1)S(1)}, u32[]{:S(2)}, u32[]{:S(2)}) collective-permute-start(bf16[256,2048]{1,0:T(8,128)(2,1)S(1)} %get-tuple-element.208), channel_id=1, source_target_pairs={{0,1},{1,0},{2,3},{3,2},{4,5},{5,4},{6,7},{7,6},{8,9},{9,8},{10,11... | collective-permute-start | bytes 3145736 | tf_op jit(solution)/shard_map/ppermute | solution.py:212
  596.6 55.6 %collective-permute-start.51 = (bf16[256,2048]{1,0:T(8,128)(2,1)S(1)}, bf16[256,2048]{1,0:T(8,128)(2,1)S(1)}, u32[]{:S(2)}, u32[]{:S(2)}) collective-permute-start(bf16[256,2048]{1,0:T(8,128)(2,1)S(1)} %get-tuple-element.200.refs_6_), channel_id=1, source_target_pairs={{0,2},{1,3},{2,0},{3,1},{4,6},{5,7},{6,4},{7,5},{8,10},{9,11},{10,... | collective-permute-start | bytes 3145736 | tf_op jit(solution)/shard_map/ppermute | solution.py:213
  696.1 62.7 %collective-permute-start.54 = (bf16[256,2048]{1,0:T(8,128)(2,1)S(1)}, bf16[256,2048]{1,0:T(8,128)(2,1)S(1)}, u32[]{:S(2)}, u32[]{:S(2)}) collective-permute-start(bf16[256,2048]{1,0:T(8,128)(2,1)S(1)} %get-tuple-element.215), channel_id=1, source_target_pairs={{0,1},{1,0},{2,3},{3,2},{4,5},{5,4},{6,7},{7,6},{8,9},{9,8},{10,11... | collective-permute-start | bytes 3145736 | tf_op jit(solution)/shard_map/ppermute | solution.py:212
  697.4 61.9 %collective-permute-start.55 = (bf16[256,2048]{1,0:T(8,128)(2,1)S(1)}, bf16[256,2048]{1,0:T(8,128)(2,1)S(1)}, u32[]{:S(2)}, u32[]{:S(2)}) collective-permute-start(bf16[256,2048]{1,0:T(8,128)(2,1)S(1)} %get-tuple-element.210.refs_4_), channel_id=1, source_target_pairs={{0,2},{1,3},{2,0},{3,1},{4,6},{5,7},{6,4},{7,5},{8,10},{9,11},{10,... | collective-permute-start | bytes 3145736 | tf_op jit(solution)/shard_map/ppermute | solution.py:213
  705.0 58.0 %collective-permute-start.52 = (bf16[256,2048]{1,0:T(8,128)(2,1)S(1)}, bf16[256,2048]{1,0:T(8,128)(2,1)S(1)}, u32[]{:S(2)}, u32[]{:S(2)}) collective-permute-start(bf16[256,2048]{1,0:T(8,128)(2,1)S(1)} %get-tuple-element.211), channel_id=1, source_target_pairs={{0,1},{1,0},{2,3},{3,2},{4,5},{5,4},{6,7},{7,6},{8,9},{9,8},{10,11... | collective-permute-start | bytes 3145736 | tf_op jit(solution)/shard_map/ppermute | solution.py:212
  706.7 56.4 %collective-permute-start.53 = (bf16[256,2048]{1,0:T(8,128)(2,1)S(1)}, bf16[256,2048]{1,0:T(8,128)(2,1)S(1)}, u32[]{:S(2)}, u32[]{:S(2)}) collective-permute-start(bf16[256,2048]{1,0:T(8,128)(2,1)S(1)} %get-tuple-element.212.refs_4_), channel_id=1, source_target_pairs={{0,2},{1,3},{2,0},{3,1},{4,6},{5,7},{6,4},{7,5},{8,10},{9,11},{10,... | collective-permute-start | bytes 3145736 | tf_op jit(solution)/shard_map/ppermute | solution.py:213
  714.6 40.7 %collective-permute-start.57 = (bf16[256,1024]{1,0:T(8,128)(2,1)S(1)}, bf16[256,1024]{1,0:T(8,128)(2,1)S(1)}, u32[]{:S(2)}, u32[]{:S(2)}) collective-permute-start(bf16[256,1024]{1,0:T(8,128)(2,1)S(1)} %get-tuple-element.219), channel_id=1, source_target_pairs={{0,1},{1,0},{2,3},{3,2},{4,5},{5,4},{6,7},{7,6},{8,9},{9,8},{10,11... | collective-permute-start | bytes 1572872 | tf_op jit(solution)/shard_map/ppermute | solution.py:203
  (106 other events, 1832.1 us)
Sparse Core Ops, SparseCore 0:
  10.8 84.7 all-gather.6
  97.2 149.6 all-gather.8
  248.5 80.2 all-gather.10
  386.3 89.4 reduce-scatter.3
  479.8 168.1 reduce-scatter.5
  678.7 89.2 reduce-scatter.7
